TPU v7x, 32 devices: a whole 2x2x4 slice. The times are simulated.
32 devices in a mesh: vocab: 16 (over z, x, core), tok: 2 (over y).
Axes of the slice: x: 2, y: 2, z: 4, core: 2. Of those that a mesh axis runs over, the one named last changes fastest.
Arguments:
- hidden: bfloat16 [256, 3584], P('tok'), may hold values from -320 to 320
- head: bfloat16 [3584, 24576], P('tok', 'vocab'), may hold values from -2 to 2
- teacher: bfloat16 [256, 24576], P('tok', 'vocab'), may hold values from 0 to 1, as said below
- block_ids: int32 [2, 16], P('tok'), may hold values from -1 to 47, as said below
- counts: int32 [2], P('tok'), may hold values from 8 to 16
Outputs:
- lse: float32 [256], P('tok')
- kl: float32 [256], P('tok')
- grad_hidden: float32 [256, 3584], P('tok', 'vocab')
- grad_head: bfloat16 [3584, 24576], P('tok', 'vocab')
Inputs may be any that keep to these rules, and one draw needn't show every extreme that they name: `block_ids`: row b lists counts[b] distinct teacher blocks (block k covers columns 512 * k to 512 * k + 511) in its first counts[b] entries; the rest of the row is -1. `teacher`: every entry is positive.
All inputs are finite; a program needn't handle non-finite values.
Results may differ from a plain program's by a relative error of at most 0.0055.
Values may be sent and summed in bfloat16 or wider, within the bound.
No kernel may reach another device: no remote copies, remote signals or barrier semaphores. Data moves between devices by JAX's collectives and lax.ppermute only.
A program may use at most 64 MiB of HBM per device.

v0:
```python
import jax
import jax.numpy as jnp
from jax import lax
from jax.sharding import PartitionSpec as P

BLK = 512


loss_scale = 1024.0


def local_stats(logits, teacher, listed):
    teacher_f = teacher.astype(jnp.float32)
    kept = jnp.where(listed, teacher_f, 0.0)
    local_top = jnp.max(logits, axis=1)
    local_sum = jnp.sum(jnp.exp(logits - local_top[:, None]), axis=1)
    local_mass = jnp.sum(kept, axis=1)
    local_part = jnp.sum(jnp.where(listed, teacher_f * (jnp.log(teacher_f) - logits), 0.0), axis=1)
    return (kept, (local_top, local_sum, local_mass, local_part))


def finish_stats(logits, kept, global_top, total_sum, total_mass, total_part):
    lse = global_top + jnp.log(total_sum)
    kl = total_part / total_mass - jnp.log(total_mass) + lse
    student = jnp.exp(logits - lse[:, None])
    delta = (loss_scale * (student - kept / total_mass[:, None])).astype(jnp.bfloat16)
    return (lse, kl, delta)


def listed_columns(block_ids, counts, column_block, token_count):
    live_slot = jnp.arange(block_ids.shape[1], dtype=jnp.int32)[None, :] < counts[:, None]
    block_hit = jnp.any(
        (block_ids[:, :, None] == column_block[None, None, :]) & live_slot[:, :, None], axis=1
    )
    token_blocks = block_hit.shape[0]
    width = column_block.shape[0]
    return jnp.broadcast_to(
        block_hit[:, None, :], (token_blocks, token_count // token_blocks, width)
    ).reshape(token_count, width)


def per_device(hidden, head, teacher, block_ids, counts):
    token_count = hidden.shape[0]
    column_count = head.shape[1]
    full_head = lax.all_gather(head, "tok", axis=0, tiled=True)
    logits = jnp.dot(hidden, full_head, preferred_element_type=jnp.float32)
    first_column = lax.axis_index("vocab") * column_count
    column_block = (first_column + jnp.arange(column_count, dtype=jnp.int32)) // BLK
    listed = listed_columns(block_ids, counts, column_block, token_count)
    kept, stats_here = local_stats(logits, teacher, listed)
    local_top, local_sum, local_mass, local_part = stats_here
    global_top = lax.pmax(local_top, "vocab")
    scaled_sum = local_sum * jnp.exp(local_top - global_top)
    total_sum, total_mass, total_part = lax.psum((scaled_sum, local_mass, local_part), "vocab")
    lse, kl, delta = finish_stats(logits, kept, global_top, total_sum, total_mass, total_part)
    grad_hidden = lax.psum_scatter(
        lax.dot_general(
            full_head, delta, (((1,), (1,)), ((), ())), preferred_element_type=jnp.float32
        ),
        "vocab",
        scatter_dimension=0,
        tiled=True,
    ).T
    slices = lax.all_to_all(hidden, "tok", split_axis=1, concat_axis=0, tiled=True)
    grad_head = lax.dot_general(
        slices,
        lax.all_gather(delta, "tok", axis=0, tiled=True),
        (((0,), (0,)), ((), ())),
        preferred_element_type=jnp.float32,
    ).astype(jnp.bfloat16)
    return (lse, kl, grad_hidden, grad_head)


def solution(mesh):
    placed = (P("tok", None), P("tok", "vocab"), P("tok", "vocab"), P("tok", None), P("tok"))
    return jax.shard_map(
        per_device,
        mesh=mesh,
        in_specs=placed,
        out_specs=(P("tok"), P("tok"), P("tok", "vocab"), P("tok", "vocab")),
        check_vma=False,
    )
```

profile of v0, /device:TPU:0, one launch (start us, length us, event | category | flops | bytes accessed | tf_op | source)
XLA Modules:
  0.0 291.0 jit_solution(8800380667704613106)
XLA Ops:
  7.2 0.0 copy-start.1
  7.2 0.0 all-gather.2.cloned.1.call-start
  7.2 0.7 all-gather.2.cloned.1.call-update
  7.9 0.0 reduce-scatter.4.cloned.1.call-start
  8.6 0.8 and_reduce_fusion
  9.4 138.2 %all-gather.2.cloned.1.call-done = bf16[3584,1536]{1,0:T(8,128)(2,1)} async-done(((bf16[1792,1536]{1,0:T(8,128)(2,1)}), bf16[3584,1536]{1,0:T(8,128)(2,1)}) %all-gather.2.cloned.1.call-update) | async-done | bytes 11010064 | tf_op jit(solution)/shard_map/all_gather | solution.py:45
  147.6 6.1 %fusion.12 = (f32[128]{0:T(128)S(1)}, f32[128,1536]{1,0:T(8,128)S(1)}) fusion(bf16[128,3584]{1,0:T(8,128)(2,1)} %param.5, bf16[3584,1536]{1,0:T(8,128)(2,1)} %all-gather.2.cloned.1.call-done), kind=kOutput, calls=%fused_computation.29 | convolution fusion | flops 1409482624 | bytes 12714496 | tf_op jit(solution)/shard_map/dot_general | solution.py:46
  153.7 0.0 copy-start
  153.7 33.3 %pmax.7 = f32[128]{0:T(128)S(1)} all-reduce(f32[128]{0:T(128)S(1)} %get-tuple-element.32), channel_id=1, replica_groups=mesh['vocab'=16,'tok'=2] {'vocab'}, use_global_device_ids=true, to_apply=%region_1.2 | all-reduce | flops 128 | bytes 1024 | tf_op jit(solution)/shard_map/pmax | solution.py:52
  187.0 0.0 copy-done.1
  187.0 0.4 fusion.7
  187.4 29.5 %all-reduce = (f32[128]{0:T(128)S(1)}, f32[128]{0:T(128)S(1)}, f32[128]{0:T(128)S(1)}) all-reduce(f32[128]{0:T(128)S(1)} %exponential_multiply_fusion, f32[128]{0:T(128)S(1)} %get-tuple-element.26, f32[128]{0:T(128)S(1)} %get-tuple-element.24), channel_id=1, replica_groups=mesh['vocab'=16,'tok'=2] {'vocab'}, use_global_device_ids=true, to_apply=%region_3.4 | all-reduce | flops 384 | bytes 3072 | tf_op jit(solution)/shard_map/psum | solution.py:54
  216.9 0.5 subtract_add_fusion
  217.4 0.0 copy-start.2
  217.4 0.3 fusion.8
  217.7 7.7 %convolution_bitcast_fusion = f32[3584,128]{0,1:T(8,128)S(1)} fusion(bf16[128,1536]{1,0:T(8,128)(2,1)S(1)} %fusion.8, bf16[3584,1536]{1,0:T(8,128)(2,1)} %all-gather.2.cloned.1.call-done), kind=kOutput, calls=%fused_computation.2 | convolution fusion | flops 1409286144 | bytes 13238272 | tf_op jit(solution)/shard_map/dot_general | solution.py:57
  225.4 1.7 copy.25
  227.2 0.0 reduce-scatter.4.cloned.1.call-update
  227.2 0.0 copy-done
  227.2 0.6 copy.21
  227.8 0.0 copy-done.2
  227.8 14.9 %all_to_all.19 = bf16[128,2,1792]{0,2,1:T(8,128)(2,1)S(1)} all-to-all(bf16[128,2,1792]{0,2,1:T(8,128)(2,1)S(1)} %bitcast.21), channel_id=1, replica_groups=mesh['vocab'=16,'tok'=2] {'tok'}, dimensions={1} | all-to-all | bytes 1835008 | tf_op jit(solution)/shard_map/all_to_all | solution.py:64
  242.8 0.5 copy.22
  243.3 10.7 %all_gather.7 = bf16[256,1536]{1,0:T(8,128)(2,1)S(1)} all-gather(bf16[128,1536]{1,0:T(8,128)(2,1)S(1)} %fusion.8), channel_id=1, replica_groups=mesh['vocab'=16,'tok'=2] {'tok'}, dimensions={0}, use_global_device_ids=true | all-gather | bytes 1179648 | tf_op jit(solution)/shard_map/all_gather | solution.py:67
  254.0 4.0 %fusion = bf16[1792,1536]{0,1:T(8,128)(2,1)} fusion(bf16[256,1536]{1,0:T(8,128)(2,1)S(1)} %all_gather.7, bf16[256,1792]{1,0:T(8,128)(2,1)S(1)} %bitcast.19), kind=kOutput, calls=%fused_computation.1 | convolution fusion | flops 1412038656 | bytes 7208960 | tf_op jit(solution)/shard_map/dot_general | solution.py:65
  258.0 8.3 %copy.24 = bf16[1792,1536]{1,0:T(8,128)(2,1)} copy(bf16[1792,1536]{0,1:T(8,128)(2,1)} %fusion) | data formatting | bytes 11010048
  266.3 17.8 %reduce-scatter.4.cloned.1.call-done = f32[224,128]{1,0:T(8,128)} async-done(((f32[3584,128]{1,0:T(8,128)}), f32[224,128]{1,0:T(8,128)}) %reduce-scatter.4.cloned.1.call-update) | async-done | bytes 114704
  (3 shorter events, 0.0 us)
Async XLA Ops:
  7.2 179.8 %copy-start.1 = (bf16[128,1536]{1,0:T(8,128)(2,1)S(1)}, bf16[128,1536]{1,0:T(8,128)(2,1)}, u32[]{:S(2)}) copy-start(bf16[128,1536]{1,0:T(8,128)(2,1)} %param.7) | copy-start | bytes 1179652
  7.2 140.4 %all-gather.2.cloned.1.call-start = ((), (), s32[]{:S(2)}) async-start(), calls=%async_computation.2 | async-start | bytes 16515072 | tf_op jit(solution)/shard_map/all_gather | solution.py:45
  7.9 276.2 %reduce-scatter.4.cloned.1.call-start = ((), (), s32[]{:S(2)}) async-start(), calls=%async_computation.3 | async-start | bytes 1949696
  153.7 73.5 %copy-start = (bf16[128,3584]{1,0:T(8,128)(2,1)S(1)}, bf16[128,3584]{1,0:T(8,128)(2,1)}, u32[]{:S(2)}) copy-start(bf16[128,3584]{1,0:T(8,128)(2,1)} %param.5) | copy-start | bytes 2752516
  217.4 10.4 %copy-start.2 = (f32[128]{0:T(128)}, f32[128]{0:T(128)S(1)}, u32[]{:S(2)}) copy-start(f32[128]{0:T(128)S(1)} %get-tuple-element.31) | copy-start | bytes 1540
Sparse Core Ops, SparseCore 0:
  9.6 137.9 all-gather.1
  227.3 56.7 reduce-scatter.3
where the time goes:
time: 291 us
  waiting for transfers between devices  157 us (54%)
  blocking collectives  88.4 us (30%)
  matrix products  17.8 us (6%)
  between operations  14.8 us (5%)
  local copies, waits for them, and re-layouts  11.2 us (4%)
    all_gather x1, waiting for transfers between devices, per_device(): full_head = lax.all_gather(head, 'tok', axis=0, tiled=True)  138 us
    pmax x1, blocking collectives, per_device(): global_top = lax.pmax(local_top, 'vocab')  33.3 us
    psum x1, blocking collectives, per_device(): lax.psum((scaled_sum, local_mass, local_part), 'vocab')  29.5 us
    unnamed x3, waiting for transfers between devices  18.5 us
    all_to_all x1, blocking collectives, per_device(): lax.all_to_all(hidden, 'tok', split_axis=1, concat_axis=0, tiled=True)  14.9 us
    all_gather x1, blocking collectives, per_device(): lax.all_gather(delta, 'tok', axis=0, tiled=True)  10.7 us
    unnamed x9, local copies, waits for them, and re-layouts  10.7 us
    dot_general x1, matrix products, per_device(): lax.dot_general(full_head, delta, (((1,), (1,)), ((), ())), preferred_ele...  7.69 us
  transfers between devices with their start and end apart: 2, of which 2 were waited for; matrix products, arithmetic and copies ran while one was open for 5% of the time, Pallas kernels for 0%

commit v1 on v0

v1 whole, which is shorter than its diff:
```python
import jax
import jax.numpy as jnp
from jax import lax
from jax.sharding import PartitionSpec as P

BLK = 512


loss_scale = 1024.0


def shift_tok(x, offset, size):
    return lax.ppermute(x, "tok", [(i, (i + offset) % size) for i in range(size)])


def swap_vocab(x, bit, size):
    return lax.ppermute(x, "vocab", [(i, i ^ bit) for i in range(size)])


def listed_columns(block_ids, counts, column_block, token_count):
    live_slot = jnp.arange(block_ids.shape[1], dtype=jnp.int32)[None, :] < counts[:, None]
    block_hit = jnp.any(
        (block_ids[:, :, None] == column_block[None, None, :]) & live_slot[:, :, None], axis=1
    )
    token_blocks = block_hit.shape[0]
    width = column_block.shape[0]
    return jnp.broadcast_to(
        block_hit[:, None, :], (token_blocks, token_count // token_blocks, width)
    ).reshape(token_count, width)


def gather_vocab(stats, vocab_index, size):
    gathered = stats[None]
    bit = 1
    while bit < size:
        other = swap_vocab(gathered, bit, size)
        upper = (vocab_index & bit) != 0
        gathered = jnp.concatenate(
            [jnp.where(upper, other, gathered), jnp.where(upper, gathered, other)], axis=0
        )
        bit *= 2
    return gathered


def sum_vocab(partial, vocab_index, tok_index, vocab_size, tok_size, token_count):
    run = vocab_size // tok_size
    rows = partial.shape[0] // run
    held = partial.reshape(run, rows, partial.shape[1])
    bit = 1
    while bit < run:
        pairs = held.reshape(held.shape[0] // 2, 2, rows, held.shape[2])
        mine = (vocab_index // bit) % 2
        keep = lax.dynamic_index_in_dim(pairs, mine, 1, keepdims=False)
        send = lax.dynamic_index_in_dim(pairs, 1 - mine, 1, keepdims=False)
        other = swap_vocab(send.astype(jnp.bfloat16), bit, vocab_size)
        held = keep + other.astype(jnp.float32)
        bit *= 2
    held = held.reshape(rows, tok_size, token_count)
    blocks = [lax.dynamic_index_in_dim(held, tok_index, 1, keepdims=False)]
    for d in range(1, tok_size):
        send = lax.dynamic_index_in_dim(held, (tok_index + d) % tok_size, 1, keepdims=False)
        blocks.append(shift_tok(send, d, tok_size))
    blocks = jnp.stack(blocks)
    high = vocab_index // run
    total = lax.dynamic_index_in_dim(blocks, (tok_index - high) % tok_size, 0, keepdims=False)
    for d in range(1, tok_size):
        target = (high + d) % tok_size
        send = lax.dynamic_index_in_dim(blocks, (tok_index - target) % tok_size, 0, keepdims=False)
        total = total + lax.ppermute(
            send, "vocab", [(i, (i + d * run) % vocab_size) for i in range(vocab_size)]
        )
    return total


def per_device(hidden, head, teacher, block_ids, counts):
    tok_size = lax.axis_size("tok")
    vocab_size = lax.axis_size("vocab")
    tok_index = lax.axis_index("tok")
    vocab_index = lax.axis_index("vocab")
    token_count = hidden.shape[0]
    rows, column_count = head.shape

    def columns_of(index):
        return lax.dynamic_slice_in_dim(hidden, index * rows, rows, axis=1)

    features = [columns_of(tok_index)]
    for d in range(1, tok_size):
        features.append(shift_tok(columns_of((tok_index + d) % tok_size), d, tok_size))
    returned = []
    for d in range(1, tok_size):
        partial = jnp.dot(features[d], head, preferred_element_type=jnp.float32)
        returned.append(shift_tok(partial, -d, tok_size))
    logits = jnp.dot(features[0], head, preferred_element_type=jnp.float32)
    for partial in returned:
        logits = logits + partial

    first_column = vocab_index * column_count
    column_block = (first_column + jnp.arange(column_count, dtype=jnp.int32)) // BLK
    listed = listed_columns(block_ids, counts, column_block, token_count)
    teacher_f = teacher.astype(jnp.float32)
    kept = jnp.where(listed, teacher_f, 0.0)
    local_top = jnp.max(logits, axis=1)
    local_sum = jnp.sum(jnp.exp(logits - local_top[:, None]), axis=1)
    local_mass = jnp.sum(kept, axis=1)
    local_part = jnp.sum(jnp.where(listed, teacher_f * (jnp.log(teacher_f) - logits), 0.0), axis=1)

    stats = gather_vocab(
        jnp.stack([local_top, local_sum, local_mass, local_part]), vocab_index, vocab_size
    )
    tops = stats[:, 0]
    global_top = jnp.max(tops, axis=0)
    total_sum = jnp.sum(stats[:, 1] * jnp.exp(tops - global_top[None, :]), axis=0)
    total_mass = jnp.sum(stats[:, 2], axis=0)
    total_part = jnp.sum(stats[:, 3], axis=0)
    lse = global_top + jnp.log(total_sum)
    kl = total_part / total_mass - jnp.log(total_mass) + lse
    student = jnp.exp(logits - lse[:, None])
    delta = (loss_scale * (student - kept / total_mass[:, None])).astype(jnp.bfloat16)

    deltas = [delta] + [shift_tok(delta, d, tok_size) for d in range(1, tok_size)]
    all_delta = jnp.concatenate(deltas, axis=0)
    all_features = jnp.concatenate(features, axis=0)

    partial = lax.dot_general(
        head, all_delta, (((1,), (1,)), ((), ())), preferred_element_type=jnp.float32
    )
    partial = partial.reshape(rows, tok_size, token_count)
    partial = jnp.stack(
        [
            lax.dynamic_index_in_dim(partial, (tok_index - owner) % tok_size, 1, keepdims=False)
            for owner in range(tok_size)
        ],
        axis=1,
    ).reshape(rows, tok_size * token_count)
    grad_hidden = sum_vocab(
        partial, vocab_index, tok_index, vocab_size, tok_size, token_count
    ).T
    grad_head = lax.dot_general(
        all_features, all_delta, (((0,), (0,)), ((), ())), preferred_element_type=jnp.float32
    ).astype(jnp.bfloat16)
    return (lse, kl, grad_hidden, grad_head)


def solution(mesh):
    placed = (P("tok", None), P("tok", "vocab"), P("tok", "vocab"), P("tok", None), P("tok"))
    return jax.shard_map(
        per_device,
        mesh=mesh,
        in_specs=placed,
        out_specs=(P("tok"), P("tok"), P("tok", "vocab"), P("tok", "vocab")),
        check_vma=False,
    )
```

time: 291 us -> 104 us (0.36)
  waiting for transfers between devices: 157 us -> 52.3 us
  blocking collectives: 88.4 us -> 0 us
  starting transfers between devices: 0.08 us -> 19.1 us
  between operations: 14.8 us -> 1.62 us
  other arithmetic: 2.02 us -> 6.52 us
    all_gather x1 -> x0, waiting for transfers between devices: 138 us -> none  [per_device(): full_head = lax.all_gather(head, 'tok', axis=0, tiled=True)]
    ppermute x0 -> x12, waiting for transfers between devices: none -> 52.3 us  [the longest x4 33 us: shift_tok(): lax.ppermute(x, 'tok', [(i, (i + offset) % size) for i in range(size)])]
    pmax x1 -> x0, blocking collectives: 33.3 us -> none  [per_device(): global_top = lax.pmax(local_top, 'vocab')]
    psum x1 -> x0, blocking collectives: 29.5 us -> none  [per_device(): lax.psum((scaled_sum, local_mass, local_part), 'vocab')]
    ppermute x0 -> x12, starting transfers between devices: none -> 19.1 us  [the longest x7 8.7 us: swap_vocab(): return lax.ppermute(x, 'vocab', [(i, i ^ bit) for i in range(size)])]
    unnamed x3 -> x0, waiting for transfers between devices: 18.5 us -> none
    all_to_all x1 -> x0, blocking collectives: 14.9 us -> none  [per_device(): lax.all_to_all(hidden, 'tok', split_axis=1, concat_axis=0, tiled=True)]
    all_gather x1 -> x0, blocking collectives: 10.7 us -> none  [per_device(): lax.all_gather(delta, 'tok', axis=0, tiled=True)]
  transfers between devices with their start and end apart: 2 -> 12, of which waited for: 2 -> 12; matrix products, arithmetic and copies ran while one was open for 5% -> 7% of each run, Pallas kernels for 0% -> 0%
where the time goes in v1:
time: 104 us; the launch traced here: 103 us
  waiting for transfers between devices  52.3 us (50%)
  starting transfers between devices  19.1 us (18%)
  matrix products  15.4 us (15%)
  local copies, waits for them, and re-layouts  8.53 us (8%)
  other arithmetic  6.52 us (6%)
  between operations  1.62 us (2%)
    ppermute x4, waiting for transfers between devices, shift_tok(): lax.ppermute(x, 'tok', [(i, (i + offset) % size) for i in range(size)])  33 us
    ppermute x7, waiting for transfers between devices, swap_vocab(): return lax.ppermute(x, 'vocab', [(i, i ^ bit) for i in range(size)])  19 us
    ppermute x7, starting transfers between devices, swap_vocab(): return lax.ppermute(x, 'vocab', [(i, i ^ bit) for i in range(size)])  8.7 us
    ppermute x4, starting transfers between devices, shift_tok(): lax.ppermute(x, 'tok', [(i, (i + offset) % size) for i in range(size)])  7.82 us
    dot_general x1, matrix products, per_device(): lax.dot_general(head, all_delta, (((1,), (1,)), ((), ())), preferred_elem...  4.31 us
    dot_general x1, matrix products, per_device(): lax.dot_general(all_features, all_delta, (((0,), (0,)), ((), ())), prefer...  4.07 us
    dot_general x1, matrix products, per_device(): partial = jnp.dot(features[d], head, preferred_element_type=jnp.float32)  3.61 us
    dot_general x1, matrix products, per_device(): logits = jnp.dot(features[0], head, preferred_element_type=jnp.float32)  3.44 us
  transfers between devices with their start and end apart: 12, of which 12 were waited for; matrix products, arithmetic and copies ran while one was open for 7% of the time, Pallas kernels for 0%

profile of v1, /device:TPU:0, one launch (start us, length us, event | category | flops | bytes accessed | tf_op | source)
XLA Modules:
  0.0 103.5 jit_solution(17200616036641261231)
XLA Ops:
  0.7 1.2 %constant_dynamic-slice_fusion.4 = (bf16[128,1792]{1,0:T(8,128)(2,1)S(1)}, bf16[128,1792]{1,0:T(8,128)(2,1)S(1)}) fusion(bf16[128,3584]{1,0:T(8,128)(2,1)} %param.5, s32[]{:T(128)S(6)} %select_n.170, s32[]{:T(128)S(6)} %select_n.168), kind=kLoop, calls=%fused_computation.69 | loop fusion | bytes 1835016 | tf_op jit(solution)/shard_map/dynamic_slice | solution.py:84
  1.9 0.0 copy-start.8
  1.9 3.0 %collective-permute-start = (bf16[128,1792]{1,0:T(8,128)(2,1)S(1)}, bf16[128,1792]{1,0:T(8,128)(2,1)S(1)}, u32[]{:S(2)}, u32[]{:S(2)}) collective-permute-start(bf16[128,1792]{1,0:T(8,128)(2,1)S(1)} %get-tuple-element.15), channel_id=1, source_target_pairs={{0,1},{1,0},{2,3},{3,2},{4,5},{5,4},{6,7},{7,6},{8,9},{9,8},{10,11... | collective-permute-start | bytes 1376264 | tf_op jit(solution)/shard_map/ppermute | solution.py:13
  4.9 10.5 %collective-permute-done = bf16[128,1792]{1,0:T(8,128)(2,1)S(1)} collective-permute-done((bf16[128,1792]{1,0:T(8,128)(2,1)S(1)}, bf16[128,1792]{1,0:T(8,128)(2,1)S(1)}, u32[]{:S(2)}, u32[]{:S(2)}) %collective-permute-start) | collective-permute-done | bytes 458784 | tf_op jit(solution)/shard_map/ppermute | solution.py:13
  15.4 0.0 copy-start
  15.4 3.6 %fusion.32 = f32[128,1536]{1,0:T(8,128)S(1)} fusion(bf16[128,1792]{1,0:T(8,128)(2,1)S(1)} %collective-permute-done, bf16[1792,1536]{1,0:T(8,128)(2,1)} %param.6), kind=kOutput, calls=%fused_computation.85 | convolution fusion | flops 704643072 | bytes 6750208 | tf_op jit(solution)/shard_map/dot_general | solution.py:91
  19.1 0.0 copy-done
  19.1 1.8 %collective-permute-start.1 = (f32[128,1536]{1,0:T(8,128)S(1)}, f32[128,1536]{1,0:T(8,128)S(1)}, u32[]{:S(2)}, u32[]{:S(2)}) collective-permute-start(f32[128,1536]{1,0:T(8,128)S(1)} %fusion.32), channel_id=1, source_target_pairs={{0,1},{1,0},{2,3},{3,2},{4,5},{5,4},{6,7},{7,6},{8,9},{9,8},{10,11... | collective-permute-start | bytes 2359304 | tf_op jit(solution)/shard_map/ppermute | solution.py:13
  21.6 0.0 copy-done.8
  21.6 0.1 and_reduce_fusion
  21.7 3.4 %fusion.31 = f32[128,1536]{1,0:T(8,128)S(1)} fusion(bf16[128,1792]{1,0:T(8,128)(2,1)S(1)} %get-tuple-element.16, bf16[1792,1536]{1,0:T(8,128)(2,1)} %param.6), kind=kOutput, calls=%fused_computation.84 | convolution fusion | flops 704643072 | bytes 6750208 | tf_op jit(solution)/shard_map/dot_general | solution.py:93
  25.1 0.0 copy-start.4
  25.1 12.7 %collective-permute-done.1 = f32[128,1536]{1,0:T(8,128)S(1)} collective-permute-done((f32[128,1536]{1,0:T(8,128)S(1)}, f32[128,1536]{1,0:T(8,128)S(1)}, u32[]{:S(2)}, u32[]{:S(2)}) %collective-permute-start.1) | collective-permute-done | bytes 786464 | tf_op jit(solution)/shard_map/ppermute | solution.py:13
  37.9 0.2 fusion.30
  38.1 0.0 copy-done.4
  38.1 0.5 exponential_reduce_fusion
  38.6 0.1 collective-permute-start.2
  38.6 1.1 %collective-permute-done.2 = f32[1,4,128]{2,1,0:T(4,128)S(1)} collective-permute-done((f32[1,4,128]{2,1,0:T(4,128)S(1)}, f32[1,4,128]{2,1,0:T(4,128)S(1)}, u32[]{:S(2)}, u32[]{:S(2)}) %collective-permute-start.2) | collective-permute-done | bytes 2080 | tf_op jit(solution)/shard_map/ppermute | solution.py:17
  39.8 1.5 %collective-permute-start.3 = (f32[2,4,128]{2,1,0:T(4,128)S(1)}, f32[2,4,128]{2,1,0:T(4,128)S(1)}, u32[]{:S(2)}, u32[]{:S(2)}) collective-permute-start(f32[2,4,128]{2,1,0:T(4,128)S(1)} %pad_maximum_fusion.7), channel_id=1, source_target_pairs={{0,4},{2,6},{4,0},{6,2},{8,12},{10,14},{12,8},{14,10},{16,20},{18,... | collective-permute-start | bytes 12296 | tf_op jit(solution)/shard_map/ppermute | solution.py:17
  41.3 2.2 %collective-permute-done.3 = f32[2,4,128]{2,1,0:T(4,128)S(1)} collective-permute-done((f32[2,4,128]{2,1,0:T(4,128)S(1)}, f32[2,4,128]{2,1,0:T(4,128)S(1)}, u32[]{:S(2)}, u32[]{:S(2)}) %collective-permute-start.3) | collective-permute-done | bytes 4128 | tf_op jit(solution)/shard_map/ppermute | solution.py:17
  43.5 1.5 %collective-permute-start.4 = (f32[4,4,128]{2,1,0:T(4,128)S(1)}, f32[4,4,128]{2,1,0:T(4,128)S(1)}, u32[]{:S(2)}, u32[]{:S(2)}) collective-permute-start(f32[4,4,128]{2,1,0:T(4,128)S(1)} %pad_maximum_fusion.6), channel_id=1, source_target_pairs={{0,8},{2,10},{4,12},{6,14},{8,0},{10,2},{12,4},{14,6},{16,24},{18,... | collective-permute-start | bytes 24584 | tf_op jit(solution)/shard_map/ppermute | solution.py:17
  45.0 2.2 %collective-permute-done.4 = f32[4,4,128]{2,1,0:T(4,128)S(1)} collective-permute-done((f32[4,4,128]{2,1,0:T(4,128)S(1)}, f32[4,4,128]{2,1,0:T(4,128)S(1)}, u32[]{:S(2)}, u32[]{:S(2)}) %collective-permute-start.4) | collective-permute-done | bytes 8224 | tf_op jit(solution)/shard_map/ppermute | solution.py:17
  47.2 2.6 %collective-permute-start.5 = (f32[8,4,128]{2,1,0:T(4,128)S(1)}, f32[8,4,128]{2,1,0:T(4,128)S(1)}, u32[]{:S(2)}, u32[]{:S(2)}) collective-permute-start(f32[8,4,128]{2,1,0:T(4,128)S(1)} %pad_maximum_fusion.4), channel_id=1, source_target_pairs={{0,16},{2,18},{4,20},{6,22},{8,24},{10,26},{12,28},{14,30},{16,0},... | collective-permute-start | bytes 49160 | tf_op jit(solution)/shard_map/ppermute | solution.py:17
  49.8 2.1 %collective-permute-done.5 = f32[8,4,128]{2,1,0:T(4,128)S(1)} collective-permute-done((f32[8,4,128]{2,1,0:T(4,128)S(1)}, f32[8,4,128]{2,1,0:T(4,128)S(1)}, u32[]{:S(2)}, u32[]{:S(2)}) %collective-permute-start.5) | collective-permute-done | bytes 16416 | tf_op jit(solution)/shard_map/ppermute | solution.py:17
  52.0 0.5 subtract_add_fusion
  52.6 0.0 copy-start.7
  52.6 0.3 fusion.10
  52.9 0.0 copy-start.2
  52.9 1.5 %collective-permute-start.6 = (bf16[128,1536]{1,0:T(8,128)(2,1)S(1)}, bf16[128,1536]{1,0:T(8,128)(2,1)S(1)}, u32[]{:S(2)}, u32[]{:S(2)}) collective-permute-start(bf16[128,1536]{1,0:T(8,128)(2,1)S(1)} %fusion.10), channel_id=1, source_target_pairs={{0,1},{1,0},{2,3},{3,2},{4,5},{5,4},{6,7},{7,6},{8,9},{9,8},{10,11... | collective-permute-start | bytes 1179656 | tf_op jit(solution)/shard_map/ppermute | solution.py:13
  54.3 6.4 %collective-permute-done.6 = bf16[128,1536]{1,0:T(8,128)(2,1)S(1)} collective-permute-done((bf16[128,1536]{1,0:T(8,128)(2,1)S(1)}, bf16[128,1536]{1,0:T(8,128)(2,1)S(1)}, u32[]{:S(2)}, u32[]{:S(2)}) %collective-permute-start.6) | collective-permute-done | bytes 393248 | tf_op jit(solution)/shard_map/ppermute | solution.py:13
  60.7 0.0 copy-start.5
  60.7 4.3 %fusion.11 = f32[256,1792]{1,0:T(8,128)S(1)} fusion(bf16[1792,1536]{1,0:T(8,128)(2,1)} %param.6, bf16[128,1536]{1,0:T(8,128)(2,1)S(1)} %collective-permute-done.6, bf16[128,1536]{1,0:T(8,128)(2,1)S(1)} %fusion.10), kind=kOutput, calls=%fused_computation.20 | convolution fusion | flops 1410859008 | bytes 8126464 | tf_op jit(solution)/shard_map/dot_general | solution.py:124
  65.0 0.0 copy-done.7
  65.0 0.0 copy-done.2
  65.0 0.0 copy-done.5
  65.1 0.1 constant_dynamic-slice_fusion.3
  65.2 1.0 copy.17
  66.2 1.9 %copy.18 = f32[1792,1,128]{2,1,0:T(1,128)} copy(f32[1792,1,128]{0,2,1:T(8,128)S(1)} %get-tuple-element.14) | data formatting | bytes 1835008
  68.0 2.7 %pad_maximum_fusion = f32[1792,2,128]{2,1,0:T(2,128)S(1)} fusion(f32[1792,1,128]{2,1,0:T(1,128)} %copy.18, f32[1792,1,128]{2,1,0:T(1,128)S(1)} %copy.17), kind=kLoop, calls=%fused_computation.1 | loop fusion | flops 458752 | bytes 3670016 | tf_op jit(solution)/shard_map/stack | solution.py:128
  70.8 2.7 %reshape_reshape_reshape.3 = f32[4,2,224,256]{3,2,1,0:T(8,128)} reshape(f32[1792,2,128]{2,1,0:T(2,128)S(1)} %pad_maximum_fusion) | data formatting | bytes 3670016 | tf_op jit(solution)/shard_map/reshape;reshape;reshape | solution.py:51
  73.5 1.2 %fusion.12 = bf16[4,224,256]{2,1,0:T(8,128)(2,1)S(1)} fusion(f32[4,2,224,256]{3,2,1,0:T(8,128)} %reshape_reshape_reshape.3, s32[]{:T(128)S(6)} %select_n.188), kind=kLoop, calls=%fused_computation.21 | loop fusion | bytes 917508 | tf_op jit(solution)/shard_map/convert_element_type | solution.py:55
  74.7 0.1 collective-permute-start.7
  74.8 1.8 %collective-permute-done.7 = bf16[4,224,256]{2,1,0:T(8,128)(2,1)S(1)} collective-permute-done((bf16[4,224,256]{2,1,0:T(8,128)(2,1)S(1)}, bf16[4,224,256]{2,1,0:T(8,128)(2,1)S(1)}, u32[]{:S(2)}, u32[]{:S(2)}) %collective-permute-start.7) | collective-permute-done | bytes 458784 | tf_op jit(solution)/shard_map/ppermute | solution.py:17
  76.6 1.3 %bitcast_add_fusion = f32[4,224,256]{2,1,0:T(8,128)S(1)} fusion(bf16[4,224,256]{2,1,0:T(8,128)(2,1)S(1)} %collective-permute-done.7, f32[4,2,224,256]{3,2,1,0:T(8,128)} %reshape_reshape_reshape.3, s32[]{:T(128)S(6)} %select_n.187), kind=kLoop, calls=%fused_computation.10 | loop fusion | flops 458752 | bytes 2293764 | tf_op jit(solution)/shard_map/add | solution.py:56
  77.8 0.0 copy-start.1
  77.9 0.0 copy-start.3
  77.9 0.0 copy-start.6
  77.9 1.5 %collective-permute-start.8 = (bf16[2,224,256]{2,1,0:T(8,128)(2,1)S(1)}, bf16[2,224,256]{2,1,0:T(8,128)(2,1)S(1)}, u32[]{:S(2)}, u32[]{:S(2)}) collective-permute-start(bf16[2,224,256]{2,1,0:T(8,128)(2,1)S(1)} %fusion.13), channel_id=1, source_target_pairs={{0,4},{2,6},{4,0},{6,2},{8,12},{10,14},{12,8},{14,10},{16,20},{18,... | collective-permute-start | bytes 688136 | tf_op jit(solution)/shard_map/ppermute | solution.py:17
  79.4 6.2 %collective-permute-done.8 = bf16[2,224,256]{2,1,0:T(8,128)(2,1)S(1)} collective-permute-done((bf16[2,224,256]{2,1,0:T(8,128)(2,1)S(1)}, bf16[2,224,256]{2,1,0:T(8,128)(2,1)S(1)}, u32[]{:S(2)}, u32[]{:S(2)}) %collective-permute-start.8) | collective-permute-done | bytes 229408 | tf_op jit(solution)/shard_map/ppermute | solution.py:17
  85.7 1.5 %collective-permute-start.9 = (bf16[1,224,256]{2,1,0:T(8,128)(2,1)S(1)}, bf16[1,224,256]{2,1,0:T(8,128)(2,1)S(1)}, u32[]{:S(2)}, u32[]{:S(2)}) collective-permute-start(bf16[1,224,256]{2,1,0:T(8,128)(2,1)S(1)} %dynamic-slice_convert_fusion.2), channel_id=1, source_target_pairs={{0,8},{2,10},{4,12},{6,14},{8,0},{10,2},{12,4},{14,6},{16,24},{18,... | collective-permute-start | bytes 344072 | tf_op jit(solution)/shard_map/ppermute | solution.py:17
  87.3 3.3 %collective-permute-done.9 = bf16[1,224,256]{2,1,0:T(8,128)(2,1)S(1)} collective-permute-done((bf16[1,224,256]{2,1,0:T(8,128)(2,1)S(1)}, bf16[1,224,256]{2,1,0:T(8,128)(2,1)S(1)}, u32[]{:S(2)}, u32[]{:S(2)}) %collective-permute-start.9) | collective-permute-done | bytes 114720 | tf_op jit(solution)/shard_map/ppermute | solution.py:17
  90.6 0.1 reshape.154
  90.7 0.2 constant_dynamic-slice_fusion
  90.9 1.5 %collective-permute-start.10 = (f32[224,128]{1,0:T(8,128)S(1)}, f32[224,128]{1,0:T(8,128)S(1)}, u32[]{:S(2)}, u32[]{:S(2)}) collective-permute-start(f32[224,128]{1,0:T(8,128)S(1)} %bitcast.54), channel_id=1, source_target_pairs={{0,1},{1,0},{2,3},{3,2},{4,5},{5,4},{6,7},{7,6},{8,9},{9,8},{10,11... | collective-permute-start | bytes 344072 | tf_op jit(solution)/shard_map/ppermute | solution.py:13
  92.4 3.4 %collective-permute-done.10 = f32[224,128]{1,0:T(8,128)S(1)} collective-permute-done((f32[224,128]{1,0:T(8,128)S(1)}, f32[224,128]{1,0:T(8,128)S(1)}, u32[]{:S(2)}, u32[]{:S(2)}) %collective-permute-start.10) | collective-permute-done | bytes 114720 | tf_op jit(solution)/shard_map/ppermute | solution.py:13
  95.8 2.6 %collective-permute-start.11 = (f32[224,128]{1,0:T(8,128)S(1)}, f32[224,128]{1,0:T(8,128)S(1)}, u32[]{:S(2)}, u32[]{:S(2)}) collective-permute-start(f32[224,128]{1,0:T(8,128)S(1)} %fusion.15), channel_id=1, source_target_pairs={{0,16},{2,18},{4,20},{6,22},{8,24},{10,26},{12,28},{14,30},{16,0},... | collective-permute-start | bytes 344072 | tf_op jit(solution)/shard_map/ppermute | solution.py:69
  98.4 0.0 copy-done.1
  98.4 0.0 copy-done.3
  98.4 0.0 copy-done.6
  98.4 4.1 %convolution_convert_fusion = bf16[1792,1536]{1,0:T(8,128)(2,1)} fusion(bf16[128,1792]{1,0:T(8,128)(2,1)S(1)} %copy-done.1, bf16[128,1792]{1,0:T(8,128)(2,1)S(1)} %get-tuple-element.16, bf16[128,1536]{1,0:T(8,128)(2,1)S(1)} %copy-done.6, bf16[128,1536]{1,0:T(8,128)(2,1)S(1)} %copy-done.3), kind=kOutput, calls=%fused_computation | convolution fusion | flops 1415446528 | bytes 7208960 | tf_op jit(solution)/shard_map/dot_general | solution.py:138
  102.5 0.3 collective-permute-done.11
  102.8 0.7 fusion.19
  (18 shorter events, 0.3 us)
Async XLA Ops:
  1.9 19.7 %copy-start.8 = (s32[1,16]{1,0:T(1,128)S(1)}, s32[1,16]{1,0:T(1,128)}, u32[]{:S(2)}) copy-start(s32[1,16]{1,0:T(1,128)} %param.8) | copy-start | bytes 196
  1.9 13.6 %collective-permute-start = (bf16[128,1792]{1,0:T(8,128)(2,1)S(1)}, bf16[128,1792]{1,0:T(8,128)(2,1)S(1)}, u32[]{:S(2)}, u32[]{:S(2)}) collective-permute-start(bf16[128,1792]{1,0:T(8,128)(2,1)S(1)} %get-tuple-element.15), channel_id=1, source_target_pairs={{0,1},{1,0},{2,3},{3,2},{4,5},{5,4},{6,7},{7,6},{8,9},{9,8},{10,11... | collective-permute-start | bytes 1376264 | tf_op jit(solution)/shard_map/ppermute | solution.py:13
  15.4 3.6 %copy-start = (bf16[128,1792]{1,0:T(8,128)(2,1)}, bf16[128,1792]{1,0:T(8,128)(2,1)S(1)}, u32[]{:S(2)}) copy-start(bf16[128,1792]{1,0:T(8,128)(2,1)S(1)} %collective-permute-done) | copy-start | bytes 1376260
  19.1 18.8 %collective-permute-start.1 = (f32[128,1536]{1,0:T(8,128)S(1)}, f32[128,1536]{1,0:T(8,128)S(1)}, u32[]{:S(2)}, u32[]{:S(2)}) collective-permute-start(f32[128,1536]{1,0:T(8,128)S(1)} %fusion.32), channel_id=1, source_target_pairs={{0,1},{1,0},{2,3},{3,2},{4,5},{5,4},{6,7},{7,6},{8,9},{9,8},{10,11... | collective-permute-start | bytes 2359304 | tf_op jit(solution)/shard_map/ppermute | solution.py:13
  25.1 12.9 %copy-start.4 = (bf16[128,1536]{1,0:T(8,128)(2,1)S(1)}, bf16[128,1536]{1,0:T(8,128)(2,1)}, u32[]{:S(2)}) copy-start(bf16[128,1536]{1,0:T(8,128)(2,1)} %param.7) | copy-start | bytes 1179652
  38.6 1.2 %collective-permute-start.2 = (f32[1,4,128]{2,1,0:T(4,128)S(1)}, f32[1,4,128]{2,1,0:T(4,128)S(1)}, u32[]{:S(2)}, u32[]{:S(2)}) collective-permute-start(f32[1,4,128]{2,1,0:T(4,128)S(1)} %maximum_bitcast_fusion), channel_id=1, source_target_pairs={{0,2},{2,0},{4,6},{6,4},{8,10},{10,8},{12,14},{14,12},{16,18},{18,... | collective-permute-start | bytes 6152 | tf_op jit(solution)/shard_map/ppermute | solution.py:17
  39.8 3.7 %collective-permute-start.3 = (f32[2,4,128]{2,1,0:T(4,128)S(1)}, f32[2,4,128]{2,1,0:T(4,128)S(1)}, u32[]{:S(2)}, u32[]{:S(2)}) collective-permute-start(f32[2,4,128]{2,1,0:T(4,128)S(1)} %pad_maximum_fusion.7), channel_id=1, source_target_pairs={{0,4},{2,6},{4,0},{6,2},{8,12},{10,14},{12,8},{14,10},{16,20},{18,... | collective-permute-start | bytes 12296 | tf_op jit(solution)/shard_map/ppermute | solution.py:17
  43.5 3.7 %collective-permute-start.4 = (f32[4,4,128]{2,1,0:T(4,128)S(1)}, f32[4,4,128]{2,1,0:T(4,128)S(1)}, u32[]{:S(2)}, u32[]{:S(2)}) collective-permute-start(f32[4,4,128]{2,1,0:T(4,128)S(1)} %pad_maximum_fusion.6), channel_id=1, source_target_pairs={{0,8},{2,10},{4,12},{6,14},{8,0},{10,2},{12,4},{14,6},{16,24},{18,... | collective-permute-start | bytes 24584 | tf_op jit(solution)/shard_map/ppermute | solution.py:17
  47.2 4.7 %collective-permute-start.5 = (f32[8,4,128]{2,1,0:T(4,128)S(1)}, f32[8,4,128]{2,1,0:T(4,128)S(1)}, u32[]{:S(2)}, u32[]{:S(2)}) collective-permute-start(f32[8,4,128]{2,1,0:T(4,128)S(1)} %pad_maximum_fusion.4), channel_id=1, source_target_pairs={{0,16},{2,18},{4,20},{6,22},{8,24},{10,26},{12,28},{14,30},{16,0},... | collective-permute-start | bytes 49160 | tf_op jit(solution)/shard_map/ppermute | solution.py:17
  52.6 12.5 %copy-start.7 = (f32[128]{0:T(128)}, f32[128]{0:T(128)S(1)}, u32[]{:S(2)}) copy-start(f32[128]{0:T(128)S(1)} %get-tuple-element.10) | copy-start | bytes 1540
  52.9 12.2 %copy-start.2 = (bf16[128,1536]{1,0:T(8,128)(2,1)}, bf16[128,1536]{1,0:T(8,128)(2,1)S(1)}, u32[]{:S(2)}) copy-start(bf16[128,1536]{1,0:T(8,128)(2,1)S(1)} %fusion.10) | copy-start | bytes 1179652
  52.9 7.8 %collective-permute-start.6 = (bf16[128,1536]{1,0:T(8,128)(2,1)S(1)}, bf16[128,1536]{1,0:T(8,128)(2,1)S(1)}, u32[]{:S(2)}, u32[]{:S(2)}) collective-permute-start(bf16[128,1536]{1,0:T(8,128)(2,1)S(1)} %fusion.10), channel_id=1, source_target_pairs={{0,1},{1,0},{2,3},{3,2},{4,5},{5,4},{6,7},{7,6},{8,9},{9,8},{10,11... | collective-permute-start | bytes 1179656 | tf_op jit(solution)/shard_map/ppermute | solution.py:13
  60.7 4.3 %copy-start.5 = (bf16[128,1536]{1,0:T(8,128)(2,1)}, bf16[128,1536]{1,0:T(8,128)(2,1)S(1)}, u32[]{:S(2)}) copy-start(bf16[128,1536]{1,0:T(8,128)(2,1)S(1)} %collective-permute-done.6) | copy-start | bytes 1179652
  74.7 1.9 %collective-permute-start.7 = (bf16[4,224,256]{2,1,0:T(8,128)(2,1)S(1)}, bf16[4,224,256]{2,1,0:T(8,128)(2,1)S(1)}, u32[]{:S(2)}, u32[]{:S(2)}) collective-permute-start(bf16[4,224,256]{2,1,0:T(8,128)(2,1)S(1)} %fusion.12), channel_id=1, source_target_pairs={{0,2},{2,0},{4,6},{6,4},{8,10},{10,8},{12,14},{14,12},{16,18},{18,... | collective-permute-start | bytes 1376264 | tf_op jit(solution)/shard_map/ppermute | solution.py:17
  77.8 20.5 %copy-start.1 = (bf16[128,1792]{1,0:T(8,128)(2,1)S(1)}, bf16[128,1792]{1,0:T(8,128)(2,1)}, u32[]{:S(2)}) copy-start(bf16[128,1792]{1,0:T(8,128)(2,1)} %copy-done) | copy-start | bytes 1376260
  77.9 20.5 %copy-start.3 = (bf16[128,1536]{1,0:T(8,128)(2,1)S(1)}, bf16[128,1536]{1,0:T(8,128)(2,1)}, u32[]{:S(2)}) copy-start(bf16[128,1536]{1,0:T(8,128)(2,1)} %copy-done.2) | copy-start | bytes 1179652
  77.9 20.5 %copy-start.6 = (bf16[128,1536]{1,0:T(8,128)(2,1)S(1)}, bf16[128,1536]{1,0:T(8,128)(2,1)}, u32[]{:S(2)}) copy-start(bf16[128,1536]{1,0:T(8,128)(2,1)} %copy-done.5) | copy-start | bytes 1179652
  77.9 7.7 %collective-permute-start.8 = (bf16[2,224,256]{2,1,0:T(8,128)(2,1)S(1)}, bf16[2,224,256]{2,1,0:T(8,128)(2,1)S(1)}, u32[]{:S(2)}, u32[]{:S(2)}) collective-permute-start(bf16[2,224,256]{2,1,0:T(8,128)(2,1)S(1)} %fusion.13), channel_id=1, source_target_pairs={{0,4},{2,6},{4,0},{6,2},{8,12},{10,14},{12,8},{14,10},{16,20},{18,... | collective-permute-start | bytes 688136 | tf_op jit(solution)/shard_map/ppermute | solution.py:17
  85.7 4.9 %collective-permute-start.9 = (bf16[1,224,256]{2,1,0:T(8,128)(2,1)S(1)}, bf16[1,224,256]{2,1,0:T(8,128)(2,1)S(1)}, u32[]{:S(2)}, u32[]{:S(2)}) collective-permute-start(bf16[1,224,256]{2,1,0:T(8,128)(2,1)S(1)} %dynamic-slice_convert_fusion.2), channel_id=1, source_target_pairs={{0,8},{2,10},{4,12},{6,14},{8,0},{10,2},{12,4},{14,6},{16,24},{18,... | collective-permute-start | bytes 344072 | tf_op jit(solution)/shard_map/ppermute | solution.py:17
  90.9 4.9 %collective-permute-start.10 = (f32[224,128]{1,0:T(8,128)S(1)}, f32[224,128]{1,0:T(8,128)S(1)}, u32[]{:S(2)}, u32[]{:S(2)}) collective-permute-start(f32[224,128]{1,0:T(8,128)S(1)} %bitcast.54), channel_id=1, source_target_pairs={{0,1},{1,0},{2,3},{3,2},{4,5},{5,4},{6,7},{7,6},{8,9},{9,8},{10,11... | collective-permute-start | bytes 344072 | tf_op jit(solution)/shard_map/ppermute | solution.py:13
  95.8 7.0 %collective-permute-start.11 = (f32[224,128]{1,0:T(8,128)S(1)}, f32[224,128]{1,0:T(8,128)S(1)}, u32[]{:S(2)}, u32[]{:S(2)}) collective-permute-start(f32[224,128]{1,0:T(8,128)S(1)} %fusion.15), channel_id=1, source_target_pairs={{0,16},{2,18},{4,20},{6,22},{8,24},{10,26},{12,28},{14,30},{16,0},... | collective-permute-start | bytes 344072 | tf_op jit(solution)/shard_map/ppermute | solution.py:69

commit v2 on v1

v2 whole, which is shorter than its diff:
```python
import jax
import jax.numpy as jnp
from jax import lax
from jax.sharding import PartitionSpec as P

BLK = 512


loss_scale = 1024.0


def shift_tok(x, offset, size):
    return lax.ppermute(x, "tok", [(i, (i + offset) % size) for i in range(size)])


def swap_vocab(x, bit, size):
    return lax.ppermute(x, "vocab", [(i, i ^ bit) for i in range(size)])


def pick(x, index, axis=0):
    return lax.dynamic_index_in_dim(x, index, axis, keepdims=False)


def listed_columns(block_ids, counts, column_block, token_count):
    live_slot = jnp.arange(block_ids.shape[1], dtype=jnp.int32)[None, :] < counts[:, None]
    block_hit = jnp.any(
        (block_ids[:, :, None] == column_block[None, None, :]) & live_slot[:, :, None], axis=1
    )
    token_blocks = block_hit.shape[0]
    width = column_block.shape[0]
    return jnp.broadcast_to(
        block_hit[:, None, :], (token_blocks, token_count // token_blocks, width)
    ).reshape(token_count, width)


def in_order(mine, other, upper):
    return jnp.concatenate(
        [jnp.where(upper, other, mine), jnp.where(upper, mine, other)], axis=0
    )


def gather_vocab(stats, vocab_index, size):
    gathered = stats[None]
    bit = 1
    while bit < size:
        other = swap_vocab(gathered, bit, size)
        gathered = in_order(gathered, other, (vocab_index & bit) != 0)
        bit *= 2
    return gathered


def halve(partial, vocab_index, vocab_size, run):
    rows = partial.shape[0] // run
    held = partial.reshape(run, rows, partial.shape[1])
    bit = 1
    while bit < run:
        pairs = held.reshape(held.shape[0] // 2, 2, rows, held.shape[2])
        mine = (vocab_index // bit) % 2
        send = pick(pairs, 1 - mine, 1).astype(jnp.bfloat16)
        other = swap_vocab(send, bit, vocab_size)
        held = pick(pairs, mine, 1) + other.astype(jnp.float32)
        bit *= 2
    return held[0]


def per_device(hidden, head, teacher, block_ids, counts):
    tok_size = lax.axis_size("tok")
    vocab_size = lax.axis_size("vocab")
    tok_index = lax.axis_index("tok")
    vocab_index = lax.axis_index("vocab")
    token_count = hidden.shape[0]
    rows, column_count = head.shape
    run = vocab_size // tok_size
    half = token_count // 2
    core = vocab_index % 2

    def columns_of(index, first, count):
        return lax.dynamic_slice(hidden, (first, index * rows), (count, rows))

    near = [
        shift_tok(columns_of((tok_index + d) % tok_size, core * half, half), d, tok_size)
        for d in range(1, tok_size)
    ]
    far = [swap_vocab(x, 1, vocab_size) for x in near]
    returned = []
    for d in range(1, tok_size):
        first = shift_tok(
            jnp.dot(near[d - 1], head, preferred_element_type=jnp.float32), -d, tok_size
        )
        second = shift_tok(
            jnp.dot(far[d - 1], head, preferred_element_type=jnp.float32), -d, tok_size
        )
        returned.append((first, second))
    own = columns_of(tok_index, 0, token_count)
    logits = jnp.dot(own, head, preferred_element_type=jnp.float32)
    for first, second in returned:
        logits = logits + in_order(first, second, core != 0)

    first_column = vocab_index * column_count
    column_block = (first_column + jnp.arange(column_count, dtype=jnp.int32)) // BLK
    listed = listed_columns(block_ids, counts, column_block, token_count)
    teacher_f = teacher.astype(jnp.float32)
    kept = jnp.where(listed, teacher_f, 0.0)
    local_top = jnp.max(logits, axis=1)
    local_sum = jnp.sum(jnp.exp(logits - local_top[:, None]), axis=1)
    local_mass = jnp.sum(kept, axis=1)
    local_part = jnp.sum(jnp.where(listed, teacher_f * (jnp.log(teacher_f) - logits), 0.0), axis=1)

    stats = gather_vocab(
        jnp.stack([local_top, local_sum, local_mass, local_part]), vocab_index, vocab_size
    )
    tops = stats[:, 0]
    global_top = jnp.max(tops, axis=0)
    total_sum = jnp.sum(stats[:, 1] * jnp.exp(tops - global_top[None, :]), axis=0)
    total_mass = jnp.sum(stats[:, 2], axis=0)
    total_part = jnp.sum(stats[:, 3], axis=0)
    lse = global_top + jnp.log(total_sum)
    kl = total_part / total_mass - jnp.log(total_mass) + lse
    student = jnp.exp(logits - lse[:, None])
    delta = (loss_scale * (student - kept / total_mass[:, None])).astype(jnp.bfloat16)

    deltas = [delta] + [shift_tok(delta, d, tok_size) for d in range(1, tok_size)]
    sums = [
        halve(
            lax.dot_general(
                head, x, (((1,), (1,)), ((), ())), preferred_element_type=jnp.float32
            ),
            vocab_index,
            vocab_size,
            run,
        )
        for x in deltas
    ]
    blocks = [sums[0]] + [
        shift_tok(sums[d].astype(jnp.bfloat16), -d, tok_size).astype(jnp.float32)
        for d in range(1, tok_size)
    ]
    blocks = jnp.stack(blocks)
    high = vocab_index // run
    total = pick(blocks, (high - tok_index) % tok_size)
    for d in range(1, tok_size):
        send = pick(blocks, (high + d - tok_index) % tok_size).astype(jnp.bfloat16)
        total = total + lax.ppermute(
            send, "vocab", [(i, (i + d * run) % vocab_size) for i in range(vocab_size)]
        ).astype(jnp.float32)
    grad_hidden = total.T

    all_delta = jnp.concatenate(deltas, axis=0)
    features = [own] + [in_order(n, f, core != 0) for n, f in zip(near, far)]
    grad_head = lax.dot_general(
        jnp.concatenate(features, axis=0),
        all_delta,
        (((0,), (0,)), ((), ())),
        preferred_element_type=jnp.float32,
    ).astype(jnp.bfloat16)
    return (lse, kl, grad_hidden, grad_head)


def solution(mesh):
    placed = (P("tok", None), P("tok", "vocab"), P("tok", "vocab"), P("tok", None), P("tok"))
    return jax.shard_map(
        per_device,
        mesh=mesh,
        in_specs=placed,
        out_specs=(P("tok"), P("tok"), P("tok", "vocab"), P("tok", "vocab")),
        check_vma=False,
    )
```

time: 104 us -> 92.8 us (0.89)
  waiting for transfers between devices: 52.3 us -> 38.6 us
  matrix products: 15.4 us -> 22.5 us
  local copies, waits for them, and re-layouts: 8.53 us -> 2.72 us
  starting transfers between devices: 19.1 us -> 22.5 us
  other arithmetic: 6.52 us -> 4.46 us
    ppermute x4 -> x5, waiting for transfers between devices: 33 us -> 24.3 us  [shift_tok(): lax.ppermute(x, 'tok', [(i, (i + offset) % size) for i in range(size)])]
    dot_general x4 -> x6, matrix products: 15.4 us -> 22.5 us  [the longest x2 8.93 us: per_device(): lax.dot_general(head, x, (((1,), (1,)), ((), ())), preferred_element_type...]
    ppermute x7 -> x11, waiting for transfers between devices: 19 us -> 14.2 us  [swap_vocab(): return lax.ppermute(x, 'vocab', [(i, i ^ bit) for i in range(size)])]
    another operation x1, other arithmetic: 2.71 us -> 0.01 us  [per_device(): blocks = jnp.stack(blocks)]
    another operation x1 -> x0, local copies, waits for them, and re-layouts: 2.7 us -> none  [sum_vocab(): pairs = held.reshape(held.shape[0] // 2, 2, rows, held.shape[2])]
    unnamed x20 -> x14, local copies, waits for them, and re-layouts: 2.88 us -> 0.23 us
    ppermute x7 -> x11, starting transfers between devices: 8.7 us -> 11 us  [swap_vocab(): return lax.ppermute(x, 'vocab', [(i, i ^ bit) for i in range(size)])]
    ppermute x4 -> x5, starting transfers between devices: 7.82 us -> 8.73 us  [shift_tok(): lax.ppermute(x, 'tok', [(i, (i + offset) % size) for i in range(size)])]
  transfers between devices with their start and end apart: 12 -> 17, of which waited for: 12 -> 12; matrix products, arithmetic and copies ran while one was open for 7% -> 24% of each run, Pallas kernels for 0% -> 0%
where the time goes in v2:
time: 92.8 us; the launch traced here: 92.5 us
  waiting for transfers between devices  38.6 us (42%)
  starting transfers between devices  22.5 us (24%)
  matrix products  22.5 us (24%)
  other arithmetic  4.46 us (5%)
  local copies, waits for them, and re-layouts  2.72 us (3%)
  between operations  1.73 us (2%)
    ppermute x5, waiting for transfers between devices, shift_tok(): lax.ppermute(x, 'tok', [(i, (i + offset) % size) for i in range(size)])  24.3 us
    ppermute x11, waiting for transfers between devices, swap_vocab(): return lax.ppermute(x, 'vocab', [(i, i ^ bit) for i in range(size)])  14.2 us
    ppermute x11, starting transfers between devices, swap_vocab(): return lax.ppermute(x, 'vocab', [(i, i ^ bit) for i in range(size)])  11 us
    dot_general x2, matrix products, per_device(): lax.dot_general(head, x, (((1,), (1,)), ((), ())), preferred_element_type...  8.93 us
    ppermute x5, starting transfers between devices, shift_tok(): lax.ppermute(x, 'tok', [(i, (i + offset) % size) for i in range(size)])  8.73 us
    dot_general x1, matrix products, per_device(): lax.dot_general(jnp.concatenate(features, axis=0), all_delta, (((0,), (0,...  5.3 us
    dot_general x1, matrix products, per_device(): jnp.dot(near[d - 1], head, preferred_element_type=jnp.float32)  3.62 us
    dot_general x1, matrix products, per_device(): logits = jnp.dot(own, head, preferred_element_type=jnp.float32)  3.6 us
  transfers between devices with their start and end apart: 17, of which 12 were waited for; matrix products, arithmetic and copies ran while one was open for 24% of the time, Pallas kernels for 0%

profile of v2, /device:TPU:0, one launch (start us, length us, event | category | flops | bytes accessed | tf_op | source)
XLA Modules:
  0.0 92.5 jit_solution(1534545822352343145)
XLA Ops:
  0.7 1.0 %dynamic_slice.45 = bf16[64,1792]{1,0:T(8,128)(2,1)S(1)} dynamic-slice(bf16[128,3584]{1,0:T(8,128)(2,1)} %param.5, s32[]{:T(128)S(6)} %select_n.187, s32[]{:T(128)S(6)} %select_n.189), dynamic_slice_sizes={64,1792} | dynamic-slice | bytes 458756 | tf_op jit(solution)/shard_map/dynamic_slice | solution.py:78
  1.6 3.0 %collective-permute-start = (bf16[64,1792]{1,0:T(8,128)(2,1)S(1)}, bf16[64,1792]{1,0:T(8,128)(2,1)S(1)}, u32[]{:S(2)}, u32[]{:S(2)}) collective-permute-start(bf16[64,1792]{1,0:T(8,128)(2,1)S(1)} %dynamic_slice.45), channel_id=1, source_target_pairs={{0,1},{1,0},{2,3},{3,2},{4,5},{5,4},{6,7},{7,6},{8,9},{9,8},{10,11... | collective-permute-start | bytes 688136 | tf_op jit(solution)/shard_map/ppermute | solution.py:13
  4.7 0.0 copy-start
  5.5 0.0 copy-start.6
  5.5 0.0 copy-start.3
  5.5 4.8 %collective-permute-done = bf16[64,1792]{1,0:T(8,128)(2,1)S(1)} collective-permute-done((bf16[64,1792]{1,0:T(8,128)(2,1)S(1)}, bf16[64,1792]{1,0:T(8,128)(2,1)S(1)}, u32[]{:S(2)}, u32[]{:S(2)}) %collective-permute-start) | collective-permute-done | bytes 229408 | tf_op jit(solution)/shard_map/ppermute | solution.py:13
  10.3 0.0 collective-permute-start.1
  10.3 3.6 %fusion.39 = f32[64,1536]{1,0:T(8,128)S(1)} fusion(bf16[64,1792]{1,0:T(8,128)(2,1)S(1)} %collective-permute-done, bf16[1792,1536]{1,0:T(8,128)(2,1)} %param.6), kind=kOutput, calls=%fused_computation.99 | convolution fusion | flops 352321536 | bytes 6127616 | tf_op jit(solution)/shard_map/dot_general | solution.py:88
  13.9 1.8 %collective-permute-start.3 = (f32[64,1536]{1,0:T(8,128)S(1)}, f32[64,1536]{1,0:T(8,128)S(1)}, u32[]{:S(2)}, u32[]{:S(2)}) collective-permute-start(f32[64,1536]{1,0:T(8,128)S(1)} %fusion.39), channel_id=1, source_target_pairs={{0,1},{1,0},{2,3},{3,2},{4,5},{5,4},{6,7},{7,6},{8,9},{9,8},{10,11... | collective-permute-start | bytes 1179656 | tf_op jit(solution)/shard_map/ppermute | solution.py:13
  15.7 0.0 collective-permute-done.1
  15.7 0.0 copy-done
  15.7 1.1 %fusion.38 = f32[64,1536]{1,0:T(8,128)S(1)} fusion(bf16[64,1792]{1,0:T(8,128)(2,1)S(1)} %collective-permute-done.1, bf16[1792,1536]{1,0:T(8,128)(2,1)S(1)} %copy-done), kind=kOutput, calls=%fused_computation.98 | convolution fusion | flops 352321536 | bytes 6127616 | tf_op jit(solution)/shard_map/dot_general | solution.py:91
  16.8 0.4 collective-permute-start.2
  17.1 0.0 copy-done.6
  17.1 0.1 and_reduce_fusion
  17.2 0.0 copy-done.3
  17.3 8.6 %collective-permute-done.3 = f32[64,1536]{1,0:T(8,128)S(1)} collective-permute-done((f32[64,1536]{1,0:T(8,128)S(1)}, f32[64,1536]{1,0:T(8,128)S(1)}, u32[]{:S(2)}, u32[]{:S(2)}) %collective-permute-start.3) | collective-permute-done | bytes 393248 | tf_op jit(solution)/shard_map/ppermute | solution.py:13
  25.9 8.0 %collective-permute-done.2 = f32[64,1536]{1,0:T(8,128)S(1)} collective-permute-done((f32[64,1536]{1,0:T(8,128)S(1)}, f32[64,1536]{1,0:T(8,128)S(1)}, u32[]{:S(2)}, u32[]{:S(2)}) %collective-permute-start.2) | collective-permute-done | bytes 393248 | tf_op jit(solution)/shard_map/ppermute | solution.py:13
  33.9 0.1 broadcast_select_fusion.3
  34.0 0.0 copy-start.2
  34.0 3.6 %fusion.37 = (f32[128]{0:T(128)S(1)}, f32[128,1536]{1,0:T(8,128)S(1)}) fusion(f32[64,1536]{1,0:T(8,128)S(1)} %get-tuple-element.14, f32[64,1536]{1,0:T(8,128)S(1)} %get-tuple-element.13, bf16[128,1792]{1,0:T(8,128)(2,1)S(1)} %constant_dynamic-slice_fusion, bf16[1792,1536]{1,0:T(8,128)(2,1)} %param.6), kind=kOutput, calls=%fused_computation.97 | convolution fusion | flops 705232768 | bytes 7537152 | tf_op jit(solution)/shard_map/dot_general | solution.py:95
  37.6 0.0 copy-done.2
  37.6 0.5 exponential_reduce_fusion
  38.1 0.1 collective-permute-start.4
  38.2 1.1 %collective-permute-done.4 = f32[1,4,128]{2,1,0:T(4,128)S(1)} collective-permute-done((f32[1,4,128]{2,1,0:T(4,128)S(1)}, f32[1,4,128]{2,1,0:T(4,128)S(1)}, u32[]{:S(2)}, u32[]{:S(2)}) %collective-permute-start.4) | collective-permute-done | bytes 2080 | tf_op jit(solution)/shard_map/ppermute | solution.py:17
  39.4 1.8 %collective-permute-start.5 = (f32[2,4,128]{2,1,0:T(4,128)S(1)}, f32[2,4,128]{2,1,0:T(4,128)S(1)}, u32[]{:S(2)}, u32[]{:S(2)}) collective-permute-start(f32[2,4,128]{2,1,0:T(4,128)S(1)} %pad_maximum_fusion.3), channel_id=1, source_target_pairs={{0,4},{2,6},{4,0},{6,2},{8,12},{10,14},{12,8},{14,10},{16,20},{18,... | collective-permute-start | bytes 12296 | tf_op jit(solution)/shard_map/ppermute | solution.py:17
  41.1 1.9 %collective-permute-done.5 = f32[2,4,128]{2,1,0:T(4,128)S(1)} collective-permute-done((f32[2,4,128]{2,1,0:T(4,128)S(1)}, f32[2,4,128]{2,1,0:T(4,128)S(1)}, u32[]{:S(2)}, u32[]{:S(2)}) %collective-permute-start.5) | collective-permute-done | bytes 4128 | tf_op jit(solution)/shard_map/ppermute | solution.py:17
  43.0 1.9 %collective-permute-start.6 = (f32[4,4,128]{2,1,0:T(4,128)S(1)}, f32[4,4,128]{2,1,0:T(4,128)S(1)}, u32[]{:S(2)}, u32[]{:S(2)}) collective-permute-start(f32[4,4,128]{2,1,0:T(4,128)S(1)} %pad_maximum_fusion.2), channel_id=1, source_target_pairs={{0,8},{2,10},{4,12},{6,14},{8,0},{10,2},{12,4},{14,6},{16,24},{18,... | collective-permute-start | bytes 24584 | tf_op jit(solution)/shard_map/ppermute | solution.py:17
  44.9 1.9 %collective-permute-done.6 = f32[4,4,128]{2,1,0:T(4,128)S(1)} collective-permute-done((f32[4,4,128]{2,1,0:T(4,128)S(1)}, f32[4,4,128]{2,1,0:T(4,128)S(1)}, u32[]{:S(2)}, u32[]{:S(2)}) %collective-permute-start.6) | collective-permute-done | bytes 8224 | tf_op jit(solution)/shard_map/ppermute | solution.py:17
  46.8 2.9 %collective-permute-start.7 = (f32[8,4,128]{2,1,0:T(4,128)S(1)}, f32[8,4,128]{2,1,0:T(4,128)S(1)}, u32[]{:S(2)}, u32[]{:S(2)}) collective-permute-start(f32[8,4,128]{2,1,0:T(4,128)S(1)} %pad_maximum_fusion), channel_id=1, source_target_pairs={{0,16},{2,18},{4,20},{6,22},{8,24},{10,26},{12,28},{14,30},{16,0},... | collective-permute-start | bytes 49160 | tf_op jit(solution)/shard_map/ppermute | solution.py:17
  49.6 0.8 broadcast_select_fusion.1
  50.5 1.0 %collective-permute-done.7 = f32[8,4,128]{2,1,0:T(4,128)S(1)} collective-permute-done((f32[8,4,128]{2,1,0:T(4,128)S(1)}, f32[8,4,128]{2,1,0:T(4,128)S(1)}, u32[]{:S(2)}, u32[]{:S(2)}) %collective-permute-start.7) | collective-permute-done | bytes 16416 | tf_op jit(solution)/shard_map/ppermute | solution.py:17
  51.6 0.5 subtract_add_fusion
  52.1 0.3 fusion.15
  52.4 1.8 %collective-permute-start.11 = (bf16[128,1536]{1,0:T(8,128)(2,1)S(1)}, bf16[128,1536]{1,0:T(8,128)(2,1)S(1)}, u32[]{:S(2)}, u32[]{:S(2)}) collective-permute-start(bf16[128,1536]{1,0:T(8,128)(2,1)S(1)} %fusion.15), channel_id=1, source_target_pairs={{0,1},{1,0},{2,3},{3,2},{4,5},{5,4},{6,7},{7,6},{8,9},{9,8},{10,11... | collective-permute-start | bytes 1179656 | tf_op jit(solution)/shard_map/ppermute | solution.py:13
  54.2 4.4 %convolution_bitcast_fusion.1 = f32[1792,128]{0,1:T(8,128)S(1)} fusion(bf16[128,1536]{1,0:T(8,128)(2,1)S(1)} %fusion.15, bf16[1792,1536]{1,0:T(8,128)(2,1)} %param.6), kind=kOutput, calls=%fused_computation.2 | convolution fusion | flops 704643072 | bytes 6815744 | tf_op jit(solution)/shard_map/dot_general | solution.py:125
  58.6 0.3 copy.15
  58.9 0.0 copy-start.1
  58.9 0.8 fusion.16
  59.7 0.0 collective-permute-start.8
  59.7 0.2 copy-done.1
  59.9 0.5 collective-permute-done.11
  60.4 4.5 %convolution_bitcast_fusion = f32[1792,128]{0,1:T(8,128)S(1)} fusion(bf16[128,1536]{1,0:T(8,128)(2,1)S(1)} %collective-permute-done.11, bf16[1792,1536]{1,0:T(8,128)(2,1)} %param.6), kind=kOutput, calls=%fused_computation.1 | convolution fusion | flops 704643072 | bytes 6815744 | tf_op jit(solution)/shard_map/dot_general | solution.py:125
  64.9 0.0 copy-done.5
  64.9 0.3 copy.16
  65.3 0.1 collective-permute-start.12
  65.4 0.0 copy-done.4
  65.4 0.0 collective-permute-done.8
  65.4 1.2 %bitcast_add_fusion.1 = f32[4,224,128]{2,1,0:T(8,128)S(1)} fusion(bf16[4,224,128]{2,1,0:T(8,128)(2,1)} %collective-permute-done.8, f32[4,2,224,128]{3,2,1,0:T(8,128)} %bitcast.73, s32[]{:T(128)S(6)} %select_n.203), kind=kLoop, calls=%fused_computation.25 | loop fusion | flops 229376 | bytes 1146884 | tf_op jit(solution)/shard_map/add | solution.py:61
  66.6 1.6 %collective-permute-start.9 = (bf16[2,224,128]{2,1,0:T(8,128)(2,1)S(1)}, bf16[2,224,128]{2,1,0:T(8,128)(2,1)S(1)}, u32[]{:S(2)}, u32[]{:S(2)}) collective-permute-start(bf16[2,224,128]{2,1,0:T(8,128)(2,1)S(1)} %fusion.18), channel_id=1, source_target_pairs={{0,4},{2,6},{4,0},{6,2},{8,12},{10,14},{12,8},{14,10},{16,20},{18,... | collective-permute-start | bytes 344072 | tf_op jit(solution)/shard_map/ppermute | solution.py:17
  68.2 0.0 collective-permute-done.12
  68.3 0.5 collective-permute-start.13
  68.8 3.8 %collective-permute-done.9 = bf16[2,224,128]{2,1,0:T(8,128)(2,1)S(1)} collective-permute-done((bf16[2,224,128]{2,1,0:T(8,128)(2,1)S(1)}, bf16[2,224,128]{2,1,0:T(8,128)(2,1)S(1)}, u32[]{:S(2)}, u32[]{:S(2)}) %collective-permute-start.9) | collective-permute-done | bytes 114720 | tf_op jit(solution)/shard_map/ppermute | solution.py:17
  72.6 2.0 %collective-permute-done.13 = bf16[2,224,128]{2,1,0:T(8,128)(2,1)S(1)} collective-permute-done((bf16[2,224,128]{2,1,0:T(8,128)(2,1)S(1)}, bf16[2,224,128]{2,1,0:T(8,128)(2,1)S(1)}, u32[]{:S(2)}, u32[]{:S(2)}) %collective-permute-start.13) | collective-permute-done | bytes 114720 | tf_op jit(solution)/shard_map/ppermute | solution.py:17
  74.7 1.7 %collective-permute-start.14 = (bf16[1,224,128]{2,1,0:T(8,128)(2,1)S(1)}, bf16[1,224,128]{2,1,0:T(8,128)(2,1)S(1)}, u32[]{:S(2)}, u32[]{:S(2)}) collective-permute-start(bf16[1,224,128]{2,1,0:T(8,128)(2,1)S(1)} %dynamic-slice_convert_fusion.3), channel_id=1, source_target_pairs={{0,8},{2,10},{4,12},{6,14},{8,0},{10,2},{12,4},{14,6},{16,24},{18,... | collective-permute-start | bytes 172040 | tf_op jit(solution)/shard_map/ppermute | solution.py:17
  76.4 0.4 collective-permute-start.10
  76.9 2.5 %collective-permute-done.14 = bf16[1,224,128]{2,1,0:T(8,128)(2,1)S(1)} collective-permute-done((bf16[1,224,128]{2,1,0:T(8,128)(2,1)S(1)}, bf16[1,224,128]{2,1,0:T(8,128)(2,1)S(1)}, u32[]{:S(2)}, u32[]{:S(2)}) %collective-permute-start.14) | collective-permute-done | bytes 57376 | tf_op jit(solution)/shard_map/ppermute | solution.py:17
  79.4 1.7 %collective-permute-start.15 = (bf16[224,128]{1,0:T(8,128)(2,1)S(1)}, bf16[224,128]{1,0:T(8,128)(2,1)S(1)}, u32[]{:S(2)}, u32[]{:S(2)}) collective-permute-start(bf16[224,128]{1,0:T(8,128)(2,1)S(1)} %fusion.26), channel_id=1, source_target_pairs={{0,1},{1,0},{2,3},{3,2},{4,5},{5,4},{6,7},{7,6},{8,9},{9,8},{10,11... | collective-permute-start | bytes 172040 | tf_op jit(solution)/shard_map/ppermute | solution.py:13
  81.2 0.0 collective-permute-done.10
  81.2 2.5 %collective-permute-done.15 = bf16[224,128]{1,0:T(8,128)(2,1)S(1)} collective-permute-done((bf16[224,128]{1,0:T(8,128)(2,1)S(1)}, bf16[224,128]{1,0:T(8,128)(2,1)S(1)}, u32[]{:S(2)}, u32[]{:S(2)}) %collective-permute-start.15) | collective-permute-done | bytes 57376 | tf_op jit(solution)/shard_map/ppermute | solution.py:13
  83.7 2.8 %collective-permute-start.16 = (bf16[224,128]{1,0:T(8,128)(2,1)S(1)}, bf16[224,128]{1,0:T(8,128)(2,1)S(1)}, u32[]{:S(2)}, u32[]{:S(2)}) collective-permute-start(bf16[224,128]{1,0:T(8,128)(2,1)S(1)} %fusion.27), channel_id=1, source_target_pairs={{0,16},{2,18},{4,20},{6,22},{8,24},{10,26},{12,28},{14,30},{16,0},... | collective-permute-start | bytes 172040 | tf_op jit(solution)/shard_map/ppermute | solution.py:143
  86.5 5.3 %convolution_convert_fusion = bf16[1792,1536]{1,0:T(8,128)(2,1)} fusion(bf16[64,1792]{1,0:T(8,128)(2,1)} %get-tuple-element.16, bf16[64,1792]{1,0:T(8,128)(2,1)} %get-tuple-element.15, bf16[128,1792]{1,0:T(8,128)(2,1)S(1)} %constant_dynamic-slice_fusion, bf16[128,1536]{1,0:T(8,128)(2,1)} %copy-done.4, bf16[128,1536]{1,0:T(8,128)(2,1)S(1)} %fusion.15), kind=kOutput, calls=%fused_computation | convolution fusion | flops 1416364032 | bytes 7208960 | tf_op jit(solution)/shard_map/dot_general | solution.py:150
  91.8 0.0 collective-permute-done.16
  91.8 0.7 fusion.25
  (28 shorter events, 0.5 us)
Async XLA Ops:
  1.6 8.6 %collective-permute-start = (bf16[64,1792]{1,0:T(8,128)(2,1)S(1)}, bf16[64,1792]{1,0:T(8,128)(2,1)S(1)}, u32[]{:S(2)}, u32[]{:S(2)}) collective-permute-start(bf16[64,1792]{1,0:T(8,128)(2,1)S(1)} %dynamic_slice.45), channel_id=1, source_target_pairs={{0,1},{1,0},{2,3},{3,2},{4,5},{5,4},{6,7},{7,6},{8,9},{9,8},{10,11... | collective-permute-start | bytes 688136 | tf_op jit(solution)/shard_map/ppermute | solution.py:13
  4.7 11.0 %copy-start = (bf16[1792,1536]{1,0:T(8,128)(2,1)S(1)}, bf16[1792,1536]{1,0:T(8,128)(2,1)}, u32[]{:S(2)}) copy-start(bf16[1792,1536]{1,0:T(8,128)(2,1)} %param.6) | copy-start | bytes 16515076
  5.5 11.6 %copy-start.6 = (s32[1,16]{1,0:T(1,128)S(1)}, s32[1,16]{1,0:T(1,128)}, u32[]{:S(2)}) copy-start(s32[1,16]{1,0:T(1,128)} %param.8) | copy-start | bytes 196
  5.5 11.7 %copy-start.3 = (bf16[128,3584]{1,0:T(8,128)(2,1)S(1)}, bf16[128,3584]{1,0:T(8,128)(2,1)}, u32[]{:S(2)}) copy-start(bf16[128,3584]{1,0:T(8,128)(2,1)} %param.5) | copy-start | bytes 2752516
  10.3 5.4 %collective-permute-start.1 = (bf16[64,1792]{1,0:T(8,128)(2,1)S(1)}, bf16[64,1792]{1,0:T(8,128)(2,1)S(1)}, u32[]{:S(2)}, u32[]{:S(2)}) collective-permute-start(bf16[64,1792]{1,0:T(8,128)(2,1)S(1)} %collective-permute-done), channel_id=1, source_target_pairs={{0,2},{2,0},{4,6},{6,4},{8,10},{10,8},{12,14},{14,12},{16,18},{18,... | collective-permute-start | bytes 688136 | tf_op jit(solution)/shard_map/ppermute | solution.py:17
  13.9 12.0 %collective-permute-start.3 = (f32[64,1536]{1,0:T(8,128)S(1)}, f32[64,1536]{1,0:T(8,128)S(1)}, u32[]{:S(2)}, u32[]{:S(2)}) collective-permute-start(f32[64,1536]{1,0:T(8,128)S(1)} %fusion.39), channel_id=1, source_target_pairs={{0,1},{1,0},{2,3},{3,2},{4,5},{5,4},{6,7},{7,6},{8,9},{9,8},{10,11... | collective-permute-start | bytes 1179656 | tf_op jit(solution)/shard_map/ppermute | solution.py:13
  16.8 17.1 %collective-permute-start.2 = (f32[64,1536]{1,0:T(8,128)S(1)}, f32[64,1536]{1,0:T(8,128)S(1)}, u32[]{:S(2)}, u32[]{:S(2)}) collective-permute-start(f32[64,1536]{1,0:T(8,128)S(1)} %fusion.38), channel_id=1, source_target_pairs={{0,1},{1,0},{2,3},{3,2},{4,5},{5,4},{6,7},{7,6},{8,9},{9,8},{10,11... | collective-permute-start | bytes 1179656 | tf_op jit(solution)/shard_map/ppermute | solution.py:13
  34.0 3.6 %copy-start.2 = (bf16[128,1536]{1,0:T(8,128)(2,1)S(1)}, bf16[128,1536]{1,0:T(8,128)(2,1)}, u32[]{:S(2)}) copy-start(bf16[128,1536]{1,0:T(8,128)(2,1)} %param.7) | copy-start | bytes 1179652
  38.1 1.2 %collective-permute-start.4 = (f32[1,4,128]{2,1,0:T(4,128)S(1)}, f32[1,4,128]{2,1,0:T(4,128)S(1)}, u32[]{:S(2)}, u32[]{:S(2)}) collective-permute-start(f32[1,4,128]{2,1,0:T(4,128)S(1)} %maximum_bitcast_fusion), channel_id=1, source_target_pairs={{0,2},{2,0},{4,6},{6,4},{8,10},{10,8},{12,14},{14,12},{16,18},{18,... | collective-permute-start | bytes 6152 | tf_op jit(solution)/shard_map/ppermute | solution.py:17
  39.4 3.7 %collective-permute-start.5 = (f32[2,4,128]{2,1,0:T(4,128)S(1)}, f32[2,4,128]{2,1,0:T(4,128)S(1)}, u32[]{:S(2)}, u32[]{:S(2)}) collective-permute-start(f32[2,4,128]{2,1,0:T(4,128)S(1)} %pad_maximum_fusion.3), channel_id=1, source_target_pairs={{0,4},{2,6},{4,0},{6,2},{8,12},{10,14},{12,8},{14,10},{16,20},{18,... | collective-permute-start | bytes 12296 | tf_op jit(solution)/shard_map/ppermute | solution.py:17
  43.0 3.7 %collective-permute-start.6 = (f32[4,4,128]{2,1,0:T(4,128)S(1)}, f32[4,4,128]{2,1,0:T(4,128)S(1)}, u32[]{:S(2)}, u32[]{:S(2)}) collective-permute-start(f32[4,4,128]{2,1,0:T(4,128)S(1)} %pad_maximum_fusion.2), channel_id=1, source_target_pairs={{0,8},{2,10},{4,12},{6,14},{8,0},{10,2},{12,4},{14,6},{16,24},{18,... | collective-permute-start | bytes 24584 | tf_op jit(solution)/shard_map/ppermute | solution.py:17
  46.8 4.7 %collective-permute-start.7 = (f32[8,4,128]{2,1,0:T(4,128)S(1)}, f32[8,4,128]{2,1,0:T(4,128)S(1)}, u32[]{:S(2)}, u32[]{:S(2)}) collective-permute-start(f32[8,4,128]{2,1,0:T(4,128)S(1)} %pad_maximum_fusion), channel_id=1, source_target_pairs={{0,16},{2,18},{4,20},{6,22},{8,24},{10,26},{12,28},{14,30},{16,0},... | collective-permute-start | bytes 49160 | tf_op jit(solution)/shard_map/ppermute | solution.py:17
  52.1 12.8 %copy-start.5 = (f32[128]{0:T(128)}, f32[128]{0:T(128)S(1)}, u32[]{:S(2)}) copy-start(f32[128]{0:T(128)S(1)} %get-tuple-element.10) | copy-start | bytes 1540
  52.4 8.0 %collective-permute-start.11 = (bf16[128,1536]{1,0:T(8,128)(2,1)S(1)}, bf16[128,1536]{1,0:T(8,128)(2,1)S(1)}, u32[]{:S(2)}, u32[]{:S(2)}) collective-permute-start(bf16[128,1536]{1,0:T(8,128)(2,1)S(1)} %fusion.15), channel_id=1, source_target_pairs={{0,1},{1,0},{2,3},{3,2},{4,5},{5,4},{6,7},{7,6},{8,9},{9,8},{10,11... | collective-permute-start | bytes 1179656 | tf_op jit(solution)/shard_map/ppermute | solution.py:13
  58.9 1.0 %copy-start.1 = (f32[1792,128]{1,0:T(8,128)}, f32[1792,128]{1,0:T(8,128)S(1)}, u32[]{:S(2)}) copy-start(f32[1792,128]{1,0:T(8,128)S(1)} %copy.15) | copy-start | bytes 2752516
  59.7 5.7 %collective-permute-start.8 = (bf16[4,224,128]{2,1,0:T(8,128)(2,1)}, bf16[4,224,128]{2,1,0:T(8,128)(2,1)}, u32[]{:S(2)}, u32[]{:S(2)}) collective-permute-start(bf16[4,224,128]{2,1,0:T(8,128)(2,1)} %fusion.16), channel_id=1, source_target_pairs={{0,2},{2,0},{4,6},{6,4},{8,10},{10,8},{12,14},{14,12},{16,18},{18,... | collective-permute-start | bytes 688136 | tf_op jit(solution)/shard_map/ppermute | solution.py:17
  60.4 5.0 %copy-start.4 = (bf16[128,1536]{1,0:T(8,128)(2,1)}, bf16[128,1536]{1,0:T(8,128)(2,1)S(1)}, u32[]{:S(2)}) copy-start(bf16[128,1536]{1,0:T(8,128)(2,1)S(1)} %collective-permute-done.11) | copy-start | bytes 1179652
  65.3 3.0 %collective-permute-start.12 = (bf16[4,224,128]{2,1,0:T(8,128)(2,1)S(1)}, bf16[4,224,128]{2,1,0:T(8,128)(2,1)S(1)}, u32[]{:S(2)}, u32[]{:S(2)}) collective-permute-start(bf16[4,224,128]{2,1,0:T(8,128)(2,1)S(1)} %fusion.17), channel_id=1, source_target_pairs={{0,2},{2,0},{4,6},{6,4},{8,10},{10,8},{12,14},{14,12},{16,18},{18,... | collective-permute-start | bytes 688136 | tf_op jit(solution)/shard_map/ppermute | solution.py:17
  66.6 6.0 %collective-permute-start.9 = (bf16[2,224,128]{2,1,0:T(8,128)(2,1)S(1)}, bf16[2,224,128]{2,1,0:T(8,128)(2,1)S(1)}, u32[]{:S(2)}, u32[]{:S(2)}) collective-permute-start(bf16[2,224,128]{2,1,0:T(8,128)(2,1)S(1)} %fusion.18), channel_id=1, source_target_pairs={{0,4},{2,6},{4,0},{6,2},{8,12},{10,14},{12,8},{14,10},{16,20},{18,... | collective-permute-start | bytes 344072 | tf_op jit(solution)/shard_map/ppermute | solution.py:17
  68.3 6.3 %collective-permute-start.13 = (bf16[2,224,128]{2,1,0:T(8,128)(2,1)S(1)}, bf16[2,224,128]{2,1,0:T(8,128)(2,1)S(1)}, u32[]{:S(2)}, u32[]{:S(2)}) collective-permute-start(bf16[2,224,128]{2,1,0:T(8,128)(2,1)S(1)} %fusion.19), channel_id=1, source_target_pairs={{0,4},{2,6},{4,0},{6,2},{8,12},{10,14},{12,8},{14,10},{16,20},{18,... | collective-permute-start | bytes 344072 | tf_op jit(solution)/shard_map/ppermute | solution.py:17
  74.7 4.7 %collective-permute-start.14 = (bf16[1,224,128]{2,1,0:T(8,128)(2,1)S(1)}, bf16[1,224,128]{2,1,0:T(8,128)(2,1)S(1)}, u32[]{:S(2)}, u32[]{:S(2)}) collective-permute-start(bf16[1,224,128]{2,1,0:T(8,128)(2,1)S(1)} %dynamic-slice_convert_fusion.3), channel_id=1, source_target_pairs={{0,8},{2,10},{4,12},{6,14},{8,0},{10,2},{12,4},{14,6},{16,24},{18,... | collective-permute-start | bytes 172040 | tf_op jit(solution)/shard_map/ppermute | solution.py:17
  76.4 4.7 %collective-permute-start.10 = (bf16[1,224,128]{2,1,0:T(8,128)(2,1)S(1)}, bf16[1,224,128]{2,1,0:T(8,128)(2,1)S(1)}, u32[]{:S(2)}, u32[]{:S(2)}) collective-permute-start(bf16[1,224,128]{2,1,0:T(8,128)(2,1)S(1)} %dynamic-slice_convert_fusion.4), channel_id=1, source_target_pairs={{0,8},{2,10},{4,12},{6,14},{8,0},{10,2},{12,4},{14,6},{16,24},{18,... | collective-permute-start | bytes 172040 | tf_op jit(solution)/shard_map/ppermute | solution.py:17
  79.4 4.2 %collective-permute-start.15 = (bf16[224,128]{1,0:T(8,128)(2,1)S(1)}, bf16[224,128]{1,0:T(8,128)(2,1)S(1)}, u32[]{:S(2)}, u32[]{:S(2)}) collective-permute-start(bf16[224,128]{1,0:T(8,128)(2,1)S(1)} %fusion.26), channel_id=1, source_target_pairs={{0,1},{1,0},{2,3},{3,2},{4,5},{5,4},{6,7},{7,6},{8,9},{9,8},{10,11... | collective-permute-start | bytes 172040 | tf_op jit(solution)/shard_map/ppermute | solution.py:13
  83.7 8.1 %collective-permute-start.16 = (bf16[224,128]{1,0:T(8,128)(2,1)S(1)}, bf16[224,128]{1,0:T(8,128)(2,1)S(1)}, u32[]{:S(2)}, u32[]{:S(2)}) collective-permute-start(bf16[224,128]{1,0:T(8,128)(2,1)S(1)} %fusion.27), channel_id=1, source_target_pairs={{0,16},{2,18},{4,20},{6,22},{8,24},{10,26},{12,28},{14,30},{16,0},... | collective-permute-start | bytes 172040 | tf_op jit(solution)/shard_map/ppermute | solution.py:143

commit v3 on v2

--- a/solution.py
+++ b/solution.py
@@ -1,12 +1,15 @@
 import jax
 import jax.numpy as jnp
 from jax import lax
+from jax.experimental import pallas as pl
+from jax.experimental.pallas import tpu as pltpu
 from jax.sharding import PartitionSpec as P
 
 BLK = 512
 
 
 loss_scale = 1024.0
+VMEM_LIMIT = 8 << 20
 
 
 def shift_tok(x, offset, size):
@@ -15,6 +18,25 @@
 
 def swap_vocab(x, bit, size):
     return lax.ppermute(x, "vocab", [(i, i ^ bit) for i in range(size)])
+
+
+def load_kernel(head_ref, out_ref, sem):
+    copy = pltpu.make_async_copy(head_ref, out_ref, sem)
+    copy.start()
+    copy.wait()
+
+
+def load(head):
+    return pl.pallas_call(
+        load_kernel,
+        out_shape=pltpu.VMEM(head.shape, head.dtype),
+        in_specs=[pl.BlockSpec(memory_space=pl.ANY)],
+        out_specs=pl.BlockSpec(memory_space=pl.ANY),
+        scratch_shapes=[pltpu.SemaphoreType.DMA],
+        compiler_params=pltpu.CompilerParams(vmem_limit_bytes=1 << 20),
+        cost_estimate=pl.CostEstimate(flops=0, bytes_accessed=2 * head.size, transcendentals=0),
+        name="load_head",
+    )(pltpu.with_memory_space_constraint(head, pltpu.HBM))
 
 
 def pick(x, index, axis=0):
@@ -39,22 +61,62 @@
     )
 
 
-def gather_vocab(stats, vocab_index, size):
-    gathered = stats[None]
-    bit = 1
-    while bit < size:
-        other = swap_vocab(gathered, bit, size)
-        gathered = in_order(gathered, other, (vocab_index & bit) != 0)
-        bit *= 2
-    return gathered
-
-
-def halve(partial, vocab_index, vocab_size, run):
-    rows = partial.shape[0] // run
-    held = partial.reshape(run, rows, partial.shape[1])
-    bit = 1
-    while bit < run:
-        pairs = held.reshape(held.shape[0] // 2, 2, rows, held.shape[2])
+def gather_vocab(stats, size):
+    pair = jnp.stack([stats, swap_vocab(stats, 1, size)])
+    pairs = [pair] + [swap_vocab(pair, bit, size) for bit in range(2, size, 2)]
+    return jnp.concatenate(pairs, axis=0)
+
+
+def tree_sum(x):
+    while x.shape[0] > 1:
+        half = x.shape[0] // 2
+        x = x[:half] + x[half:]
+    return x[0]
+
+
+def gradient_kernel(core_ref, head_ref, delta_ref, send_ref, keep_ref):
+    upper = core_ref[0] == 1
+    pairs, rows, _ = send_ref.shape
+    for k in range(pairs):
+        block = lax.dot_general(
+            head_ref[2 * k * rows : 2 * (k + 1) * rows, :],
+            delta_ref[...],
+            (((1,), (1,)), ((), ())),
+            preferred_element_type=jnp.float32,
+        )
+        low, high = block[:rows], block[rows:]
+        send_ref[k] = jnp.where(upper, low, high).astype(jnp.bfloat16)
+        keep_ref[k] = jnp.where(upper, high, low)
+
+
+def gradient(core, head, delta, run):
+    rows = head.shape[0] // run
+    shape = (run // 2, rows, delta.shape[0])
+    in_vmem = pl.BlockSpec(memory_space=pltpu.VMEM)
+    return pl.pallas_call(
+        gradient_kernel,
+        out_shape=(pltpu.VMEM(shape, jnp.bfloat16), pltpu.VMEM(shape, jnp.float32)),
+        in_specs=[pl.BlockSpec(memory_space=pltpu.SMEM), in_vmem, in_vmem],
+        out_specs=(in_vmem, in_vmem),
+        compiler_params=pltpu.CompilerParams(vmem_limit_bytes=VMEM_LIMIT),
+        cost_estimate=pl.CostEstimate(
+            flops=2 * head.size * delta.shape[0],
+            bytes_accessed=2 * (head.size + delta.size),
+            transcendentals=0,
+        ),
+        name="partial_gradient",
+    )(
+        core.reshape(1),
+        pltpu.with_memory_space_constraint(head, pltpu.VMEM),
+        pltpu.with_memory_space_constraint(delta, pltpu.VMEM),
+    )
+
+
+def halve(send, keep, vocab_index, vocab_size):
+    held = keep + swap_vocab(send, 1, vocab_size).astype(jnp.float32)
+    bit = 2
+    while held.shape[0] > 1:
+        pairs = held.reshape(held.shape[0] // 2, 2, *held.shape[1:])
         mine = (vocab_index // bit) % 2
         send = pick(pairs, 1 - mine, 1).astype(jnp.bfloat16)
         other = swap_vocab(send, bit, vocab_size)
@@ -72,6 +134,7 @@
     rows, column_count = head.shape
     run = vocab_size // tok_size
     half = token_count // 2
+    head = load(head)
     core = vocab_index % 2
 
     def columns_of(index, first, count):
@@ -92,7 +155,7 @@
         )
         returned.append((first, second))
     own = columns_of(tok_index, 0, token_count)
-    logits = jnp.dot(own, head, preferred_element_type=jnp.float32)
+    logits = lax.optimization_barrier(jnp.dot(own, head, preferred_element_type=jnp.float32))
     for first, second in returned:
         logits = logits + in_order(first, second, core != 0)
 
@@ -106,31 +169,18 @@
     local_mass = jnp.sum(kept, axis=1)
     local_part = jnp.sum(jnp.where(listed, teacher_f * (jnp.log(teacher_f) - logits), 0.0), axis=1)
 
-    stats = gather_vocab(
-        jnp.stack([local_top, local_sum, local_mass, local_part]), vocab_index, vocab_size
-    )
+    stats = gather_vocab(jnp.stack([local_top, local_sum, local_mass, local_part]), vocab_size)
     tops = stats[:, 0]
     global_top = jnp.max(tops, axis=0)
-    total_sum = jnp.sum(stats[:, 1] * jnp.exp(tops - global_top[None, :]), axis=0)
-    total_mass = jnp.sum(stats[:, 2], axis=0)
-    total_part = jnp.sum(stats[:, 3], axis=0)
+    total_sum = tree_sum(stats[:, 1] * jnp.exp(tops - global_top[None, :]))
+    total_mass, total_part = tree_sum(stats[:, 2]), tree_sum(stats[:, 3])
     lse = global_top + jnp.log(total_sum)
     kl = total_part / total_mass - jnp.log(total_mass) + lse
     student = jnp.exp(logits - lse[:, None])
     delta = (loss_scale * (student - kept / total_mass[:, None])).astype(jnp.bfloat16)
 
     deltas = [delta] + [shift_tok(delta, d, tok_size) for d in range(1, tok_size)]
-    sums = [
-        halve(
-            lax.dot_general(
-                head, x, (((1,), (1,)), ((), ())), preferred_element_type=jnp.float32
-            ),
-            vocab_index,
-            vocab_size,
-            run,
-        )
-        for x in deltas
-    ]
+    sums = [halve(*gradient(core, head, x, run), vocab_index, vocab_size) for x in deltas]
     blocks = [sums[0]] + [
         shift_tok(sums[d].astype(jnp.bfloat16), -d, tok_size).astype(jnp.float32)
         for d in range(1, tok_size)

time: 92.8 us -> 91.2 us (0.983)
  matrix products: 22.5 us -> 9.87 us
  local copies, waits for them, and re-layouts: 2.72 us -> 8.74 us
  Pallas kernels: 0 us -> 5.81 us
    dot_general x3 -> x1, matrix products: 12.5 us -> 0.88 us  [per_device(): jnp.dot(own, head, preferred_element_type=jnp.float32)]
    unnamed x14 -> x23, local copies, waits for them, and re-layouts: 0.23 us -> 7.64 us
    pallas_call x0 -> x3, Pallas kernels: none -> 5.81 us  [the longest x2 3.16 us: gradient(): pl.pallas_call(gradient_kernel, out_shape=(pltpu.VMEM(shape, jnp.bfloat16...]
    ppermute x11 -> x15, starting transfers between devices: 11 us -> 14.9 us  [swap_vocab(): return lax.ppermute(x, 'vocab', [(i, i ^ bit) for i in range(size)])]
    ppermute x5, waiting for transfers between devices: 24.3 us -> 20.7 us  [shift_tok(): lax.ppermute(x, 'tok', [(i, (i + offset) % size) for i in range(size)])]
    ppermute x1, starting transfers between devices: 2.76 us -> 0.07 us  [per_device(): lax.ppermute(send, 'vocab', [(i, (i + d * run) % vocab_size) for i in ran...]
    ppermute x11 -> x15, waiting for transfers between devices: 14.2 us -> 15.9 us  [swap_vocab(): return lax.ppermute(x, 'vocab', [(i, i ^ bit) for i in range(size)])]
    add x5 -> x3, other arithmetic: 1.29 us -> 0.06 us  [halve(): held = pick(pairs, mine, 1) + other.astype(jnp.float32)]
  transfers between devices with their start and end apart: 17 -> 21, of which waited for: 12 -> 14; matrix products, arithmetic and copies ran while one was open for 24% -> 11% of each run, Pallas kernels for 0% -> 6%
where the time goes in v3:
time: 91.2 us; the launch traced here: 90.9 us
  waiting for transfers between devices  37.7 us (41%)
  starting transfers between devices  23.3 us (26%)
  matrix products  9.87 us (11%)
  local copies, waits for them, and re-layouts  8.74 us (10%)
  Pallas kernels  5.81 us (6%)
  other arithmetic  3.68 us (4%)
  between operations  1.77 us (2%)
    ppermute x5, waiting for transfers between devices, shift_tok(): lax.ppermute(x, 'tok', [(i, (i + offset) % size) for i in range(size)])  20.7 us
    ppermute x15, waiting for transfers between devices, swap_vocab(): return lax.ppermute(x, 'vocab', [(i, i ^ bit) for i in range(size)])  15.9 us
    ppermute x15, starting transfers between devices, swap_vocab(): return lax.ppermute(x, 'vocab', [(i, i ^ bit) for i in range(size)])  14.9 us
    ppermute x5, starting transfers between devices, shift_tok(): lax.ppermute(x, 'tok', [(i, (i + offset) % size) for i in range(size)])  8.35 us
    unnamed x23, local copies, waits for them, and re-layouts  7.64 us
    dot_general x1, matrix products, per_device(): lax.dot_general(jnp.concatenate(features, axis=0), all_delta, (((0,), (0,...  4.08 us
    dot_general x1, matrix products, per_device(): jnp.dot(near[d - 1], head, preferred_element_type=jnp.float32)  3.85 us
    pallas_call x2, Pallas kernels, gradient(): pl.pallas_call(gradient_kernel, out_shape=(pltpu.VMEM(shape, jnp.bfloat16...  3.16 us
  transfers between devices with their start and end apart: 21, of which 14 were waited for; matrix products, arithmetic and copies ran while one was open for 11% of the time, Pallas kernels for 6%

profile of v3, /device:TPU:0, one launch (start us, length us, event | category | flops | bytes accessed | tf_op | source)
XLA Modules:
  0.0 90.9 jit_solution(7816343718764724610)
XLA Ops:
  0.7 1.0 %dynamic_slice.32 = bf16[64,1792]{1,0:T(8,128)(2,1)S(1)} dynamic-slice(bf16[128,3584]{1,0:T(8,128)(2,1)} %param.5, s32[]{:T(128)S(6)} %select_n.120, s32[]{:T(128)S(6)} %select_n.122), dynamic_slice_sizes={64,1792} | dynamic-slice | bytes 458756 | tf_op jit(solution)/shard_map/dynamic_slice | solution.py:141
  1.6 3.0 %collective-permute-start = (bf16[64,1792]{1,0:T(8,128)(2,1)S(1)}, bf16[64,1792]{1,0:T(8,128)(2,1)S(1)}, u32[]{:S(2)}, u32[]{:S(2)}) collective-permute-start(bf16[64,1792]{1,0:T(8,128)(2,1)S(1)} %dynamic_slice.32), channel_id=1, source_target_pairs={{0,1},{1,0},{2,3},{3,2},{4,5},{5,4},{6,7},{7,6},{8,9},{9,8},{10,11... | collective-permute-start | bytes 688136 | tf_op jit(solution)/shard_map/ppermute | solution.py:16
  4.7 2.6 %load_head.1.head_ref = bf16[1792,1536]{1,0:T(8,128)(2,1)S(1)} custom-call(bf16[1792,1536]{1,0:T(8,128)(2,1)} %head_ref.1), custom_call_target="tpu_custom_call" | custom-call | bytes 5505024 | tf_op jit(solution)/shard_map/load_head/pallas_call | solution.py:30
  7.3 0.0 copy-start
  7.3 2.4 %copy-done = bf16[1792,1536]{1,0:T(8,128)(2,1)} copy-done((bf16[1792,1536]{1,0:T(8,128)(2,1)}, bf16[1792,1536]{1,0:T(8,128)(2,1)S(1)}, u32[]{:S(2)}) %copy-start) | copy-done | bytes 5505048
  9.8 0.5 collective-permute-done
  10.3 0.0 collective-permute-start.1
  10.3 3.9 %fusion.39 = f32[64,1536]{1,0:T(8,128)S(1)} fusion(bf16[64,1792]{1,0:T(8,128)(2,1)S(1)} %collective-permute-done, bf16[1792,1536]{1,0:T(8,128)(2,1)} %copy-done), kind=kOutput, calls=%fused_computation.106 | convolution fusion | flops 352321536 | bytes 6127616 | tf_op jit(solution)/shard_map/dot_general | solution.py:151
  14.1 0.0 copy-start.7
  14.1 1.6 %collective-permute-start.3 = (f32[64,1536]{1,0:T(8,128)S(1)}, f32[64,1536]{1,0:T(8,128)S(1)}, u32[]{:S(2)}, u32[]{:S(2)}) collective-permute-start(f32[64,1536]{1,0:T(8,128)S(1)} %fusion.39), channel_id=1, source_target_pairs={{0,1},{1,0},{2,3},{3,2},{4,5},{5,4},{6,7},{7,6},{8,9},{9,8},{10,11... | collective-permute-start | bytes 1179656 | tf_op jit(solution)/shard_map/ppermute | solution.py:16
  15.7 0.0 collective-permute-done.1
  15.7 1.1 %fusion.38 = f32[64,1536]{1,0:T(8,128)S(1)} fusion(bf16[64,1792]{1,0:T(8,128)(2,1)S(1)} %collective-permute-done.1, bf16[1792,1536]{1,0:T(8,128)(2,1)S(1)} %copy-done.1), kind=kOutput, calls=%fused_computation.105 | convolution fusion | flops 352321536 | bytes 6127616 | tf_op jit(solution)/shard_map/dot_general | solution.py:154
  16.8 0.0 copy-start.4
  16.8 0.6 collective-permute-start.2
  17.4 0.9 fusion.37
  19.1 0.1 and_reduce_fusion
  19.2 6.9 %collective-permute-done.3 = f32[64,1536]{1,0:T(8,128)S(1)} collective-permute-done((f32[64,1536]{1,0:T(8,128)S(1)}, f32[64,1536]{1,0:T(8,128)S(1)}, u32[]{:S(2)}, u32[]{:S(2)}) %collective-permute-start.3) | collective-permute-done | bytes 393248 | tf_op jit(solution)/shard_map/ppermute | solution.py:16
  26.1 8.1 %collective-permute-done.2 = f32[64,1536]{1,0:T(8,128)} collective-permute-done((f32[64,1536]{1,0:T(8,128)S(1)}, f32[64,1536]{1,0:T(8,128)}, u32[]{:S(2)}, u32[]{:S(2)}) %collective-permute-start.2) | collective-permute-done | bytes 393248 | tf_op jit(solution)/shard_map/ppermute | solution.py:16
  34.2 1.1 %broadcast_select_fusion.3 = (f32[64,1536]{1,0:T(8,128)S(1)}, f32[64,1536]{1,0:T(8,128)S(1)}) fusion(f32[64,1536]{1,0:T(8,128)} %collective-permute-done.2, f32[64,1536]{1,0:T(8,128)S(1)} %collective-permute-done.3, pred[]{:T(512)S(6)} %ne.75), kind=kLoop, calls=%fused_computation.35 | loop fusion | flops 196608 | bytes 1572865 | tf_op jit(solution)/shard_map/jit(_where)/select_n | solution.py:60
  35.3 0.2 fusion.35
  35.4 0.5 exponential_reduce_fusion
  36.0 0.1 collective-permute-start.4
  36.0 1.1 %collective-permute-done.4 = f32[4,128]{1,0:T(4,128)S(1)} collective-permute-done((f32[4,128]{1,0:T(4,128)S(1)}, f32[4,128]{1,0:T(4,128)S(1)}, u32[]{:S(2)}, u32[]{:S(2)}) %collective-permute-start.4) | collective-permute-done | bytes 2080 | tf_op jit(solution)/shard_map/ppermute | solution.py:20
  37.2 1.5 %collective-permute-start.5 = (f32[2,4,128]{2,1,0:T(4,128)S(1)}, f32[2,4,128]{2,1,0:T(4,128)S(1)}, u32[]{:S(2)}, u32[]{:S(2)}) collective-permute-start(f32[2,4,128]{2,1,0:T(4,128)S(1)} %pad_maximum_fusion), channel_id=1, source_target_pairs={{0,4},{2,6},{4,0},{6,2},{8,12},{10,14},{12,8},{14,10},{16,20},{18,... | collective-permute-start | bytes 12296 | tf_op jit(solution)/shard_map/ppermute | solution.py:20
  38.7 1.6 %collective-permute-start.6 = (f32[2,4,128]{2,1,0:T(4,128)S(1)}, f32[2,4,128]{2,1,0:T(4,128)S(1)}, u32[]{:S(2)}, u32[]{:S(2)}) collective-permute-start(f32[2,4,128]{2,1,0:T(4,128)S(1)} %pad_maximum_fusion), channel_id=1, source_target_pairs={{0,8},{2,10},{4,12},{6,14},{8,0},{10,2},{12,4},{14,6},{16,24},{18,... | collective-permute-start | bytes 12296 | tf_op jit(solution)/shard_map/ppermute | solution.py:20
  40.3 0.4 collective-permute-start.7
  40.7 2.6 %collective-permute-start.8 = (f32[2,4,128]{2,1,0:T(4,128)S(1)}, f32[2,4,128]{2,1,0:T(4,128)S(1)}, u32[]{:S(2)}, u32[]{:S(2)}) collective-permute-start(f32[2,4,128]{2,1,0:T(4,128)S(1)} %pad_maximum_fusion), channel_id=1, source_target_pairs={{0,16},{2,18},{4,20},{6,22},{8,24},{10,26},{12,28},{14,30},{16,0},... | collective-permute-start | bytes 12296 | tf_op jit(solution)/shard_map/ppermute | solution.py:20
  43.3 1.3 %collective-permute-start.9 = (f32[2,4,128]{2,1,0:T(4,128)S(1)}, f32[2,4,128]{2,1,0:T(4,128)S(1)}, u32[]{:S(2)}, u32[]{:S(2)}) collective-permute-start(f32[2,4,128]{2,1,0:T(4,128)S(1)} %pad_maximum_fusion), channel_id=1, source_target_pairs={{0,20},{2,22},{4,16},{6,18},{8,28},{10,30},{12,24},{14,26},{16,4},... | collective-permute-start | bytes 12296 | tf_op jit(solution)/shard_map/ppermute | solution.py:20
  44.6 0.0 collective-permute-done.5
  44.6 3.6 %collective-permute-start.10 = (f32[2,4,128]{2,1,0:T(4,128)S(1)}, f32[2,4,128]{2,1,0:T(4,128)S(1)}, u32[]{:S(2)}, u32[]{:S(2)}) collective-permute-start(f32[2,4,128]{2,1,0:T(4,128)S(1)} %pad_maximum_fusion), channel_id=1, source_target_pairs={{0,24},{2,26},{4,28},{6,30},{8,16},{10,18},{12,20},{14,22},{16,8},... | collective-permute-start | bytes 12296 | tf_op jit(solution)/shard_map/ppermute | solution.py:20
  48.2 0.0 collective-permute-done.6
  48.2 0.1 collective-permute-start.11
  48.3 0.0 collective-permute-done.7
  48.4 0.3 collective-permute-done.9
  48.7 1.3 %collective-permute-done.10 = f32[2,4,128]{2,1,0:T(4,128)S(1)} collective-permute-done((f32[2,4,128]{2,1,0:T(4,128)S(1)}, f32[2,4,128]{2,1,0:T(4,128)S(1)}, u32[]{:S(2)}, u32[]{:S(2)}) %collective-permute-start.10) | collective-permute-done | bytes 4128 | tf_op jit(solution)/shard_map/ppermute | solution.py:20
  50.0 4.5 %collective-permute-done.11 = f32[2,4,128]{2,1,0:T(4,128)S(1)} collective-permute-done((f32[2,4,128]{2,1,0:T(4,128)S(1)}, f32[2,4,128]{2,1,0:T(4,128)S(1)}, u32[]{:S(2)}, u32[]{:S(2)}) %collective-permute-start.11) | collective-permute-done | bytes 4128 | tf_op jit(solution)/shard_map/ppermute | solution.py:20
  54.7 0.5 subtract_add_fusion
  55.2 0.3 fusion.15.delta_ref
  55.5 1.6 %collective-permute-start.15 = (bf16[128,1536]{1,0:T(8,128)(2,1)S(1)}, bf16[128,1536]{1,0:T(8,128)(2,1)S(1)}, u32[]{:S(2)}, u32[]{:S(2)}) collective-permute-start(bf16[128,1536]{1,0:T(8,128)(2,1)S(1)} %fusion.15.delta_ref), channel_id=1, source_target_pairs={{0,1},{1,0},{2,3},{3,2},{4,5},{5,4},{6,7},{7,6},{8,9},{9,8},{10,11... | collective-permute-start | bytes 1179656 | tf_op jit(solution)/shard_map/ppermute | solution.py:16
  57.0 2.6 %copy-done.2 = bf16[1792,1536]{1,0:T(8,128)(2,1)S(1)} copy-done((bf16[1792,1536]{1,0:T(8,128)(2,1)S(1)}, bf16[1792,1536]{1,0:T(8,128)(2,1)}, u32[]{:S(2)}) %copy-start.2) | copy-done | bytes 5505048
  59.6 1.6 %partial_gradient.2 = (bf16[4,224,128]{2,1,0:T(8,128)(2,1)S(1)}, f32[4,224,128]{2,1,0:T(8,128)S(1)}) custom-call(s32[1]{0:T(128)} %bitcast.13.core_ref, bf16[1792,1536]{1,0:T(8,128)(2,1)S(1)} %copy-done.2, bf16[128,1536]{1,0:T(8,128)(2,1)S(1)} %fusion.15.delta_ref), custom_call_target="tpu_custom_call" | custom-call | flops 704643072 | bytes 5898240 | tf_op jit(solution)/shard_map/partial_gradient/pallas_call | solution.py:96
  61.2 0.1 collective-permute-start.12
  61.3 2.6 %collective-permute-done.15.delta_ref = bf16[128,1536]{1,0:T(8,128)(2,1)S(1)} collective-permute-done((bf16[128,1536]{1,0:T(8,128)(2,1)S(1)}, bf16[128,1536]{1,0:T(8,128)(2,1)S(1)}, u32[]{:S(2)}, u32[]{:S(2)}) %collective-permute-start.15) | collective-permute-done | bytes 393248 | tf_op jit(solution)/shard_map/ppermute | solution.py:16
  63.9 2.6 %copy-done.3 = bf16[1792,1536]{1,0:T(8,128)(2,1)S(1)} copy-done((bf16[1792,1536]{1,0:T(8,128)(2,1)S(1)}, bf16[1792,1536]{1,0:T(8,128)(2,1)}, u32[]{:S(2)}) %copy-start.3) | copy-done | bytes 5505048
  66.5 1.6 %partial_gradient.3 = (bf16[4,224,128]{2,1,0:T(8,128)(2,1)S(1)}, f32[4,224,128]{2,1,0:T(8,128)S(1)}) custom-call(s32[1]{0:T(128)} %bitcast.13.core_ref, bf16[1792,1536]{1,0:T(8,128)(2,1)S(1)} %copy-done.3, bf16[128,1536]{1,0:T(8,128)(2,1)S(1)} %collective-permute-done.15.delta_ref), custom_call_target="tpu_custom_call" | custom-call | flops 704643072 | bytes 5898240 | tf_op jit(solution)/shard_map/partial_gradient/pallas_call | solution.py:96
  68.0 0.1 collective-permute-start.16
  68.1 0.0 collective-permute-done.12
  68.1 0.1 convert_add_fusion.1
  68.2 0.6 collective-permute-start.13
  68.8 0.8 collective-permute-done.16
  69.6 0.1 convert_add_fusion
  69.7 0.8 collective-permute-start.17
  70.5 3.8 %collective-permute-done.13 = bf16[2,224,128]{2,1,0:T(8,128)(2,1)S(1)} collective-permute-done((bf16[2,224,128]{2,1,0:T(8,128)(2,1)S(1)}, bf16[2,224,128]{2,1,0:T(8,128)(2,1)S(1)}, u32[]{:S(2)}, u32[]{:S(2)}) %collective-permute-start.13) | collective-permute-done | bytes 114720 | tf_op jit(solution)/shard_map/ppermute | solution.py:20
  74.3 2.0 %collective-permute-done.17 = bf16[2,224,128]{2,1,0:T(8,128)(2,1)S(1)} collective-permute-done((bf16[2,224,128]{2,1,0:T(8,128)(2,1)S(1)}, bf16[2,224,128]{2,1,0:T(8,128)(2,1)S(1)}, u32[]{:S(2)}, u32[]{:S(2)}) %collective-permute-start.17) | collective-permute-done | bytes 114720 | tf_op jit(solution)/shard_map/ppermute | solution.py:20
  76.3 0.1 collective-permute-start.18
  76.4 2.1 %collective-permute-start.14 = (bf16[1,224,128]{2,1,0:T(8,128)(2,1)S(1)}, bf16[1,224,128]{2,1,0:T(8,128)(2,1)S(1)}, u32[]{:S(2)}, u32[]{:S(2)}) collective-permute-start(bf16[1,224,128]{2,1,0:T(8,128)(2,1)S(1)} %dynamic-slice_convert_fusion.1), channel_id=1, source_target_pairs={{0,8},{2,10},{4,12},{6,14},{8,0},{10,2},{12,4},{14,6},{16,24},{18,... | collective-permute-start | bytes 172040 | tf_op jit(solution)/shard_map/ppermute | solution.py:20
  78.5 2.1 %collective-permute-done.18 = bf16[1,224,128]{2,1,0:T(8,128)(2,1)S(1)} collective-permute-done((bf16[1,224,128]{2,1,0:T(8,128)(2,1)S(1)}, bf16[1,224,128]{2,1,0:T(8,128)(2,1)S(1)}, u32[]{:S(2)}, u32[]{:S(2)}) %collective-permute-start.18) | collective-permute-done | bytes 57376 | tf_op jit(solution)/shard_map/ppermute | solution.py:20
  80.6 1.6 %collective-permute-start.19 = (bf16[224,128]{1,0:T(8,128)(2,1)S(1)}, bf16[224,128]{1,0:T(8,128)(2,1)S(1)}, u32[]{:S(2)}, u32[]{:S(2)}) collective-permute-start(bf16[224,128]{1,0:T(8,128)(2,1)S(1)} %fusion.24), channel_id=1, source_target_pairs={{0,1},{1,0},{2,3},{3,2},{4,5},{5,4},{6,7},{7,6},{8,9},{9,8},{10,11... | collective-permute-start | bytes 172040 | tf_op jit(solution)/shard_map/ppermute | solution.py:16
  82.2 0.0 collective-permute-done.14
  82.2 2.6 %collective-permute-done.19 = bf16[224,128]{1,0:T(8,128)(2,1)S(1)} collective-permute-done((bf16[224,128]{1,0:T(8,128)(2,1)S(1)}, bf16[224,128]{1,0:T(8,128)(2,1)S(1)}, u32[]{:S(2)}, u32[]{:S(2)}) %collective-permute-start.19) | collective-permute-done | bytes 57376 | tf_op jit(solution)/shard_map/ppermute | solution.py:16
  84.9 0.1 collective-permute-start.20
  85.0 4.1 %convolution_convert_fusion = bf16[1792,1536]{1,0:T(8,128)(2,1)} fusion(bf16[64,1792]{1,0:T(8,128)(2,1)S(1)} %get-tuple-element.23, bf16[64,1792]{1,0:T(8,128)(2,1)S(1)} %get-tuple-element.22, bf16[128,1792]{1,0:T(8,128)(2,1)S(1)} %constant_dynamic-slice_fusion, bf16[128,1536]{1,0:T(8,128)(2,1)S(1)} %collective-permute-done.15.delta_ref, ...), kind=kOutput, calls=%fused_computation | convolution fusion | flops 1416364032 | bytes 7208960 | tf_op jit(solution)/shard_map/dot_general | solution.py:200
  89.1 1.2 %collective-permute-done.20 = bf16[224,128]{1,0:T(8,128)(2,1)S(1)} collective-permute-done((bf16[224,128]{1,0:T(8,128)(2,1)S(1)}, bf16[224,128]{1,0:T(8,128)(2,1)S(1)}, u32[]{:S(2)}, u32[]{:S(2)}) %collective-permute-start.20) | collective-permute-done | bytes 57376 | tf_op jit(solution)/shard_map/ppermute | solution.py:193
  90.2 0.7 fusion.23
  (46 shorter events, 0.5 us)
Async XLA Ops:
  1.6 8.6 %collective-permute-start = (bf16[64,1792]{1,0:T(8,128)(2,1)S(1)}, bf16[64,1792]{1,0:T(8,128)(2,1)S(1)}, u32[]{:S(2)}, u32[]{:S(2)}) collective-permute-start(bf16[64,1792]{1,0:T(8,128)(2,1)S(1)} %dynamic_slice.32), channel_id=1, source_target_pairs={{0,1},{1,0},{2,3},{3,2},{4,5},{5,4},{6,7},{7,6},{8,9},{9,8},{10,11... | collective-permute-start | bytes 688136 | tf_op jit(solution)/shard_map/ppermute | solution.py:16
  4.7 5.1 %copy-start.5 = (bf16[128,3584]{1,0:T(8,128)(2,1)S(1)}, bf16[128,3584]{1,0:T(8,128)(2,1)}, u32[]{:S(2)}) copy-start(bf16[128,3584]{1,0:T(8,128)(2,1)} %param.5) | copy-start | bytes 2752516
  7.3 2.4 %copy-start = (bf16[1792,1536]{1,0:T(8,128)(2,1)}, bf16[1792,1536]{1,0:T(8,128)(2,1)S(1)}, u32[]{:S(2)}) copy-start(bf16[1792,1536]{1,0:T(8,128)(2,1)S(1)} %load_head.1.head_ref) | copy-start | bytes 16515076
  9.8 5.9 %copy-start.1 = (bf16[1792,1536]{1,0:T(8,128)(2,1)S(1)}, bf16[1792,1536]{1,0:T(8,128)(2,1)}, u32[]{:S(2)}) copy-start(bf16[1792,1536]{1,0:T(8,128)(2,1)} %copy-done) | copy-start | bytes 16515076
  10.3 5.5 %collective-permute-start.1 = (bf16[64,1792]{1,0:T(8,128)(2,1)S(1)}, bf16[64,1792]{1,0:T(8,128)(2,1)S(1)}, u32[]{:S(2)}, u32[]{:S(2)}) collective-permute-start(bf16[64,1792]{1,0:T(8,128)(2,1)S(1)} %collective-permute-done), channel_id=1, source_target_pairs={{0,2},{2,0},{4,6},{6,4},{8,10},{10,8},{12,14},{14,12},{16,18},{18,... | collective-permute-start | bytes 688136 | tf_op jit(solution)/shard_map/ppermute | solution.py:20
  14.1 5.0 %copy-start.7 = (s32[1,16]{1,0:T(1,128)S(1)}, s32[1,16]{1,0:T(1,128)}, u32[]{:S(2)}) copy-start(s32[1,16]{1,0:T(1,128)} %param.8) | copy-start | bytes 196
  14.1 12.0 %collective-permute-start.3 = (f32[64,1536]{1,0:T(8,128)S(1)}, f32[64,1536]{1,0:T(8,128)S(1)}, u32[]{:S(2)}, u32[]{:S(2)}) collective-permute-start(f32[64,1536]{1,0:T(8,128)S(1)} %fusion.39), channel_id=1, source_target_pairs={{0,1},{1,0},{2,3},{3,2},{4,5},{5,4},{6,7},{7,6},{8,9},{9,8},{10,11... | collective-permute-start | bytes 1179656 | tf_op jit(solution)/shard_map/ppermute | solution.py:16
  16.8 18.7 %copy-start.4 = (bf16[128,1536]{1,0:T(8,128)(2,1)S(1)}, bf16[128,1536]{1,0:T(8,128)(2,1)}, u32[]{:S(2)}) copy-start(bf16[128,1536]{1,0:T(8,128)(2,1)} %param.7) | copy-start | bytes 1179652
  16.8 17.4 %collective-permute-start.2 = (f32[64,1536]{1,0:T(8,128)S(1)}, f32[64,1536]{1,0:T(8,128)}, u32[]{:S(2)}, u32[]{:S(2)}) collective-permute-start(f32[64,1536]{1,0:T(8,128)S(1)} %fusion.38), channel_id=1, source_target_pairs={{0,1},{1,0},{2,3},{3,2},{4,5},{5,4},{6,7},{7,6},{8,9},{9,8},{10,11... | collective-permute-start | bytes 1179656 | tf_op jit(solution)/shard_map/ppermute | solution.py:16
  36.0 1.2 %collective-permute-start.4 = (f32[4,128]{1,0:T(4,128)S(1)}, f32[4,128]{1,0:T(4,128)S(1)}, u32[]{:S(2)}, u32[]{:S(2)}) collective-permute-start(f32[4,128]{1,0:T(4,128)S(1)} %get-tuple-element.47), channel_id=1, source_target_pairs={{0,2},{2,0},{4,6},{6,4},{8,10},{10,8},{12,14},{14,12},{16,18},{18,... | collective-permute-start | bytes 6152 | tf_op jit(solution)/shard_map/ppermute | solution.py:20
  37.2 7.4 %collective-permute-start.5 = (f32[2,4,128]{2,1,0:T(4,128)S(1)}, f32[2,4,128]{2,1,0:T(4,128)S(1)}, u32[]{:S(2)}, u32[]{:S(2)}) collective-permute-start(f32[2,4,128]{2,1,0:T(4,128)S(1)} %pad_maximum_fusion), channel_id=1, source_target_pairs={{0,4},{2,6},{4,0},{6,2},{8,12},{10,14},{12,8},{14,10},{16,20},{18,... | collective-permute-start | bytes 12296 | tf_op jit(solution)/shard_map/ppermute | solution.py:20
  38.7 9.5 %collective-permute-start.6 = (f32[2,4,128]{2,1,0:T(4,128)S(1)}, f32[2,4,128]{2,1,0:T(4,128)S(1)}, u32[]{:S(2)}, u32[]{:S(2)}) collective-permute-start(f32[2,4,128]{2,1,0:T(4,128)S(1)} %pad_maximum_fusion), channel_id=1, source_target_pairs={{0,8},{2,10},{4,12},{6,14},{8,0},{10,2},{12,4},{14,6},{16,24},{18,... | collective-permute-start | bytes 12296 | tf_op jit(solution)/shard_map/ppermute | solution.py:20
  40.3 8.1 %collective-permute-start.7 = (f32[2,4,128]{2,1,0:T(4,128)S(1)}, f32[2,4,128]{2,1,0:T(4,128)S(1)}, u32[]{:S(2)}, u32[]{:S(2)}) collective-permute-start(f32[2,4,128]{2,1,0:T(4,128)S(1)} %pad_maximum_fusion), channel_id=1, source_target_pairs={{0,12},{2,14},{4,8},{6,10},{8,4},{10,6},{12,0},{14,2},{16,28},{18,... | collective-permute-start | bytes 12296 | tf_op jit(solution)/shard_map/ppermute | solution.py:20
  40.7 7.7 %collective-permute-start.8 = (f32[2,4,128]{2,1,0:T(4,128)S(1)}, f32[2,4,128]{2,1,0:T(4,128)S(1)}, u32[]{:S(2)}, u32[]{:S(2)}) collective-permute-start(f32[2,4,128]{2,1,0:T(4,128)S(1)} %pad_maximum_fusion), channel_id=1, source_target_pairs={{0,16},{2,18},{4,20},{6,22},{8,24},{10,26},{12,28},{14,30},{16,0},... | collective-permute-start | bytes 12296 | tf_op jit(solution)/shard_map/ppermute | solution.py:20
  43.3 5.4 %collective-permute-start.9 = (f32[2,4,128]{2,1,0:T(4,128)S(1)}, f32[2,4,128]{2,1,0:T(4,128)S(1)}, u32[]{:S(2)}, u32[]{:S(2)}) collective-permute-start(f32[2,4,128]{2,1,0:T(4,128)S(1)} %pad_maximum_fusion), channel_id=1, source_target_pairs={{0,20},{2,22},{4,16},{6,18},{8,28},{10,30},{12,24},{14,26},{16,4},... | collective-permute-start | bytes 12296 | tf_op jit(solution)/shard_map/ppermute | solution.py:20
  44.6 5.4 %collective-permute-start.10 = (f32[2,4,128]{2,1,0:T(4,128)S(1)}, f32[2,4,128]{2,1,0:T(4,128)S(1)}, u32[]{:S(2)}, u32[]{:S(2)}) collective-permute-start(f32[2,4,128]{2,1,0:T(4,128)S(1)} %pad_maximum_fusion), channel_id=1, source_target_pairs={{0,24},{2,26},{4,28},{6,30},{8,16},{10,18},{12,20},{14,22},{16,8},... | collective-permute-start | bytes 12296 | tf_op jit(solution)/shard_map/ppermute | solution.py:20
  48.2 6.3 %collective-permute-start.11 = (f32[2,4,128]{2,1,0:T(4,128)S(1)}, f32[2,4,128]{2,1,0:T(4,128)S(1)}, u32[]{:S(2)}, u32[]{:S(2)}) collective-permute-start(f32[2,4,128]{2,1,0:T(4,128)S(1)} %pad_maximum_fusion), channel_id=1, source_target_pairs={{0,28},{2,30},{4,24},{6,26},{8,20},{10,22},{12,16},{14,18},{16,12}... | collective-permute-start | bytes 12296 | tf_op jit(solution)/shard_map/ppermute | solution.py:20
  55.2 12.9 %copy-start.6 = (f32[128]{0:T(128)}, f32[128]{0:T(128)S(1)}, u32[]{:S(2)}) copy-start(f32[128]{0:T(128)S(1)} %get-tuple-element.17) | copy-start | bytes 1540
  55.5 8.4 %collective-permute-start.15 = (bf16[128,1536]{1,0:T(8,128)(2,1)S(1)}, bf16[128,1536]{1,0:T(8,128)(2,1)S(1)}, u32[]{:S(2)}, u32[]{:S(2)}) collective-permute-start(bf16[128,1536]{1,0:T(8,128)(2,1)S(1)} %fusion.15.delta_ref), channel_id=1, source_target_pairs={{0,1},{1,0},{2,3},{3,2},{4,5},{5,4},{6,7},{7,6},{8,9},{9,8},{10,11... | collective-permute-start | bytes 1179656 | tf_op jit(solution)/shard_map/ppermute | solution.py:16
  57.0 2.6 %copy-start.2 = (bf16[1792,1536]{1,0:T(8,128)(2,1)S(1)}, bf16[1792,1536]{1,0:T(8,128)(2,1)}, u32[]{:S(2)}) copy-start(bf16[1792,1536]{1,0:T(8,128)(2,1)} %copy-done) | copy-start | bytes 16515076
  61.2 6.9 %collective-permute-start.12 = (bf16[4,224,128]{2,1,0:T(8,128)(2,1)S(1)}, bf16[4,224,128]{2,1,0:T(8,128)(2,1)S(1)}, u32[]{:S(2)}, u32[]{:S(2)}) collective-permute-start(bf16[4,224,128]{2,1,0:T(8,128)(2,1)S(1)} %get-tuple-element.9), channel_id=1, source_target_pairs={{0,2},{2,0},{4,6},{6,4},{8,10},{10,8},{12,14},{14,12},{16,18},{18,... | collective-permute-start | bytes 688136 | tf_op jit(solution)/shard_map/ppermute | solution.py:20
  63.9 2.6 %copy-start.3 = (bf16[1792,1536]{1,0:T(8,128)(2,1)S(1)}, bf16[1792,1536]{1,0:T(8,128)(2,1)}, u32[]{:S(2)}) copy-start(bf16[1792,1536]{1,0:T(8,128)(2,1)} %copy-done) | copy-start | bytes 16515076
  68.0 1.6 %collective-permute-start.16 = (bf16[4,224,128]{2,1,0:T(8,128)(2,1)S(1)}, bf16[4,224,128]{2,1,0:T(8,128)(2,1)S(1)}, u32[]{:S(2)}, u32[]{:S(2)}) collective-permute-start(bf16[4,224,128]{2,1,0:T(8,128)(2,1)S(1)} %get-tuple-element.11), channel_id=1, source_target_pairs={{0,2},{2,0},{4,6},{6,4},{8,10},{10,8},{12,14},{14,12},{16,18},{18,... | collective-permute-start | bytes 688136 | tf_op jit(solution)/shard_map/ppermute | solution.py:20
  68.2 6.0 %collective-permute-start.13 = (bf16[2,224,128]{2,1,0:T(8,128)(2,1)S(1)}, bf16[2,224,128]{2,1,0:T(8,128)(2,1)S(1)}, u32[]{:S(2)}, u32[]{:S(2)}) collective-permute-start(bf16[2,224,128]{2,1,0:T(8,128)(2,1)S(1)} %fusion.16), channel_id=1, source_target_pairs={{0,4},{2,6},{4,0},{6,2},{8,12},{10,14},{12,8},{14,10},{16,20},{18,... | collective-permute-start | bytes 344072 | tf_op jit(solution)/shard_map/ppermute | solution.py:20
  69.7 6.6 %collective-permute-start.17 = (bf16[2,224,128]{2,1,0:T(8,128)(2,1)S(1)}, bf16[2,224,128]{2,1,0:T(8,128)(2,1)S(1)}, u32[]{:S(2)}, u32[]{:S(2)}) collective-permute-start(bf16[2,224,128]{2,1,0:T(8,128)(2,1)S(1)} %fusion.17), channel_id=1, source_target_pairs={{0,4},{2,6},{4,0},{6,2},{8,12},{10,14},{12,8},{14,10},{16,20},{18,... | collective-permute-start | bytes 344072 | tf_op jit(solution)/shard_map/ppermute | solution.py:20
  76.3 4.2 %collective-permute-start.18 = (bf16[1,224,128]{2,1,0:T(8,128)(2,1)S(1)}, bf16[1,224,128]{2,1,0:T(8,128)(2,1)S(1)}, u32[]{:S(2)}, u32[]{:S(2)}) collective-permute-start(bf16[1,224,128]{2,1,0:T(8,128)(2,1)S(1)} %dynamic-slice_convert_fusion), channel_id=1, source_target_pairs={{0,8},{2,10},{4,12},{6,14},{8,0},{10,2},{12,4},{14,6},{16,24},{18,... | collective-permute-start | bytes 172040 | tf_op jit(solution)/shard_map/ppermute | solution.py:20
  76.4 5.7 %collective-permute-start.14 = (bf16[1,224,128]{2,1,0:T(8,128)(2,1)S(1)}, bf16[1,224,128]{2,1,0:T(8,128)(2,1)S(1)}, u32[]{:S(2)}, u32[]{:S(2)}) collective-permute-start(bf16[1,224,128]{2,1,0:T(8,128)(2,1)S(1)} %dynamic-slice_convert_fusion.1), channel_id=1, source_target_pairs={{0,8},{2,10},{4,12},{6,14},{8,0},{10,2},{12,4},{14,6},{16,24},{18,... | collective-permute-start | bytes 172040 | tf_op jit(solution)/shard_map/ppermute | solution.py:20
  80.6 4.2 %collective-permute-start.19 = (bf16[224,128]{1,0:T(8,128)(2,1)S(1)}, bf16[224,128]{1,0:T(8,128)(2,1)S(1)}, u32[]{:S(2)}, u32[]{:S(2)}) collective-permute-start(bf16[224,128]{1,0:T(8,128)(2,1)S(1)} %fusion.24), channel_id=1, source_target_pairs={{0,1},{1,0},{2,3},{3,2},{4,5},{5,4},{6,7},{7,6},{8,9},{9,8},{10,11... | collective-permute-start | bytes 172040 | tf_op jit(solution)/shard_map/ppermute | solution.py:16
  84.9 5.3 %collective-permute-start.20 = (bf16[224,128]{1,0:T(8,128)(2,1)S(1)}, bf16[224,128]{1,0:T(8,128)(2,1)S(1)}, u32[]{:S(2)}, u32[]{:S(2)}) collective-permute-start(bf16[224,128]{1,0:T(8,128)(2,1)S(1)} %fusion.25), channel_id=1, source_target_pairs={{0,16},{2,18},{4,20},{6,22},{8,24},{10,26},{12,28},{14,30},{16,0},... | collective-permute-start | bytes 172040 | tf_op jit(solution)/shard_map/ppermute | solution.py:193

commit v4 on v3

--- a/solution.py
+++ b/solution.py
@@ -9,7 +9,7 @@
 
 
 loss_scale = 1024.0
-VMEM_LIMIT = 8 << 20
+VMEM_LIMIT = 16 << 20
 
 
 def shift_tok(x, offset, size):
@@ -18,25 +18,6 @@
 
 def swap_vocab(x, bit, size):
     return lax.ppermute(x, "vocab", [(i, i ^ bit) for i in range(size)])
-
-
-def load_kernel(head_ref, out_ref, sem):
-    copy = pltpu.make_async_copy(head_ref, out_ref, sem)
-    copy.start()
-    copy.wait()
-
-
-def load(head):
-    return pl.pallas_call(
-        load_kernel,
-        out_shape=pltpu.VMEM(head.shape, head.dtype),
-        in_specs=[pl.BlockSpec(memory_space=pl.ANY)],
-        out_specs=pl.BlockSpec(memory_space=pl.ANY),
-        scratch_shapes=[pltpu.SemaphoreType.DMA],
-        compiler_params=pltpu.CompilerParams(vmem_limit_bytes=1 << 20),
-        cost_estimate=pl.CostEstimate(flops=0, bytes_accessed=2 * head.size, transcendentals=0),
-        name="load_head",
-    )(pltpu.with_memory_space_constraint(head, pltpu.HBM))
 
 
 def pick(x, index, axis=0):
@@ -61,25 +42,30 @@
     )
 
 
-def gather_vocab(stats, size):
-    pair = jnp.stack([stats, swap_vocab(stats, 1, size)])
-    pairs = [pair] + [swap_vocab(pair, bit, size) for bit in range(2, size, 2)]
-    return jnp.concatenate(pairs, axis=0)
-
-
-def tree_sum(x):
-    while x.shape[0] > 1:
-        half = x.shape[0] // 2
-        x = x[:half] + x[half:]
-    return x[0]
-
-
-def gradient_kernel(core_ref, head_ref, delta_ref, send_ref, keep_ref):
+def gather_vocab(stats, vocab_index, size):
+    gathered = stats[None]
+    bit = 1
+    while bit < size:
+        other = swap_vocab(gathered, bit, size)
+        gathered = in_order(gathered, other, (vocab_index & bit) != 0)
+        bit *= 2
+    return gathered
+
+
+def gradient_kernel(core_ref, head_ref, delta_ref, send_ref, keep_ref, held_ref, sems):
     upper = core_ref[0] == 1
     pairs, rows, _ = send_ref.shape
+    parts = [pl.ds(2 * k * rows, 2 * rows) for k in range(pairs)]
+    copies = [
+        pltpu.make_async_copy(head_ref.at[part], held_ref.at[part], sems.at[k])
+        for k, part in enumerate(parts)
+    ]
+    for copy in copies:
+        copy.start()
     for k in range(pairs):
+        copies[k].wait()
         block = lax.dot_general(
-            head_ref[2 * k * rows : 2 * (k + 1) * rows, :],
+            held_ref[2 * k * rows : 2 * (k + 1) * rows, :],
             delta_ref[...],
             (((1,), (1,)), ((), ())),
             preferred_element_type=jnp.float32,
@@ -96,8 +82,16 @@
     return pl.pallas_call(
         gradient_kernel,
         out_shape=(pltpu.VMEM(shape, jnp.bfloat16), pltpu.VMEM(shape, jnp.float32)),
-        in_specs=[pl.BlockSpec(memory_space=pltpu.SMEM), in_vmem, in_vmem],
+        in_specs=[
+            pl.BlockSpec(memory_space=pltpu.SMEM),
+            pl.BlockSpec(memory_space=pltpu.HBM),
+            in_vmem,
+        ],
         out_specs=(in_vmem, in_vmem),
+        scratch_shapes=[
+            pltpu.VMEM(head.shape, head.dtype),
+            pltpu.SemaphoreType.DMA((run // 2,)),
+        ],
         compiler_params=pltpu.CompilerParams(vmem_limit_bytes=VMEM_LIMIT),
         cost_estimate=pl.CostEstimate(
             flops=2 * head.size * delta.shape[0],
@@ -107,7 +101,7 @@
         name="partial_gradient",
     )(
         core.reshape(1),
-        pltpu.with_memory_space_constraint(head, pltpu.VMEM),
+        pltpu.with_memory_space_constraint(head, pltpu.HBM),
         pltpu.with_memory_space_constraint(delta, pltpu.VMEM),
     )
 
@@ -134,7 +128,6 @@
     rows, column_count = head.shape
     run = vocab_size // tok_size
     half = token_count // 2
-    head = load(head)
     core = vocab_index % 2
 
     def columns_of(index, first, count):
@@ -144,6 +137,9 @@
         shift_tok(columns_of((tok_index + d) % tok_size, core * half, half), d, tok_size)
         for d in range(1, tok_size)
     ]
+    own = columns_of(tok_index, 0, token_count)
+    logits = jnp.dot(own, head, preferred_element_type=jnp.float32)
+    near, logits = lax.optimization_barrier((near, logits))
     far = [swap_vocab(x, 1, vocab_size) for x in near]
     returned = []
     for d in range(1, tok_size):
@@ -154,8 +150,6 @@
             jnp.dot(far[d - 1], head, preferred_element_type=jnp.float32), -d, tok_size
         )
         returned.append((first, second))
-    own = columns_of(tok_index, 0, token_count)
-    logits = lax.optimization_barrier(jnp.dot(own, head, preferred_element_type=jnp.float32))
     for first, second in returned:
         logits = logits + in_order(first, second, core != 0)
 
@@ -169,11 +163,13 @@
     local_mass = jnp.sum(kept, axis=1)
     local_part = jnp.sum(jnp.where(listed, teacher_f * (jnp.log(teacher_f) - logits), 0.0), axis=1)
 
-    stats = gather_vocab(jnp.stack([local_top, local_sum, local_mass, local_part]), vocab_size)
+    stats = gather_vocab(
+        jnp.stack([local_top, local_sum, local_mass, local_part]), vocab_index, vocab_size
+    )
     tops = stats[:, 0]
     global_top = jnp.max(tops, axis=0)
-    total_sum = tree_sum(stats[:, 1] * jnp.exp(tops - global_top[None, :]))
-    total_mass, total_part = tree_sum(stats[:, 2]), tree_sum(stats[:, 3])
+    total_sum = jnp.sum(stats[:, 1] * jnp.exp(tops - global_top[None, :]), axis=0)
+    total_mass, total_part = jnp.sum(stats[:, 2], axis=0), jnp.sum(stats[:, 3], axis=0)
     lse = global_top + jnp.log(total_sum)
     kl = total_part / total_mass - jnp.log(total_mass) + lse
     student = jnp.exp(logits - lse[:, None])
@@ -181,17 +177,20 @@
 
     deltas = [delta] + [shift_tok(delta, d, tok_size) for d in range(1, tok_size)]
     sums = [halve(*gradient(core, head, x, run), vocab_index, vocab_size) for x in deltas]
-    blocks = [sums[0]] + [
-        shift_tok(sums[d].astype(jnp.bfloat16), -d, tok_size).astype(jnp.float32)
-        for d in range(1, tok_size)
-    ]
-    blocks = jnp.stack(blocks)
     high = vocab_index // run
-    total = pick(blocks, (high - tok_index) % tok_size)
-    for d in range(1, tok_size):
-        send = pick(blocks, (high + d - tok_index) % tok_size).astype(jnp.bfloat16)
+    apart = (tok_index - high) % tok_size
+    total = jnp.where(apart == 0, sums[0], 0.0)
+    sums = jnp.stack([x.astype(jnp.bfloat16) for x in sums])
+    for k in range(tok_size):
+        pairs = []
+        for v in range(vocab_size):
+            for t in range(tok_size):
+                d = (k + t - v // run) % tok_size
+                target = (t * run + v % run) * tok_size + (t - d) % tok_size
+                if target != v * tok_size + t:
+                    pairs.append((v * tok_size + t, target))
         total = total + lax.ppermute(
-            send, "vocab", [(i, (i + d * run) % vocab_size) for i in range(vocab_size)]
+            pick(sums, (k + apart) % tok_size), ("vocab", "tok"), pairs
         ).astype(jnp.float32)
     grad_hidden = total.T
 

time: 91.2 us -> 84 us (0.921)
  waiting for transfers between devices: 37.7 us -> 30.3 us
  local copies, waits for them, and re-layouts: 8.74 us -> 2.26 us
  Pallas kernels: 5.81 us -> 9.65 us
  starting transfers between devices: 23.3 us -> 26.3 us
    unnamed x23 -> x8, local copies, waits for them, and re-layouts: 7.64 us -> 0.02 us
    pallas_call x2, Pallas kernels: 3.16 us -> 9.65 us  [gradient(): pl.pallas_call(gradient_kernel, out_shape=(pltpu.VMEM(shape, jnp.bfloat16...]
    ppermute x1 -> x2, starting transfers between devices: 0.07 us -> 6.1 us  [per_device(): lax.ppermute(pick(sums, (k + apart) % tok_size), ('vocab', 'tok'), pairs)]
    ppermute x15 -> x11, waiting for transfers between devices: 15.9 us -> 12.4 us  [swap_vocab(): return lax.ppermute(x, 'vocab', [(i, i ^ bit) for i in range(size)])]
    dot_general x1, matrix products: 0.88 us -> 3.71 us  [per_device(): logits = jnp.dot(own, head, preferred_element_type=jnp.float32)]
    dot_general x1, matrix products: 3.85 us -> 1.07 us  [per_device(): jnp.dot(near[d - 1], head, preferred_element_type=jnp.float32)]
    ppermute x5 -> x4, waiting for transfers between devices: 20.7 us -> 17.9 us  [shift_tok(): lax.ppermute(x, 'tok', [(i, (i + offset) % size) for i in range(size)])]
    pallas_call x1 -> x0, Pallas kernels: 2.65 us -> none  [load(): pl.pallas_call(load_kernel, out_shape=pltpu.VMEM(head.shape, head.dtype),...]
  transfers between devices with their start and end apart: 21 -> 17, of which waited for: 14 -> 12; matrix products, arithmetic and copies ran while one was open for 11% -> 14% of each run, Pallas kernels for 6% -> 12%
where the time goes in v4:
time: 84 us; the launch traced here: 83.8 us
  waiting for transfers between devices  30.3 us (36%)
  starting transfers between devices  26.3 us (31%)
  matrix products  9.92 us (12%)
  Pallas kernels  9.65 us (11%)
  other arithmetic  3.77 us (4%)
  local copies, waits for them, and re-layouts  2.26 us (3%)
  between operations  1.55 us (2%)
    ppermute x4, waiting for transfers between devices, shift_tok(): lax.ppermute(x, 'tok', [(i, (i + offset) % size) for i in range(size)])  17.9 us
    ppermute x11, starting transfers between devices, swap_vocab(): return lax.ppermute(x, 'vocab', [(i, i ^ bit) for i in range(size)])  13.2 us
    ppermute x11, waiting for transfers between devices, swap_vocab(): return lax.ppermute(x, 'vocab', [(i, i ^ bit) for i in range(size)])  12.4 us
    pallas_call x2, Pallas kernels, gradient(): pl.pallas_call(gradient_kernel, out_shape=(pltpu.VMEM(shape, jnp.bfloat16...  9.65 us
    ppermute x4, starting transfers between devices, shift_tok(): lax.ppermute(x, 'tok', [(i, (i + offset) % size) for i in range(size)])  7.04 us
    ppermute x2, starting transfers between devices, per_device(): lax.ppermute(pick(sums, (k + apart) % tok_size), ('vocab', 'tok'), pairs)  6.1 us
    dot_general x1, matrix products, per_device(): lax.dot_general(jnp.concatenate(features, axis=0), all_delta, (((0,), (0,...  4.08 us
    dot_general x1, matrix products, per_device(): logits = jnp.dot(own, head, preferred_element_type=jnp.float32)  3.71 us
  transfers between devices with their start and end apart: 17, of which 12 were waited for; matrix products, arithmetic and copies ran while one was open for 14% of the time, Pallas kernels for 12%

profile of v4, /device:TPU:0, one launch (start us, length us, event | category | flops | bytes accessed | tf_op | source)
XLA Modules:
  0.0 83.8 jit_solution(3794344691957234236)
XLA Ops:
  0.7 1.0 %dynamic_slice.31 = bf16[64,1792]{1,0:T(8,128)(2,1)S(1)} dynamic-slice(bf16[128,3584]{1,0:T(8,128)(2,1)} %param.5, s32[]{:T(128)S(6)} %select_n.185, s32[]{:T(128)S(6)} %select_n.187), dynamic_slice_sizes={64,1792} | dynamic-slice | bytes 458756 | tf_op jit(solution)/shard_map/dynamic_slice | solution.py:134
  1.6 3.0 %collective-permute-start = (bf16[64,1792]{1,0:T(8,128)(2,1)S(1)}, bf16[64,1792]{1,0:T(8,128)(2,1)S(1)}, u32[]{:S(2)}, u32[]{:S(2)}) collective-permute-start(bf16[64,1792]{1,0:T(8,128)(2,1)S(1)} %dynamic_slice.31), channel_id=1, source_target_pairs={{0,1},{1,0},{2,3},{3,2},{4,5},{5,4},{6,7},{7,6},{8,9},{9,8},{10,11... | collective-permute-start | bytes 688136 | tf_op jit(solution)/shard_map/ppermute | solution.py:16
  4.7 0.0 copy-start
  4.7 1.2 %constant_dynamic-slice_fusion = bf16[128,1792]{1,0:T(8,128)(2,1)S(1)} fusion(bf16[128,3584]{1,0:T(8,128)(2,1)} %param.5, s32[]{:T(128)S(6)} %select_n.188), kind=kLoop, calls=%fused_computation.80 | loop fusion | bytes 917508 | tf_op jit(solution)/shard_map/dynamic_slice | solution.py:134
  5.9 3.7 %fusion.35 = f32[128,1536]{1,0:T(8,128)S(1)} fusion(bf16[128,1792]{1,0:T(8,128)(2,1)S(1)} %constant_dynamic-slice_fusion, bf16[1792,1536]{1,0:T(8,128)(2,1)} %head_ref.3), kind=kOutput, calls=%fused_computation.91 | convolution fusion | flops 704643072 | bytes 6750208 | tf_op jit(solution)/shard_map/dot_general | solution.py:141
  9.6 0.0 copy-start.3
  9.6 0.7 collective-permute-done
  10.3 0.0 collective-permute-start.1
  10.3 0.0 copy-done
  10.3 1.1 %fusion.37 = f32[64,1536]{1,0:T(8,128)S(1)} fusion(bf16[64,1792]{1,0:T(8,128)(2,1)S(1)} %collective-permute-done, bf16[1792,1536]{1,0:T(8,128)(2,1)S(1)} %copy-done), kind=kOutput, calls=%fused_computation.93 | convolution fusion | flops 352321536 | bytes 6127616 | tf_op jit(solution)/shard_map/dot_general | solution.py:147
  11.3 0.0 copy-start.1
  11.3 1.8 %collective-permute-start.3 = (f32[64,1536]{1,0:T(8,128)S(1)}, f32[64,1536]{1,0:T(8,128)S(1)}, u32[]{:S(2)}, u32[]{:S(2)}) collective-permute-start(f32[64,1536]{1,0:T(8,128)S(1)} %fusion.37), channel_id=1, source_target_pairs={{0,1},{1,0},{2,3},{3,2},{4,5},{5,4},{6,7},{7,6},{8,9},{9,8},{10,11... | collective-permute-start | bytes 1179656 | tf_op jit(solution)/shard_map/ppermute | solution.py:16
  13.2 0.0 collective-permute-done.1
  13.2 1.1 %fusion.36 = f32[64,1536]{1,0:T(8,128)S(1)} fusion(bf16[64,1792]{1,0:T(8,128)(2,1)S(1)} %collective-permute-done.1, bf16[1792,1536]{1,0:T(8,128)(2,1)S(1)} %copy-done), kind=kOutput, calls=%fused_computation.92 | convolution fusion | flops 352321536 | bytes 6127616 | tf_op jit(solution)/shard_map/dot_general | solution.py:150
  14.2 0.4 collective-permute-start.2
  15.3 0.0 copy-done.3
  15.3 0.1 and_reduce_fusion
  15.4 7.9 %collective-permute-done.3 = f32[64,1536]{1,0:T(8,128)S(1)} collective-permute-done((f32[64,1536]{1,0:T(8,128)S(1)}, f32[64,1536]{1,0:T(8,128)S(1)}, u32[]{:S(2)}, u32[]{:S(2)}) %collective-permute-start.3) | collective-permute-done | bytes 393248 | tf_op jit(solution)/shard_map/ppermute | solution.py:16
  23.3 8.1 %collective-permute-done.2 = f32[64,1536]{1,0:T(8,128)} collective-permute-done((f32[64,1536]{1,0:T(8,128)S(1)}, f32[64,1536]{1,0:T(8,128)}, u32[]{:S(2)}, u32[]{:S(2)}) %collective-permute-start.2) | collective-permute-done | bytes 393248 | tf_op jit(solution)/shard_map/ppermute | solution.py:16
  31.5 1.1 %broadcast_select_fusion.3 = (f32[64,1536]{1,0:T(8,128)S(1)}, f32[64,1536]{1,0:T(8,128)S(1)}) fusion(f32[64,1536]{1,0:T(8,128)} %collective-permute-done.2, f32[64,1536]{1,0:T(8,128)S(1)} %collective-permute-done.3, pred[]{:T(512)S(6)} %ne.96), kind=kLoop, calls=%fused_computation.31 | loop fusion | flops 196608 | bytes 1572865 | tf_op jit(solution)/shard_map/jit(_where)/select_n | solution.py:41
  32.5 0.2 fusion.34
  32.7 0.0 copy-done.1
  32.7 0.5 exponential_reduce_fusion
  33.2 0.1 collective-permute-start.4
  33.3 1.1 %collective-permute-done.4 = f32[1,4,128]{2,1,0:T(4,128)S(1)} collective-permute-done((f32[1,4,128]{2,1,0:T(4,128)S(1)}, f32[1,4,128]{2,1,0:T(4,128)S(1)}, u32[]{:S(2)}, u32[]{:S(2)}) %collective-permute-start.4) | collective-permute-done | bytes 2080 | tf_op jit(solution)/shard_map/ppermute | solution.py:20
  34.5 1.8 %collective-permute-start.5 = (f32[2,4,128]{2,1,0:T(4,128)S(1)}, f32[2,4,128]{2,1,0:T(4,128)S(1)}, u32[]{:S(2)}, u32[]{:S(2)}) collective-permute-start(f32[2,4,128]{2,1,0:T(4,128)S(1)} %pad_maximum_fusion.3), channel_id=1, source_target_pairs={{0,4},{2,6},{4,0},{6,2},{8,12},{10,14},{12,8},{14,10},{16,20},{18,... | collective-permute-start | bytes 12296 | tf_op jit(solution)/shard_map/ppermute | solution.py:20
  36.2 1.9 %collective-permute-done.5 = f32[2,4,128]{2,1,0:T(4,128)S(1)} collective-permute-done((f32[2,4,128]{2,1,0:T(4,128)S(1)}, f32[2,4,128]{2,1,0:T(4,128)S(1)}, u32[]{:S(2)}, u32[]{:S(2)}) %collective-permute-start.5) | collective-permute-done | bytes 4128 | tf_op jit(solution)/shard_map/ppermute | solution.py:20
  38.1 1.9 %collective-permute-start.6 = (f32[4,4,128]{2,1,0:T(4,128)S(1)}, f32[4,4,128]{2,1,0:T(4,128)S(1)}, u32[]{:S(2)}, u32[]{:S(2)}) collective-permute-start(f32[4,4,128]{2,1,0:T(4,128)S(1)} %pad_maximum_fusion.2), channel_id=1, source_target_pairs={{0,8},{2,10},{4,12},{6,14},{8,0},{10,2},{12,4},{14,6},{16,24},{18,... | collective-permute-start | bytes 24584 | tf_op jit(solution)/shard_map/ppermute | solution.py:20
  40.0 1.9 %collective-permute-done.6 = f32[4,4,128]{2,1,0:T(4,128)S(1)} collective-permute-done((f32[4,4,128]{2,1,0:T(4,128)S(1)}, f32[4,4,128]{2,1,0:T(4,128)S(1)}, u32[]{:S(2)}, u32[]{:S(2)}) %collective-permute-start.6) | collective-permute-done | bytes 8224 | tf_op jit(solution)/shard_map/ppermute | solution.py:20
  41.9 2.9 %collective-permute-start.7 = (f32[8,4,128]{2,1,0:T(4,128)S(1)}, f32[8,4,128]{2,1,0:T(4,128)S(1)}, u32[]{:S(2)}, u32[]{:S(2)}) collective-permute-start(f32[8,4,128]{2,1,0:T(4,128)S(1)} %pad_maximum_fusion), channel_id=1, source_target_pairs={{0,16},{2,18},{4,20},{6,22},{8,24},{10,26},{12,28},{14,30},{16,0},... | collective-permute-start | bytes 49160 | tf_op jit(solution)/shard_map/ppermute | solution.py:20
  44.8 1.8 %collective-permute-done.7 = f32[8,4,128]{2,1,0:T(4,128)S(1)} collective-permute-done((f32[8,4,128]{2,1,0:T(4,128)S(1)}, f32[8,4,128]{2,1,0:T(4,128)S(1)}, u32[]{:S(2)}, u32[]{:S(2)}) %collective-permute-start.7) | collective-permute-done | bytes 16416 | tf_op jit(solution)/shard_map/ppermute | solution.py:20
  46.7 0.5 subtract_add_fusion
  47.2 0.0 copy-start.2
  47.2 0.3 fusion.15.delta_ref
  47.5 1.8 %collective-permute-start.11 = (bf16[128,1536]{1,0:T(8,128)(2,1)S(1)}, bf16[128,1536]{1,0:T(8,128)(2,1)S(1)}, u32[]{:S(2)}, u32[]{:S(2)}) collective-permute-start(bf16[128,1536]{1,0:T(8,128)(2,1)S(1)} %fusion.15.delta_ref), channel_id=1, source_target_pairs={{0,1},{1,0},{2,3},{3,2},{4,5},{5,4},{6,7},{7,6},{8,9},{9,8},{10,11... | collective-permute-start | bytes 1179656 | tf_op jit(solution)/shard_map/ppermute | solution.py:16
  49.3 4.8 %partial_gradient.2 = (bf16[4,224,128]{2,1,0:T(8,128)(2,1)S(1)}, f32[4,224,128]{2,1,0:T(8,128)S(1)}) custom-call(s32[1]{0:T(128)} %bitcast.9.core_ref, bf16[1792,1536]{1,0:T(8,128)(2,1)} %head_ref.3, bf16[128,1536]{1,0:T(8,128)(2,1)S(1)} %fusion.15.delta_ref), custom_call_target="tpu_custom_call" | custom-call | flops 704643072 | bytes 5898240 | tf_op jit(solution)/shard_map/partial_gradient/pallas_call | solution.py:82
  54.1 0.1 collective-permute-start.8
  54.3 1.2 %collective-permute-done.11.delta_ref = bf16[128,1536]{1,0:T(8,128)(2,1)S(1)} collective-permute-done((bf16[128,1536]{1,0:T(8,128)(2,1)S(1)}, bf16[128,1536]{1,0:T(8,128)(2,1)S(1)}, u32[]{:S(2)}, u32[]{:S(2)}) %collective-permute-start.11) | collective-permute-done | bytes 393248 | tf_op jit(solution)/shard_map/ppermute | solution.py:16
  55.5 4.8 %partial_gradient.3 = (bf16[4,224,128]{2,1,0:T(8,128)(2,1)S(1)}, f32[4,224,128]{2,1,0:T(8,128)S(1)}) custom-call(s32[1]{0:T(128)} %bitcast.9.core_ref, bf16[1792,1536]{1,0:T(8,128)(2,1)} %head_ref.3, bf16[128,1536]{1,0:T(8,128)(2,1)S(1)} %collective-permute-done.11.delta_ref), custom_call_target="tpu_custom_call" | custom-call | flops 704643072 | bytes 5898240 | tf_op jit(solution)/shard_map/partial_gradient/pallas_call | solution.py:82
  60.3 0.0 copy-done.2
  60.3 0.1 collective-permute-start.12
  60.4 0.0 collective-permute-done.8
  60.4 0.1 convert_add_fusion.1
  60.5 1.6 %collective-permute-start.9 = (bf16[2,224,128]{2,1,0:T(8,128)(2,1)S(1)}, bf16[2,224,128]{2,1,0:T(8,128)(2,1)S(1)}, u32[]{:S(2)}, u32[]{:S(2)}) collective-permute-start(bf16[2,224,128]{2,1,0:T(8,128)(2,1)S(1)} %fusion.16), channel_id=1, source_target_pairs={{0,4},{2,6},{4,0},{6,2},{8,12},{10,14},{12,8},{14,10},{16,20},{18,... | collective-permute-start | bytes 344072 | tf_op jit(solution)/shard_map/ppermute | solution.py:20
  62.1 0.0 collective-permute-done.12
  62.1 0.1 convert_add_fusion
  62.2 1.4 %collective-permute-start.13 = (bf16[2,224,128]{2,1,0:T(8,128)(2,1)S(1)}, bf16[2,224,128]{2,1,0:T(8,128)(2,1)S(1)}, u32[]{:S(2)}, u32[]{:S(2)}) collective-permute-start(bf16[2,224,128]{2,1,0:T(8,128)(2,1)S(1)} %fusion.17), channel_id=1, source_target_pairs={{0,4},{2,6},{4,0},{6,2},{8,12},{10,14},{12,8},{14,10},{16,20},{18,... | collective-permute-start | bytes 344072 | tf_op jit(solution)/shard_map/ppermute | solution.py:20
  63.6 2.9 %collective-permute-done.9 = bf16[2,224,128]{2,1,0:T(8,128)(2,1)S(1)} collective-permute-done((bf16[2,224,128]{2,1,0:T(8,128)(2,1)S(1)}, bf16[2,224,128]{2,1,0:T(8,128)(2,1)S(1)}, u32[]{:S(2)}, u32[]{:S(2)}) %collective-permute-start.9) | collective-permute-done | bytes 114720 | tf_op jit(solution)/shard_map/ppermute | solution.py:20
  66.6 1.7 %collective-permute-start.10 = (bf16[1,224,128]{2,1,0:T(8,128)(2,1)S(1)}, bf16[1,224,128]{2,1,0:T(8,128)(2,1)S(1)}, u32[]{:S(2)}, u32[]{:S(2)}) collective-permute-start(bf16[1,224,128]{2,1,0:T(8,128)(2,1)S(1)} %dynamic-slice_convert_fusion.1), channel_id=1, source_target_pairs={{0,8},{2,10},{4,12},{6,14},{8,0},{10,2},{12,4},{14,6},{16,24},{18,... | collective-permute-start | bytes 172040 | tf_op jit(solution)/shard_map/ppermute | solution.py:20
  68.3 0.3 collective-permute-done.13
  68.6 1.7 %collective-permute-start.14 = (bf16[1,224,128]{2,1,0:T(8,128)(2,1)S(1)}, bf16[1,224,128]{2,1,0:T(8,128)(2,1)S(1)}, u32[]{:S(2)}, u32[]{:S(2)}) collective-permute-start(bf16[1,224,128]{2,1,0:T(8,128)(2,1)S(1)} %dynamic-slice_convert_fusion), channel_id=1, source_target_pairs={{0,8},{2,10},{4,12},{6,14},{8,0},{10,2},{12,4},{14,6},{16,24},{18,... | collective-permute-start | bytes 172040 | tf_op jit(solution)/shard_map/ppermute | solution.py:20
  70.3 0.5 collective-permute-done.10
  70.8 2.0 %collective-permute-done.14 = bf16[1,224,128]{2,1,0:T(8,128)(2,1)S(1)} collective-permute-done((bf16[1,224,128]{2,1,0:T(8,128)(2,1)S(1)}, bf16[1,224,128]{2,1,0:T(8,128)(2,1)S(1)}, u32[]{:S(2)}, u32[]{:S(2)}) %collective-permute-start.14) | collective-permute-done | bytes 57376 | tf_op jit(solution)/shard_map/ppermute | solution.py:20
  72.9 0.1 fusion.24
  73.0 0.7 collective-permute-start.15
  73.6 5.4 %collective-permute-start.16 = (bf16[224,128]{1,0:T(8,128)(2,1)S(1)}, bf16[224,128]{1,0:T(8,128)(2,1)S(1)}, u32[]{:S(2)}, u32[]{:S(2)}) collective-permute-start(bf16[224,128]{1,0:T(8,128)(2,1)S(1)} %get-tuple-element.30), channel_id=1, source_target_pairs={{0,1},{1,17},{2,3},{3,19},{4,5},{5,21},{6,7},{7,23},{8,9},{9,25},{... | collective-permute-start | bytes 172040 | tf_op jit(solution)/shard_map/ppermute | solution.py:192
  79.1 4.1 %convolution_convert_fusion = bf16[1792,1536]{1,0:T(8,128)(2,1)} fusion(bf16[64,1792]{1,0:T(8,128)(2,1)S(1)} %get-tuple-element.28, bf16[64,1792]{1,0:T(8,128)(2,1)S(1)} %get-tuple-element.27, bf16[128,1792]{1,0:T(8,128)(2,1)S(1)} %constant_dynamic-slice_fusion, bf16[128,1536]{1,0:T(8,128)(2,1)S(1)} %collective-permute-done.11.delta_ref, ...), kind=kOutput, calls=%fused_computation | convolution fusion | flops 1416364032 | bytes 7208960 | tf_op jit(solution)/shard_map/dot_general | solution.py:199
  83.1 0.0 collective-permute-done.15
  83.1 0.0 collective-permute-done.16
  83.1 0.7 fusion.19
  (22 shorter events, 0.4 us)
Async XLA Ops:
  1.6 8.6 %collective-permute-start = (bf16[64,1792]{1,0:T(8,128)(2,1)S(1)}, bf16[64,1792]{1,0:T(8,128)(2,1)S(1)}, u32[]{:S(2)}, u32[]{:S(2)}) collective-permute-start(bf16[64,1792]{1,0:T(8,128)(2,1)S(1)} %dynamic_slice.31), channel_id=1, source_target_pairs={{0,1},{1,0},{2,3},{3,2},{4,5},{5,4},{6,7},{7,6},{8,9},{9,8},{10,11... | collective-permute-start | bytes 688136 | tf_op jit(solution)/shard_map/ppermute | solution.py:16
  4.7 5.6 %copy-start = (bf16[1792,1536]{1,0:T(8,128)(2,1)S(1)}, bf16[1792,1536]{1,0:T(8,128)(2,1)}, u32[]{:S(2)}) copy-start(bf16[1792,1536]{1,0:T(8,128)(2,1)} %head_ref.3) | copy-start | bytes 16515076
  9.6 5.7 %copy-start.3 = (s32[1,16]{1,0:T(1,128)S(1)}, s32[1,16]{1,0:T(1,128)}, u32[]{:S(2)}) copy-start(s32[1,16]{1,0:T(1,128)} %param.8) | copy-start | bytes 196
  10.3 2.9 %collective-permute-start.1 = (bf16[64,1792]{1,0:T(8,128)(2,1)S(1)}, bf16[64,1792]{1,0:T(8,128)(2,1)S(1)}, u32[]{:S(2)}, u32[]{:S(2)}) collective-permute-start(bf16[64,1792]{1,0:T(8,128)(2,1)S(1)} %collective-permute-done), channel_id=1, source_target_pairs={{0,2},{2,0},{4,6},{6,4},{8,10},{10,8},{12,14},{14,12},{16,18},{18,... | collective-permute-start | bytes 688136 | tf_op jit(solution)/shard_map/ppermute | solution.py:20
  11.3 21.4 %copy-start.1 = (bf16[128,1536]{1,0:T(8,128)(2,1)S(1)}, bf16[128,1536]{1,0:T(8,128)(2,1)}, u32[]{:S(2)}) copy-start(bf16[128,1536]{1,0:T(8,128)(2,1)} %param.7) | copy-start | bytes 1179652
  11.3 12.0 %collective-permute-start.3 = (f32[64,1536]{1,0:T(8,128)S(1)}, f32[64,1536]{1,0:T(8,128)S(1)}, u32[]{:S(2)}, u32[]{:S(2)}) collective-permute-start(f32[64,1536]{1,0:T(8,128)S(1)} %fusion.37), channel_id=1, source_target_pairs={{0,1},{1,0},{2,3},{3,2},{4,5},{5,4},{6,7},{7,6},{8,9},{9,8},{10,11... | collective-permute-start | bytes 1179656 | tf_op jit(solution)/shard_map/ppermute | solution.py:16
  14.2 17.2 %collective-permute-start.2 = (f32[64,1536]{1,0:T(8,128)S(1)}, f32[64,1536]{1,0:T(8,128)}, u32[]{:S(2)}, u32[]{:S(2)}) collective-permute-start(f32[64,1536]{1,0:T(8,128)S(1)} %fusion.36), channel_id=1, source_target_pairs={{0,1},{1,0},{2,3},{3,2},{4,5},{5,4},{6,7},{7,6},{8,9},{9,8},{10,11... | collective-permute-start | bytes 1179656 | tf_op jit(solution)/shard_map/ppermute | solution.py:16
  33.2 1.2 %collective-permute-start.4 = (f32[1,4,128]{2,1,0:T(4,128)S(1)}, f32[1,4,128]{2,1,0:T(4,128)S(1)}, u32[]{:S(2)}, u32[]{:S(2)}) collective-permute-start(f32[1,4,128]{2,1,0:T(4,128)S(1)} %maximum_bitcast_fusion), channel_id=1, source_target_pairs={{0,2},{2,0},{4,6},{6,4},{8,10},{10,8},{12,14},{14,12},{16,18},{18,... | collective-permute-start | bytes 6152 | tf_op jit(solution)/shard_map/ppermute | solution.py:20
  34.5 3.7 %collective-permute-start.5 = (f32[2,4,128]{2,1,0:T(4,128)S(1)}, f32[2,4,128]{2,1,0:T(4,128)S(1)}, u32[]{:S(2)}, u32[]{:S(2)}) collective-permute-start(f32[2,4,128]{2,1,0:T(4,128)S(1)} %pad_maximum_fusion.3), channel_id=1, source_target_pairs={{0,4},{2,6},{4,0},{6,2},{8,12},{10,14},{12,8},{14,10},{16,20},{18,... | collective-permute-start | bytes 12296 | tf_op jit(solution)/shard_map/ppermute | solution.py:20
  38.1 3.7 %collective-permute-start.6 = (f32[4,4,128]{2,1,0:T(4,128)S(1)}, f32[4,4,128]{2,1,0:T(4,128)S(1)}, u32[]{:S(2)}, u32[]{:S(2)}) collective-permute-start(f32[4,4,128]{2,1,0:T(4,128)S(1)} %pad_maximum_fusion.2), channel_id=1, source_target_pairs={{0,8},{2,10},{4,12},{6,14},{8,0},{10,2},{12,4},{14,6},{16,24},{18,... | collective-permute-start | bytes 24584 | tf_op jit(solution)/shard_map/ppermute | solution.py:20
  41.9 4.7 %collective-permute-start.7 = (f32[8,4,128]{2,1,0:T(4,128)S(1)}, f32[8,4,128]{2,1,0:T(4,128)S(1)}, u32[]{:S(2)}, u32[]{:S(2)}) collective-permute-start(f32[8,4,128]{2,1,0:T(4,128)S(1)} %pad_maximum_fusion), channel_id=1, source_target_pairs={{0,16},{2,18},{4,20},{6,22},{8,24},{10,26},{12,28},{14,30},{16,0},... | collective-permute-start | bytes 49160 | tf_op jit(solution)/shard_map/ppermute | solution.py:20
  47.2 13.1 %copy-start.2 = (f32[128]{0:T(128)}, f32[128]{0:T(128)S(1)}, u32[]{:S(2)}) copy-start(f32[128]{0:T(128)S(1)} %get-tuple-element.22) | copy-start | bytes 1540
  47.5 8.0 %collective-permute-start.11 = (bf16[128,1536]{1,0:T(8,128)(2,1)S(1)}, bf16[128,1536]{1,0:T(8,128)(2,1)S(1)}, u32[]{:S(2)}, u32[]{:S(2)}) collective-permute-start(bf16[128,1536]{1,0:T(8,128)(2,1)S(1)} %fusion.15.delta_ref), channel_id=1, source_target_pairs={{0,1},{1,0},{2,3},{3,2},{4,5},{5,4},{6,7},{7,6},{8,9},{9,8},{10,11... | collective-permute-start | bytes 1179656 | tf_op jit(solution)/shard_map/ppermute | solution.py:16
  54.1 6.3 %collective-permute-start.8 = (bf16[4,224,128]{2,1,0:T(8,128)(2,1)S(1)}, bf16[4,224,128]{2,1,0:T(8,128)(2,1)S(1)}, u32[]{:S(2)}, u32[]{:S(2)}) collective-permute-start(bf16[4,224,128]{2,1,0:T(8,128)(2,1)S(1)} %get-tuple-element.13), channel_id=1, source_target_pairs={{0,2},{2,0},{4,6},{6,4},{8,10},{10,8},{12,14},{14,12},{16,18},{18,... | collective-permute-start | bytes 688136 | tf_op jit(solution)/shard_map/ppermute | solution.py:20
  60.3 1.8 %collective-permute-start.12 = (bf16[4,224,128]{2,1,0:T(8,128)(2,1)S(1)}, bf16[4,224,128]{2,1,0:T(8,128)(2,1)S(1)}, u32[]{:S(2)}, u32[]{:S(2)}) collective-permute-start(bf16[4,224,128]{2,1,0:T(8,128)(2,1)S(1)} %get-tuple-element.15), channel_id=1, source_target_pairs={{0,2},{2,0},{4,6},{6,4},{8,10},{10,8},{12,14},{14,12},{16,18},{18,... | collective-permute-start | bytes 688136 | tf_op jit(solution)/shard_map/ppermute | solution.py:20
  60.5 6.0 %collective-permute-start.9 = (bf16[2,224,128]{2,1,0:T(8,128)(2,1)S(1)}, bf16[2,224,128]{2,1,0:T(8,128)(2,1)S(1)}, u32[]{:S(2)}, u32[]{:S(2)}) collective-permute-start(bf16[2,224,128]{2,1,0:T(8,128)(2,1)S(1)} %fusion.16), channel_id=1, source_target_pairs={{0,4},{2,6},{4,0},{6,2},{8,12},{10,14},{12,8},{14,10},{16,20},{18,... | collective-permute-start | bytes 344072 | tf_op jit(solution)/shard_map/ppermute | solution.py:20
  62.2 6.3 %collective-permute-start.13 = (bf16[2,224,128]{2,1,0:T(8,128)(2,1)S(1)}, bf16[2,224,128]{2,1,0:T(8,128)(2,1)S(1)}, u32[]{:S(2)}, u32[]{:S(2)}) collective-permute-start(bf16[2,224,128]{2,1,0:T(8,128)(2,1)S(1)} %fusion.17), channel_id=1, source_target_pairs={{0,4},{2,6},{4,0},{6,2},{8,12},{10,14},{12,8},{14,10},{16,20},{18,... | collective-permute-start | bytes 344072 | tf_op jit(solution)/shard_map/ppermute | solution.py:20
  66.6 4.2 %collective-permute-start.10 = (bf16[1,224,128]{2,1,0:T(8,128)(2,1)S(1)}, bf16[1,224,128]{2,1,0:T(8,128)(2,1)S(1)}, u32[]{:S(2)}, u32[]{:S(2)}) collective-permute-start(bf16[1,224,128]{2,1,0:T(8,128)(2,1)S(1)} %dynamic-slice_convert_fusion.1), channel_id=1, source_target_pairs={{0,8},{2,10},{4,12},{6,14},{8,0},{10,2},{12,4},{14,6},{16,24},{18,... | collective-permute-start | bytes 172040 | tf_op jit(solution)/shard_map/ppermute | solution.py:20
  68.6 4.2 %collective-permute-start.14 = (bf16[1,224,128]{2,1,0:T(8,128)(2,1)S(1)}, bf16[1,224,128]{2,1,0:T(8,128)(2,1)S(1)}, u32[]{:S(2)}, u32[]{:S(2)}) collective-permute-start(bf16[1,224,128]{2,1,0:T(8,128)(2,1)S(1)} %dynamic-slice_convert_fusion), channel_id=1, source_target_pairs={{0,8},{2,10},{4,12},{6,14},{8,0},{10,2},{12,4},{14,6},{16,24},{18,... | collective-permute-start | bytes 172040 | tf_op jit(solution)/shard_map/ppermute | solution.py:20
  73.0 10.2 %collective-permute-start.15 = (bf16[224,128]{1,0:T(8,128)(2,1)S(1)}, bf16[224,128]{1,0:T(8,128)(2,1)S(1)}, u32[]{:S(2)}, u32[]{:S(2)}) collective-permute-start(bf16[224,128]{1,0:T(8,128)(2,1)S(1)} %get-tuple-element.29), channel_id=1, source_target_pairs={{1,16},{3,18},{5,20},{7,22},{9,24},{11,26},{13,28},{15,30},{16,1},... | collective-permute-start | bytes 172040 | tf_op jit(solution)/shard_map/ppermute | solution.py:192
  73.6 9.5 %collective-permute-start.16 = (bf16[224,128]{1,0:T(8,128)(2,1)S(1)}, bf16[224,128]{1,0:T(8,128)(2,1)S(1)}, u32[]{:S(2)}, u32[]{:S(2)}) collective-permute-start(bf16[224,128]{1,0:T(8,128)(2,1)S(1)} %get-tuple-element.30), channel_id=1, source_target_pairs={{0,1},{1,17},{2,3},{3,19},{4,5},{5,21},{6,7},{7,23},{8,9},{9,25},{... | collective-permute-start | bytes 172040 | tf_op jit(solution)/shard_map/ppermute | solution.py:192

commit v5 on v4

--- a/solution.py
+++ b/solution.py
@@ -1,3 +1,5 @@
+import functools
+
 import jax
 import jax.numpy as jnp
 from jax import lax
@@ -52,7 +54,17 @@
     return gathered
 
 
-def gradient_kernel(core_ref, head_ref, delta_ref, send_ref, keep_ref, held_ref, sems):
+def write_pieces(k, head_rows, delta_ref, upper, send_ref, keep_ref):
+    rows = send_ref.shape[1]
+    block = lax.dot_general(
+        head_rows, delta_ref[...], (((1,), (1,)), ((), ())), preferred_element_type=jnp.float32
+    )
+    low, high = block[:rows], block[rows:]
+    send_ref[k] = jnp.where(upper, low, high).astype(jnp.bfloat16)
+    keep_ref[k] = jnp.where(upper, high, low)
+
+
+def first_gradient_kernel(core_ref, head_ref, delta_ref, send_ref, keep_ref, held_ref, sems):
     upper = core_ref[0] == 1
     pairs, rows, _ = send_ref.shape
     parts = [pl.ds(2 * k * rows, 2 * rows) for k in range(pairs)]
@@ -60,38 +72,42 @@
         pltpu.make_async_copy(head_ref.at[part], held_ref.at[part], sems.at[k])
         for k, part in enumerate(parts)
     ]
-    for copy in copies:
+    for copy in copies[:2]:
         copy.start()
     for k in range(pairs):
         copies[k].wait()
-        block = lax.dot_general(
-            held_ref[2 * k * rows : 2 * (k + 1) * rows, :],
-            delta_ref[...],
-            (((1,), (1,)), ((), ())),
-            preferred_element_type=jnp.float32,
-        )
-        low, high = block[:rows], block[rows:]
-        send_ref[k] = jnp.where(upper, low, high).astype(jnp.bfloat16)
-        keep_ref[k] = jnp.where(upper, high, low)
-
-
-def gradient(core, head, delta, run):
+        if k + 2 < pairs:
+            copies[k + 2].start()
+        head_rows = held_ref[2 * k * rows : 2 * (k + 1) * rows, :]
+        write_pieces(k, head_rows, delta_ref, upper, send_ref, keep_ref)
+
+
+def later_gradient_kernel(core_ref, head_ref, delta_ref, send_ref, keep_ref):
+    upper = core_ref[0] == 1
+    pairs, rows, _ = send_ref.shape
+    for k in range(pairs):
+        head_rows = head_ref[2 * k * rows : 2 * (k + 1) * rows, :]
+        write_pieces(k, head_rows, delta_ref, upper, send_ref, keep_ref)
+
+
+def gradient(core, head, delta, run, first):
     rows = head.shape[0] // run
     shape = (run // 2, rows, delta.shape[0])
     in_vmem = pl.BlockSpec(memory_space=pltpu.VMEM)
+    space = pltpu.HBM if first else pltpu.VMEM
+    outs = (pltpu.VMEM(shape, jnp.bfloat16), pltpu.VMEM(shape, jnp.float32))
+    if first:
+        outs = outs + (pltpu.VMEM(head.shape, head.dtype),)
     return pl.pallas_call(
-        gradient_kernel,
-        out_shape=(pltpu.VMEM(shape, jnp.bfloat16), pltpu.VMEM(shape, jnp.float32)),
+        first_gradient_kernel if first else later_gradient_kernel,
+        out_shape=outs,
         in_specs=[
             pl.BlockSpec(memory_space=pltpu.SMEM),
-            pl.BlockSpec(memory_space=pltpu.HBM),
+            pl.BlockSpec(memory_space=space),
             in_vmem,
         ],
-        out_specs=(in_vmem, in_vmem),
-        scratch_shapes=[
-            pltpu.VMEM(head.shape, head.dtype),
-            pltpu.SemaphoreType.DMA((run // 2,)),
-        ],
+        out_specs=(in_vmem,) * len(outs),
+        scratch_shapes=[pltpu.SemaphoreType.DMA((run // 2,))] if first else [],
         compiler_params=pltpu.CompilerParams(vmem_limit_bytes=VMEM_LIMIT),
         cost_estimate=pl.CostEstimate(
             flops=2 * head.size * delta.shape[0],
@@ -101,22 +117,53 @@
         name="partial_gradient",
     )(
         core.reshape(1),
-        pltpu.with_memory_space_constraint(head, pltpu.HBM),
+        pltpu.with_memory_space_constraint(head, space),
         pltpu.with_memory_space_constraint(delta, pltpu.VMEM),
     )
 
 
-def halve(send, keep, vocab_index, vocab_size):
-    held = keep + swap_vocab(send, 1, vocab_size).astype(jnp.float32)
-    bit = 2
-    while held.shape[0] > 1:
-        pairs = held.reshape(held.shape[0] // 2, 2, *held.shape[1:])
-        mine = (vocab_index // bit) % 2
-        send = pick(pairs, 1 - mine, 1).astype(jnp.bfloat16)
-        other = swap_vocab(send, bit, vocab_size)
-        held = pick(pairs, mine, 1) + other.astype(jnp.float32)
-        bit *= 2
-    return held[0]
+def head_gradient_kernel(steps, start, width, *refs):
+    features_ref, delta_ref, out_ref, held_ref, sems = refs[0], refs[1], *refs[-3:]
+    copies = []
+    for k in range(steps):
+        block = lax.dot_general(
+            features_ref[:, start + k * width : start + (k + 1) * width],
+            delta_ref[...],
+            (((0,), (0,)), ((), ())),
+            preferred_element_type=jnp.float32,
+        )
+        held_ref[k] = block.astype(jnp.bfloat16)
+        copy = pltpu.make_async_copy(
+            held_ref.at[k], out_ref.at[pl.ds(start + k * width, width)], sems.at[k]
+        )
+        copy.start()
+        copies.append(copy)
+    for copy in copies:
+        copy.wait()
+
+
+def head_gradient(features, delta, out, start, steps, width):
+    columns = delta.shape[1]
+    in_vmem = pl.BlockSpec(memory_space=pltpu.VMEM)
+    in_hbm = pl.BlockSpec(memory_space=pltpu.HBM)
+    return pl.pallas_call(
+        functools.partial(head_gradient_kernel, steps, start, width),
+        out_shape=jax.ShapeDtypeStruct((features.shape[1], columns), jnp.bfloat16),
+        in_specs=[in_vmem, in_vmem] + ([] if out is None else [in_hbm]),
+        out_specs=in_hbm,
+        scratch_shapes=[
+            pltpu.VMEM((steps, width, columns), jnp.bfloat16),
+            pltpu.SemaphoreType.DMA((steps,)),
+        ],
+        input_output_aliases={} if out is None else {2: 0},
+        compiler_params=pltpu.CompilerParams(vmem_limit_bytes=VMEM_LIMIT),
+        cost_estimate=pl.CostEstimate(
+            flops=2 * steps * width * delta.size,
+            bytes_accessed=2 * (features.size + delta.size + steps * width * columns),
+            transcendentals=0,
+        ),
+        name="head_gradient",
+    )(features, delta, *([] if out is None else [out]))
 
 
 def per_device(hidden, head, teacher, block_ids, counts):
@@ -150,6 +197,9 @@
             jnp.dot(far[d - 1], head, preferred_element_type=jnp.float32), -d, tok_size
         )
         returned.append((first, second))
+    features = [own] + [in_order(n, f, core != 0) for n, f in zip(near, far)]
+    all_features = jnp.concatenate(features, axis=0)
+    returned, all_features = lax.optimization_barrier((returned, all_features))
     for first, second in returned:
         logits = logits + in_order(first, second, core != 0)
 
@@ -176,11 +226,44 @@
     delta = (loss_scale * (student - kept / total_mass[:, None])).astype(jnp.bfloat16)
 
     deltas = [delta] + [shift_tok(delta, d, tok_size) for d in range(1, tok_size)]
-    sums = [halve(*gradient(core, head, x, run), vocab_index, vocab_size) for x in deltas]
+    send, keep, head_here = gradient(core, head, delta, run, True)
+    other = swap_vocab(send, 1, vocab_size)
+    state = [(keep, other)]
+    for x in deltas[1:]:
+        send, keep = gradient(core, head_here, x, run, False)
+        state[0], send = lax.optimization_barrier((state[0], send))
+        state.append((keep, swap_vocab(send, 1, vocab_size)))
+    all_delta = jnp.concatenate(deltas, axis=0)
+
+    width = 256 if rows % 256 == 0 else rows
+    chunks = rows // width
+    shares = [(chunks + 1) // 2, chunks // 4]
+    done = 0
+    grad_head = None
+    bit = 2
+    held = jnp.stack([keep + other.astype(jnp.float32) for keep, other in state])
+    while bit < run:
+        pairs = held.reshape(tok_size, held.shape[1] // 2, 2, *held.shape[2:])
+        mine = (vocab_index // bit) % 2
+        send = pick(pairs, 1 - mine, 2).astype(jnp.bfloat16)
+        send, all_delta = lax.optimization_barrier((send, all_delta))
+        other = swap_vocab(send, bit, vocab_size)
+        share = shares.pop(0) if shares else 0
+        if share:
+            grad_head = head_gradient(
+                all_features, all_delta, grad_head, done * width, share, width
+            )
+            done += share
+            other, grad_head = lax.optimization_barrier((other, grad_head))
+        held = pick(pairs, mine, 2) + other.astype(jnp.float32)
+        bit *= 2
+    sums = held[:, 0]
     high = vocab_index // run
     apart = (tok_index - high) % tok_size
     total = jnp.where(apart == 0, sums[0], 0.0)
-    sums = jnp.stack([x.astype(jnp.bfloat16) for x in sums])
+    sums = sums.astype(jnp.bfloat16)
+    sends = [pick(sums, (k + apart) % tok_size) for k in range(tok_size)]
+    sends, all_delta = lax.optimization_barrier((sends, all_delta))
     for k in range(tok_size):
         pairs = []
         for v in range(vocab_size):
@@ -189,19 +272,12 @@
                 target = (t * run + v % run) * tok_size + (t - d) % tok_size
                 if target != v * tok_size + t:
                     pairs.append((v * tok_size + t, target))
-        total = total + lax.ppermute(
-            pick(sums, (k + apart) % tok_size), ("vocab", "tok"), pairs
-        ).astype(jnp.float32)
+        total = total + lax.ppermute(sends[k], ("vocab", "tok"), pairs).astype(jnp.float32)
     grad_hidden = total.T
-
-    all_delta = jnp.concatenate(deltas, axis=0)
-    features = [own] + [in_order(n, f, core != 0) for n, f in zip(near, far)]
-    grad_head = lax.dot_general(
-        jnp.concatenate(features, axis=0),
-        all_delta,
-        (((0,), (0,)), ((), ())),
-        preferred_element_type=jnp.float32,
-    ).astype(jnp.bfloat16)
+    if done < chunks:
+        grad_head = head_gradient(
+            all_features, all_delta, grad_head, done * width, chunks - done, width
+        )
     return (lse, kl, grad_hidden, grad_head)
 
 

time: 84 us -> 86.6 us (1.031)
  local copies, waits for them, and re-layouts: 2.26 us -> 7.07 us
  starting transfers between devices: 26.3 us -> 23.4 us
  Pallas kernels: 9.65 us -> 11.3 us
  other arithmetic: 3.77 us -> 2.82 us
  waiting for transfers between devices: 30.3 us -> 29.4 us
    unnamed x8 -> x10, local copies, waits for them, and re-layouts: 0.02 us -> 5.01 us
    dot_general x1 -> x0, matrix products: 4.08 us -> none  [per_device(): lax.dot_general(jnp.concatenate(features, axis=0), all_delta, (((0,), (0,...]
    ppermute x4, waiting for transfers between devices: 17.9 us -> 14.4 us  [shift_tok(): lax.ppermute(x, 'tok', [(i, (i + offset) % size) for i in range(size)])]
    ppermute x11 -> x9, starting transfers between devices: 13.2 us -> 10.4 us  [swap_vocab(): return lax.ppermute(x, 'vocab', [(i, i ^ bit) for i in range(size)])]
    dot_general x1, matrix products: 1.07 us -> 3.63 us  [per_device(): jnp.dot(near[d - 1], head, preferred_element_type=jnp.float32)]
    dot_general x1, matrix products: 1.07 us -> 3.62 us  [per_device(): jnp.dot(far[d - 1], head, preferred_element_type=jnp.float32)]
    pallas_call x2 -> x5, Pallas kernels: 9.65 us -> 11.3 us  [the longest x2 6.37 us: gradient(): pl.pallas_call(first_gradient_kernel if first else later_gradient_kernel,...]
    ppermute x11 -> x9, waiting for transfers between devices: 12.4 us -> 13.9 us  [swap_vocab(): return lax.ppermute(x, 'vocab', [(i, i ^ bit) for i in range(size)])]
  transfers between devices with their start and end apart: 17 -> 15, of which waited for: 12 -> 11; matrix products, arithmetic and copies ran while one was open for 14% -> 14% of each run, Pallas kernels for 12% -> 13%
where the time goes in v5:
time: 86.6 us; the launch traced here: 86.3 us
  waiting for transfers between devices  29.4 us (34%)
  starting transfers between devices  23.4 us (27%)
  Pallas kernels  11.3 us (13%)
  matrix products  10.7 us (12%)
  local copies, waits for them, and re-layouts  7.07 us (8%)
  other arithmetic  2.82 us (3%)
  between operations  1.57 us (2%)
    ppermute x4, waiting for transfers between devices, shift_tok(): lax.ppermute(x, 'tok', [(i, (i + offset) % size) for i in range(size)])  14.4 us
    ppermute x9, waiting for transfers between devices, swap_vocab(): return lax.ppermute(x, 'vocab', [(i, i ^ bit) for i in range(size)])  13.9 us
    ppermute x9, starting transfers between devices, swap_vocab(): return lax.ppermute(x, 'vocab', [(i, i ^ bit) for i in range(size)])  10.4 us
    ppermute x4, starting transfers between devices, shift_tok(): lax.ppermute(x, 'tok', [(i, (i + offset) % size) for i in range(size)])  6.99 us
    pallas_call x2, Pallas kernels, gradient(): pl.pallas_call(first_gradient_kernel if first else later_gradient_kernel,...  6.37 us
    ppermute x2, starting transfers between devices, per_device(): lax.ppermute(sends[k], ('vocab', 'tok'), pairs).astype(jnp.float32)  6.02 us
    unnamed x10, local copies, waits for them, and re-layouts  5.01 us
    pallas_call x3, Pallas kernels, head_gradient(): pl.pallas_call(functools.partial(head_gradient_kernel, steps, start, widt...  4.91 us
  transfers between devices with their start and end apart: 15, of which 11 were waited for; matrix products, arithmetic and copies ran while one was open for 14% of the time, Pallas kernels for 13%

profile of v5, /device:TPU:0, one launch (start us, length us, event | category | flops | bytes accessed | tf_op | source)
XLA Modules:
  0.0 86.3 jit_solution(10559754862660520063)
XLA Ops:
  0.6 0.0 copy-start.4
  0.7 1.0 %dynamic_slice.23 = bf16[64,1792]{1,0:T(8,128)(2,1)S(1)} dynamic-slice(bf16[128,3584]{1,0:T(8,128)(2,1)} %param.5, s32[]{:T(128)S(6)} %select_n.175, s32[]{:T(128)S(6)} %select_n.177), dynamic_slice_sizes={64,1792} | dynamic-slice | bytes 458756 | tf_op jit(solution)/shard_map/dynamic_slice | solution.py:181
  1.6 3.0 %collective-permute-start = (bf16[64,1792]{1,0:T(8,128)(2,1)S(1)}, bf16[64,1792]{1,0:T(8,128)(2,1)S(1)}, u32[]{:S(2)}, u32[]{:S(2)}) collective-permute-start(bf16[64,1792]{1,0:T(8,128)(2,1)S(1)} %dynamic_slice.23), channel_id=1, source_target_pairs={{0,1},{1,0},{2,3},{3,2},{4,5},{5,4},{6,7},{7,6},{8,9},{9,8},{10,11... | collective-permute-start | bytes 688136 | tf_op jit(solution)/shard_map/ppermute | solution.py:18
  5.3 1.1 %constant_dynamic-slice_fusion = bf16[128,1792]{1,0:T(8,128)(2,1)S(1)} fusion(bf16[128,3584]{1,0:T(8,128)(2,1)} %param.5, s32[]{:T(128)S(6)} %select_n.178), kind=kLoop, calls=%fused_computation.71 | loop fusion | bytes 917508 | tf_op jit(solution)/shard_map/dynamic_slice | solution.py:181
  6.4 3.4 %fusion.29 = f32[128,1536]{1,0:T(8,128)S(1)} fusion(bf16[128,1792]{1,0:T(8,128)(2,1)S(1)} %constant_dynamic-slice_fusion, bf16[1792,1536]{1,0:T(8,128)(2,1)} %head_ref.1), kind=kOutput, calls=%fused_computation.82 | convolution fusion | flops 704643072 | bytes 6750208 | tf_op jit(solution)/shard_map/dot_general | solution.py:188
  9.9 0.0 copy-done.4
  9.9 0.1 and_reduce_fusion
  10.0 0.3 collective-permute-done
  10.3 0.0 collective-permute-start.2
  10.3 3.6 %fusion.30 = f32[64,1536]{1,0:T(8,128)S(1)} fusion(bf16[64,1792]{1,0:T(8,128)(2,1)S(1)} %collective-permute-done, bf16[1792,1536]{1,0:T(8,128)(2,1)} %head_ref.1), kind=kOutput, calls=%fused_computation.83 | convolution fusion | flops 352321536 | bytes 6127616 | tf_op jit(solution)/shard_map/dot_general | solution.py:194
  13.9 0.0 copy-start.2
  13.9 1.8 %collective-permute-start.1 = (f32[64,1536]{1,0:T(8,128)S(1)}, f32[64,1536]{1,0:T(8,128)S(1)}, u32[]{:S(2)}, u32[]{:S(2)}) collective-permute-start(f32[64,1536]{1,0:T(8,128)S(1)} %fusion.30), channel_id=1, source_target_pairs={{0,1},{1,0},{2,3},{3,2},{4,5},{5,4},{6,7},{7,6},{8,9},{9,8},{10,11... | collective-permute-start | bytes 1179656 | tf_op jit(solution)/shard_map/ppermute | solution.py:18
  15.7 0.0 collective-permute-done.2
  15.7 3.6 %fusion.31 = f32[64,1536]{1,0:T(8,128)S(1)} fusion(bf16[64,1792]{1,0:T(8,128)(2,1)S(1)} %collective-permute-done.2, bf16[1792,1536]{1,0:T(8,128)(2,1)} %head_ref.1), kind=kOutput, calls=%fused_computation.84 | convolution fusion | flops 352321536 | bytes 6127616 | tf_op jit(solution)/shard_map/dot_general | solution.py:197
  19.3 0.4 collective-permute-start.3
  19.7 0.1 pad_maximum_fusion.refs_0_
  19.8 6.1 %collective-permute-done.1 = f32[64,1536]{1,0:T(8,128)S(1)} collective-permute-done((f32[64,1536]{1,0:T(8,128)S(1)}, f32[64,1536]{1,0:T(8,128)S(1)}, u32[]{:S(2)}, u32[]{:S(2)}) %collective-permute-start.1) | collective-permute-done | bytes 393248 | tf_op jit(solution)/shard_map/ppermute | solution.py:18
  25.9 8.0 %collective-permute-done.3 = f32[64,1536]{1,0:T(8,128)S(1)} collective-permute-done((f32[64,1536]{1,0:T(8,128)S(1)}, f32[64,1536]{1,0:T(8,128)S(1)}, u32[]{:S(2)}, u32[]{:S(2)}) %collective-permute-start.3) | collective-permute-done | bytes 393248 | tf_op jit(solution)/shard_map/ppermute | solution.py:18
  33.9 0.1 broadcast_select_fusion.3
  34.0 0.2 fusion.28
  34.2 0.0 copy-done.2
  34.2 0.5 exponential_reduce_fusion
  34.7 0.1 collective-permute-start.4
  34.8 1.1 %collective-permute-done.4 = f32[1,4,128]{2,1,0:T(4,128)S(1)} collective-permute-done((f32[1,4,128]{2,1,0:T(4,128)S(1)}, f32[1,4,128]{2,1,0:T(4,128)S(1)}, u32[]{:S(2)}, u32[]{:S(2)}) %collective-permute-start.4) | collective-permute-done | bytes 2080 | tf_op jit(solution)/shard_map/ppermute | solution.py:22
  35.9 1.8 %collective-permute-start.5 = (f32[2,4,128]{2,1,0:T(4,128)S(1)}, f32[2,4,128]{2,1,0:T(4,128)S(1)}, u32[]{:S(2)}, u32[]{:S(2)}) collective-permute-start(f32[2,4,128]{2,1,0:T(4,128)S(1)} %pad_maximum_fusion.5), channel_id=1, source_target_pairs={{0,4},{2,6},{4,0},{6,2},{8,12},{10,14},{12,8},{14,10},{16,20},{18,... | collective-permute-start | bytes 12296 | tf_op jit(solution)/shard_map/ppermute | solution.py:22
  37.7 1.9 %collective-permute-done.5 = f32[2,4,128]{2,1,0:T(4,128)S(1)} collective-permute-done((f32[2,4,128]{2,1,0:T(4,128)S(1)}, f32[2,4,128]{2,1,0:T(4,128)S(1)}, u32[]{:S(2)}, u32[]{:S(2)}) %collective-permute-start.5) | collective-permute-done | bytes 4128 | tf_op jit(solution)/shard_map/ppermute | solution.py:22
  39.6 1.9 %collective-permute-start.6 = (f32[4,4,128]{2,1,0:T(4,128)S(1)}, f32[4,4,128]{2,1,0:T(4,128)S(1)}, u32[]{:S(2)}, u32[]{:S(2)}) collective-permute-start(f32[4,4,128]{2,1,0:T(4,128)S(1)} %pad_maximum_fusion.4), channel_id=1, source_target_pairs={{0,8},{2,10},{4,12},{6,14},{8,0},{10,2},{12,4},{14,6},{16,24},{18,... | collective-permute-start | bytes 24584 | tf_op jit(solution)/shard_map/ppermute | solution.py:22
  41.5 1.9 %collective-permute-done.6 = f32[4,4,128]{2,1,0:T(4,128)S(1)} collective-permute-done((f32[4,4,128]{2,1,0:T(4,128)S(1)}, f32[4,4,128]{2,1,0:T(4,128)S(1)}, u32[]{:S(2)}, u32[]{:S(2)}) %collective-permute-start.6) | collective-permute-done | bytes 8224 | tf_op jit(solution)/shard_map/ppermute | solution.py:22
  43.3 2.9 %collective-permute-start.7 = (f32[8,4,128]{2,1,0:T(4,128)S(1)}, f32[8,4,128]{2,1,0:T(4,128)S(1)}, u32[]{:S(2)}, u32[]{:S(2)}) collective-permute-start(f32[8,4,128]{2,1,0:T(4,128)S(1)} %pad_maximum_fusion.2), channel_id=1, source_target_pairs={{0,16},{2,18},{4,20},{6,22},{8,24},{10,26},{12,28},{14,30},{16,0},... | collective-permute-start | bytes 49160 | tf_op jit(solution)/shard_map/ppermute | solution.py:22
  46.2 1.8 %collective-permute-done.7 = f32[8,4,128]{2,1,0:T(4,128)S(1)} collective-permute-done((f32[8,4,128]{2,1,0:T(4,128)S(1)}, f32[8,4,128]{2,1,0:T(4,128)S(1)}, u32[]{:S(2)}, u32[]{:S(2)}) %collective-permute-start.7) | collective-permute-done | bytes 16416 | tf_op jit(solution)/shard_map/ppermute | solution.py:22
  48.2 0.5 subtract_add_fusion
  48.7 0.0 copy-start.3
  48.7 0.3 fusion.7.delta_ref
  49.0 1.8 %collective-permute-start.9 = (bf16[128,1536]{1,0:T(8,128)(2,1)S(1)}, bf16[128,1536]{1,0:T(8,128)(2,1)S(1)}, u32[]{:S(2)}, u32[]{:S(2)}) collective-permute-start(bf16[128,1536]{1,0:T(8,128)(2,1)S(1)} %fusion.7.delta_ref), channel_id=1, source_target_pairs={{0,1},{1,0},{2,3},{3,2},{4,5},{5,4},{6,7},{7,6},{8,9},{9,8},{10,11... | collective-permute-start | bytes 1179656 | tf_op jit(solution)/shard_map/ppermute | solution.py:18
  50.8 4.8 %partial_gradient.2 = (bf16[4,224,128]{2,1,0:T(8,128)(2,1)S(1)}, f32[4,224,128]{2,1,0:T(8,128)S(1)}, bf16[1792,1536]{1,0:T(8,128)(2,1)S(1)}) custom-call(s32[1]{0:T(128)} %bitcast.9.core_ref, bf16[1792,1536]{1,0:T(8,128)(2,1)} %head_ref.1, bf16[128,1536]{1,0:T(8,128)(2,1)S(1)} %fusion.7.delta_ref), custom_call_target="tpu_custom_call" | custom-call | flops 704643072 | bytes 5898240 | tf_op jit(solution)/shard_map/partial_gradient/pallas_call | solution.py:101
  55.6 0.0 copy-start
  55.6 2.4 %copy-done = bf16[1792,1536]{1,0:T(8,128)(2,1)} copy-done((bf16[1792,1536]{1,0:T(8,128)(2,1)}, bf16[1792,1536]{1,0:T(8,128)(2,1)S(1)}, u32[]{:S(2)}) %copy-start) | copy-done | bytes 5505048
  58.0 0.0 collective-permute-start.8
  58.0 0.0 collective-permute-done.9.delta_ref
  58.0 0.0 copy-start.1
  58.0 2.6 %copy-done.1 = bf16[1792,1536]{1,0:T(8,128)(2,1)S(1)} copy-done((bf16[1792,1536]{1,0:T(8,128)(2,1)S(1)}, bf16[1792,1536]{1,0:T(8,128)(2,1)}, u32[]{:S(2)}) %copy-start.1) | copy-done | bytes 5505048
  60.6 1.6 %partial_gradient.3 = (bf16[4,224,128]{2,1,0:T(8,128)(2,1)S(1)}, f32[4,224,128]{2,1,0:T(8,128)S(1)}) custom-call(s32[1]{0:T(128)} %bitcast.9.core_ref, bf16[1792,1536]{1,0:T(8,128)(2,1)S(1)} %copy-done.1, bf16[128,1536]{1,0:T(8,128)(2,1)S(1)} %collective-permute-done.9.delta_ref), custom_call_target="tpu_custom_call" | custom-call | flops 704643072 | bytes 5898240 | tf_op jit(solution)/shard_map/partial_gradient/pallas_call | solution.py:101
  62.2 0.0 copy-done.3
  62.2 0.0 collective-permute-done.8
  62.2 0.6 collective-permute-start.10
  62.8 0.1 pad_maximum_fusion.1.refs_1_
  62.9 1.0 %collective-permute-done.10 = bf16[4,224,128]{2,1,0:T(8,128)(2,1)S(1)} collective-permute-done((bf16[4,224,128]{2,1,0:T(8,128)(2,1)S(1)}, bf16[4,224,128]{2,1,0:T(8,128)(2,1)S(1)}, u32[]{:S(2)}, u32[]{:S(2)}) %collective-permute-start.10) | collective-permute-done | bytes 229408 | tf_op jit(solution)/shard_map/ppermute | solution.py:22
  64.0 1.6 %collective-permute-start.11 = (bf16[2,2,224,128]{3,2,1,0:T(8,128)(2,1)S(1)}, bf16[2,2,224,128]{3,2,1,0:T(8,128)(2,1)S(1)}, u32[]{:S(2)}, u32[]{:S(2)}) collective-permute-start(bf16[2,2,224,128]{3,2,1,0:T(8,128)(2,1)S(1)} %fusion.14), channel_id=1, source_target_pairs={{0,4},{2,6},{4,0},{6,2},{8,12},{10,14},{12,8},{14,10},{16,20},{18,... | collective-permute-start | bytes 688136 | tf_op jit(solution)/shard_map/ppermute | solution.py:22
  65.6 2.1 %head_gradient.3.refs_2_ = bf16[1792,1536]{1,0:T(8,128)(2,1)} custom-call(bf16[256,1792]{1,0:T(8,128)(2,1)S(1)} %pad_maximum_fusion.refs_0_, bf16[256,1536]{1,0:T(8,128)(2,1)S(1)} %pad_maximum_fusion.1.refs_1_), custom_call_target="tpu_custom_call" | custom-call | flops 805306368 | bytes 4849664 | tf_op jit(solution)/shard_map/head_gradient/pallas_call | solution.py:149
  67.6 4.3 %collective-permute-done.11 = bf16[2,2,224,128]{3,2,1,0:T(8,128)(2,1)S(1)} collective-permute-done((bf16[2,2,224,128]{3,2,1,0:T(8,128)(2,1)S(1)}, bf16[2,2,224,128]{3,2,1,0:T(8,128)(2,1)S(1)}, u32[]{:S(2)}, u32[]{:S(2)}) %collective-permute-start.11) | collective-permute-done | bytes 229408 | tf_op jit(solution)/shard_map/ppermute | solution.py:22
  72.0 1.6 %collective-permute-start.12 = (bf16[2,1,224,128]{3,2,1,0:T(8,128)(2,1)S(1)}, bf16[2,1,224,128]{3,2,1,0:T(8,128)(2,1)S(1)}, u32[]{:S(2)}, u32[]{:S(2)}) collective-permute-start(bf16[2,1,224,128]{3,2,1,0:T(8,128)(2,1)S(1)} %dynamic-slice_convert_fusion), channel_id=1, source_target_pairs={{0,8},{2,10},{4,12},{6,14},{8,0},{10,2},{12,4},{14,6},{16,24},{18,... | collective-permute-start | bytes 344072 | tf_op jit(solution)/shard_map/ppermute | solution.py:22
  73.6 1.3 %head_gradient.4.refs_2_ = bf16[1792,1536]{1,0:T(8,128)(2,1)} custom-call(bf16[256,1792]{1,0:T(8,128)(2,1)S(1)} %pad_maximum_fusion.refs_0_, bf16[256,1536]{1,0:T(8,128)(2,1)S(1)} %pad_maximum_fusion.1.refs_1_, bf16[1792,1536]{1,0:T(8,128)(2,1)} %head_gradient.3.refs_2_), custom_call_target="tpu_custom_call", output_to_operand_aliasing={{}: (2, {})} | custom-call | flops 201326592 | bytes 2490368 | tf_op jit(solution)/shard_map/head_gradient/pallas_call | solution.py:149
  74.9 1.9 %collective-permute-done.12 = bf16[2,1,224,128]{3,2,1,0:T(8,128)(2,1)S(1)} collective-permute-done((bf16[2,1,224,128]{3,2,1,0:T(8,128)(2,1)S(1)}, bf16[2,1,224,128]{3,2,1,0:T(8,128)(2,1)S(1)}, u32[]{:S(2)}, u32[]{:S(2)}) %collective-permute-start.12) | collective-permute-done | bytes 114720 | tf_op jit(solution)/shard_map/ppermute | solution.py:22
  76.9 0.7 collective-permute-start.13
  77.6 5.4 %collective-permute-start.14 = (bf16[224,128]{1,0:T(8,128)(2,1)S(1)}, bf16[224,128]{1,0:T(8,128)(2,1)S(1)}, u32[]{:S(2)}, u32[]{:S(2)}) collective-permute-start(bf16[224,128]{1,0:T(8,128)(2,1)S(1)} %get-tuple-element.49), channel_id=1, source_target_pairs={{0,1},{1,17},{2,3},{3,19},{4,5},{5,21},{6,7},{7,23},{8,9},{9,25},{... | collective-permute-start | bytes 172040 | tf_op jit(solution)/shard_map/ppermute | solution.py:275
  83.0 1.5 %head_gradient.5 = bf16[1792,1536]{1,0:T(8,128)(2,1)} custom-call(bf16[256,1792]{1,0:T(8,128)(2,1)S(1)} %pad_maximum_fusion.refs_0_, bf16[256,1536]{1,0:T(8,128)(2,1)S(1)} %pad_maximum_fusion.1.refs_1_, bf16[1792,1536]{1,0:T(8,128)(2,1)} %head_gradient.4.refs_2_), custom_call_target="tpu_custom_call", output_to_operand_aliasing={{}: (2, {})} | custom-call | flops 402653184 | bytes 3276800 | tf_op jit(solution)/shard_map/head_gradient/pallas_call | solution.py:149
  84.5 0.0 collective-permute-done.13
  84.5 1.1 %collective-permute-done.14 = bf16[224,128]{1,0:T(8,128)(2,1)S(1)} collective-permute-done((bf16[224,128]{1,0:T(8,128)(2,1)S(1)}, bf16[224,128]{1,0:T(8,128)(2,1)S(1)}, u32[]{:S(2)}, u32[]{:S(2)}) %collective-permute-start.14) | collective-permute-done | bytes 57376 | tf_op jit(solution)/shard_map/ppermute | solution.py:275
  85.6 0.7 fusion.18
  (21 shorter events, 0.4 us)
Async XLA Ops:
  0.6 9.2 %copy-start.4 = (s32[1,16]{1,0:T(1,128)S(1)}, s32[1,16]{1,0:T(1,128)}, u32[]{:S(2)}) copy-start(s32[1,16]{1,0:T(1,128)} %param.8) | copy-start | bytes 196
  1.6 8.6 %collective-permute-start = (bf16[64,1792]{1,0:T(8,128)(2,1)S(1)}, bf16[64,1792]{1,0:T(8,128)(2,1)S(1)}, u32[]{:S(2)}, u32[]{:S(2)}) collective-permute-start(bf16[64,1792]{1,0:T(8,128)(2,1)S(1)} %dynamic_slice.23), channel_id=1, source_target_pairs={{0,1},{1,0},{2,3},{3,2},{4,5},{5,4},{6,7},{7,6},{8,9},{9,8},{10,11... | collective-permute-start | bytes 688136 | tf_op jit(solution)/shard_map/ppermute | solution.py:18
  10.3 5.5 %collective-permute-start.2 = (bf16[64,1792]{1,0:T(8,128)(2,1)S(1)}, bf16[64,1792]{1,0:T(8,128)(2,1)S(1)}, u32[]{:S(2)}, u32[]{:S(2)}) collective-permute-start(bf16[64,1792]{1,0:T(8,128)(2,1)S(1)} %collective-permute-done), channel_id=1, source_target_pairs={{0,2},{2,0},{4,6},{6,4},{8,10},{10,8},{12,14},{14,12},{16,18},{18,... | collective-permute-start | bytes 688136 | tf_op jit(solution)/shard_map/ppermute | solution.py:22
  13.9 20.3 %copy-start.2 = (bf16[128,1536]{1,0:T(8,128)(2,1)S(1)}, bf16[128,1536]{1,0:T(8,128)(2,1)}, u32[]{:S(2)}) copy-start(bf16[128,1536]{1,0:T(8,128)(2,1)} %param.7) | copy-start | bytes 1179652
  13.9 12.0 %collective-permute-start.1 = (f32[64,1536]{1,0:T(8,128)S(1)}, f32[64,1536]{1,0:T(8,128)S(1)}, u32[]{:S(2)}, u32[]{:S(2)}) collective-permute-start(f32[64,1536]{1,0:T(8,128)S(1)} %fusion.30), channel_id=1, source_target_pairs={{0,1},{1,0},{2,3},{3,2},{4,5},{5,4},{6,7},{7,6},{8,9},{9,8},{10,11... | collective-permute-start | bytes 1179656 | tf_op jit(solution)/shard_map/ppermute | solution.py:18
  19.3 14.6 %collective-permute-start.3 = (f32[64,1536]{1,0:T(8,128)S(1)}, f32[64,1536]{1,0:T(8,128)S(1)}, u32[]{:S(2)}, u32[]{:S(2)}) collective-permute-start(f32[64,1536]{1,0:T(8,128)S(1)} %fusion.31), channel_id=1, source_target_pairs={{0,1},{1,0},{2,3},{3,2},{4,5},{5,4},{6,7},{7,6},{8,9},{9,8},{10,11... | collective-permute-start | bytes 1179656 | tf_op jit(solution)/shard_map/ppermute | solution.py:18
  34.7 1.2 %collective-permute-start.4 = (f32[1,4,128]{2,1,0:T(4,128)S(1)}, f32[1,4,128]{2,1,0:T(4,128)S(1)}, u32[]{:S(2)}, u32[]{:S(2)}) collective-permute-start(f32[1,4,128]{2,1,0:T(4,128)S(1)} %maximum_bitcast_fusion), channel_id=1, source_target_pairs={{0,2},{2,0},{4,6},{6,4},{8,10},{10,8},{12,14},{14,12},{16,18},{18,... | collective-permute-start | bytes 6152 | tf_op jit(solution)/shard_map/ppermute | solution.py:22
  35.9 3.7 %collective-permute-start.5 = (f32[2,4,128]{2,1,0:T(4,128)S(1)}, f32[2,4,128]{2,1,0:T(4,128)S(1)}, u32[]{:S(2)}, u32[]{:S(2)}) collective-permute-start(f32[2,4,128]{2,1,0:T(4,128)S(1)} %pad_maximum_fusion.5), channel_id=1, source_target_pairs={{0,4},{2,6},{4,0},{6,2},{8,12},{10,14},{12,8},{14,10},{16,20},{18,... | collective-permute-start | bytes 12296 | tf_op jit(solution)/shard_map/ppermute | solution.py:22
  39.6 3.7 %collective-permute-start.6 = (f32[4,4,128]{2,1,0:T(4,128)S(1)}, f32[4,4,128]{2,1,0:T(4,128)S(1)}, u32[]{:S(2)}, u32[]{:S(2)}) collective-permute-start(f32[4,4,128]{2,1,0:T(4,128)S(1)} %pad_maximum_fusion.4), channel_id=1, source_target_pairs={{0,8},{2,10},{4,12},{6,14},{8,0},{10,2},{12,4},{14,6},{16,24},{18,... | collective-permute-start | bytes 24584 | tf_op jit(solution)/shard_map/ppermute | solution.py:22
  43.3 4.7 %collective-permute-start.7 = (f32[8,4,128]{2,1,0:T(4,128)S(1)}, f32[8,4,128]{2,1,0:T(4,128)S(1)}, u32[]{:S(2)}, u32[]{:S(2)}) collective-permute-start(f32[8,4,128]{2,1,0:T(4,128)S(1)} %pad_maximum_fusion.2), channel_id=1, source_target_pairs={{0,16},{2,18},{4,20},{6,22},{8,24},{10,26},{12,28},{14,30},{16,0},... | collective-permute-start | bytes 49160 | tf_op jit(solution)/shard_map/ppermute | solution.py:22
  48.7 13.5 %copy-start.3 = (f32[128]{0:T(128)}, f32[128]{0:T(128)S(1)}, u32[]{:S(2)}) copy-start(f32[128]{0:T(128)S(1)} %get-tuple-element.60) | copy-start | bytes 1540
  49.0 9.1 %collective-permute-start.9 = (bf16[128,1536]{1,0:T(8,128)(2,1)S(1)}, bf16[128,1536]{1,0:T(8,128)(2,1)S(1)}, u32[]{:S(2)}, u32[]{:S(2)}) collective-permute-start(bf16[128,1536]{1,0:T(8,128)(2,1)S(1)} %fusion.7.delta_ref), channel_id=1, source_target_pairs={{0,1},{1,0},{2,3},{3,2},{4,5},{5,4},{6,7},{7,6},{8,9},{9,8},{10,11... | collective-permute-start | bytes 1179656 | tf_op jit(solution)/shard_map/ppermute | solution.py:18
  55.6 2.4 %copy-start = (bf16[1792,1536]{1,0:T(8,128)(2,1)}, bf16[1792,1536]{1,0:T(8,128)(2,1)S(1)}, u32[]{:S(2)}) copy-start(bf16[1792,1536]{1,0:T(8,128)(2,1)S(1)} %get-tuple-element.34.head_ref) | copy-start | bytes 16515076
  58.0 4.2 %collective-permute-start.8 = (bf16[4,224,128]{2,1,0:T(8,128)(2,1)S(1)}, bf16[4,224,128]{2,1,0:T(8,128)(2,1)S(1)}, u32[]{:S(2)}, u32[]{:S(2)}) collective-permute-start(bf16[4,224,128]{2,1,0:T(8,128)(2,1)S(1)} %get-tuple-element.33), channel_id=1, source_target_pairs={{0,2},{2,0},{4,6},{6,4},{8,10},{10,8},{12,14},{14,12},{16,18},{18,... | collective-permute-start | bytes 688136 | tf_op jit(solution)/shard_map/ppermute | solution.py:22
  58.0 2.6 %copy-start.1 = (bf16[1792,1536]{1,0:T(8,128)(2,1)S(1)}, bf16[1792,1536]{1,0:T(8,128)(2,1)}, u32[]{:S(2)}) copy-start(bf16[1792,1536]{1,0:T(8,128)(2,1)} %copy-done) | copy-start | bytes 16515076
  62.2 1.7 %collective-permute-start.10 = (bf16[4,224,128]{2,1,0:T(8,128)(2,1)S(1)}, bf16[4,224,128]{2,1,0:T(8,128)(2,1)S(1)}, u32[]{:S(2)}, u32[]{:S(2)}) collective-permute-start(bf16[4,224,128]{2,1,0:T(8,128)(2,1)S(1)} %get-tuple-element.39), channel_id=1, source_target_pairs={{0,2},{2,0},{4,6},{6,4},{8,10},{10,8},{12,14},{14,12},{16,18},{18,... | collective-permute-start | bytes 688136 | tf_op jit(solution)/shard_map/ppermute | solution.py:22
  64.0 7.9 %collective-permute-start.11 = (bf16[2,2,224,128]{3,2,1,0:T(8,128)(2,1)S(1)}, bf16[2,2,224,128]{3,2,1,0:T(8,128)(2,1)S(1)}, u32[]{:S(2)}, u32[]{:S(2)}) collective-permute-start(bf16[2,2,224,128]{3,2,1,0:T(8,128)(2,1)S(1)} %fusion.14), channel_id=1, source_target_pairs={{0,4},{2,6},{4,0},{6,2},{8,12},{10,14},{12,8},{14,10},{16,20},{18,... | collective-permute-start | bytes 688136 | tf_op jit(solution)/shard_map/ppermute | solution.py:22
  72.0 4.9 %collective-permute-start.12 = (bf16[2,1,224,128]{3,2,1,0:T(8,128)(2,1)S(1)}, bf16[2,1,224,128]{3,2,1,0:T(8,128)(2,1)S(1)}, u32[]{:S(2)}, u32[]{:S(2)}) collective-permute-start(bf16[2,1,224,128]{3,2,1,0:T(8,128)(2,1)S(1)} %dynamic-slice_convert_fusion), channel_id=1, source_target_pairs={{0,8},{2,10},{4,12},{6,14},{8,0},{10,2},{12,4},{14,6},{16,24},{18,... | collective-permute-start | bytes 344072 | tf_op jit(solution)/shard_map/ppermute | solution.py:22
  76.9 7.6 %collective-permute-start.13 = (bf16[224,128]{1,0:T(8,128)(2,1)S(1)}, bf16[224,128]{1,0:T(8,128)(2,1)S(1)}, u32[]{:S(2)}, u32[]{:S(2)}) collective-permute-start(bf16[224,128]{1,0:T(8,128)(2,1)S(1)} %get-tuple-element.48), channel_id=1, source_target_pairs={{1,16},{3,18},{5,20},{7,22},{9,24},{11,26},{13,28},{15,30},{16,1},... | collective-permute-start | bytes 172040 | tf_op jit(solution)/shard_map/ppermute | solution.py:275
  77.6 8.0 %collective-permute-start.14 = (bf16[224,128]{1,0:T(8,128)(2,1)S(1)}, bf16[224,128]{1,0:T(8,128)(2,1)S(1)}, u32[]{:S(2)}, u32[]{:S(2)}) collective-permute-start(bf16[224,128]{1,0:T(8,128)(2,1)S(1)} %get-tuple-element.49), channel_id=1, source_target_pairs={{0,1},{1,17},{2,3},{3,19},{4,5},{5,21},{6,7},{7,23},{8,9},{9,25},{... | collective-permute-start | bytes 172040 | tf_op jit(solution)/shard_map/ppermute | solution.py:275

commit v6 on v5

--- a/solution.py
+++ b/solution.py
@@ -22,36 +22,61 @@
     return lax.ppermute(x, "vocab", [(i, i ^ bit) for i in range(size)])
 
 
-def pick(x, index, axis=0):
-    return lax.dynamic_index_in_dim(x, index, axis, keepdims=False)
-
-
-def listed_columns(block_ids, counts, column_block, token_count):
-    live_slot = jnp.arange(block_ids.shape[1], dtype=jnp.int32)[None, :] < counts[:, None]
-    block_hit = jnp.any(
-        (block_ids[:, :, None] == column_block[None, None, :]) & live_slot[:, :, None], axis=1
-    )
-    token_blocks = block_hit.shape[0]
-    width = column_block.shape[0]
-    return jnp.broadcast_to(
-        block_hit[:, None, :], (token_blocks, token_count // token_blocks, width)
-    ).reshape(token_count, width)
-
-
 def in_order(mine, other, upper):
     return jnp.concatenate(
         [jnp.where(upper, other, mine), jnp.where(upper, mine, other)], axis=0
     )
 
 
-def gather_vocab(stats, vocab_index, size):
+def gather_vocab(stats, upper, size):
     gathered = stats[None]
-    bit = 1
-    while bit < size:
-        other = swap_vocab(gathered, bit, size)
-        gathered = in_order(gathered, other, (vocab_index & bit) != 0)
-        bit *= 2
+    for i, flag in enumerate(upper):
+        gathered = in_order(gathered, swap_vocab(gathered, 1 << i, size), flag)
     return gathered
+
+
+def own_kernel(own_ref, head_ref, out_ref, held_ref, sems):
+    steps = sems.shape[0]
+    depth = head_ref.shape[0] // steps
+    parts = [pl.ds(k * depth, depth) for k in range(steps)]
+    copies = [
+        pltpu.make_async_copy(head_ref.at[part], held_ref.at[part], sems.at[k])
+        for k, part in enumerate(parts)
+    ]
+    for copy in copies[:2]:
+        copy.start()
+    for k in range(steps):
+        copies[k].wait()
+        if k + 2 < steps:
+            copies[k + 2].start()
+        product = jnp.dot(
+            own_ref[:, k * depth : (k + 1) * depth],
+            held_ref[k * depth : (k + 1) * depth, :],
+            preferred_element_type=jnp.float32,
+        )
+        out_ref[...] = product if k == 0 else out_ref[...] + product
+
+
+def own_product(own, head):
+    steps = 7 if head.shape[0] % (7 * 128) == 0 else 1
+    in_vmem = pl.BlockSpec(memory_space=pltpu.VMEM)
+    return pl.pallas_call(
+        own_kernel,
+        out_shape=(
+            pltpu.VMEM((own.shape[0], head.shape[1]), jnp.float32),
+            pltpu.VMEM(head.shape, head.dtype),
+        ),
+        in_specs=[in_vmem, pl.BlockSpec(memory_space=pltpu.HBM)],
+        out_specs=(in_vmem, in_vmem),
+        scratch_shapes=[pltpu.SemaphoreType.DMA((steps,))],
+        compiler_params=pltpu.CompilerParams(vmem_limit_bytes=VMEM_LIMIT),
+        cost_estimate=pl.CostEstimate(
+            flops=2 * head.size * own.shape[0],
+            bytes_accessed=2 * (head.size + own.size),
+            transcendentals=0,
+        ),
+        name="own_product",
+    )(own, pltpu.with_memory_space_constraint(head, pltpu.HBM))
 
 
 def write_pieces(k, head_rows, delta_ref, upper, send_ref, keep_ref):
@@ -116,7 +141,7 @@
         ),
         name="partial_gradient",
     )(
-        core.reshape(1),
+        core,
         pltpu.with_memory_space_constraint(head, space),
         pltpu.with_memory_space_constraint(delta, pltpu.VMEM),
     )
@@ -175,37 +200,54 @@
     rows, column_count = head.shape
     run = vocab_size // tok_size
     half = token_count // 2
-    core = vocab_index % 2
+    core = vocab_index & 1
 
     def columns_of(index, first, count):
         return lax.dynamic_slice(hidden, (first, index * rows), (count, rows))
 
     near = [
-        shift_tok(columns_of((tok_index + d) % tok_size, core * half, half), d, tok_size)
+        shift_tok(columns_of(lax.rem(tok_index + d, tok_size), core * half, half), d, tok_size)
         for d in range(1, tok_size)
     ]
     own = columns_of(tok_index, 0, token_count)
-    logits = jnp.dot(own, head, preferred_element_type=jnp.float32)
+    upper = []
+    while 1 << len(upper) < vocab_size:
+        upper.append((vocab_index & (1 << len(upper))) != 0)
+    high = lax.div(vocab_index, run)
+    apart = lax.rem(tok_index + tok_size - high, tok_size)
+    apart_is = [apart == d for d in range(tok_size)]
+    first_column = vocab_index * column_count
+    column_block = (first_column + jnp.arange(column_count, dtype=jnp.int32)) // BLK
+    live_slot = jnp.arange(block_ids.shape[1], dtype=jnp.int32)[None, :] < counts[:, None]
+    block_hit = jnp.any(
+        (block_ids[:, :, None] == column_block[None, None, :]) & live_slot[:, :, None], axis=1
+    )
+    core_word = core.reshape(1)
+    own, upper, apart_is, block_hit, core_word = lax.optimization_barrier(
+        (own, upper, apart_is, block_hit, core_word)
+    )
+    logits, head_here = own_product(own, head)
     near, logits = lax.optimization_barrier((near, logits))
     far = [swap_vocab(x, 1, vocab_size) for x in near]
     returned = []
     for d in range(1, tok_size):
         first = shift_tok(
-            jnp.dot(near[d - 1], head, preferred_element_type=jnp.float32), -d, tok_size
+            jnp.dot(near[d - 1], head_here, preferred_element_type=jnp.float32), -d, tok_size
         )
         second = shift_tok(
-            jnp.dot(far[d - 1], head, preferred_element_type=jnp.float32), -d, tok_size
+            jnp.dot(far[d - 1], head_here, preferred_element_type=jnp.float32), -d, tok_size
         )
         returned.append((first, second))
-    features = [own] + [in_order(n, f, core != 0) for n, f in zip(near, far)]
+    features = [own] + [in_order(n, f, upper[0]) for n, f in zip(near, far)]
     all_features = jnp.concatenate(features, axis=0)
     returned, all_features = lax.optimization_barrier((returned, all_features))
     for first, second in returned:
-        logits = logits + in_order(first, second, core != 0)
-
-    first_column = vocab_index * column_count
-    column_block = (first_column + jnp.arange(column_count, dtype=jnp.int32)) // BLK
-    listed = listed_columns(block_ids, counts, column_block, token_count)
+        logits = logits + in_order(first, second, upper[0])
+
+    blocks = block_hit.shape[0]
+    listed = jnp.broadcast_to(
+        block_hit[:, None, :], (blocks, token_count // blocks, column_count)
+    ).reshape(token_count, column_count)
     teacher_f = teacher.astype(jnp.float32)
     kept = jnp.where(listed, teacher_f, 0.0)
     local_top = jnp.max(logits, axis=1)
@@ -214,7 +256,7 @@
     local_part = jnp.sum(jnp.where(listed, teacher_f * (jnp.log(teacher_f) - logits), 0.0), axis=1)
 
     stats = gather_vocab(
-        jnp.stack([local_top, local_sum, local_mass, local_part]), vocab_index, vocab_size
+        jnp.stack([local_top, local_sum, local_mass, local_part]), upper, vocab_size
     )
     tops = stats[:, 0]
     global_top = jnp.max(tops, axis=0)
@@ -226,11 +268,11 @@
     delta = (loss_scale * (student - kept / total_mass[:, None])).astype(jnp.bfloat16)
 
     deltas = [delta] + [shift_tok(delta, d, tok_size) for d in range(1, tok_size)]
-    send, keep, head_here = gradient(core, head, delta, run, True)
+    send, keep, head_here = gradient(core_word, head, delta, run, True)
     other = swap_vocab(send, 1, vocab_size)
     state = [(keep, other)]
     for x in deltas[1:]:
-        send, keep = gradient(core, head_here, x, run, False)
+        send, keep = gradient(core_word, head_here, x, run, False)
         state[0], send = lax.optimization_barrier((state[0], send))
         state.append((keep, swap_vocab(send, 1, vocab_size)))
     all_delta = jnp.concatenate(deltas, axis=0)
@@ -240,14 +282,15 @@
     shares = [(chunks + 1) // 2, chunks // 4]
     done = 0
     grad_head = None
-    bit = 2
     held = jnp.stack([keep + other.astype(jnp.float32) for keep, other in state])
-    while bit < run:
+    for i in range(1, len(upper)):
+        if held.shape[1] == 1:
+            break
         pairs = held.reshape(tok_size, held.shape[1] // 2, 2, *held.shape[2:])
-        mine = (vocab_index // bit) % 2
-        send = pick(pairs, 1 - mine, 2).astype(jnp.bfloat16)
+        low, high = pairs[:, :, 0], pairs[:, :, 1]
+        send = jnp.where(upper[i], low, high).astype(jnp.bfloat16)
         send, all_delta = lax.optimization_barrier((send, all_delta))
-        other = swap_vocab(send, bit, vocab_size)
+        other = swap_vocab(send, 1 << i, vocab_size)
         share = shares.pop(0) if shares else 0
         if share:
             grad_head = head_gradient(
@@ -255,14 +298,16 @@
             )
             done += share
             other, grad_head = lax.optimization_barrier((other, grad_head))
-        held = pick(pairs, mine, 2) + other.astype(jnp.float32)
-        bit *= 2
+        held = jnp.where(upper[i], high, low) + other.astype(jnp.float32)
     sums = held[:, 0]
-    high = vocab_index // run
-    apart = (tok_index - high) % tok_size
-    total = jnp.where(apart == 0, sums[0], 0.0)
+    total = jnp.where(apart_is[0], sums[0], 0.0)
     sums = sums.astype(jnp.bfloat16)
-    sends = [pick(sums, (k + apart) % tok_size) for k in range(tok_size)]
+    sends = []
+    for k in range(tok_size):
+        send = sums[k]
+        for d in range(1, tok_size):
+            send = jnp.where(apart_is[d], sums[(k + d) % tok_size], send)
+        sends.append(send)
     sends, all_delta = lax.optimization_barrier((sends, all_delta))
     for k in range(tok_size):
         pairs = []

time: 86.6 us -> 82 us (0.947)
  matrix products: 10.7 us -> 2.13 us
  waiting for transfers between devices: 29.4 us -> 35.4 us
  local copies, waits for them, and re-layouts: 7.07 us -> 2.04 us
  Pallas kernels: 11.3 us -> 16.3 us
  starting transfers between devices: 23.4 us -> 20.6 us
    dot_general x3 -> x2, matrix products: 10.7 us -> 2.13 us  [the longest x1 1.07 us: per_device(): jnp.dot(near[d - 1], head_here, preferred_element_type=jnp.float32)]
    pallas_call x0 -> x1, Pallas kernels: none -> 5.04 us  [own_product(): pl.pallas_call(own_kernel, out_shape=(pltpu.VMEM((own.shape[0], head.shap...]
    unnamed x10 -> x4, local copies, waits for them, and re-layouts: 5.01 us -> 0.01 us
    ppermute x4, waiting for transfers between devices: 14.4 us -> 19.3 us  [shift_tok(): lax.ppermute(x, 'tok', [(i, (i + offset) % size) for i in range(size)])]
    ppermute x4, starting transfers between devices: 6.99 us -> 5.25 us  [shift_tok(): lax.ppermute(x, 'tok', [(i, (i + offset) % size) for i in range(size)])]
    ppermute x9, waiting for transfers between devices: 13.9 us -> 15.1 us  [swap_vocab(): return lax.ppermute(x, 'vocab', [(i, i ^ bit) for i in range(size)])]
    ppermute x9, starting transfers between devices: 10.4 us -> 9.31 us  [swap_vocab(): return lax.ppermute(x, 'vocab', [(i, i ^ bit) for i in range(size)])]
  transfers between devices with their start and end apart: 15 -> 15, of which waited for: 11 -> 12; matrix products, arithmetic and copies ran while one was open for 14% -> 5% of each run, Pallas kernels for 13% -> 20%
where the time goes in v6:
time: 82 us; the launch traced here: 81.7 us
  waiting for transfers between devices  35.4 us (43%)
  starting transfers between devices  20.6 us (25%)
  Pallas kernels  16.3 us (20%)
  other arithmetic  3.67 us (4%)
  matrix products  2.13 us (3%)
  local copies, waits for them, and re-layouts  2.04 us (2%)
  between operations  1.56 us (2%)
    ppermute x4, waiting for transfers between devices, shift_tok(): lax.ppermute(x, 'tok', [(i, (i + offset) % size) for i in range(size)])  19.3 us
    ppermute x9, waiting for transfers between devices, swap_vocab(): return lax.ppermute(x, 'vocab', [(i, i ^ bit) for i in range(size)])  15.1 us
    ppermute x9, starting transfers between devices, swap_vocab(): return lax.ppermute(x, 'vocab', [(i, i ^ bit) for i in range(size)])  9.31 us
    pallas_call x2, Pallas kernels, gradient(): pl.pallas_call(first_gradient_kernel if first else later_gradient_kernel,...  6.38 us
    ppermute x2, starting transfers between devices, per_device(): lax.ppermute(sends[k], ('vocab', 'tok'), pairs).astype(jnp.float32)  6.01 us
    ppermute x4, starting transfers between devices, shift_tok(): lax.ppermute(x, 'tok', [(i, (i + offset) % size) for i in range(size)])  5.25 us
    pallas_call x1, Pallas kernels, own_product(): pl.pallas_call(own_kernel, out_shape=(pltpu.VMEM((own.shape[0], head.shap...  5.04 us
    pallas_call x3, Pallas kernels, head_gradient(): pl.pallas_call(functools.partial(head_gradient_kernel, steps, start, widt...  4.9 us
  transfers between devices with their start and end apart: 15, of which 12 were waited for; matrix products, arithmetic and copies ran while one was open for 5% of the time, Pallas kernels for 20%

profile of v6, /device:TPU:0, one launch (start us, length us, event | category | flops | bytes accessed | tf_op | source)
XLA Modules:
  0.0 81.7 jit_solution(2741651298647966684)
XLA Ops:
  0.6 1.0 %dynamic_slice.7 = bf16[64,1792]{1,0:T(8,128)(2,1)S(1)} dynamic-slice(bf16[128,3584]{1,0:T(8,128)(2,1)} %param.5, s32[]{:T(128)S(6)} %select_n.182, s32[]{:T(128)S(6)} %select_n.183), dynamic_slice_sizes={64,1792} | dynamic-slice | bytes 458756 | tf_op jit(solution)/shard_map/dynamic_slice | solution.py:206
  1.6 3.0 %collective-permute-start = (bf16[64,1792]{1,0:T(8,128)(2,1)S(1)}, bf16[64,1792]{1,0:T(8,128)(2,1)S(1)}, u32[]{:S(2)}, u32[]{:S(2)}) collective-permute-start(bf16[64,1792]{1,0:T(8,128)(2,1)S(1)} %dynamic_slice.7), channel_id=1, source_target_pairs={{0,1},{1,0},{2,3},{3,2},{4,5},{5,4},{6,7},{7,6},{8,9},{9,8},{10,11... | collective-permute-start | bytes 688136 | tf_op jit(solution)/shard_map/ppermute | solution.py:18
  5.3 0.8 and_reduce_fusion
  6.1 1.1 %constant_dynamic-slice_fusion.own_ref = bf16[128,1792]{1,0:T(8,128)(2,1)S(1)} fusion(bf16[128,3584]{1,0:T(8,128)(2,1)} %param.5, s32[]{:T(128)S(6)} %select_n.176), kind=kLoop, calls=%fused_computation.77 | loop fusion | bytes 917508 | tf_op jit(solution)/shard_map/dynamic_slice | solution.py:206
  7.2 5.0 %own_product.1 = (f32[128,1536]{1,0:T(8,128)S(1)}, bf16[1792,1536]{1,0:T(8,128)(2,1)S(1)}) custom-call(bf16[128,1792]{1,0:T(8,128)(2,1)S(1)} %constant_dynamic-slice_fusion.own_ref, bf16[1792,1536]{1,0:T(8,128)(2,1)} %head_ref.3), custom_call_target="tpu_custom_call" | custom-call | flops 704643072 | bytes 5963776 | tf_op jit(solution)/shard_map/own_product/pallas_call | solution.py:63
  12.2 0.0 collective-permute-done
  12.3 0.1 collective-permute-start.2
  12.3 1.1 %fusion.26 = f32[64,1536]{1,0:T(8,128)S(1)} fusion(bf16[64,1792]{1,0:T(8,128)(2,1)S(1)} %collective-permute-done, bf16[1792,1536]{1,0:T(8,128)(2,1)S(1)} %get-tuple-element.47), kind=kOutput, calls=%fused_computation.80 | convolution fusion | flops 352321536 | bytes 6127616 | tf_op jit(solution)/shard_map/dot_general | solution.py:235
  13.4 0.0 copy-start
  13.4 0.1 collective-permute-start.1
  13.5 0.3 collective-permute-done.2
  13.8 1.1 %fusion.27 = f32[64,1536]{1,0:T(8,128)S(1)} fusion(bf16[64,1792]{1,0:T(8,128)(2,1)S(1)} %collective-permute-done.2, bf16[1792,1536]{1,0:T(8,128)(2,1)S(1)} %get-tuple-element.47), kind=kOutput, calls=%fused_computation.81 | convolution fusion | flops 352321536 | bytes 6127616 | tf_op jit(solution)/shard_map/dot_general | solution.py:238
  14.9 1.8 %collective-permute-start.3 = (f32[64,1536]{1,0:T(8,128)S(1)}, f32[64,1536]{1,0:T(8,128)S(1)}, u32[]{:S(2)}, u32[]{:S(2)}) collective-permute-start(f32[64,1536]{1,0:T(8,128)S(1)} %fusion.27), channel_id=1, source_target_pairs={{0,1},{1,0},{2,3},{3,2},{4,5},{5,4},{6,7},{7,6},{8,9},{9,8},{10,11... | collective-permute-start | bytes 1179656 | tf_op jit(solution)/shard_map/ppermute | solution.py:18
  16.6 0.1 broadcast_select_fusion.1
  16.7 0.1 pad_maximum_fusion.refs_0_
  16.8 8.6 %collective-permute-done.1 = f32[64,1536]{1,0:T(8,128)S(1)} collective-permute-done((f32[64,1536]{1,0:T(8,128)S(1)}, f32[64,1536]{1,0:T(8,128)S(1)}, u32[]{:S(2)}, u32[]{:S(2)}) %collective-permute-start.1) | collective-permute-done | bytes 393248 | tf_op jit(solution)/shard_map/ppermute | solution.py:18
  25.4 8.0 %collective-permute-done.3 = f32[64,1536]{1,0:T(8,128)S(1)} collective-permute-done((f32[64,1536]{1,0:T(8,128)S(1)}, f32[64,1536]{1,0:T(8,128)S(1)}, u32[]{:S(2)}, u32[]{:S(2)}) %collective-permute-start.3) | collective-permute-done | bytes 393248 | tf_op jit(solution)/shard_map/ppermute | solution.py:18
  33.4 0.1 broadcast_select_fusion.3
  33.5 0.2 fusion.25
  33.7 0.0 copy-done
  33.7 0.5 exponential_reduce_fusion
  34.2 0.1 collective-permute-start.4
  34.2 1.1 %collective-permute-done.4 = f32[1,4,128]{2,1,0:T(4,128)S(1)} collective-permute-done((f32[1,4,128]{2,1,0:T(4,128)S(1)}, f32[1,4,128]{2,1,0:T(4,128)S(1)}, u32[]{:S(2)}, u32[]{:S(2)}) %collective-permute-start.4) | collective-permute-done | bytes 2080 | tf_op jit(solution)/shard_map/ppermute | solution.py:22
  35.4 1.6 %collective-permute-start.5 = (f32[2,4,128]{2,1,0:T(4,128)S(1)}, f32[2,4,128]{2,1,0:T(4,128)S(1)}, u32[]{:S(2)}, u32[]{:S(2)}) collective-permute-start(f32[2,4,128]{2,1,0:T(4,128)S(1)} %pad_maximum_fusion.6), channel_id=1, source_target_pairs={{0,4},{2,6},{4,0},{6,2},{8,12},{10,14},{12,8},{14,10},{16,20},{18,... | collective-permute-start | bytes 12296 | tf_op jit(solution)/shard_map/ppermute | solution.py:22
  37.0 2.1 %collective-permute-done.5 = f32[2,4,128]{2,1,0:T(4,128)S(1)} collective-permute-done((f32[2,4,128]{2,1,0:T(4,128)S(1)}, f32[2,4,128]{2,1,0:T(4,128)S(1)}, u32[]{:S(2)}, u32[]{:S(2)}) %collective-permute-start.5) | collective-permute-done | bytes 4128 | tf_op jit(solution)/shard_map/ppermute | solution.py:22
  39.1 1.6 %collective-permute-start.6 = (f32[4,4,128]{2,1,0:T(4,128)S(1)}, f32[4,4,128]{2,1,0:T(4,128)S(1)}, u32[]{:S(2)}, u32[]{:S(2)}) collective-permute-start(f32[4,4,128]{2,1,0:T(4,128)S(1)} %pad_maximum_fusion.5), channel_id=1, source_target_pairs={{0,8},{2,10},{4,12},{6,14},{8,0},{10,2},{12,4},{14,6},{16,24},{18,... | collective-permute-start | bytes 24584 | tf_op jit(solution)/shard_map/ppermute | solution.py:22
  40.7 2.1 %collective-permute-done.6 = f32[4,4,128]{2,1,0:T(4,128)S(1)} collective-permute-done((f32[4,4,128]{2,1,0:T(4,128)S(1)}, f32[4,4,128]{2,1,0:T(4,128)S(1)}, u32[]{:S(2)}, u32[]{:S(2)}) %collective-permute-start.6) | collective-permute-done | bytes 8224 | tf_op jit(solution)/shard_map/ppermute | solution.py:22
  42.8 2.7 %collective-permute-start.7 = (f32[8,4,128]{2,1,0:T(4,128)S(1)}, f32[8,4,128]{2,1,0:T(4,128)S(1)}, u32[]{:S(2)}, u32[]{:S(2)}) collective-permute-start(f32[8,4,128]{2,1,0:T(4,128)S(1)} %pad_maximum_fusion.3), channel_id=1, source_target_pairs={{0,16},{2,18},{4,20},{6,22},{8,24},{10,26},{12,28},{14,30},{16,0},... | collective-permute-start | bytes 49160 | tf_op jit(solution)/shard_map/ppermute | solution.py:22
  45.5 2.1 %collective-permute-done.7 = f32[8,4,128]{2,1,0:T(4,128)S(1)} collective-permute-done((f32[8,4,128]{2,1,0:T(4,128)S(1)}, f32[8,4,128]{2,1,0:T(4,128)S(1)}, u32[]{:S(2)}, u32[]{:S(2)}) %collective-permute-start.7) | collective-permute-done | bytes 16416 | tf_op jit(solution)/shard_map/ppermute | solution.py:22
  47.6 0.5 subtract_add_fusion
  48.2 0.0 copy-start.1
  48.2 0.3 fusion.7.delta_ref
  48.5 0.4 collective-permute-start.9
  48.8 4.8 %partial_gradient.2 = (bf16[4,224,128]{2,1,0:T(8,128)(2,1)S(1)}, f32[4,224,128]{2,1,0:T(8,128)S(1)}, bf16[1792,1536]{1,0:T(8,128)(2,1)S(1)}) custom-call(s32[1]{0:T(128)} %bitcast.2.core_ref, bf16[1792,1536]{1,0:T(8,128)(2,1)} %head_ref.3, bf16[128,1536]{1,0:T(8,128)(2,1)S(1)} %fusion.7.delta_ref), custom_call_target="tpu_custom_call" | custom-call | flops 704643072 | bytes 5898240 | tf_op jit(solution)/shard_map/partial_gradient/pallas_call | solution.py:126
  53.6 0.1 collective-permute-start.8
  53.7 2.6 %collective-permute-done.9.delta_ref = bf16[128,1536]{1,0:T(8,128)(2,1)S(1)} collective-permute-done((bf16[128,1536]{1,0:T(8,128)(2,1)S(1)}, bf16[128,1536]{1,0:T(8,128)(2,1)S(1)}, u32[]{:S(2)}, u32[]{:S(2)}) %collective-permute-start.9) | collective-permute-done | bytes 393248 | tf_op jit(solution)/shard_map/ppermute | solution.py:18
  56.3 1.6 %partial_gradient.3 = (bf16[4,224,128]{2,1,0:T(8,128)(2,1)S(1)}, f32[4,224,128]{2,1,0:T(8,128)S(1)}) custom-call(s32[1]{0:T(128)} %bitcast.2.core_ref, bf16[1792,1536]{1,0:T(8,128)(2,1)S(1)} %get-tuple-element.55.head_ref, bf16[128,1536]{1,0:T(8,128)(2,1)S(1)} %collective-permute-done.9.delta_ref), custom_call_target="tpu_custom_call" | custom-call | flops 704643072 | bytes 5898240 | tf_op jit(solution)/shard_map/partial_gradient/pallas_call | solution.py:126
  57.9 0.0 copy-done.1
  57.9 0.0 collective-permute-done.8
  57.9 0.1 collective-permute-start.10
  58.0 0.1 pad_maximum_fusion.1.refs_1_
  58.1 1.4 %collective-permute-done.10 = bf16[4,224,128]{2,1,0:T(8,128)(2,1)S(1)} collective-permute-done((bf16[4,224,128]{2,1,0:T(8,128)(2,1)S(1)}, bf16[4,224,128]{2,1,0:T(8,128)(2,1)S(1)}, u32[]{:S(2)}, u32[]{:S(2)}) %collective-permute-start.10) | collective-permute-done | bytes 229408 | tf_op jit(solution)/shard_map/ppermute | solution.py:22
  59.5 0.1 pad_maximum_fusion.2
  59.6 1.5 %collective-permute-start.11 = (bf16[2,2,224,128]{3,2,0,1:T(8,128)(2,1)S(1)}, bf16[2,2,224,128]{3,2,0,1:T(8,128)(2,1)S(1)}, u32[]{:S(2)}, u32[]{:S(2)}) collective-permute-start(bf16[2,2,224,128]{3,2,0,1:T(8,128)(2,1)S(1)} %fusion.10), channel_id=1, source_target_pairs={{0,4},{2,6},{4,0},{6,2},{8,12},{10,14},{12,8},{14,10},{16,20},{18,... | collective-permute-start | bytes 688136 | tf_op jit(solution)/shard_map/ppermute | solution.py:22
  61.2 2.1 %head_gradient.3.refs_2_ = bf16[1792,1536]{1,0:T(8,128)(2,1)} custom-call(bf16[256,1792]{1,0:T(8,128)(2,1)S(1)} %pad_maximum_fusion.refs_0_, bf16[256,1536]{1,0:T(8,128)(2,1)S(1)} %pad_maximum_fusion.1.refs_1_), custom_call_target="tpu_custom_call" | custom-call | flops 805306368 | bytes 4849664 | tf_op jit(solution)/shard_map/head_gradient/pallas_call | solution.py:174
  63.3 4.1 %collective-permute-done.11 = bf16[2,2,224,128]{3,2,0,1:T(8,128)(2,1)S(1)} collective-permute-done((bf16[2,2,224,128]{3,2,0,1:T(8,128)(2,1)S(1)}, bf16[2,2,224,128]{3,2,0,1:T(8,128)(2,1)S(1)}, u32[]{:S(2)}, u32[]{:S(2)}) %collective-permute-start.11) | collective-permute-done | bytes 229408 | tf_op jit(solution)/shard_map/ppermute | solution.py:22
  67.3 0.1 fusion.9
  67.4 1.6 %collective-permute-start.12 = (bf16[2,1,224,128]{3,2,1,0:T(8,128)(2,1)S(1)}, bf16[2,1,224,128]{3,2,1,0:T(8,128)(2,1)S(1)}, u32[]{:S(2)}, u32[]{:S(2)}) collective-permute-start(bf16[2,1,224,128]{3,2,1,0:T(8,128)(2,1)S(1)} %fusion.11), channel_id=1, source_target_pairs={{0,8},{2,10},{4,12},{6,14},{8,0},{10,2},{12,4},{14,6},{16,24},{18,... | collective-permute-start | bytes 344072 | tf_op jit(solution)/shard_map/ppermute | solution.py:22
  69.1 1.3 %head_gradient.4.refs_2_ = bf16[1792,1536]{1,0:T(8,128)(2,1)} custom-call(bf16[256,1792]{1,0:T(8,128)(2,1)S(1)} %pad_maximum_fusion.refs_0_, bf16[256,1536]{1,0:T(8,128)(2,1)S(1)} %pad_maximum_fusion.1.refs_1_, bf16[1792,1536]{1,0:T(8,128)(2,1)} %head_gradient.3.refs_2_), custom_call_target="tpu_custom_call", output_to_operand_aliasing={{}: (2, {})} | custom-call | flops 201326592 | bytes 2490368 | tf_op jit(solution)/shard_map/head_gradient/pallas_call | solution.py:174
  70.4 1.9 %collective-permute-done.12 = bf16[2,1,224,128]{3,2,1,0:T(8,128)(2,1)S(1)} collective-permute-done((bf16[2,1,224,128]{3,2,1,0:T(8,128)(2,1)S(1)}, bf16[2,1,224,128]{3,2,1,0:T(8,128)(2,1)S(1)}, u32[]{:S(2)}, u32[]{:S(2)}) %collective-permute-start.12) | collective-permute-done | bytes 114720 | tf_op jit(solution)/shard_map/ppermute | solution.py:22
  72.4 0.7 collective-permute-start.13
  73.0 5.3 %collective-permute-start.14 = (bf16[224,128]{1,0:T(8,128)(2,1)S(1)}, bf16[224,128]{1,0:T(8,128)(2,1)S(1)}, u32[]{:S(2)}, u32[]{:S(2)}) collective-permute-start(bf16[224,128]{1,0:T(8,128)(2,1)S(1)} %get-tuple-element.71), channel_id=1, source_target_pairs={{0,1},{1,17},{2,3},{3,19},{4,5},{5,21},{6,7},{7,23},{8,9},{9,25},{... | collective-permute-start | bytes 172040 | tf_op jit(solution)/shard_map/ppermute | solution.py:320
  78.4 1.5 %head_gradient.5 = bf16[1792,1536]{1,0:T(8,128)(2,1)} custom-call(bf16[256,1792]{1,0:T(8,128)(2,1)S(1)} %pad_maximum_fusion.refs_0_, bf16[256,1536]{1,0:T(8,128)(2,1)S(1)} %pad_maximum_fusion.1.refs_1_, bf16[1792,1536]{1,0:T(8,128)(2,1)} %head_gradient.4.refs_2_), custom_call_target="tpu_custom_call", output_to_operand_aliasing={{}: (2, {})} | custom-call | flops 402653184 | bytes 3276800 | tf_op jit(solution)/shard_map/head_gradient/pallas_call | solution.py:174
  79.9 0.0 collective-permute-done.13
  79.9 1.1 %collective-permute-done.14 = bf16[224,128]{1,0:T(8,128)(2,1)S(1)} collective-permute-done((bf16[224,128]{1,0:T(8,128)(2,1)S(1)}, bf16[224,128]{1,0:T(8,128)(2,1)S(1)}, u32[]{:S(2)}, u32[]{:S(2)}) %collective-permute-start.14) | collective-permute-done | bytes 57376 | tf_op jit(solution)/shard_map/ppermute | solution.py:320
  81.0 0.7 fusion.15
  (21 shorter events, 0.4 us)
Async XLA Ops:
  1.6 10.6 %collective-permute-start = (bf16[64,1792]{1,0:T(8,128)(2,1)S(1)}, bf16[64,1792]{1,0:T(8,128)(2,1)S(1)}, u32[]{:S(2)}, u32[]{:S(2)}) collective-permute-start(bf16[64,1792]{1,0:T(8,128)(2,1)S(1)} %dynamic_slice.7), channel_id=1, source_target_pairs={{0,1},{1,0},{2,3},{3,2},{4,5},{5,4},{6,7},{7,6},{8,9},{9,8},{10,11... | collective-permute-start | bytes 688136 | tf_op jit(solution)/shard_map/ppermute | solution.py:18
  12.3 1.6 %collective-permute-start.2 = (bf16[64,1792]{1,0:T(8,128)(2,1)S(1)}, bf16[64,1792]{1,0:T(8,128)(2,1)S(1)}, u32[]{:S(2)}, u32[]{:S(2)}) collective-permute-start(bf16[64,1792]{1,0:T(8,128)(2,1)S(1)} %collective-permute-done), channel_id=1, source_target_pairs={{0,2},{2,0},{4,6},{6,4},{8,10},{10,8},{12,14},{14,12},{16,18},{18,... | collective-permute-start | bytes 688136 | tf_op jit(solution)/shard_map/ppermute | solution.py:22
  13.4 20.3 %copy-start = (bf16[128,1536]{1,0:T(8,128)(2,1)S(1)}, bf16[128,1536]{1,0:T(8,128)(2,1)}, u32[]{:S(2)}) copy-start(bf16[128,1536]{1,0:T(8,128)(2,1)} %param.7) | copy-start | bytes 1179652
  13.4 12.0 %collective-permute-start.1 = (f32[64,1536]{1,0:T(8,128)S(1)}, f32[64,1536]{1,0:T(8,128)S(1)}, u32[]{:S(2)}, u32[]{:S(2)}) collective-permute-start(f32[64,1536]{1,0:T(8,128)S(1)} %fusion.26), channel_id=1, source_target_pairs={{0,1},{1,0},{2,3},{3,2},{4,5},{5,4},{6,7},{7,6},{8,9},{9,8},{10,11... | collective-permute-start | bytes 1179656 | tf_op jit(solution)/shard_map/ppermute | solution.py:18
  14.9 18.5 %collective-permute-start.3 = (f32[64,1536]{1,0:T(8,128)S(1)}, f32[64,1536]{1,0:T(8,128)S(1)}, u32[]{:S(2)}, u32[]{:S(2)}) collective-permute-start(f32[64,1536]{1,0:T(8,128)S(1)} %fusion.27), channel_id=1, source_target_pairs={{0,1},{1,0},{2,3},{3,2},{4,5},{5,4},{6,7},{7,6},{8,9},{9,8},{10,11... | collective-permute-start | bytes 1179656 | tf_op jit(solution)/shard_map/ppermute | solution.py:18
  34.2 1.2 %collective-permute-start.4 = (f32[1,4,128]{2,1,0:T(4,128)S(1)}, f32[1,4,128]{2,1,0:T(4,128)S(1)}, u32[]{:S(2)}, u32[]{:S(2)}) collective-permute-start(f32[1,4,128]{2,1,0:T(4,128)S(1)} %maximum_bitcast_fusion), channel_id=1, source_target_pairs={{0,2},{2,0},{4,6},{6,4},{8,10},{10,8},{12,14},{14,12},{16,18},{18,... | collective-permute-start | bytes 6152 | tf_op jit(solution)/shard_map/ppermute | solution.py:22
  35.4 3.7 %collective-permute-start.5 = (f32[2,4,128]{2,1,0:T(4,128)S(1)}, f32[2,4,128]{2,1,0:T(4,128)S(1)}, u32[]{:S(2)}, u32[]{:S(2)}) collective-permute-start(f32[2,4,128]{2,1,0:T(4,128)S(1)} %pad_maximum_fusion.6), channel_id=1, source_target_pairs={{0,4},{2,6},{4,0},{6,2},{8,12},{10,14},{12,8},{14,10},{16,20},{18,... | collective-permute-start | bytes 12296 | tf_op jit(solution)/shard_map/ppermute | solution.py:22
  39.1 3.7 %collective-permute-start.6 = (f32[4,4,128]{2,1,0:T(4,128)S(1)}, f32[4,4,128]{2,1,0:T(4,128)S(1)}, u32[]{:S(2)}, u32[]{:S(2)}) collective-permute-start(f32[4,4,128]{2,1,0:T(4,128)S(1)} %pad_maximum_fusion.5), channel_id=1, source_target_pairs={{0,8},{2,10},{4,12},{6,14},{8,0},{10,2},{12,4},{14,6},{16,24},{18,... | collective-permute-start | bytes 24584 | tf_op jit(solution)/shard_map/ppermute | solution.py:22
  42.8 4.7 %collective-permute-start.7 = (f32[8,4,128]{2,1,0:T(4,128)S(1)}, f32[8,4,128]{2,1,0:T(4,128)S(1)}, u32[]{:S(2)}, u32[]{:S(2)}) collective-permute-start(f32[8,4,128]{2,1,0:T(4,128)S(1)} %pad_maximum_fusion.3), channel_id=1, source_target_pairs={{0,16},{2,18},{4,20},{6,22},{8,24},{10,26},{12,28},{14,30},{16,0},... | collective-permute-start | bytes 49160 | tf_op jit(solution)/shard_map/ppermute | solution.py:22
  48.2 9.7 %copy-start.1 = (f32[128]{0:T(128)}, f32[128]{0:T(128)S(1)}, u32[]{:S(2)}) copy-start(f32[128]{0:T(128)S(1)} %get-tuple-element.82) | copy-start | bytes 1540
  48.5 7.8 %collective-permute-start.9 = (bf16[128,1536]{1,0:T(8,128)(2,1)S(1)}, bf16[128,1536]{1,0:T(8,128)(2,1)S(1)}, u32[]{:S(2)}, u32[]{:S(2)}) collective-permute-start(bf16[128,1536]{1,0:T(8,128)(2,1)S(1)} %fusion.7.delta_ref), channel_id=1, source_target_pairs={{0,1},{1,0},{2,3},{3,2},{4,5},{5,4},{6,7},{7,6},{8,9},{9,8},{10,11... | collective-permute-start | bytes 1179656 | tf_op jit(solution)/shard_map/ppermute | solution.py:18
  53.6 4.3 %collective-permute-start.8 = (bf16[4,224,128]{2,1,0:T(8,128)(2,1)S(1)}, bf16[4,224,128]{2,1,0:T(8,128)(2,1)S(1)}, u32[]{:S(2)}, u32[]{:S(2)}) collective-permute-start(bf16[4,224,128]{2,1,0:T(8,128)(2,1)S(1)} %get-tuple-element.54), channel_id=1, source_target_pairs={{0,2},{2,0},{4,6},{6,4},{8,10},{10,8},{12,14},{14,12},{16,18},{18,... | collective-permute-start | bytes 688136 | tf_op jit(solution)/shard_map/ppermute | solution.py:22
  57.9 1.6 %collective-permute-start.10 = (bf16[4,224,128]{2,1,0:T(8,128)(2,1)S(1)}, bf16[4,224,128]{2,1,0:T(8,128)(2,1)S(1)}, u32[]{:S(2)}, u32[]{:S(2)}) collective-permute-start(bf16[4,224,128]{2,1,0:T(8,128)(2,1)S(1)} %get-tuple-element.60), channel_id=1, source_target_pairs={{0,2},{2,0},{4,6},{6,4},{8,10},{10,8},{12,14},{14,12},{16,18},{18,... | collective-permute-start | bytes 688136 | tf_op jit(solution)/shard_map/ppermute | solution.py:22
  59.6 7.7 %collective-permute-start.11 = (bf16[2,2,224,128]{3,2,0,1:T(8,128)(2,1)S(1)}, bf16[2,2,224,128]{3,2,0,1:T(8,128)(2,1)S(1)}, u32[]{:S(2)}, u32[]{:S(2)}) collective-permute-start(bf16[2,2,224,128]{3,2,0,1:T(8,128)(2,1)S(1)} %fusion.10), channel_id=1, source_target_pairs={{0,4},{2,6},{4,0},{6,2},{8,12},{10,14},{12,8},{14,10},{16,20},{18,... | collective-permute-start | bytes 688136 | tf_op jit(solution)/shard_map/ppermute | solution.py:22
  67.4 4.9 %collective-permute-start.12 = (bf16[2,1,224,128]{3,2,1,0:T(8,128)(2,1)S(1)}, bf16[2,1,224,128]{3,2,1,0:T(8,128)(2,1)S(1)}, u32[]{:S(2)}, u32[]{:S(2)}) collective-permute-start(bf16[2,1,224,128]{3,2,1,0:T(8,128)(2,1)S(1)} %fusion.11), channel_id=1, source_target_pairs={{0,8},{2,10},{4,12},{6,14},{8,0},{10,2},{12,4},{14,6},{16,24},{18,... | collective-permute-start | bytes 344072 | tf_op jit(solution)/shard_map/ppermute | solution.py:22
  72.4 7.6 %collective-permute-start.13 = (bf16[224,128]{1,0:T(8,128)(2,1)S(1)}, bf16[224,128]{1,0:T(8,128)(2,1)S(1)}, u32[]{:S(2)}, u32[]{:S(2)}) collective-permute-start(bf16[224,128]{1,0:T(8,128)(2,1)S(1)} %get-tuple-element.70), channel_id=1, source_target_pairs={{1,16},{3,18},{5,20},{7,22},{9,24},{11,26},{13,28},{15,30},{16,1},... | collective-permute-start | bytes 172040 | tf_op jit(solution)/shard_map/ppermute | solution.py:320
  73.0 8.0 %collective-permute-start.14 = (bf16[224,128]{1,0:T(8,128)(2,1)S(1)}, bf16[224,128]{1,0:T(8,128)(2,1)S(1)}, u32[]{:S(2)}, u32[]{:S(2)}) collective-permute-start(bf16[224,128]{1,0:T(8,128)(2,1)S(1)} %get-tuple-element.71), channel_id=1, source_target_pairs={{0,1},{1,17},{2,3},{3,19},{4,5},{5,21},{6,7},{7,23},{8,9},{9,25},{... | collective-permute-start | bytes 172040 | tf_op jit(solution)/shard_map/ppermute | solution.py:320

commit v7 on v6

--- a/solution.py
+++ b/solution.py
@@ -35,7 +35,7 @@
     return gathered
 
 
-def own_kernel(own_ref, head_ref, out_ref, held_ref, sems):
+def load_kernel(head_ref, held_ref, sems):
     steps = sems.shape[0]
     depth = head_ref.shape[0] // steps
     parts = [pl.ds(k * depth, depth) for k in range(steps)]
@@ -43,40 +43,26 @@
         pltpu.make_async_copy(head_ref.at[part], held_ref.at[part], sems.at[k])
         for k, part in enumerate(parts)
     ]
-    for copy in copies[:2]:
+    for copy in copies:
         copy.start()
-    for k in range(steps):
-        copies[k].wait()
-        if k + 2 < steps:
-            copies[k + 2].start()
-        product = jnp.dot(
-            own_ref[:, k * depth : (k + 1) * depth],
-            held_ref[k * depth : (k + 1) * depth, :],
-            preferred_element_type=jnp.float32,
-        )
-        out_ref[...] = product if k == 0 else out_ref[...] + product
-
-
-def own_product(own, head):
-    steps = 7 if head.shape[0] % (7 * 128) == 0 else 1
-    in_vmem = pl.BlockSpec(memory_space=pltpu.VMEM)
+    for copy in copies:
+        copy.wait()
+
+
+def load(head):
+    steps = 4
     return pl.pallas_call(
-        own_kernel,
-        out_shape=(
-            pltpu.VMEM((own.shape[0], head.shape[1]), jnp.float32),
-            pltpu.VMEM(head.shape, head.dtype),
-        ),
-        in_specs=[in_vmem, pl.BlockSpec(memory_space=pltpu.HBM)],
-        out_specs=(in_vmem, in_vmem),
+        load_kernel,
+        out_shape=pltpu.VMEM(head.shape, head.dtype),
+        in_specs=[pl.BlockSpec(memory_space=pltpu.HBM)],
+        out_specs=pl.BlockSpec(memory_space=pltpu.VMEM),
         scratch_shapes=[pltpu.SemaphoreType.DMA((steps,))],
         compiler_params=pltpu.CompilerParams(vmem_limit_bytes=VMEM_LIMIT),
         cost_estimate=pl.CostEstimate(
-            flops=2 * head.size * own.shape[0],
-            bytes_accessed=2 * (head.size + own.size),
-            transcendentals=0,
+            flops=0, bytes_accessed=4 * head.size, transcendentals=0
         ),
-        name="own_product",
-    )(own, pltpu.with_memory_space_constraint(head, pltpu.HBM))
+        name="load_head",
+    )(pltpu.with_memory_space_constraint(head, pltpu.HBM))
 
 
 def write_pieces(k, head_rows, delta_ref, upper, send_ref, keep_ref):
@@ -209,7 +195,6 @@
         shift_tok(columns_of(lax.rem(tok_index + d, tok_size), core * half, half), d, tok_size)
         for d in range(1, tok_size)
     ]
-    own = columns_of(tok_index, 0, token_count)
     upper = []
     while 1 << len(upper) < vocab_size:
         upper.append((vocab_index & (1 << len(upper))) != 0)
@@ -219,15 +204,13 @@
     first_column = vocab_index * column_count
     column_block = (first_column + jnp.arange(column_count, dtype=jnp.int32)) // BLK
     live_slot = jnp.arange(block_ids.shape[1], dtype=jnp.int32)[None, :] < counts[:, None]
-    block_hit = jnp.any(
-        (block_ids[:, :, None] == column_block[None, None, :]) & live_slot[:, :, None], axis=1
-    )
     core_word = core.reshape(1)
-    own, upper, apart_is, block_hit, core_word = lax.optimization_barrier(
-        (own, upper, apart_is, block_hit, core_word)
-    )
-    logits, head_here = own_product(own, head)
-    near, logits = lax.optimization_barrier((near, logits))
+    own = columns_of(tok_index, 0, token_count)
+    own, head, upper, apart_is, column_block, live_slot, core_word = lax.optimization_barrier(
+        (own, head, upper, apart_is, column_block, live_slot, core_word)
+    )
+    head_here = load(head)
+    near, head_here = lax.optimization_barrier((near, head_here))
     far = [swap_vocab(x, 1, vocab_size) for x in near]
     returned = []
     for d in range(1, tok_size):
@@ -238,9 +221,15 @@
             jnp.dot(far[d - 1], head_here, preferred_element_type=jnp.float32), -d, tok_size
         )
         returned.append((first, second))
+    logits = jnp.dot(own, head_here, preferred_element_type=jnp.float32)
+    block_hit = jnp.any(
+        (block_ids[:, :, None] == column_block[None, None, :]) & live_slot[:, :, None], axis=1
+    )
     features = [own] + [in_order(n, f, upper[0]) for n, f in zip(near, far)]
     all_features = jnp.concatenate(features, axis=0)
-    returned, all_features = lax.optimization_barrier((returned, all_features))
+    returned, all_features, logits, block_hit = lax.optimization_barrier(
+        (returned, all_features, logits, block_hit)
+    )
     for first, second in returned:
         logits = logits + in_order(first, second, upper[0])
 
@@ -279,27 +268,26 @@
 
     width = 256 if rows % 256 == 0 else rows
     chunks = rows // width
-    shares = [(chunks + 1) // 2, chunks // 4]
-    done = 0
-    grad_head = None
-    held = jnp.stack([keep + other.astype(jnp.float32) for keep, other in state])
-    for i in range(1, len(upper)):
-        if held.shape[1] == 1:
-            break
-        pairs = held.reshape(tok_size, held.shape[1] // 2, 2, *held.shape[2:])
-        low, high = pairs[:, :, 0], pairs[:, :, 1]
-        send = jnp.where(upper[i], low, high).astype(jnp.bfloat16)
-        send, all_delta = lax.optimization_barrier((send, all_delta))
-        other = swap_vocab(send, 1 << i, vocab_size)
-        share = shares.pop(0) if shares else 0
-        if share:
-            grad_head = head_gradient(
-                all_features, all_delta, grad_head, done * width, share, width
-            )
-            done += share
-            other, grad_head = lax.optimization_barrier((other, grad_head))
-        held = jnp.where(upper[i], high, low) + other.astype(jnp.float32)
-    sums = held[:, 0]
+    held = jnp.stack([keep + other.astype(jnp.float32) for keep, other in state], axis=1)
+    pieces = held.shape[0]
+    places = [i for i in range(1, len(upper)) if 1 << i < run]
+    taken = []
+    for offset in range(pieces):
+        options = [held[j ^ offset] for j in range(pieces)]
+        for i in places:
+            options = [
+                jnp.where(upper[i], high, low) for low, high in zip(options[::2], options[1::2])
+            ]
+        taken.append(options[0])
+    sends = [x.astype(jnp.bfloat16) for x in taken[1:]]
+    sends, all_delta = lax.optimization_barrier((sends, all_delta))
+    others = [swap_vocab(x, 2 * (i + 1), vocab_size) for i, x in enumerate(sends)]
+    done = (chunks + 1) // 2
+    grad_head = head_gradient(all_features, all_delta, None, 0, done, width)
+    others, grad_head = lax.optimization_barrier((others, grad_head))
+    sums = taken[0]
+    for other in others:
+        sums = sums + other.astype(jnp.float32)
     total = jnp.where(apart_is[0], sums[0], 0.0)
     sums = sums.astype(jnp.bfloat16)
     sends = []

time: 82 us -> 78.9 us (0.962)
  the two profiles are of different devices: /device:TPU:0 before, /device:TPU:12 now
where the time goes in v7:
time: 78.9 us; the launch traced here: 78.6 us
  waiting for transfers between devices  37.5 us (48%)
  starting transfers between devices  16.6 us (21%)
  Pallas kernels  12.9 us (16%)
  other arithmetic  4.97 us (6%)
  matrix products  3.01 us (4%)
  local copies, waits for them, and re-layouts  2.03 us (3%)
  between operations  1.59 us (2%)
    ppermute x4, waiting for transfers between devices, shift_tok(): lax.ppermute(x, 'tok', [(i, (i + offset) % size) for i in range(size)])  20.5 us
    ppermute x10, waiting for transfers between devices, swap_vocab(): return lax.ppermute(x, 'vocab', [(i, i ^ bit) for i in range(size)])  13.1 us
    ppermute x10, starting transfers between devices, swap_vocab(): return lax.ppermute(x, 'vocab', [(i, i ^ bit) for i in range(size)])  8.49 us
    pallas_call x2, Pallas kernels, gradient(): pl.pallas_call(first_gradient_kernel if first else later_gradient_kernel,...  6.38 us
    ppermute x2, starting transfers between devices, per_device(): lax.ppermute(sends[k], ('vocab', 'tok'), pairs).astype(jnp.float32)  4.82 us
    ppermute x2, waiting for transfers between devices, per_device(): lax.ppermute(sends[k], ('vocab', 'tok'), pairs).astype(jnp.float32)  3.91 us
    pallas_call x2, Pallas kernels, head_gradient(): pl.pallas_call(functools.partial(head_gradient_kernel, steps, start, widt...  3.9 us
    ppermute x4, starting transfers between devices, shift_tok(): lax.ppermute(x, 'tok', [(i, (i + offset) % size) for i in range(size)])  3.3 us
  transfers between devices with their start and end apart: 16, of which 12 were waited for; matrix products, arithmetic and copies ran while one was open for 6% of the time, Pallas kernels for 16%

profile of v7, /device:TPU:12, one launch (start us, length us, event | category | flops | bytes accessed | tf_op | source)
XLA Modules:
  0.0 78.6 jit_solution(4729035736583740893)
XLA Ops:
  0.6 1.0 %dynamic_slice.7 = bf16[64,1792]{1,0:T(8,128)(2,1)S(1)} dynamic-slice(bf16[128,3584]{1,0:T(8,128)(2,1)} %param.5, s32[]{:T(128)S(6)} %select_n.184, s32[]{:T(128)S(6)} %select_n.185), dynamic_slice_sizes={64,1792} | dynamic-slice | bytes 458756 | tf_op jit(solution)/shard_map/dynamic_slice | solution.py:192
  1.6 0.6 collective-permute-start
  2.2 1.0 %constant_dynamic-slice_fusion = bf16[128,1792]{1,0:T(8,128)(2,1)S(1)} fusion(bf16[128,3584]{1,0:T(8,128)(2,1)} %param.5, s32[]{:T(128)S(6)} %select_n.178), kind=kLoop, calls=%fused_computation.93 | loop fusion | bytes 917508 | tf_op jit(solution)/shard_map/dynamic_slice | solution.py:192
  3.9 0.0 copy-start.1
  4.0 2.6 %load_head.1 = bf16[1792,1536]{1,0:T(8,128)(2,1)S(1)} custom-call(bf16[1792,1536]{1,0:T(8,128)(2,1)} %head_ref.1), custom_call_target="tpu_custom_call" | custom-call | bytes 11010048 | tf_op jit(solution)/shard_map/load_head/pallas_call | solution.py:54
  6.6 0.0 copy-done.1
  6.6 0.1 and_reduce_fusion
  6.7 2.3 %collective-permute-done = bf16[64,1792]{1,0:T(8,128)(2,1)S(1)} collective-permute-done((bf16[64,1792]{1,0:T(8,128)(2,1)S(1)}, bf16[64,1792]{1,0:T(8,128)(2,1)S(1)}, u32[]{:S(2)}, u32[]{:S(2)}) %collective-permute-start) | collective-permute-done | bytes 229408 | tf_op jit(solution)/shard_map/ppermute | solution.py:18
  9.0 0.0 collective-permute-start.2
  9.0 1.1 %fusion.38 = f32[64,1536]{1,0:T(8,128)S(1)} fusion(bf16[64,1792]{1,0:T(8,128)(2,1)S(1)} %collective-permute-done, bf16[1792,1536]{1,0:T(8,128)(2,1)S(1)} %load_head.1), kind=kOutput, calls=%fused_computation.96 | convolution fusion | flops 352321536 | bytes 6127616 | tf_op jit(solution)/shard_map/dot_general | solution.py:218
  10.1 0.6 collective-permute-start.1
  10.7 0.9 %fusion.40 = f32[128,1536]{1,0:T(8,128)S(1)} fusion(bf16[128,1792]{1,0:T(8,128)(2,1)S(1)} %constant_dynamic-slice_fusion, bf16[1792,1536]{1,0:T(8,128)(2,1)S(1)} %load_head.1), kind=kOutput, calls=%fused_computation.98 | convolution fusion | flops 704643072 | bytes 6750208 | tf_op jit(solution)/shard_map/dot_general | solution.py:224
  11.6 0.0 collective-permute-done.2
  11.6 1.1 %fusion.39 = f32[64,1536]{1,0:T(8,128)S(1)} fusion(bf16[64,1792]{1,0:T(8,128)(2,1)S(1)} %collective-permute-done.2, bf16[1792,1536]{1,0:T(8,128)(2,1)S(1)} %load_head.1), kind=kOutput, calls=%fused_computation.97 | convolution fusion | flops 352321536 | bytes 6127616 | tf_op jit(solution)/shard_map/dot_general | solution.py:221
  12.6 1.6 %collective-permute-start.3 = (f32[64,1536]{1,0:T(8,128)S(1)}, f32[64,1536]{1,0:T(8,128)S(1)}, u32[]{:S(2)}, u32[]{:S(2)}) collective-permute-start(f32[64,1536]{1,0:T(8,128)S(1)} %fusion.39), channel_id=1, source_target_pairs={{0,1},{1,0},{2,3},{3,2},{4,5},{5,4},{6,7},{7,6},{8,9},{9,8},{10,11... | collective-permute-start | bytes 1179656 | tf_op jit(solution)/shard_map/ppermute | solution.py:18
  14.3 0.1 pad_maximum_fusion.refs_0_
  14.3 7.7 %collective-permute-done.1 = f32[64,1536]{1,0:T(8,128)S(1)} collective-permute-done((f32[64,1536]{1,0:T(8,128)S(1)}, f32[64,1536]{1,0:T(8,128)S(1)}, u32[]{:S(2)}, u32[]{:S(2)}) %collective-permute-start.1) | collective-permute-done | bytes 393248 | tf_op jit(solution)/shard_map/ppermute | solution.py:18
  22.1 8.0 %collective-permute-done.3 = f32[64,1536]{1,0:T(8,128)S(1)} collective-permute-done((f32[64,1536]{1,0:T(8,128)S(1)}, f32[64,1536]{1,0:T(8,128)S(1)}, u32[]{:S(2)}, u32[]{:S(2)}) %collective-permute-start.3) | collective-permute-done | bytes 393248 | tf_op jit(solution)/shard_map/ppermute | solution.py:18
  30.1 0.1 broadcast_select_fusion.3
  30.2 0.2 fusion.37
  30.4 1.5 %exponential_reduce_fusion = (f32[128]{0:T(128)S(1)}, f32[128]{0:T(128)S(1)}, f32[128]{0:T(128)S(1)}) fusion(f32[128,1536]{1,0:T(8,128)S(1)} %get-tuple-element.93, f32[128]{0:T(128)S(1)} %get-tuple-element.92, bf16[128,1536]{1,0:T(8,128)(2,1)} %param.7, pred[1536]{0:T(1024)(128)(4,1)S(1)} %reduce.4), kind=kLoop, calls=%fused_computation.19 | loop fusion | flops 1769088 | bytes 1183232 | tf_op jit(solution)/shard_map/reduce_sum | solution.py:243
  31.9 0.1 collective-permute-start.4
  32.0 1.1 %collective-permute-done.4 = f32[1,4,128]{2,1,0:T(4,128)S(1)} collective-permute-done((f32[1,4,128]{2,1,0:T(4,128)S(1)}, f32[1,4,128]{2,1,0:T(4,128)S(1)}, u32[]{:S(2)}, u32[]{:S(2)}) %collective-permute-start.4) | collective-permute-done | bytes 2080 | tf_op jit(solution)/shard_map/ppermute | solution.py:22
  33.1 1.6 %collective-permute-start.5 = (f32[2,4,128]{2,1,0:T(4,128)S(1)}, f32[2,4,128]{2,1,0:T(4,128)S(1)}, u32[]{:S(2)}, u32[]{:S(2)}) collective-permute-start(f32[2,4,128]{2,1,0:T(4,128)S(1)} %pad_maximum_fusion.6), channel_id=1, source_target_pairs={{0,4},{2,6},{4,0},{6,2},{8,12},{10,14},{12,8},{14,10},{16,20},{18,... | collective-permute-start | bytes 12296 | tf_op jit(solution)/shard_map/ppermute | solution.py:22
  34.7 2.1 %collective-permute-done.5 = f32[2,4,128]{2,1,0:T(4,128)S(1)} collective-permute-done((f32[2,4,128]{2,1,0:T(4,128)S(1)}, f32[2,4,128]{2,1,0:T(4,128)S(1)}, u32[]{:S(2)}, u32[]{:S(2)}) %collective-permute-start.5) | collective-permute-done | bytes 4128 | tf_op jit(solution)/shard_map/ppermute | solution.py:22
  36.8 0.5 collective-permute-start.6
  37.3 3.2 %collective-permute-done.6 = f32[4,4,128]{2,1,0:T(4,128)S(1)} collective-permute-done((f32[4,4,128]{2,1,0:T(4,128)S(1)}, f32[4,4,128]{2,1,0:T(4,128)S(1)}, u32[]{:S(2)}, u32[]{:S(2)}) %collective-permute-start.6) | collective-permute-done | bytes 8224 | tf_op jit(solution)/shard_map/ppermute | solution.py:22
  40.5 2.7 %collective-permute-start.7 = (f32[8,4,128]{2,1,0:T(4,128)S(1)}, f32[8,4,128]{2,1,0:T(4,128)S(1)}, u32[]{:S(2)}, u32[]{:S(2)}) collective-permute-start(f32[8,4,128]{2,1,0:T(4,128)S(1)} %pad_maximum_fusion.3), channel_id=1, source_target_pairs={{0,16},{2,18},{4,20},{6,22},{8,24},{10,26},{12,28},{14,30},{16,0},... | collective-permute-start | bytes 49160 | tf_op jit(solution)/shard_map/ppermute | solution.py:22
  43.2 2.0 %collective-permute-done.7 = f32[8,4,128]{2,1,0:T(4,128)S(1)} collective-permute-done((f32[8,4,128]{2,1,0:T(4,128)S(1)}, f32[8,4,128]{2,1,0:T(4,128)S(1)}, u32[]{:S(2)}, u32[]{:S(2)}) %collective-permute-start.7) | collective-permute-done | bytes 16416 | tf_op jit(solution)/shard_map/ppermute | solution.py:22
  45.4 0.5 subtract_add_fusion
  45.9 0.0 copy-start
  45.9 1.3 %fusion.7.delta_ref = bf16[128,1536]{1,0:T(8,128)(2,1)S(1)} fusion(bf16[128,1536]{1,0:T(8,128)(2,1)} %param.7, f32[128,1536]{1,0:T(8,128)S(1)} %get-tuple-element.93, f32[128]{0:T(128)S(1)} %get-tuple-element.104, f32[128]{0:T(128)S(1)} %get-tuple-element.91, pred[1536]{0:T(1024)(128)(4,1)S(1)} %reduce.4), kind=kLoop, calls=%fused_computation.20 | loop fusion | flops 1376256 | bytes 1575424 | tf_op jit(solution)/shard_map/convert_element_type | solution.py:257
  47.2 0.6 collective-permute-start.9
  47.7 4.8 %partial_gradient.2 = (bf16[4,224,128]{2,1,0:T(8,128)(2,1)S(1)}, f32[4,224,128]{2,1,0:T(8,128)S(1)}, bf16[1792,1536]{1,0:T(8,128)(2,1)S(1)}) custom-call(s32[1]{0:T(128)} %bitcast.1.core_ref, bf16[1792,1536]{1,0:T(8,128)(2,1)} %head_ref.1, bf16[128,1536]{1,0:T(8,128)(2,1)S(1)} %fusion.7.delta_ref), custom_call_target="tpu_custom_call" | custom-call | flops 704643072 | bytes 5898240 | tf_op jit(solution)/shard_map/partial_gradient/pallas_call | solution.py:112
  52.5 0.1 collective-permute-start.8
  52.6 2.4 %collective-permute-done.9.delta_ref = bf16[128,1536]{1,0:T(8,128)(2,1)S(1)} collective-permute-done((bf16[128,1536]{1,0:T(8,128)(2,1)S(1)}, bf16[128,1536]{1,0:T(8,128)(2,1)S(1)}, u32[]{:S(2)}, u32[]{:S(2)}) %collective-permute-start.9) | collective-permute-done | bytes 393248 | tf_op jit(solution)/shard_map/ppermute | solution.py:18
  55.0 1.6 %partial_gradient.3 = (bf16[4,224,128]{2,1,0:T(8,128)(2,1)S(1)}, f32[4,224,128]{2,1,0:T(8,128)S(1)}) custom-call(s32[1]{0:T(128)} %bitcast.1.core_ref, bf16[1792,1536]{1,0:T(8,128)(2,1)S(1)} %get-tuple-element.59.head_ref, bf16[128,1536]{1,0:T(8,128)(2,1)S(1)} %collective-permute-done.9.delta_ref), custom_call_target="tpu_custom_call" | custom-call | flops 704643072 | bytes 5898240 | tf_op jit(solution)/shard_map/partial_gradient/pallas_call | solution.py:112
  56.6 0.0 copy-done
  56.6 0.0 collective-permute-done.8
  56.6 0.1 collective-permute-start.10
  56.7 0.1 pad_maximum_fusion.1.refs_1_
  56.8 1.4 %collective-permute-done.10 = bf16[4,224,128]{2,1,0:T(8,128)(2,1)S(1)} collective-permute-done((bf16[4,224,128]{2,1,0:T(8,128)(2,1)S(1)}, bf16[4,224,128]{2,1,0:T(8,128)(2,1)S(1)}, u32[]{:S(2)}, u32[]{:S(2)}) %collective-permute-start.10) | collective-permute-done | bytes 229408 | tf_op jit(solution)/shard_map/ppermute | solution.py:22
  58.2 0.1 fusion.19
  58.3 0.1 fusion.17
  58.4 1.6 %collective-permute-start.11 = (bf16[2,224,128]{2,1,0:T(8,128)(2,1)S(1)}, bf16[2,224,128]{2,1,0:T(8,128)(2,1)S(1)}, u32[]{:S(2)}, u32[]{:S(2)}) collective-permute-start(bf16[2,224,128]{2,1,0:T(8,128)(2,1)S(1)} %get-tuple-element.65), channel_id=1, source_target_pairs={{0,4},{2,6},{4,0},{6,2},{8,12},{10,14},{12,8},{14,10},{16,20},{18,... | collective-permute-start | bytes 344072 | tf_op jit(solution)/shard_map/ppermute | solution.py:22
  59.9 0.4 collective-permute-start.12
  60.4 1.5 %collective-permute-start.13 = (bf16[2,224,128]{2,1,0:T(8,128)(2,1)S(1)}, bf16[2,224,128]{2,1,0:T(8,128)(2,1)S(1)}, u32[]{:S(2)}, u32[]{:S(2)}) collective-permute-start(bf16[2,224,128]{2,1,0:T(8,128)(2,1)S(1)} %get-tuple-element.67), channel_id=1, source_target_pairs={{0,12},{2,14},{4,8},{6,10},{8,4},{10,6},{12,0},{14,2},{16,28},{18,... | collective-permute-start | bytes 344072 | tf_op jit(solution)/shard_map/ppermute | solution.py:22
  61.9 2.1 %head_gradient.2.refs_2_ = bf16[1792,1536]{1,0:T(8,128)(2,1)} custom-call(bf16[256,1792]{1,0:T(8,128)(2,1)S(1)} %pad_maximum_fusion.refs_0_, bf16[256,1536]{1,0:T(8,128)(2,1)S(1)} %pad_maximum_fusion.1.refs_1_), custom_call_target="tpu_custom_call" | custom-call | flops 805306368 | bytes 4849664 | tf_op jit(solution)/shard_map/head_gradient/pallas_call | solution.py:160
  64.0 0.0 collective-permute-done.11
  64.0 1.9 %collective-permute-done.12 = bf16[2,224,128]{2,1,0:T(8,128)(2,1)S(1)} collective-permute-done((bf16[2,224,128]{2,1,0:T(8,128)(2,1)S(1)}, bf16[2,224,128]{2,1,0:T(8,128)(2,1)S(1)}, u32[]{:S(2)}, u32[]{:S(2)}) %collective-permute-start.12) | collective-permute-done | bytes 114720 | tf_op jit(solution)/shard_map/ppermute | solution.py:22
  66.0 1.3 %collective-permute-done.13 = bf16[2,224,128]{2,1,0:T(8,128)(2,1)S(1)} collective-permute-done((bf16[2,224,128]{2,1,0:T(8,128)(2,1)S(1)}, bf16[2,224,128]{2,1,0:T(8,128)(2,1)S(1)}, u32[]{:S(2)}, u32[]{:S(2)}) %collective-permute-start.13) | collective-permute-done | bytes 114720 | tf_op jit(solution)/shard_map/ppermute | solution.py:22
  67.3 0.1 fusion.32
  67.4 2.7 %collective-permute-start.15 = (bf16[224,128]{1,0:T(8,128)(2,1)S(1)}, bf16[224,128]{1,0:T(8,128)(2,1)S(1)}, u32[]{:S(2)}, u32[]{:S(2)}) collective-permute-start(bf16[224,128]{1,0:T(8,128)(2,1)S(1)} %get-tuple-element.75), channel_id=1, source_target_pairs={{0,1},{1,17},{2,3},{3,19},{4,5},{5,21},{6,7},{7,23},{8,9},{9,25},{... | collective-permute-start | bytes 172040 | tf_op jit(solution)/shard_map/ppermute | solution.py:308
  70.1 2.1 %collective-permute-start.14 = (bf16[224,128]{1,0:T(8,128)(2,1)S(1)}, bf16[224,128]{1,0:T(8,128)(2,1)S(1)}, u32[]{:S(2)}, u32[]{:S(2)}) collective-permute-start(bf16[224,128]{1,0:T(8,128)(2,1)S(1)} %get-tuple-element.74), channel_id=1, source_target_pairs={{1,16},{3,18},{5,20},{7,22},{9,24},{11,26},{13,28},{15,30},{16,1},... | collective-permute-start | bytes 172040 | tf_op jit(solution)/shard_map/ppermute | solution.py:308
  72.2 1.8 %head_gradient.3 = bf16[1792,1536]{1,0:T(8,128)(2,1)} custom-call(bf16[256,1792]{1,0:T(8,128)(2,1)S(1)} %pad_maximum_fusion.refs_0_, bf16[256,1536]{1,0:T(8,128)(2,1)S(1)} %pad_maximum_fusion.1.refs_1_, bf16[1792,1536]{1,0:T(8,128)(2,1)} %head_gradient.2.refs_2_), custom_call_target="tpu_custom_call", output_to_operand_aliasing={{}: (2, {})} | custom-call | flops 603979776 | bytes 4063232 | tf_op jit(solution)/shard_map/head_gradient/pallas_call | solution.py:160
  74.0 0.0 collective-permute-done.15
  74.0 3.9 %collective-permute-done.14 = bf16[224,128]{1,0:T(8,128)(2,1)S(1)} collective-permute-done((bf16[224,128]{1,0:T(8,128)(2,1)S(1)}, bf16[224,128]{1,0:T(8,128)(2,1)S(1)}, u32[]{:S(2)}, u32[]{:S(2)}) %collective-permute-start.14) | collective-permute-done | bytes 57376 | tf_op jit(solution)/shard_map/ppermute | solution.py:308
  77.9 0.7 fusion.23
  (19 shorter events, 0.3 us)
Async XLA Ops:
  1.6 7.4 %collective-permute-start = (bf16[64,1792]{1,0:T(8,128)(2,1)S(1)}, bf16[64,1792]{1,0:T(8,128)(2,1)S(1)}, u32[]{:S(2)}, u32[]{:S(2)}) collective-permute-start(bf16[64,1792]{1,0:T(8,128)(2,1)S(1)} %dynamic_slice.7), channel_id=1, source_target_pairs={{0,1},{1,0},{2,3},{3,2},{4,5},{5,4},{6,7},{7,6},{8,9},{9,8},{10,11... | collective-permute-start | bytes 688136 | tf_op jit(solution)/shard_map/ppermute | solution.py:18
  3.9 2.6 %copy-start.1 = (s32[1,16]{1,0:T(1,128)S(1)}, s32[1,16]{1,0:T(1,128)}, u32[]{:S(2)}) copy-start(s32[1,16]{1,0:T(1,128)} %param.8) | copy-start | bytes 196
  9.0 2.5 %collective-permute-start.2 = (bf16[64,1792]{1,0:T(8,128)(2,1)S(1)}, bf16[64,1792]{1,0:T(8,128)(2,1)S(1)}, u32[]{:S(2)}, u32[]{:S(2)}) collective-permute-start(bf16[64,1792]{1,0:T(8,128)(2,1)S(1)} %collective-permute-done), channel_id=1, source_target_pairs={{0,2},{2,0},{4,6},{6,4},{8,10},{10,8},{12,14},{14,12},{16,18},{18,... | collective-permute-start | bytes 688136 | tf_op jit(solution)/shard_map/ppermute | solution.py:22
  10.1 12.0 %collective-permute-start.1 = (f32[64,1536]{1,0:T(8,128)S(1)}, f32[64,1536]{1,0:T(8,128)S(1)}, u32[]{:S(2)}, u32[]{:S(2)}) collective-permute-start(f32[64,1536]{1,0:T(8,128)S(1)} %fusion.38), channel_id=1, source_target_pairs={{0,1},{1,0},{2,3},{3,2},{4,5},{5,4},{6,7},{7,6},{8,9},{9,8},{10,11... | collective-permute-start | bytes 1179656 | tf_op jit(solution)/shard_map/ppermute | solution.py:18
  12.6 17.5 %collective-permute-start.3 = (f32[64,1536]{1,0:T(8,128)S(1)}, f32[64,1536]{1,0:T(8,128)S(1)}, u32[]{:S(2)}, u32[]{:S(2)}) collective-permute-start(f32[64,1536]{1,0:T(8,128)S(1)} %fusion.39), channel_id=1, source_target_pairs={{0,1},{1,0},{2,3},{3,2},{4,5},{5,4},{6,7},{7,6},{8,9},{9,8},{10,11... | collective-permute-start | bytes 1179656 | tf_op jit(solution)/shard_map/ppermute | solution.py:18
  31.9 1.2 %collective-permute-start.4 = (f32[1,4,128]{2,1,0:T(4,128)S(1)}, f32[1,4,128]{2,1,0:T(4,128)S(1)}, u32[]{:S(2)}, u32[]{:S(2)}) collective-permute-start(f32[1,4,128]{2,1,0:T(4,128)S(1)} %maximum_bitcast_fusion), channel_id=1, source_target_pairs={{0,2},{2,0},{4,6},{6,4},{8,10},{10,8},{12,14},{14,12},{16,18},{18,... | collective-permute-start | bytes 6152 | tf_op jit(solution)/shard_map/ppermute | solution.py:22
  33.1 3.7 %collective-permute-start.5 = (f32[2,4,128]{2,1,0:T(4,128)S(1)}, f32[2,4,128]{2,1,0:T(4,128)S(1)}, u32[]{:S(2)}, u32[]{:S(2)}) collective-permute-start(f32[2,4,128]{2,1,0:T(4,128)S(1)} %pad_maximum_fusion.6), channel_id=1, source_target_pairs={{0,4},{2,6},{4,0},{6,2},{8,12},{10,14},{12,8},{14,10},{16,20},{18,... | collective-permute-start | bytes 12296 | tf_op jit(solution)/shard_map/ppermute | solution.py:22
  36.8 3.7 %collective-permute-start.6 = (f32[4,4,128]{2,1,0:T(4,128)S(1)}, f32[4,4,128]{2,1,0:T(4,128)S(1)}, u32[]{:S(2)}, u32[]{:S(2)}) collective-permute-start(f32[4,4,128]{2,1,0:T(4,128)S(1)} %pad_maximum_fusion.5), channel_id=1, source_target_pairs={{0,8},{2,10},{4,12},{6,14},{8,0},{10,2},{12,4},{14,6},{16,24},{18,... | collective-permute-start | bytes 24584 | tf_op jit(solution)/shard_map/ppermute | solution.py:22
  40.5 4.7 %collective-permute-start.7 = (f32[8,4,128]{2,1,0:T(4,128)S(1)}, f32[8,4,128]{2,1,0:T(4,128)S(1)}, u32[]{:S(2)}, u32[]{:S(2)}) collective-permute-start(f32[8,4,128]{2,1,0:T(4,128)S(1)} %pad_maximum_fusion.3), channel_id=1, source_target_pairs={{0,16},{2,18},{4,20},{6,22},{8,24},{10,26},{12,28},{14,30},{16,0},... | collective-permute-start | bytes 49160 | tf_op jit(solution)/shard_map/ppermute | solution.py:22
  45.9 10.7 %copy-start = (f32[128]{0:T(128)}, f32[128]{0:T(128)S(1)}, u32[]{:S(2)}) copy-start(f32[128]{0:T(128)S(1)} %get-tuple-element.91) | copy-start | bytes 1540
  47.2 7.8 %collective-permute-start.9 = (bf16[128,1536]{1,0:T(8,128)(2,1)S(1)}, bf16[128,1536]{1,0:T(8,128)(2,1)S(1)}, u32[]{:S(2)}, u32[]{:S(2)}) collective-permute-start(bf16[128,1536]{1,0:T(8,128)(2,1)S(1)} %fusion.7.delta_ref), channel_id=1, source_target_pairs={{0,1},{1,0},{2,3},{3,2},{4,5},{5,4},{6,7},{7,6},{8,9},{9,8},{10,11... | collective-permute-start | bytes 1179656 | tf_op jit(solution)/shard_map/ppermute | solution.py:18
  52.5 4.0 %collective-permute-start.8 = (bf16[4,224,128]{2,1,0:T(8,128)(2,1)S(1)}, bf16[4,224,128]{2,1,0:T(8,128)(2,1)S(1)}, u32[]{:S(2)}, u32[]{:S(2)}) collective-permute-start(bf16[4,224,128]{2,1,0:T(8,128)(2,1)S(1)} %get-tuple-element.58), channel_id=1, source_target_pairs={{0,2},{2,0},{4,6},{6,4},{8,10},{10,8},{12,14},{14,12},{16,18},{18,... | collective-permute-start | bytes 688136 | tf_op jit(solution)/shard_map/ppermute | solution.py:22
  56.6 1.6 %collective-permute-start.10 = (bf16[4,224,128]{2,1,0:T(8,128)(2,1)S(1)}, bf16[4,224,128]{2,1,0:T(8,128)(2,1)S(1)}, u32[]{:S(2)}, u32[]{:S(2)}) collective-permute-start(bf16[4,224,128]{2,1,0:T(8,128)(2,1)S(1)} %get-tuple-element.64), channel_id=1, source_target_pairs={{0,2},{2,0},{4,6},{6,4},{8,10},{10,8},{12,14},{14,12},{16,18},{18,... | collective-permute-start | bytes 688136 | tf_op jit(solution)/shard_map/ppermute | solution.py:22
  58.4 5.6 %collective-permute-start.11 = (bf16[2,224,128]{2,1,0:T(8,128)(2,1)S(1)}, bf16[2,224,128]{2,1,0:T(8,128)(2,1)S(1)}, u32[]{:S(2)}, u32[]{:S(2)}) collective-permute-start(bf16[2,224,128]{2,1,0:T(8,128)(2,1)S(1)} %get-tuple-element.65), channel_id=1, source_target_pairs={{0,4},{2,6},{4,0},{6,2},{8,12},{10,14},{12,8},{14,10},{16,20},{18,... | collective-permute-start | bytes 344072 | tf_op jit(solution)/shard_map/ppermute | solution.py:22
  59.9 6.0 %collective-permute-start.12 = (bf16[2,224,128]{2,1,0:T(8,128)(2,1)S(1)}, bf16[2,224,128]{2,1,0:T(8,128)(2,1)S(1)}, u32[]{:S(2)}, u32[]{:S(2)}) collective-permute-start(bf16[2,224,128]{2,1,0:T(8,128)(2,1)S(1)} %get-tuple-element.66), channel_id=1, source_target_pairs={{0,8},{2,10},{4,12},{6,14},{8,0},{10,2},{12,4},{14,6},{16,24},{18,... | collective-permute-start | bytes 344072 | tf_op jit(solution)/shard_map/ppermute | solution.py:22
  60.4 6.9 %collective-permute-start.13 = (bf16[2,224,128]{2,1,0:T(8,128)(2,1)S(1)}, bf16[2,224,128]{2,1,0:T(8,128)(2,1)S(1)}, u32[]{:S(2)}, u32[]{:S(2)}) collective-permute-start(bf16[2,224,128]{2,1,0:T(8,128)(2,1)S(1)} %get-tuple-element.67), channel_id=1, source_target_pairs={{0,12},{2,14},{4,8},{6,10},{8,4},{10,6},{12,0},{14,2},{16,28},{18,... | collective-permute-start | bytes 344072 | tf_op jit(solution)/shard_map/ppermute | solution.py:22
  67.4 6.7 %collective-permute-start.15 = (bf16[224,128]{1,0:T(8,128)(2,1)S(1)}, bf16[224,128]{1,0:T(8,128)(2,1)S(1)}, u32[]{:S(2)}, u32[]{:S(2)}) collective-permute-start(bf16[224,128]{1,0:T(8,128)(2,1)S(1)} %get-tuple-element.75), channel_id=1, source_target_pairs={{0,1},{1,17},{2,3},{3,19},{4,5},{5,21},{6,7},{7,23},{8,9},{9,25},{... | collective-permute-start | bytes 172040 | tf_op jit(solution)/shard_map/ppermute | solution.py:308
  70.1 7.9 %collective-permute-start.14 = (bf16[224,128]{1,0:T(8,128)(2,1)S(1)}, bf16[224,128]{1,0:T(8,128)(2,1)S(1)}, u32[]{:S(2)}, u32[]{:S(2)}) collective-permute-start(bf16[224,128]{1,0:T(8,128)(2,1)S(1)} %get-tuple-element.74), channel_id=1, source_target_pairs={{1,16},{3,18},{5,20},{7,22},{9,24},{11,26},{13,28},{15,30},{16,1},... | collective-permute-start | bytes 172040 | tf_op jit(solution)/shard_map/ppermute | solution.py:308

commit v8 on v7

--- a/solution.py
+++ b/solution.py
@@ -12,6 +12,7 @@
 
 loss_scale = 1024.0
 VMEM_LIMIT = 16 << 20
+STEP = 16
 
 
 def shift_tok(x, offset, size):
@@ -63,6 +64,96 @@
         ),
         name="load_head",
     )(pltpu.with_memory_space_constraint(head, pltpu.HBM))
+
+
+def stats_kernel(core_ref, own_ref, kept_ref, early_ref, *refs):
+    parts, (logits_ref, stats_ref, turned_ref) = refs[:-3], refs[-3:]
+    half = own_ref.shape[0] // 2
+    lane = lax.broadcasted_iota(jnp.int32, (STEP, 128), 1)
+    for place in range(2):
+        start = (core_ref[0] if place == 0 else 1 - core_ref[0]) * half
+        for r in range(0, half, STEP):
+            rows = pl.ds(pl.multiple_of(start + r, STEP), STEP)
+            logits = own_ref[rows, :]
+            for part in parts[place::2]:
+                logits = logits + part[r : r + STEP, :]
+            logits_ref[rows, :] = logits
+            top = jnp.max(logits, axis=1, keepdims=True)
+            total = jnp.sum(jnp.exp(logits - top), axis=1, keepdims=True)
+            dot = jnp.sum(kept_ref[rows, :].astype(jnp.float32) * logits, axis=1, keepdims=True)
+            turned_ref[rows, :] = jnp.where(lane == 0, top, jnp.where(lane == 1, total, dot))
+    turned = turned_ref[...].T
+    stats_ref[0:2, :] = turned[0:2]
+    stats_ref[2:3, :] = early_ref[0:1, :]
+    stats_ref[3:4, :] = early_ref[1:2, :] - turned[2:3]
+
+
+def local_stats(core, own_logits, kept, early, returned):
+    in_vmem = pl.BlockSpec(memory_space=pltpu.VMEM)
+    parts = [x for pair in returned for x in pair]
+    arrays = [
+        pltpu.with_memory_space_constraint(x, pltpu.VMEM) for x in (own_logits, kept, early, *parts)
+    ]
+    return pl.pallas_call(
+        stats_kernel,
+        out_shape=(
+            pltpu.VMEM(own_logits.shape, jnp.float32),
+            pltpu.VMEM((4, own_logits.shape[0]), jnp.float32),
+        ),
+        in_specs=[pl.BlockSpec(memory_space=pltpu.SMEM)] + [in_vmem] * len(arrays),
+        out_specs=(in_vmem, in_vmem),
+        scratch_shapes=[pltpu.VMEM((own_logits.shape[0], 128), jnp.float32)],
+        compiler_params=pltpu.CompilerParams(vmem_limit_bytes=VMEM_LIMIT),
+        cost_estimate=pl.CostEstimate(
+            flops=8 * own_logits.size,
+            bytes_accessed=12 * own_logits.size,
+            transcendentals=own_logits.size,
+        ),
+        name="local_stats",
+    )(core, *arrays)
+
+
+def delta_kernel(gathered_ref, logits_ref, kept_ref, delta_ref, lse_ref, kl_ref):
+    shards = [gathered_ref[i] for i in range(gathered_ref.shape[0])]
+    top = shards[0][0:1]
+    for x in shards[1:]:
+        top = jnp.maximum(top, x[0:1])
+    total, mass, part = 0.0, 0.0, 0.0
+    for x in shards:
+        total = total + x[1:2] * jnp.exp(x[0:1] - top)
+        mass, part = mass + x[2:3], part + x[3:4]
+    lse = top + jnp.log(total)
+    lse_ref[...] = lse
+    kl_ref[...] = part / mass - jnp.log(mass) + lse
+    row = lax.broadcasted_iota(jnp.int32, (128, lse.shape[1]), 0)
+    turned = jnp.where(row == 0, lse, 1.0 / mass).T
+    lse_column, scale_column = turned[:, 0:1], turned[:, 1:2]
+    for r in range(0, logits_ref.shape[0], STEP):
+        rows = slice(r, r + STEP)
+        student = jnp.exp(logits_ref[rows, :] - lse_column[rows])
+        kept = kept_ref[rows, :].astype(jnp.float32) * scale_column[rows]
+        delta_ref[rows, :] = (loss_scale * (student - kept)).astype(jnp.bfloat16)
+
+
+def finish(gathered, logits, kept):
+    tokens = logits.shape[0]
+    in_vmem = pl.BlockSpec(memory_space=pltpu.VMEM)
+    delta, lse, kl = pl.pallas_call(
+        delta_kernel,
+        out_shape=(
+            pltpu.VMEM(logits.shape, jnp.bfloat16),
+            jax.ShapeDtypeStruct((1, tokens), jnp.float32),
+            jax.ShapeDtypeStruct((1, tokens), jnp.float32),
+        ),
+        in_specs=[in_vmem] * 3,
+        out_specs=(in_vmem, in_vmem, in_vmem),
+        compiler_params=pltpu.CompilerParams(vmem_limit_bytes=VMEM_LIMIT),
+        cost_estimate=pl.CostEstimate(
+            flops=8 * logits.size, bytes_accessed=8 * logits.size, transcendentals=logits.size
+        ),
+        name="delta",
+    )(*[pltpu.with_memory_space_constraint(x, pltpu.VMEM) for x in (gathered, logits, kept)])
+    return delta, lse.reshape(tokens), kl.reshape(tokens)
 
 
 def write_pieces(k, head_rows, delta_ref, upper, send_ref, keep_ref):
@@ -227,34 +318,20 @@
     )
     features = [own] + [in_order(n, f, upper[0]) for n, f in zip(near, far)]
     all_features = jnp.concatenate(features, axis=0)
-    returned, all_features, logits, block_hit = lax.optimization_barrier(
-        (returned, all_features, logits, block_hit)
-    )
-    for first, second in returned:
-        logits = logits + in_order(first, second, upper[0])
-
     blocks = block_hit.shape[0]
     listed = jnp.broadcast_to(
         block_hit[:, None, :], (blocks, token_count // blocks, column_count)
     ).reshape(token_count, column_count)
     teacher_f = teacher.astype(jnp.float32)
     kept = jnp.where(listed, teacher_f, 0.0)
-    local_top = jnp.max(logits, axis=1)
-    local_sum = jnp.sum(jnp.exp(logits - local_top[:, None]), axis=1)
-    local_mass = jnp.sum(kept, axis=1)
-    local_part = jnp.sum(jnp.where(listed, teacher_f * (jnp.log(teacher_f) - logits), 0.0), axis=1)
-
-    stats = gather_vocab(
-        jnp.stack([local_top, local_sum, local_mass, local_part]), upper, vocab_size
-    )
-    tops = stats[:, 0]
-    global_top = jnp.max(tops, axis=0)
-    total_sum = jnp.sum(stats[:, 1] * jnp.exp(tops - global_top[None, :]), axis=0)
-    total_mass, total_part = jnp.sum(stats[:, 2], axis=0), jnp.sum(stats[:, 3], axis=0)
-    lse = global_top + jnp.log(total_sum)
-    kl = total_part / total_mass - jnp.log(total_mass) + lse
-    student = jnp.exp(logits - lse[:, None])
-    delta = (loss_scale * (student - kept / total_mass[:, None])).astype(jnp.bfloat16)
+    mass = jnp.sum(kept, axis=1)
+    entropy = jnp.sum(jnp.where(listed, teacher_f * jnp.log(teacher_f), 0.0), axis=1)
+    kept, early = kept.astype(jnp.bfloat16), jnp.stack([mass, entropy])
+    returned, all_features, logits, kept, early = lax.optimization_barrier(
+        (returned, all_features, logits, kept, early)
+    )
+    logits, stats = local_stats(core_word, logits, kept, early, returned)
+    delta, lse, kl = finish(gather_vocab(stats, upper, vocab_size), logits, kept)
 
     deltas = [delta] + [shift_tok(delta, d, tok_size) for d in range(1, tok_size)]
     send, keep, head_here = gradient(core_word, head, delta, run, True)
@@ -288,29 +365,30 @@
     sums = taken[0]
     for other in others:
         sums = sums + other.astype(jnp.float32)
-    total = jnp.where(apart_is[0], sums[0], 0.0)
-    sums = sums.astype(jnp.bfloat16)
-    sends = []
+    sums = [
+        sums[d]
+        if d == 0
+        else shift_tok(sums[d].astype(jnp.bfloat16), -d, tok_size).astype(jnp.float32)
+        for d in range(tok_size)
+    ]
+    blocks = []
     for k in range(tok_size):
-        send = sums[k]
+        block = sums[k]
         for d in range(1, tok_size):
-            send = jnp.where(apart_is[d], sums[(k + d) % tok_size], send)
-        sends.append(send)
-    sends, all_delta = lax.optimization_barrier((sends, all_delta))
-    for k in range(tok_size):
-        pairs = []
-        for v in range(vocab_size):
-            for t in range(tok_size):
-                d = (k + t - v // run) % tok_size
-                target = (t * run + v % run) * tok_size + (t - d) % tok_size
-                if target != v * tok_size + t:
-                    pairs.append((v * tok_size + t, target))
-        total = total + lax.ppermute(sends[k], ("vocab", "tok"), pairs).astype(jnp.float32)
-    grad_hidden = total.T
+            block = jnp.where(apart_is[d], sums[(k - d) % tok_size], block)
+        blocks.append(block)
+    total = blocks[0]
     if done < chunks:
+        blocks[1:], all_delta = lax.optimization_barrier((blocks[1:], all_delta))
         grad_head = head_gradient(
             all_features, all_delta, grad_head, done * width, chunks - done, width
         )
+    for k in range(1, tok_size):
+        pairs = [(v, (v + k * run) % vocab_size) for v in range(vocab_size)]
+        total = total + lax.ppermute(
+            blocks[k].astype(jnp.bfloat16), "vocab", pairs
+        ).astype(jnp.float32)
+    grad_hidden = total.T
     return (lse, kl, grad_hidden, grad_head)
 
 

time: 78.9 us -> 77.4 us (0.981)
  the two profiles are of different devices: /device:TPU:12 before, /device:TPU:0 now
where the time goes in v8:
time: 77.4 us; the launch traced here: 77.2 us
  waiting for transfers between devices  33.9 us (44%)
  starting transfers between devices  19.2 us (25%)
  Pallas kernels  14.2 us (18%)
  other arithmetic  3.3 us (4%)
  matrix products  3.01 us (4%)
  local copies, waits for them, and re-layouts  2.02 us (3%)
  between operations  1.54 us (2%)
    ppermute x5, waiting for transfers between devices, shift_tok(): lax.ppermute(x, 'tok', [(i, (i + offset) % size) for i in range(size)])  21.2 us
    ppermute x10, waiting for transfers between devices, swap_vocab(): return lax.ppermute(x, 'vocab', [(i, i ^ bit) for i in range(size)])  12 us
    ppermute x10, starting transfers between devices, swap_vocab(): return lax.ppermute(x, 'vocab', [(i, i ^ bit) for i in range(size)])  9.66 us
    ppermute x5, starting transfers between devices, shift_tok(): lax.ppermute(x, 'tok', [(i, (i + offset) % size) for i in range(size)])  6.87 us
    pallas_call x2, Pallas kernels, gradient(): pl.pallas_call(first_gradient_kernel if first else later_gradient_kernel,...  6.41 us
    pallas_call x2, Pallas kernels, head_gradient(): pl.pallas_call(functools.partial(head_gradient_kernel, steps, start, widt...  3.89 us
    ppermute x1, starting transfers between devices, per_device(): lax.ppermute(blocks[k].astype(jnp.bfloat16), 'vocab', pairs)  2.65 us
    pallas_call x1, Pallas kernels, load(): pl.pallas_call(load_kernel, out_shape=pltpu.VMEM(head.shape, head.dtype),...  2.62 us
  transfers between devices with their start and end apart: 16, of which 12 were waited for; matrix products, arithmetic and copies ran while one was open for 8% of the time, Pallas kernels for 17%

profile of v8, /device:TPU:0, one launch (start us, length us, event | category | flops | bytes accessed | tf_op | source)
XLA Modules:
  0.0 77.2 jit_solution(13080641509598518402)
XLA Ops:
  0.6 1.0 %dynamic_slice.7 = bf16[64,1792]{1,0:T(8,128)(2,1)S(1)} dynamic-slice(bf16[128,3584]{1,0:T(8,128)(2,1)} %param.5, s32[]{:T(128)S(6)} %select_n.155, s32[]{:T(128)S(6)} %select_n.156), dynamic_slice_sizes={64,1792} | dynamic-slice | bytes 458756 | tf_op jit(solution)/shard_map/dynamic_slice | solution.py:283
  1.6 3.0 %collective-permute-start = (bf16[64,1792]{1,0:T(8,128)(2,1)S(1)}, bf16[64,1792]{1,0:T(8,128)(2,1)S(1)}, u32[]{:S(2)}, u32[]{:S(2)}) collective-permute-start(bf16[64,1792]{1,0:T(8,128)(2,1)S(1)} %dynamic_slice.7), channel_id=1, source_target_pairs={{0,1},{1,0},{2,3},{3,2},{4,5},{5,4},{6,7},{7,6},{8,9},{9,8},{10,11... | collective-permute-start | bytes 688136 | tf_op jit(solution)/shard_map/ppermute | solution.py:19
  4.6 1.0 %constant_dynamic-slice_fusion = bf16[128,1792]{1,0:T(8,128)(2,1)S(1)} fusion(bf16[128,3584]{1,0:T(8,128)(2,1)} %param.5, s32[]{:T(128)S(6)} %select_n.149), kind=kLoop, calls=%fused_computation.70 | loop fusion | bytes 917508 | tf_op jit(solution)/shard_map/dynamic_slice | solution.py:283
  6.4 0.8 and_reduce_fusion
  7.2 1.3 %fusion = (f32[128]{0:T(128)S(1)}, f32[128]{0:T(128)S(1)}, bf16[128,1536]{1,0:T(8,128)(2,1)S(1)}) fusion(bf16[128,1536]{1,0:T(8,128)(2,1)} %param.7, pred[1536]{0:T(1024)(128)(4,1)S(1)} %and_reduce_fusion), kind=kLoop, calls=%fused_computation.8 | loop fusion | flops 1376000 | bytes 788992 | tf_op jit(solution)/shard_map/reduce_sum | solution.py:327
  8.5 2.6 %load_head.1 = bf16[1792,1536]{1,0:T(8,128)(2,1)S(1)} custom-call(bf16[1792,1536]{1,0:T(8,128)(2,1)} %head_ref.1), custom_call_target="tpu_custom_call" | custom-call | bytes 11010048 | tf_op jit(solution)/shard_map/load_head/pallas_call | solution.py:55
  11.1 0.0 collective-permute-done
  11.1 0.1 collective-permute-start.2
  11.2 1.1 %fusion.25 = f32[64,1536]{1,0:T(8,128)S(1)} fusion(bf16[64,1792]{1,0:T(8,128)(2,1)S(1)} %collective-permute-done, bf16[1792,1536]{1,0:T(8,128)(2,1)S(1)} %load_head.1), kind=kOutput, calls=%fused_computation.71 | convolution fusion | flops 352321536 | bytes 6127616 | tf_op jit(solution)/shard_map/dot_general | solution.py:309
  12.3 0.9 %collective-permute-start.1 = (f32[64,1536]{1,0:T(8,128)S(1)}, f32[64,1536]{1,0:T(8,128)S(1)}, u32[]{:S(2)}, u32[]{:S(2)}) collective-permute-start(f32[64,1536]{1,0:T(8,128)S(1)} %fusion.25), channel_id=1, source_target_pairs={{0,1},{1,0},{2,3},{3,2},{4,5},{5,4},{6,7},{7,6},{8,9},{9,8},{10,11... | collective-permute-start | bytes 1179656 | tf_op jit(solution)/shard_map/ppermute | solution.py:19
  13.1 0.9 %fusion.27.own_ref = f32[128,1536]{1,0:T(8,128)S(1)} fusion(bf16[128,1792]{1,0:T(8,128)(2,1)S(1)} %constant_dynamic-slice_fusion, bf16[1792,1536]{1,0:T(8,128)(2,1)S(1)} %load_head.1), kind=kOutput, calls=%fused_computation.73 | convolution fusion | flops 704643072 | bytes 6750208 | tf_op jit(solution)/shard_map/dot_general | solution.py:315
  14.0 0.0 collective-permute-done.2
  14.0 1.1 %fusion.26 = f32[64,1536]{1,0:T(8,128)S(1)} fusion(bf16[64,1792]{1,0:T(8,128)(2,1)S(1)} %collective-permute-done.2, bf16[1792,1536]{1,0:T(8,128)(2,1)S(1)} %load_head.1), kind=kOutput, calls=%fused_computation.72 | convolution fusion | flops 352321536 | bytes 6127616 | tf_op jit(solution)/shard_map/dot_general | solution.py:312
  15.1 1.3 %collective-permute-start.3 = (f32[64,1536]{1,0:T(8,128)S(1)}, f32[64,1536]{1,0:T(8,128)S(1)}, u32[]{:S(2)}, u32[]{:S(2)}) collective-permute-start(f32[64,1536]{1,0:T(8,128)S(1)} %fusion.26), channel_id=1, source_target_pairs={{0,1},{1,0},{2,3},{3,2},{4,5},{5,4},{6,7},{7,6},{8,9},{9,8},{10,11... | collective-permute-start | bytes 1179656 | tf_op jit(solution)/shard_map/ppermute | solution.py:19
  16.4 0.1 pad_maximum_fusion.refs_0_
  16.5 7.7 %collective-permute-done.1.refs_0_ = f32[64,1536]{1,0:T(8,128)S(1)} collective-permute-done((f32[64,1536]{1,0:T(8,128)S(1)}, f32[64,1536]{1,0:T(8,128)S(1)}, u32[]{:S(2)}, u32[]{:S(2)}) %collective-permute-start.1) | collective-permute-done | bytes 393248 | tf_op jit(solution)/shard_map/ppermute | solution.py:19
  24.2 8.0 %collective-permute-done.3.refs_1_ = f32[64,1536]{1,0:T(8,128)S(1)} collective-permute-done((f32[64,1536]{1,0:T(8,128)S(1)}, f32[64,1536]{1,0:T(8,128)S(1)}, u32[]{:S(2)}, u32[]{:S(2)}) %collective-permute-start.3) | collective-permute-done | bytes 393248 | tf_op jit(solution)/shard_map/ppermute | solution.py:19
  32.3 0.4 local_stats.1
  32.7 0.0 collective-permute-start.4
  32.7 1.1 %collective-permute-done.4 = f32[1,4,128]{2,1,0:T(4,128)S(1)} collective-permute-done((f32[1,4,128]{2,1,0:T(4,128)S(1)}, f32[1,4,128]{2,1,0:T(4,128)S(1)}, u32[]{:S(2)}, u32[]{:S(2)}) %collective-permute-start.4) | collective-permute-done | bytes 2080 | tf_op jit(solution)/shard_map/ppermute | solution.py:23
  33.9 1.6 %collective-permute-start.5 = (f32[2,4,128]{2,1,0:T(4,128)S(1)}, f32[2,4,128]{2,1,0:T(4,128)S(1)}, u32[]{:S(2)}, u32[]{:S(2)}) collective-permute-start(f32[2,4,128]{2,1,0:T(4,128)S(1)} %pad_maximum_fusion.6), channel_id=1, source_target_pairs={{0,4},{2,6},{4,0},{6,2},{8,12},{10,14},{12,8},{14,10},{16,20},{18,... | collective-permute-start | bytes 12296 | tf_op jit(solution)/shard_map/ppermute | solution.py:23
  35.4 2.1 %collective-permute-done.5 = f32[2,4,128]{2,1,0:T(4,128)S(1)} collective-permute-done((f32[2,4,128]{2,1,0:T(4,128)S(1)}, f32[2,4,128]{2,1,0:T(4,128)S(1)}, u32[]{:S(2)}, u32[]{:S(2)}) %collective-permute-start.5) | collective-permute-done | bytes 4128 | tf_op jit(solution)/shard_map/ppermute | solution.py:23
  37.6 1.6 %collective-permute-start.6 = (f32[4,4,128]{2,1,0:T(4,128)S(1)}, f32[4,4,128]{2,1,0:T(4,128)S(1)}, u32[]{:S(2)}, u32[]{:S(2)}) collective-permute-start(f32[4,4,128]{2,1,0:T(4,128)S(1)} %pad_maximum_fusion.5), channel_id=1, source_target_pairs={{0,8},{2,10},{4,12},{6,14},{8,0},{10,2},{12,4},{14,6},{16,24},{18,... | collective-permute-start | bytes 24584 | tf_op jit(solution)/shard_map/ppermute | solution.py:23
  39.2 2.1 %collective-permute-done.6 = f32[4,4,128]{2,1,0:T(4,128)S(1)} collective-permute-done((f32[4,4,128]{2,1,0:T(4,128)S(1)}, f32[4,4,128]{2,1,0:T(4,128)S(1)}, u32[]{:S(2)}, u32[]{:S(2)}) %collective-permute-start.6) | collective-permute-done | bytes 8224 | tf_op jit(solution)/shard_map/ppermute | solution.py:23
  41.3 2.7 %collective-permute-start.7 = (f32[8,4,128]{2,1,0:T(4,128)S(1)}, f32[8,4,128]{2,1,0:T(4,128)S(1)}, u32[]{:S(2)}, u32[]{:S(2)}) collective-permute-start(f32[8,4,128]{2,1,0:T(4,128)S(1)} %pad_maximum_fusion.4), channel_id=1, source_target_pairs={{0,16},{2,18},{4,20},{6,22},{8,24},{10,26},{12,28},{14,30},{16,0},... | collective-permute-start | bytes 49160 | tf_op jit(solution)/shard_map/ppermute | solution.py:23
  44.0 2.0 %collective-permute-done.7 = f32[8,4,128]{2,1,0:T(4,128)S(1)} collective-permute-done((f32[8,4,128]{2,1,0:T(4,128)S(1)}, f32[8,4,128]{2,1,0:T(4,128)S(1)}, u32[]{:S(2)}, u32[]{:S(2)}) %collective-permute-start.7) | collective-permute-done | bytes 16416 | tf_op jit(solution)/shard_map/ppermute | solution.py:23
  46.0 0.9 %delta.1 = (bf16[128,1536]{1,0:T(8,128)(2,1)S(1)}, f32[1,128]{1,0:T(1,128)}, f32[1,128]{1,0:T(1,128)}) custom-call(f32[16,4,128]{2,1,0:T(4,128)S(1)} %pad_maximum_fusion.3.gathered_ref, f32[128,1536]{1,0:T(8,128)S(1)} %get-tuple-element.62.logits_ref, bf16[128,1536]{1,0:T(8,128)(2,1)S(1)} %get-tuple-element.57.kept_ref), custom_call_target="tpu_custom_call" | custom-call | flops 1572864 | bytes 1572864 | tf_op jit(solution)/shard_map/delta/pallas_call | solution.py:141
  46.9 0.8 %collective-permute-start.9 = (bf16[128,1536]{1,0:T(8,128)(2,1)S(1)}, bf16[128,1536]{1,0:T(8,128)(2,1)S(1)}, u32[]{:S(2)}, u32[]{:S(2)}) collective-permute-start(bf16[128,1536]{1,0:T(8,128)(2,1)S(1)} %get-tuple-element.66.delta_ref), channel_id=1, source_target_pairs={{0,1},{1,0},{2,3},{3,2},{4,5},{5,4},{6,7},{7,6},{8,9},{9,8},{10,11... | collective-permute-start | bytes 1179656 | tf_op jit(solution)/shard_map/ppermute | solution.py:19
  47.8 4.8 %partial_gradient.2 = (bf16[4,224,128]{2,1,0:T(8,128)(2,1)S(1)}, f32[4,224,128]{2,1,0:T(8,128)S(1)}, bf16[1792,1536]{1,0:T(8,128)(2,1)S(1)}) custom-call(s32[1]{0:T(128)} %bitcast.1.core_ref, bf16[1792,1536]{1,0:T(8,128)(2,1)} %head_ref.1, bf16[128,1536]{1,0:T(8,128)(2,1)S(1)} %get-tuple-element.66.delta_ref), custom_call_target="tpu_custom_call" | custom-call | flops 704643072 | bytes 5898240 | tf_op jit(solution)/shard_map/partial_gradient/pallas_call | solution.py:203
  52.6 0.1 collective-permute-start.8
  52.7 2.1 %collective-permute-done.9.delta_ref = bf16[128,1536]{1,0:T(8,128)(2,1)S(1)} collective-permute-done((bf16[128,1536]{1,0:T(8,128)(2,1)S(1)}, bf16[128,1536]{1,0:T(8,128)(2,1)S(1)}, u32[]{:S(2)}, u32[]{:S(2)}) %collective-permute-start.9) | collective-permute-done | bytes 393248 | tf_op jit(solution)/shard_map/ppermute | solution.py:19
  54.7 1.6 %partial_gradient.3 = (bf16[4,224,128]{2,1,0:T(8,128)(2,1)S(1)}, f32[4,224,128]{2,1,0:T(8,128)S(1)}) custom-call(s32[1]{0:T(128)} %bitcast.1.core_ref, bf16[1792,1536]{1,0:T(8,128)(2,1)S(1)} %get-tuple-element.69.head_ref, bf16[128,1536]{1,0:T(8,128)(2,1)S(1)} %collective-permute-done.9.delta_ref), custom_call_target="tpu_custom_call" | custom-call | flops 704643072 | bytes 5898240 | tf_op jit(solution)/shard_map/partial_gradient/pallas_call | solution.py:203
  56.3 0.0 collective-permute-done.8
  56.3 0.1 collective-permute-start.10
  56.5 0.1 pad_maximum_fusion.1.refs_1_
  56.5 1.4 %collective-permute-done.10 = bf16[4,224,128]{2,1,0:T(8,128)(2,1)S(1)} collective-permute-done((bf16[4,224,128]{2,1,0:T(8,128)(2,1)S(1)}, bf16[4,224,128]{2,1,0:T(8,128)(2,1)S(1)}, u32[]{:S(2)}, u32[]{:S(2)}) %collective-permute-start.10) | collective-permute-done | bytes 229408 | tf_op jit(solution)/shard_map/ppermute | solution.py:23
  57.9 0.1 fusion.17
  58.0 0.1 fusion.15
  58.1 1.6 %collective-permute-start.11 = (bf16[2,224,128]{2,1,0:T(8,128)(2,1)S(1)}, bf16[2,224,128]{2,1,0:T(8,128)(2,1)S(1)}, u32[]{:S(2)}, u32[]{:S(2)}) collective-permute-start(bf16[2,224,128]{2,1,0:T(8,128)(2,1)S(1)} %get-tuple-element.75), channel_id=1, source_target_pairs={{0,4},{2,6},{4,0},{6,2},{8,12},{10,14},{12,8},{14,10},{16,20},{18,... | collective-permute-start | bytes 344072 | tf_op jit(solution)/shard_map/ppermute | solution.py:23
  59.6 1.6 %collective-permute-start.12 = (bf16[2,224,128]{2,1,0:T(8,128)(2,1)S(1)}, bf16[2,224,128]{2,1,0:T(8,128)(2,1)S(1)}, u32[]{:S(2)}, u32[]{:S(2)}) collective-permute-start(bf16[2,224,128]{2,1,0:T(8,128)(2,1)S(1)} %get-tuple-element.76), channel_id=1, source_target_pairs={{0,8},{2,10},{4,12},{6,14},{8,0},{10,2},{12,4},{14,6},{16,24},{18,... | collective-permute-start | bytes 344072 | tf_op jit(solution)/shard_map/ppermute | solution.py:23
  61.2 0.4 collective-permute-start.13
  61.7 2.1 %head_gradient.2.refs_2_ = bf16[1792,1536]{1,0:T(8,128)(2,1)} custom-call(bf16[256,1792]{1,0:T(8,128)(2,1)S(1)} %pad_maximum_fusion.refs_0_, bf16[256,1536]{1,0:T(8,128)(2,1)S(1)} %pad_maximum_fusion.1.refs_1_), custom_call_target="tpu_custom_call" | custom-call | flops 805306368 | bytes 4849664 | tf_op jit(solution)/shard_map/head_gradient/pallas_call | solution.py:251
  63.7 0.0 collective-permute-done.11
  63.8 1.9 %collective-permute-done.12 = bf16[2,224,128]{2,1,0:T(8,128)(2,1)S(1)} collective-permute-done((bf16[2,224,128]{2,1,0:T(8,128)(2,1)S(1)}, bf16[2,224,128]{2,1,0:T(8,128)(2,1)S(1)}, u32[]{:S(2)}, u32[]{:S(2)}) %collective-permute-start.12) | collective-permute-done | bytes 114720 | tf_op jit(solution)/shard_map/ppermute | solution.py:23
  65.7 1.3 %collective-permute-done.13 = bf16[2,224,128]{2,1,0:T(8,128)(2,1)S(1)} collective-permute-done((bf16[2,224,128]{2,1,0:T(8,128)(2,1)S(1)}, bf16[2,224,128]{2,1,0:T(8,128)(2,1)S(1)}, u32[]{:S(2)}, u32[]{:S(2)}) %collective-permute-start.13) | collective-permute-done | bytes 114720 | tf_op jit(solution)/shard_map/ppermute | solution.py:23
  67.0 0.1 fusion.12
  67.1 0.9 %collective-permute-start.14 = (bf16[224,128]{1,0:T(8,128)(2,1)S(1)}, bf16[224,128]{1,0:T(8,128)(2,1)S(1)}, u32[]{:S(2)}, u32[]{:S(2)}) collective-permute-start(bf16[224,128]{1,0:T(8,128)(2,1)S(1)} %fusion.18), channel_id=1, source_target_pairs={{0,1},{1,0},{2,3},{3,2},{4,5},{5,4},{6,7},{7,6},{8,9},{9,8},{10,11... | collective-permute-start | bytes 172040 | tf_op jit(solution)/shard_map/ppermute | solution.py:19
  68.0 3.4 %collective-permute-done.14 = bf16[224,128]{1,0:T(8,128)(2,1)S(1)} collective-permute-done((bf16[224,128]{1,0:T(8,128)(2,1)S(1)}, bf16[224,128]{1,0:T(8,128)(2,1)S(1)}, u32[]{:S(2)}, u32[]{:S(2)}) %collective-permute-start.14) | collective-permute-done | bytes 57376 | tf_op jit(solution)/shard_map/ppermute | solution.py:19
  71.3 2.6 %collective-permute-start.15 = (bf16[224,128]{1,0:T(8,128)(2,1)S(1)}, bf16[224,128]{1,0:T(8,128)(2,1)S(1)}, u32[]{:S(2)}, u32[]{:S(2)}) collective-permute-start(bf16[224,128]{1,0:T(8,128)(2,1)S(1)} %convert_select_fusion.1), channel_id=1, source_target_pairs={{0,16},{2,18},{4,20},{6,22},{8,24},{10,26},{12,28},{14,30},{16,0},... | collective-permute-start | bytes 172040 | tf_op jit(solution)/shard_map/ppermute | solution.py:388
  74.0 1.8 %head_gradient.3 = bf16[1792,1536]{1,0:T(8,128)(2,1)} custom-call(bf16[256,1792]{1,0:T(8,128)(2,1)S(1)} %pad_maximum_fusion.refs_0_, bf16[256,1536]{1,0:T(8,128)(2,1)S(1)} %pad_maximum_fusion.1.refs_1_, bf16[1792,1536]{1,0:T(8,128)(2,1)} %head_gradient.2.refs_2_), custom_call_target="tpu_custom_call", output_to_operand_aliasing={{}: (2, {})} | custom-call | flops 603979776 | bytes 4063232 | tf_op jit(solution)/shard_map/head_gradient/pallas_call | solution.py:251
  75.8 0.7 collective-permute-done.15
  76.5 0.7 fusion.14
  (16 shorter events, 0.2 us)
Async XLA Ops:
  1.6 9.5 %collective-permute-start = (bf16[64,1792]{1,0:T(8,128)(2,1)S(1)}, bf16[64,1792]{1,0:T(8,128)(2,1)S(1)}, u32[]{:S(2)}, u32[]{:S(2)}) collective-permute-start(bf16[64,1792]{1,0:T(8,128)(2,1)S(1)} %dynamic_slice.7), channel_id=1, source_target_pairs={{0,1},{1,0},{2,3},{3,2},{4,5},{5,4},{6,7},{7,6},{8,9},{9,8},{10,11... | collective-permute-start | bytes 688136 | tf_op jit(solution)/shard_map/ppermute | solution.py:19
  11.1 2.9 %collective-permute-start.2 = (bf16[64,1792]{1,0:T(8,128)(2,1)S(1)}, bf16[64,1792]{1,0:T(8,128)(2,1)S(1)}, u32[]{:S(2)}, u32[]{:S(2)}) collective-permute-start(bf16[64,1792]{1,0:T(8,128)(2,1)S(1)} %collective-permute-done), channel_id=1, source_target_pairs={{0,2},{2,0},{4,6},{6,4},{8,10},{10,8},{12,14},{14,12},{16,18},{18,... | collective-permute-start | bytes 688136 | tf_op jit(solution)/shard_map/ppermute | solution.py:23
  12.3 12.0 %collective-permute-start.1 = (f32[64,1536]{1,0:T(8,128)S(1)}, f32[64,1536]{1,0:T(8,128)S(1)}, u32[]{:S(2)}, u32[]{:S(2)}) collective-permute-start(f32[64,1536]{1,0:T(8,128)S(1)} %fusion.25), channel_id=1, source_target_pairs={{0,1},{1,0},{2,3},{3,2},{4,5},{5,4},{6,7},{7,6},{8,9},{9,8},{10,11... | collective-permute-start | bytes 1179656 | tf_op jit(solution)/shard_map/ppermute | solution.py:19
  15.1 17.2 %collective-permute-start.3 = (f32[64,1536]{1,0:T(8,128)S(1)}, f32[64,1536]{1,0:T(8,128)S(1)}, u32[]{:S(2)}, u32[]{:S(2)}) collective-permute-start(f32[64,1536]{1,0:T(8,128)S(1)} %fusion.26), channel_id=1, source_target_pairs={{0,1},{1,0},{2,3},{3,2},{4,5},{5,4},{6,7},{7,6},{8,9},{9,8},{10,11... | collective-permute-start | bytes 1179656 | tf_op jit(solution)/shard_map/ppermute | solution.py:19
  32.7 1.2 %collective-permute-start.4 = (f32[1,4,128]{2,1,0:T(4,128)S(1)}, f32[1,4,128]{2,1,0:T(4,128)S(1)}, u32[]{:S(2)}, u32[]{:S(2)}) collective-permute-start(f32[1,4,128]{2,1,0:T(4,128)S(1)} %bitcast.86), channel_id=1, source_target_pairs={{0,2},{2,0},{4,6},{6,4},{8,10},{10,8},{12,14},{14,12},{16,18},{18,... | collective-permute-start | bytes 6152 | tf_op jit(solution)/shard_map/ppermute | solution.py:23
  33.9 3.7 %collective-permute-start.5 = (f32[2,4,128]{2,1,0:T(4,128)S(1)}, f32[2,4,128]{2,1,0:T(4,128)S(1)}, u32[]{:S(2)}, u32[]{:S(2)}) collective-permute-start(f32[2,4,128]{2,1,0:T(4,128)S(1)} %pad_maximum_fusion.6), channel_id=1, source_target_pairs={{0,4},{2,6},{4,0},{6,2},{8,12},{10,14},{12,8},{14,10},{16,20},{18,... | collective-permute-start | bytes 12296 | tf_op jit(solution)/shard_map/ppermute | solution.py:23
  37.6 3.7 %collective-permute-start.6 = (f32[4,4,128]{2,1,0:T(4,128)S(1)}, f32[4,4,128]{2,1,0:T(4,128)S(1)}, u32[]{:S(2)}, u32[]{:S(2)}) collective-permute-start(f32[4,4,128]{2,1,0:T(4,128)S(1)} %pad_maximum_fusion.5), channel_id=1, source_target_pairs={{0,8},{2,10},{4,12},{6,14},{8,0},{10,2},{12,4},{14,6},{16,24},{18,... | collective-permute-start | bytes 24584 | tf_op jit(solution)/shard_map/ppermute | solution.py:23
  41.3 4.7 %collective-permute-start.7 = (f32[8,4,128]{2,1,0:T(4,128)S(1)}, f32[8,4,128]{2,1,0:T(4,128)S(1)}, u32[]{:S(2)}, u32[]{:S(2)}) collective-permute-start(f32[8,4,128]{2,1,0:T(4,128)S(1)} %pad_maximum_fusion.4), channel_id=1, source_target_pairs={{0,16},{2,18},{4,20},{6,22},{8,24},{10,26},{12,28},{14,30},{16,0},... | collective-permute-start | bytes 49160 | tf_op jit(solution)/shard_map/ppermute | solution.py:23
  46.9 7.8 %collective-permute-start.9 = (bf16[128,1536]{1,0:T(8,128)(2,1)S(1)}, bf16[128,1536]{1,0:T(8,128)(2,1)S(1)}, u32[]{:S(2)}, u32[]{:S(2)}) collective-permute-start(bf16[128,1536]{1,0:T(8,128)(2,1)S(1)} %get-tuple-element.66.delta_ref), channel_id=1, source_target_pairs={{0,1},{1,0},{2,3},{3,2},{4,5},{5,4},{6,7},{7,6},{8,9},{9,8},{10,11... | collective-permute-start | bytes 1179656 | tf_op jit(solution)/shard_map/ppermute | solution.py:19
  52.6 3.7 %collective-permute-start.8 = (bf16[4,224,128]{2,1,0:T(8,128)(2,1)S(1)}, bf16[4,224,128]{2,1,0:T(8,128)(2,1)S(1)}, u32[]{:S(2)}, u32[]{:S(2)}) collective-permute-start(bf16[4,224,128]{2,1,0:T(8,128)(2,1)S(1)} %get-tuple-element.68), channel_id=1, source_target_pairs={{0,2},{2,0},{4,6},{6,4},{8,10},{10,8},{12,14},{14,12},{16,18},{18,... | collective-permute-start | bytes 688136 | tf_op jit(solution)/shard_map/ppermute | solution.py:23
  56.3 1.6 %collective-permute-start.10 = (bf16[4,224,128]{2,1,0:T(8,128)(2,1)S(1)}, bf16[4,224,128]{2,1,0:T(8,128)(2,1)S(1)}, u32[]{:S(2)}, u32[]{:S(2)}) collective-permute-start(bf16[4,224,128]{2,1,0:T(8,128)(2,1)S(1)} %get-tuple-element.74), channel_id=1, source_target_pairs={{0,2},{2,0},{4,6},{6,4},{8,10},{10,8},{12,14},{14,12},{16,18},{18,... | collective-permute-start | bytes 688136 | tf_op jit(solution)/shard_map/ppermute | solution.py:23
  58.1 5.6 %collective-permute-start.11 = (bf16[2,224,128]{2,1,0:T(8,128)(2,1)S(1)}, bf16[2,224,128]{2,1,0:T(8,128)(2,1)S(1)}, u32[]{:S(2)}, u32[]{:S(2)}) collective-permute-start(bf16[2,224,128]{2,1,0:T(8,128)(2,1)S(1)} %get-tuple-element.75), channel_id=1, source_target_pairs={{0,4},{2,6},{4,0},{6,2},{8,12},{10,14},{12,8},{14,10},{16,20},{18,... | collective-permute-start | bytes 344072 | tf_op jit(solution)/shard_map/ppermute | solution.py:23
  59.6 6.0 %collective-permute-start.12 = (bf16[2,224,128]{2,1,0:T(8,128)(2,1)S(1)}, bf16[2,224,128]{2,1,0:T(8,128)(2,1)S(1)}, u32[]{:S(2)}, u32[]{:S(2)}) collective-permute-start(bf16[2,224,128]{2,1,0:T(8,128)(2,1)S(1)} %get-tuple-element.76), channel_id=1, source_target_pairs={{0,8},{2,10},{4,12},{6,14},{8,0},{10,2},{12,4},{14,6},{16,24},{18,... | collective-permute-start | bytes 344072 | tf_op jit(solution)/shard_map/ppermute | solution.py:23
  61.2 5.8 %collective-permute-start.13 = (bf16[2,224,128]{2,1,0:T(8,128)(2,1)S(1)}, bf16[2,224,128]{2,1,0:T(8,128)(2,1)S(1)}, u32[]{:S(2)}, u32[]{:S(2)}) collective-permute-start(bf16[2,224,128]{2,1,0:T(8,128)(2,1)S(1)} %get-tuple-element.77), channel_id=1, source_target_pairs={{0,12},{2,14},{4,8},{6,10},{8,4},{10,6},{12,0},{14,2},{16,28},{18,... | collective-permute-start | bytes 344072 | tf_op jit(solution)/shard_map/ppermute | solution.py:23
  67.1 4.2 %collective-permute-start.14 = (bf16[224,128]{1,0:T(8,128)(2,1)S(1)}, bf16[224,128]{1,0:T(8,128)(2,1)S(1)}, u32[]{:S(2)}, u32[]{:S(2)}) collective-permute-start(bf16[224,128]{1,0:T(8,128)(2,1)S(1)} %fusion.18), channel_id=1, source_target_pairs={{0,1},{1,0},{2,3},{3,2},{4,5},{5,4},{6,7},{7,6},{8,9},{9,8},{10,11... | collective-permute-start | bytes 172040 | tf_op jit(solution)/shard_map/ppermute | solution.py:19
  71.3 5.1 %collective-permute-start.15 = (bf16[224,128]{1,0:T(8,128)(2,1)S(1)}, bf16[224,128]{1,0:T(8,128)(2,1)S(1)}, u32[]{:S(2)}, u32[]{:S(2)}) collective-permute-start(bf16[224,128]{1,0:T(8,128)(2,1)S(1)} %convert_select_fusion.1), channel_id=1, source_target_pairs={{0,16},{2,18},{4,20},{6,22},{8,24},{10,26},{12,28},{14,30},{16,0},... | collective-permute-start | bytes 172040 | tf_op jit(solution)/shard_map/ppermute | solution.py:388

commit v9 on v8

--- a/solution.py
+++ b/solution.py
@@ -29,10 +29,22 @@
     )
 
 
-def gather_vocab(stats, upper, size):
-    gathered = stats[None]
-    for i, flag in enumerate(upper):
-        gathered = in_order(gathered, swap_vocab(gathered, 1 << i, size), flag)
+def select(options, flags):
+    for flag in flags:
+        options = [jnp.where(flag, high, low) for low, high in zip(options[::2], options[1::2])]
+    return options[0]
+
+
+def gather_vocab(stats, upper, places, size):
+    pair = in_order(stats[None], swap_vocab(stats[None], 1, size), upper[0])
+    count = 1 << len(places)
+    options = [pair] + [swap_vocab(pair, 2 * offset, size) for offset in range(1, count)]
+    flags = [upper[i] for i in places]
+    gathered = jnp.concatenate(
+        [select([options[j ^ i] for i in range(count)], flags) for j in range(count)], axis=0
+    )
+    for i in range(len(places) + 1, len(upper)):
+        gathered = in_order(gathered, swap_vocab(gathered, 1 << i, size), upper[i])
     return gathered
 
 
@@ -166,25 +178,7 @@
     keep_ref[k] = jnp.where(upper, high, low)
 
 
-def first_gradient_kernel(core_ref, head_ref, delta_ref, send_ref, keep_ref, held_ref, sems):
-    upper = core_ref[0] == 1
-    pairs, rows, _ = send_ref.shape
-    parts = [pl.ds(2 * k * rows, 2 * rows) for k in range(pairs)]
-    copies = [
-        pltpu.make_async_copy(head_ref.at[part], held_ref.at[part], sems.at[k])
-        for k, part in enumerate(parts)
-    ]
-    for copy in copies[:2]:
-        copy.start()
-    for k in range(pairs):
-        copies[k].wait()
-        if k + 2 < pairs:
-            copies[k + 2].start()
-        head_rows = held_ref[2 * k * rows : 2 * (k + 1) * rows, :]
-        write_pieces(k, head_rows, delta_ref, upper, send_ref, keep_ref)
-
-
-def later_gradient_kernel(core_ref, head_ref, delta_ref, send_ref, keep_ref):
+def gradient_kernel(core_ref, head_ref, delta_ref, send_ref, keep_ref):
     upper = core_ref[0] == 1
     pairs, rows, _ = send_ref.shape
     for k in range(pairs):
@@ -192,24 +186,15 @@
         write_pieces(k, head_rows, delta_ref, upper, send_ref, keep_ref)
 
 
-def gradient(core, head, delta, run, first):
+def gradient(core, head, delta, run):
     rows = head.shape[0] // run
     shape = (run // 2, rows, delta.shape[0])
     in_vmem = pl.BlockSpec(memory_space=pltpu.VMEM)
-    space = pltpu.HBM if first else pltpu.VMEM
-    outs = (pltpu.VMEM(shape, jnp.bfloat16), pltpu.VMEM(shape, jnp.float32))
-    if first:
-        outs = outs + (pltpu.VMEM(head.shape, head.dtype),)
     return pl.pallas_call(
-        first_gradient_kernel if first else later_gradient_kernel,
-        out_shape=outs,
-        in_specs=[
-            pl.BlockSpec(memory_space=pltpu.SMEM),
-            pl.BlockSpec(memory_space=space),
-            in_vmem,
-        ],
-        out_specs=(in_vmem,) * len(outs),
-        scratch_shapes=[pltpu.SemaphoreType.DMA((run // 2,))] if first else [],
+        gradient_kernel,
+        out_shape=(pltpu.VMEM(shape, jnp.bfloat16), pltpu.VMEM(shape, jnp.float32)),
+        in_specs=[pl.BlockSpec(memory_space=pltpu.SMEM), in_vmem, in_vmem],
+        out_specs=(in_vmem, in_vmem),
         compiler_params=pltpu.CompilerParams(vmem_limit_bytes=VMEM_LIMIT),
         cost_estimate=pl.CostEstimate(
             flops=2 * head.size * delta.shape[0],
@@ -219,7 +204,7 @@
         name="partial_gradient",
     )(
         core,
-        pltpu.with_memory_space_constraint(head, space),
+        pltpu.with_memory_space_constraint(head, pltpu.VMEM),
         pltpu.with_memory_space_constraint(delta, pltpu.VMEM),
     )
 
@@ -301,7 +286,9 @@
         (own, head, upper, apart_is, column_block, live_slot, core_word)
     )
     head_here = load(head)
-    near, head_here = lax.optimization_barrier((near, head_here))
+    near, head_here, column_block, teacher = lax.optimization_barrier(
+        (near, head_here, column_block, teacher)
+    )
     far = [swap_vocab(x, 1, vocab_size) for x in near]
     returned = []
     for d in range(1, tok_size):
@@ -330,15 +317,16 @@
     returned, all_features, logits, kept, early = lax.optimization_barrier(
         (returned, all_features, logits, kept, early)
     )
+    places = [i for i in range(1, len(upper)) if 1 << i < run]
     logits, stats = local_stats(core_word, logits, kept, early, returned)
-    delta, lse, kl = finish(gather_vocab(stats, upper, vocab_size), logits, kept)
+    delta, lse, kl = finish(gather_vocab(stats, upper, places, vocab_size), logits, kept)
 
     deltas = [delta] + [shift_tok(delta, d, tok_size) for d in range(1, tok_size)]
-    send, keep, head_here = gradient(core_word, head, delta, run, True)
+    send, keep = gradient(core_word, head_here, delta, run)
     other = swap_vocab(send, 1, vocab_size)
     state = [(keep, other)]
     for x in deltas[1:]:
-        send, keep = gradient(core_word, head_here, x, run, False)
+        send, keep = gradient(core_word, head_here, x, run)
         state[0], send = lax.optimization_barrier((state[0], send))
         state.append((keep, swap_vocab(send, 1, vocab_size)))
     all_delta = jnp.concatenate(deltas, axis=0)
@@ -347,15 +335,10 @@
     chunks = rows // width
     held = jnp.stack([keep + other.astype(jnp.float32) for keep, other in state], axis=1)
     pieces = held.shape[0]
-    places = [i for i in range(1, len(upper)) if 1 << i < run]
-    taken = []
-    for offset in range(pieces):
-        options = [held[j ^ offset] for j in range(pieces)]
-        for i in places:
-            options = [
-                jnp.where(upper[i], high, low) for low, high in zip(options[::2], options[1::2])
-            ]
-        taken.append(options[0])
+    flags = [upper[i] for i in places]
+    taken = [
+        select([held[j ^ offset] for j in range(pieces)], flags) for offset in range(pieces)
+    ]
     sends = [x.astype(jnp.bfloat16) for x in taken[1:]]
     sends, all_delta = lax.optimization_barrier((sends, all_delta))
     others = [swap_vocab(x, 2 * (i + 1), vocab_size) for i, x in enumerate(sends)]
@@ -365,12 +348,15 @@
     sums = taken[0]
     for other in others:
         sums = sums + other.astype(jnp.float32)
-    sums = [
-        sums[d]
-        if d == 0
-        else shift_tok(sums[d].astype(jnp.bfloat16), -d, tok_size).astype(jnp.float32)
-        for d in range(tok_size)
-    ]
+    sends = [x.astype(jnp.bfloat16) for x in (sums[d] for d in range(1, tok_size))]
+    sends, all_delta = lax.optimization_barrier((sends, all_delta))
+    others = [shift_tok(x, -d, tok_size) for d, x in enumerate(sends, 1)]
+    if done < chunks:
+        grad_head = head_gradient(
+            all_features, all_delta, grad_head, done * width, chunks - done, width
+        )
+        others, grad_head = lax.optimization_barrier((others, grad_head))
+    sums = [sums[0]] + [x.astype(jnp.float32) for x in others]
     blocks = []
     for k in range(tok_size):
         block = sums[k]
@@ -378,11 +364,6 @@
             block = jnp.where(apart_is[d], sums[(k - d) % tok_size], block)
         blocks.append(block)
     total = blocks[0]
-    if done < chunks:
-        blocks[1:], all_delta = lax.optimization_barrier((blocks[1:], all_delta))
-        grad_head = head_gradient(
-            all_features, all_delta, grad_head, done * width, chunks - done, width
-        )
     for k in range(1, tok_size):
         pairs = [(v, (v + k * run) % vocab_size) for v in range(vocab_size)]
         total = total + lax.ppermute(

time: 77.4 us -> 77.9 us (level)
  waiting for transfers between devices: 33.9 us -> 37.7 us
  Pallas kernels: 14.2 us -> 11 us
  other arithmetic: 3.3 us -> 1.68 us
  starting transfers between devices: 19.2 us -> 20.8 us
    pallas_call x2, Pallas kernels: 6.41 us -> 3.15 us  [gradient(): pl.pallas_call(gradient_kernel, out_shape=(pltpu.VMEM(shape, jnp.bfloat16...]
    ppermute x1, waiting for transfers between devices: 0.67 us -> 3.01 us  [per_device(): lax.ppermute(blocks[k].astype(jnp.bfloat16), 'vocab', pairs)]
    ppermute x5, starting transfers between devices: 6.87 us -> 8.28 us  [shift_tok(): lax.ppermute(x, 'tok', [(i, (i + offset) % size) for i in range(size)])]
    ppermute x5, waiting for transfers between devices: 21.2 us -> 22.5 us  [shift_tok(): lax.ppermute(x, 'tok', [(i, (i + offset) % size) for i in range(size)])]
    reduce_sum x1, other arithmetic: 1.31 us -> 0.31 us  [per_device(): mass = jnp.sum(kept, axis=1)]
    ppermute x10 -> x11, starting transfers between devices: 9.66 us -> 9.94 us  [swap_vocab(): return lax.ppermute(x, 'vocab', [(i, i ^ bit) for i in range(size)])]
    ppermute x10 -> x11, waiting for transfers between devices: 12 us -> 12.2 us  [swap_vocab(): return lax.ppermute(x, 'vocab', [(i, i ^ bit) for i in range(size)])]
  transfers between devices with their start and end apart: 16 -> 17, of which waited for: 12 -> 14; matrix products, arithmetic and copies ran while one was open for 8% -> 6% of each run, Pallas kernels for 17% -> 12%
where the time goes in v9:
time: 77.9 us; the launch traced here: 77.7 us
  waiting for transfers between devices  37.7 us (48%)
  starting transfers between devices  20.8 us (27%)
  Pallas kernels  11 us (14%)
  matrix products  3.01 us (4%)
  local copies, waits for them, and re-layouts  2.04 us (3%)
  other arithmetic  1.68 us (2%)
  between operations  1.52 us (2%)
    ppermute x5, waiting for transfers between devices, shift_tok(): lax.ppermute(x, 'tok', [(i, (i + offset) % size) for i in range(size)])  22.5 us
    ppermute x11, waiting for transfers between devices, swap_vocab(): return lax.ppermute(x, 'vocab', [(i, i ^ bit) for i in range(size)])  12.2 us
    ppermute x11, starting transfers between devices, swap_vocab(): return lax.ppermute(x, 'vocab', [(i, i ^ bit) for i in range(size)])  9.94 us
    ppermute x5, starting transfers between devices, shift_tok(): lax.ppermute(x, 'tok', [(i, (i + offset) % size) for i in range(size)])  8.28 us
    pallas_call x2, Pallas kernels, head_gradient(): pl.pallas_call(functools.partial(head_gradient_kernel, steps, start, widt...  3.89 us
    pallas_call x2, Pallas kernels, gradient(): pl.pallas_call(gradient_kernel, out_shape=(pltpu.VMEM(shape, jnp.bfloat16...  3.15 us
    ppermute x1, waiting for transfers between devices, per_device(): lax.ppermute(blocks[k].astype(jnp.bfloat16), 'vocab', pairs)  3.01 us
    pallas_call x1, Pallas kernels, load(): pl.pallas_call(load_kernel, out_shape=pltpu.VMEM(head.shape, head.dtype),...  2.62 us
  transfers between devices with their start and end apart: 17, of which 14 were waited for; matrix products, arithmetic and copies ran while one was open for 6% of the time, Pallas kernels for 12%

profile of v9, /device:TPU:0, one launch (start us, length us, event | category | flops | bytes accessed | tf_op | source)
XLA Modules:
  0.0 77.7 jit_solution(17889266340063388791)
XLA Ops:
  0.6 1.0 %dynamic_slice.7 = bf16[64,1792]{1,0:T(8,128)(2,1)S(1)} dynamic-slice(bf16[128,3584]{1,0:T(8,128)(2,1)} %param.5, s32[]{:T(128)S(6)} %select_n.177, s32[]{:T(128)S(6)} %select_n.178), dynamic_slice_sizes={64,1792} | dynamic-slice | bytes 458756 | tf_op jit(solution)/shard_map/dynamic_slice | solution.py:268
  1.6 3.0 %collective-permute-start = (bf16[64,1792]{1,0:T(8,128)(2,1)S(1)}, bf16[64,1792]{1,0:T(8,128)(2,1)S(1)}, u32[]{:S(2)}, u32[]{:S(2)}) collective-permute-start(bf16[64,1792]{1,0:T(8,128)(2,1)S(1)} %dynamic_slice.7), channel_id=1, source_target_pairs={{0,1},{1,0},{2,3},{3,2},{4,5},{5,4},{6,7},{7,6},{8,9},{9,8},{10,11... | collective-permute-start | bytes 688136 | tf_op jit(solution)/shard_map/ppermute | solution.py:19
  5.3 1.1 %constant_dynamic-slice_fusion = bf16[128,1792]{1,0:T(8,128)(2,1)S(1)} fusion(bf16[128,3584]{1,0:T(8,128)(2,1)} %param.5, s32[]{:T(128)S(6)} %select_n.171), kind=kLoop, calls=%fused_computation.74 | loop fusion | bytes 917508 | tf_op jit(solution)/shard_map/dynamic_slice | solution.py:268
  6.4 2.6 %load_head.1.head_ref = bf16[1792,1536]{1,0:T(8,128)(2,1)S(1)} custom-call(bf16[1792,1536]{1,0:T(8,128)(2,1)} %head_ref), custom_call_target="tpu_custom_call" | custom-call | bytes 11010048 | tf_op jit(solution)/shard_map/load_head/pallas_call | solution.py:67
  9.0 0.0 copy-start.1
  9.0 0.0 copy-start
  9.0 1.2 %collective-permute-done = bf16[64,1792]{1,0:T(8,128)(2,1)S(1)} collective-permute-done((bf16[64,1792]{1,0:T(8,128)(2,1)S(1)}, bf16[64,1792]{1,0:T(8,128)(2,1)S(1)}, u32[]{:S(2)}, u32[]{:S(2)}) %collective-permute-start) | collective-permute-done | bytes 229408 | tf_op jit(solution)/shard_map/ppermute | solution.py:19
  10.2 0.0 collective-permute-start.2
  10.3 1.1 %fusion.26 = f32[64,1536]{1,0:T(8,128)S(1)} fusion(bf16[64,1792]{1,0:T(8,128)(2,1)S(1)} %collective-permute-done, bf16[1792,1536]{1,0:T(8,128)(2,1)S(1)} %load_head.1.head_ref), kind=kOutput, calls=%fused_computation.75 | convolution fusion | flops 352321536 | bytes 6127616 | tf_op jit(solution)/shard_map/dot_general | solution.py:296
  11.3 1.8 %collective-permute-start.1 = (f32[64,1536]{1,0:T(8,128)S(1)}, f32[64,1536]{1,0:T(8,128)S(1)}, u32[]{:S(2)}, u32[]{:S(2)}) collective-permute-start(f32[64,1536]{1,0:T(8,128)S(1)} %fusion.26), channel_id=1, source_target_pairs={{0,1},{1,0},{2,3},{3,2},{4,5},{5,4},{6,7},{7,6},{8,9},{9,8},{10,11... | collective-permute-start | bytes 1179656 | tf_op jit(solution)/shard_map/ppermute | solution.py:19
  13.1 0.9 %fusion.28.own_ref = f32[128,1536]{1,0:T(8,128)S(1)} fusion(bf16[128,1792]{1,0:T(8,128)(2,1)S(1)} %constant_dynamic-slice_fusion, bf16[1792,1536]{1,0:T(8,128)(2,1)S(1)} %load_head.1.head_ref), kind=kOutput, calls=%fused_computation.77 | convolution fusion | flops 704643072 | bytes 6750208 | tf_op jit(solution)/shard_map/dot_general | solution.py:302
  14.0 0.0 copy-done.1
  14.0 0.1 and_reduce_fusion
  14.1 0.0 copy-done
  14.1 0.3 fusion
  14.5 0.0 collective-permute-done.2
  14.5 1.1 %fusion.27 = f32[64,1536]{1,0:T(8,128)S(1)} fusion(bf16[64,1792]{1,0:T(8,128)(2,1)S(1)} %collective-permute-done.2, bf16[1792,1536]{1,0:T(8,128)(2,1)S(1)} %load_head.1.head_ref), kind=kOutput, calls=%fused_computation.76 | convolution fusion | flops 352321536 | bytes 6127616 | tf_op jit(solution)/shard_map/dot_general | solution.py:299
  15.5 0.3 collective-permute-start.3
  15.9 0.1 broadcast_select_fusion.1
  15.9 0.1 pad_maximum_fusion.refs_0_
  16.0 7.3 %collective-permute-done.1.refs_0_ = f32[64,1536]{1,0:T(8,128)S(1)} collective-permute-done((f32[64,1536]{1,0:T(8,128)S(1)}, f32[64,1536]{1,0:T(8,128)S(1)}, u32[]{:S(2)}, u32[]{:S(2)}) %collective-permute-start.1) | collective-permute-done | bytes 393248 | tf_op jit(solution)/shard_map/ppermute | solution.py:19
  23.3 8.0 %collective-permute-done.3.refs_1_ = f32[64,1536]{1,0:T(8,128)S(1)} collective-permute-done((f32[64,1536]{1,0:T(8,128)S(1)}, f32[64,1536]{1,0:T(8,128)S(1)}, u32[]{:S(2)}, u32[]{:S(2)}) %collective-permute-start.3) | collective-permute-done | bytes 393248 | tf_op jit(solution)/shard_map/ppermute | solution.py:19
  31.3 0.4 local_stats.1
  31.8 0.0 collective-permute-start.4
  31.8 1.1 %collective-permute-done.4 = f32[1,4,128]{2,1,0:T(4,128)S(1)} collective-permute-done((f32[1,4,128]{2,1,0:T(4,128)S(1)}, f32[1,4,128]{2,1,0:T(4,128)S(1)}, u32[]{:S(2)}, u32[]{:S(2)}) %collective-permute-start.4) | collective-permute-done | bytes 2080 | tf_op jit(solution)/shard_map/ppermute | solution.py:23
  33.0 1.8 %collective-permute-start.7 = (f32[2,4,128]{2,1,0:T(4,128)S(1)}, f32[2,4,128]{2,1,0:T(4,128)S(1)}, u32[]{:S(2)}, u32[]{:S(2)}) collective-permute-start(f32[2,4,128]{2,1,0:T(4,128)S(1)} %pad_maximum_fusion.5), channel_id=1, source_target_pairs={{0,4},{2,6},{4,0},{6,2},{8,12},{10,14},{12,8},{14,10},{16,20},{18,... | collective-permute-start | bytes 12296 | tf_op jit(solution)/shard_map/ppermute | solution.py:23
  34.7 1.6 %collective-permute-start.6 = (f32[2,4,128]{2,1,0:T(4,128)S(1)}, f32[2,4,128]{2,1,0:T(4,128)S(1)}, u32[]{:S(2)}, u32[]{:S(2)}) collective-permute-start(f32[2,4,128]{2,1,0:T(4,128)S(1)} %pad_maximum_fusion.5), channel_id=1, source_target_pairs={{0,8},{2,10},{4,12},{6,14},{8,0},{10,2},{12,4},{14,6},{16,24},{18,... | collective-permute-start | bytes 12296 | tf_op jit(solution)/shard_map/ppermute | solution.py:23
  36.3 0.2 collective-permute-start.5
  36.5 0.1 collective-permute-done.7
  36.6 1.7 %collective-permute-done.6 = f32[2,4,128]{2,1,0:T(4,128)S(1)} collective-permute-done((f32[2,4,128]{2,1,0:T(4,128)S(1)}, f32[2,4,128]{2,1,0:T(4,128)S(1)}, u32[]{:S(2)}, u32[]{:S(2)}) %collective-permute-start.6) | collective-permute-done | bytes 4128 | tf_op jit(solution)/shard_map/ppermute | solution.py:23
  38.3 2.5 %collective-permute-done.5 = f32[2,4,128]{2,1,0:T(4,128)S(1)} collective-permute-done((f32[2,4,128]{2,1,0:T(4,128)S(1)}, f32[2,4,128]{2,1,0:T(4,128)S(1)}, u32[]{:S(2)}, u32[]{:S(2)}) %collective-permute-start.5) | collective-permute-done | bytes 4128 | tf_op jit(solution)/shard_map/ppermute | solution.py:23
  40.8 2.7 %collective-permute-start.8 = (f32[8,4,128]{2,1,0:T(4,128)S(1)}, f32[8,4,128]{2,1,0:T(4,128)S(1)}, u32[]{:S(2)}, u32[]{:S(2)}) collective-permute-start(f32[8,4,128]{2,1,0:T(4,128)S(1)} %pad_maximum_fusion.4), channel_id=1, source_target_pairs={{0,16},{2,18},{4,20},{6,22},{8,24},{10,26},{12,28},{14,30},{16,0},... | collective-permute-start | bytes 49160 | tf_op jit(solution)/shard_map/ppermute | solution.py:23
  43.5 2.1 %collective-permute-done.8 = f32[8,4,128]{2,1,0:T(4,128)S(1)} collective-permute-done((f32[8,4,128]{2,1,0:T(4,128)S(1)}, f32[8,4,128]{2,1,0:T(4,128)S(1)}, u32[]{:S(2)}, u32[]{:S(2)}) %collective-permute-start.8) | collective-permute-done | bytes 16416 | tf_op jit(solution)/shard_map/ppermute | solution.py:23
  45.6 0.9 %delta.1 = (bf16[128,1536]{1,0:T(8,128)(2,1)S(1)}, f32[1,128]{1,0:T(1,128)}, f32[1,128]{1,0:T(1,128)}) custom-call(f32[16,4,128]{2,1,0:T(4,128)S(1)} %pad_maximum_fusion.3.gathered_ref, f32[128,1536]{1,0:T(8,128)S(1)} %get-tuple-element.67.logits_ref, bf16[128,1536]{1,0:T(8,128)(2,1)S(1)} %get-tuple-element.62.kept_ref), custom_call_target="tpu_custom_call" | custom-call | flops 1572864 | bytes 1572864 | tf_op jit(solution)/shard_map/delta/pallas_call | solution.py:153
  46.5 1.5 %collective-permute-start.10 = (bf16[128,1536]{1,0:T(8,128)(2,1)S(1)}, bf16[128,1536]{1,0:T(8,128)(2,1)S(1)}, u32[]{:S(2)}, u32[]{:S(2)}) collective-permute-start(bf16[128,1536]{1,0:T(8,128)(2,1)S(1)} %get-tuple-element.71.delta_ref), channel_id=1, source_target_pairs={{0,1},{1,0},{2,3},{3,2},{4,5},{5,4},{6,7},{7,6},{8,9},{9,8},{10,11... | collective-permute-start | bytes 1179656 | tf_op jit(solution)/shard_map/ppermute | solution.py:19
  48.1 1.6 %partial_gradient.2 = (bf16[4,224,128]{2,1,0:T(8,128)(2,1)S(1)}, f32[4,224,128]{2,1,0:T(8,128)S(1)}) custom-call(s32[1]{0:T(128)} %bitcast.1.core_ref, bf16[1792,1536]{1,0:T(8,128)(2,1)S(1)} %load_head.1.head_ref, bf16[128,1536]{1,0:T(8,128)(2,1)S(1)} %get-tuple-element.71.delta_ref), custom_call_target="tpu_custom_call" | custom-call | flops 704643072 | bytes 5898240 | tf_op jit(solution)/shard_map/partial_gradient/pallas_call | solution.py:193
  49.6 0.1 collective-permute-start.9
  49.7 5.1 %collective-permute-done.10.delta_ref = bf16[128,1536]{1,0:T(8,128)(2,1)S(1)} collective-permute-done((bf16[128,1536]{1,0:T(8,128)(2,1)S(1)}, bf16[128,1536]{1,0:T(8,128)(2,1)S(1)}, u32[]{:S(2)}, u32[]{:S(2)}) %collective-permute-start.10) | collective-permute-done | bytes 393248 | tf_op jit(solution)/shard_map/ppermute | solution.py:19
  54.8 1.6 %partial_gradient.3 = (bf16[4,224,128]{2,1,0:T(8,128)(2,1)S(1)}, f32[4,224,128]{2,1,0:T(8,128)S(1)}) custom-call(s32[1]{0:T(128)} %bitcast.1.core_ref, bf16[1792,1536]{1,0:T(8,128)(2,1)S(1)} %load_head.1.head_ref, bf16[128,1536]{1,0:T(8,128)(2,1)S(1)} %collective-permute-done.10.delta_ref), custom_call_target="tpu_custom_call" | custom-call | flops 704643072 | bytes 5898240 | tf_op jit(solution)/shard_map/partial_gradient/pallas_call | solution.py:193
  56.4 0.0 collective-permute-done.9
  56.4 0.1 collective-permute-start.11
  56.5 0.1 add_bitcast_fusion.1
  56.6 0.1 pad_maximum_fusion.1.refs_1_
  56.6 1.4 %collective-permute-done.11 = bf16[4,224,128]{2,1,0:T(8,128)(2,1)S(1)} collective-permute-done((bf16[4,224,128]{2,1,0:T(8,128)(2,1)S(1)}, bf16[4,224,128]{2,1,0:T(8,128)(2,1)S(1)}, u32[]{:S(2)}, u32[]{:S(2)}) %collective-permute-start.11) | collective-permute-done | bytes 229408 | tf_op jit(solution)/shard_map/ppermute | solution.py:23
  58.0 0.1 add_bitcast_fusion
  58.0 0.1 fusion.18
  58.1 0.1 fusion.16
  58.2 0.5 collective-permute-start.12
  58.7 0.4 collective-permute-start.13
  59.1 2.6 %collective-permute-start.14 = (bf16[2,224,128]{2,1,0:T(8,128)(2,1)S(1)}, bf16[2,224,128]{2,1,0:T(8,128)(2,1)S(1)}, u32[]{:S(2)}, u32[]{:S(2)}) collective-permute-start(bf16[2,224,128]{2,1,0:T(8,128)(2,1)S(1)} %get-tuple-element.81), channel_id=1, source_target_pairs={{0,12},{2,14},{4,8},{6,10},{8,4},{10,6},{12,0},{14,2},{16,28},{18,... | collective-permute-start | bytes 344072 | tf_op jit(solution)/shard_map/ppermute | solution.py:23
  61.8 2.1 %head_gradient.2.refs_2_ = bf16[1792,1536]{1,0:T(8,128)(2,1)} custom-call(bf16[256,1792]{1,0:T(8,128)(2,1)S(1)} %pad_maximum_fusion.refs_0_, bf16[256,1536]{1,0:T(8,128)(2,1)S(1)} %pad_maximum_fusion.1.refs_1_), custom_call_target="tpu_custom_call" | custom-call | flops 805306368 | bytes 4849664 | tf_op jit(solution)/shard_map/head_gradient/pallas_call | solution.py:236
  63.8 0.0 collective-permute-done.12
  63.9 0.9 %collective-permute-done.13 = bf16[2,224,128]{2,1,0:T(8,128)(2,1)S(1)} collective-permute-done((bf16[2,224,128]{2,1,0:T(8,128)(2,1)S(1)}, bf16[2,224,128]{2,1,0:T(8,128)(2,1)S(1)}, u32[]{:S(2)}, u32[]{:S(2)}) %collective-permute-start.13) | collective-permute-done | bytes 114720 | tf_op jit(solution)/shard_map/ppermute | solution.py:23
  64.8 2.3 %collective-permute-done.14 = bf16[2,224,128]{2,1,0:T(8,128)(2,1)S(1)} collective-permute-done((bf16[2,224,128]{2,1,0:T(8,128)(2,1)S(1)}, bf16[2,224,128]{2,1,0:T(8,128)(2,1)S(1)}, u32[]{:S(2)}, u32[]{:S(2)}) %collective-permute-start.14) | collective-permute-done | bytes 114720 | tf_op jit(solution)/shard_map/ppermute | solution.py:23
  67.1 0.1 fusion.12
  67.2 1.6 %collective-permute-start.15 = (bf16[224,128]{1,0:T(8,128)(2,1)S(1)}, bf16[224,128]{1,0:T(8,128)(2,1)S(1)}, u32[]{:S(2)}, u32[]{:S(2)}) collective-permute-start(bf16[224,128]{1,0:T(8,128)(2,1)S(1)} %fusion.19), channel_id=1, source_target_pairs={{0,1},{1,0},{2,3},{3,2},{4,5},{5,4},{6,7},{7,6},{8,9},{9,8},{10,11... | collective-permute-start | bytes 172040 | tf_op jit(solution)/shard_map/ppermute | solution.py:19
  68.8 1.8 %head_gradient.3 = bf16[1792,1536]{1,0:T(8,128)(2,1)} custom-call(bf16[256,1792]{1,0:T(8,128)(2,1)S(1)} %pad_maximum_fusion.refs_0_, bf16[256,1536]{1,0:T(8,128)(2,1)S(1)} %pad_maximum_fusion.1.refs_1_, bf16[1792,1536]{1,0:T(8,128)(2,1)} %head_gradient.2.refs_2_), custom_call_target="tpu_custom_call", output_to_operand_aliasing={{}: (2, {})} | custom-call | flops 603979776 | bytes 4063232 | tf_op jit(solution)/shard_map/head_gradient/pallas_call | solution.py:236
  70.6 0.8 %collective-permute-done.15 = bf16[224,128]{1,0:T(8,128)(2,1)S(1)} collective-permute-done((bf16[224,128]{1,0:T(8,128)(2,1)S(1)}, bf16[224,128]{1,0:T(8,128)(2,1)S(1)}, u32[]{:S(2)}, u32[]{:S(2)}) %collective-permute-start.15) | collective-permute-done | bytes 57376 | tf_op jit(solution)/shard_map/ppermute | solution.py:19
  71.5 2.6 %collective-permute-start.16 = (bf16[224,128]{1,0:T(8,128)(2,1)S(1)}, bf16[224,128]{1,0:T(8,128)(2,1)S(1)}, u32[]{:S(2)}, u32[]{:S(2)}) collective-permute-start(bf16[224,128]{1,0:T(8,128)(2,1)S(1)} %fusion.15), channel_id=1, source_target_pairs={{0,16},{2,18},{4,20},{6,22},{8,24},{10,26},{12,28},{14,30},{16,0},... | collective-permute-start | bytes 172040 | tf_op jit(solution)/shard_map/ppermute | solution.py:369
  74.0 3.0 %collective-permute-done.16 = bf16[224,128]{1,0:T(8,128)(2,1)S(1)} collective-permute-done((bf16[224,128]{1,0:T(8,128)(2,1)S(1)}, bf16[224,128]{1,0:T(8,128)(2,1)S(1)}, u32[]{:S(2)}, u32[]{:S(2)}) %collective-permute-start.16) | collective-permute-done | bytes 57376 | tf_op jit(solution)/shard_map/ppermute | solution.py:369
  77.0 0.7 fusion.14
  (11 shorter events, 0.1 us)
Async XLA Ops:
  1.6 8.6 %collective-permute-start = (bf16[64,1792]{1,0:T(8,128)(2,1)S(1)}, bf16[64,1792]{1,0:T(8,128)(2,1)S(1)}, u32[]{:S(2)}, u32[]{:S(2)}) collective-permute-start(bf16[64,1792]{1,0:T(8,128)(2,1)S(1)} %dynamic_slice.7), channel_id=1, source_target_pairs={{0,1},{1,0},{2,3},{3,2},{4,5},{5,4},{6,7},{7,6},{8,9},{9,8},{10,11... | collective-permute-start | bytes 688136 | tf_op jit(solution)/shard_map/ppermute | solution.py:19
  9.0 5.0 %copy-start.1 = (s32[1,16]{1,0:T(1,128)S(1)}, s32[1,16]{1,0:T(1,128)}, u32[]{:S(2)}) copy-start(s32[1,16]{1,0:T(1,128)} %param.8) | copy-start | bytes 196
  9.0 5.1 %copy-start = (bf16[128,1536]{1,0:T(8,128)(2,1)S(1)}, bf16[128,1536]{1,0:T(8,128)(2,1)}, u32[]{:S(2)}) copy-start(bf16[128,1536]{1,0:T(8,128)(2,1)} %param.7) | copy-start | bytes 1179652
  10.2 4.2 %collective-permute-start.2 = (bf16[64,1792]{1,0:T(8,128)(2,1)S(1)}, bf16[64,1792]{1,0:T(8,128)(2,1)S(1)}, u32[]{:S(2)}, u32[]{:S(2)}) collective-permute-start(bf16[64,1792]{1,0:T(8,128)(2,1)S(1)} %collective-permute-done), channel_id=1, source_target_pairs={{0,2},{2,0},{4,6},{6,4},{8,10},{10,8},{12,14},{14,12},{16,18},{18,... | collective-permute-start | bytes 688136 | tf_op jit(solution)/shard_map/ppermute | solution.py:23
  11.3 12.0 %collective-permute-start.1 = (f32[64,1536]{1,0:T(8,128)S(1)}, f32[64,1536]{1,0:T(8,128)S(1)}, u32[]{:S(2)}, u32[]{:S(2)}) collective-permute-start(f32[64,1536]{1,0:T(8,128)S(1)} %fusion.26), channel_id=1, source_target_pairs={{0,1},{1,0},{2,3},{3,2},{4,5},{5,4},{6,7},{7,6},{8,9},{9,8},{10,11... | collective-permute-start | bytes 1179656 | tf_op jit(solution)/shard_map/ppermute | solution.py:19
  15.5 15.8 %collective-permute-start.3 = (f32[64,1536]{1,0:T(8,128)S(1)}, f32[64,1536]{1,0:T(8,128)S(1)}, u32[]{:S(2)}, u32[]{:S(2)}) collective-permute-start(f32[64,1536]{1,0:T(8,128)S(1)} %fusion.27), channel_id=1, source_target_pairs={{0,1},{1,0},{2,3},{3,2},{4,5},{5,4},{6,7},{7,6},{8,9},{9,8},{10,11... | collective-permute-start | bytes 1179656 | tf_op jit(solution)/shard_map/ppermute | solution.py:19
  31.8 1.2 %collective-permute-start.4 = (f32[1,4,128]{2,1,0:T(4,128)S(1)}, f32[1,4,128]{2,1,0:T(4,128)S(1)}, u32[]{:S(2)}, u32[]{:S(2)}) collective-permute-start(f32[1,4,128]{2,1,0:T(4,128)S(1)} %bitcast.86), channel_id=1, source_target_pairs={{0,2},{2,0},{4,6},{6,4},{8,10},{10,8},{12,14},{14,12},{16,18},{18,... | collective-permute-start | bytes 6152 | tf_op jit(solution)/shard_map/ppermute | solution.py:23
  33.0 3.7 %collective-permute-start.7 = (f32[2,4,128]{2,1,0:T(4,128)S(1)}, f32[2,4,128]{2,1,0:T(4,128)S(1)}, u32[]{:S(2)}, u32[]{:S(2)}) collective-permute-start(f32[2,4,128]{2,1,0:T(4,128)S(1)} %pad_maximum_fusion.5), channel_id=1, source_target_pairs={{0,4},{2,6},{4,0},{6,2},{8,12},{10,14},{12,8},{14,10},{16,20},{18,... | collective-permute-start | bytes 12296 | tf_op jit(solution)/shard_map/ppermute | solution.py:23
  34.7 3.6 %collective-permute-start.6 = (f32[2,4,128]{2,1,0:T(4,128)S(1)}, f32[2,4,128]{2,1,0:T(4,128)S(1)}, u32[]{:S(2)}, u32[]{:S(2)}) collective-permute-start(f32[2,4,128]{2,1,0:T(4,128)S(1)} %pad_maximum_fusion.5), channel_id=1, source_target_pairs={{0,8},{2,10},{4,12},{6,14},{8,0},{10,2},{12,4},{14,6},{16,24},{18,... | collective-permute-start | bytes 12296 | tf_op jit(solution)/shard_map/ppermute | solution.py:23
  36.3 4.5 %collective-permute-start.5 = (f32[2,4,128]{2,1,0:T(4,128)S(1)}, f32[2,4,128]{2,1,0:T(4,128)S(1)}, u32[]{:S(2)}, u32[]{:S(2)}) collective-permute-start(f32[2,4,128]{2,1,0:T(4,128)S(1)} %pad_maximum_fusion.5), channel_id=1, source_target_pairs={{0,12},{2,14},{4,8},{6,10},{8,4},{10,6},{12,0},{14,2},{16,28},{18,... | collective-permute-start | bytes 12296 | tf_op jit(solution)/shard_map/ppermute | solution.py:23
  40.8 4.8 %collective-permute-start.8 = (f32[8,4,128]{2,1,0:T(4,128)S(1)}, f32[8,4,128]{2,1,0:T(4,128)S(1)}, u32[]{:S(2)}, u32[]{:S(2)}) collective-permute-start(f32[8,4,128]{2,1,0:T(4,128)S(1)} %pad_maximum_fusion.4), channel_id=1, source_target_pairs={{0,16},{2,18},{4,20},{6,22},{8,24},{10,26},{12,28},{14,30},{16,0},... | collective-permute-start | bytes 49160 | tf_op jit(solution)/shard_map/ppermute | solution.py:23
  46.5 8.3 %collective-permute-start.10 = (bf16[128,1536]{1,0:T(8,128)(2,1)S(1)}, bf16[128,1536]{1,0:T(8,128)(2,1)S(1)}, u32[]{:S(2)}, u32[]{:S(2)}) collective-permute-start(bf16[128,1536]{1,0:T(8,128)(2,1)S(1)} %get-tuple-element.71.delta_ref), channel_id=1, source_target_pairs={{0,1},{1,0},{2,3},{3,2},{4,5},{5,4},{6,7},{7,6},{8,9},{9,8},{10,11... | collective-permute-start | bytes 1179656 | tf_op jit(solution)/shard_map/ppermute | solution.py:19
  49.6 6.8 %collective-permute-start.9 = (bf16[4,224,128]{2,1,0:T(8,128)(2,1)S(1)}, bf16[4,224,128]{2,1,0:T(8,128)(2,1)S(1)}, u32[]{:S(2)}, u32[]{:S(2)}) collective-permute-start(bf16[4,224,128]{2,1,0:T(8,128)(2,1)S(1)} %get-tuple-element.73), channel_id=1, source_target_pairs={{0,2},{2,0},{4,6},{6,4},{8,10},{10,8},{12,14},{14,12},{16,18},{18,... | collective-permute-start | bytes 688136 | tf_op jit(solution)/shard_map/ppermute | solution.py:23
  56.4 1.6 %collective-permute-start.11 = (bf16[4,224,128]{2,1,0:T(8,128)(2,1)S(1)}, bf16[4,224,128]{2,1,0:T(8,128)(2,1)S(1)}, u32[]{:S(2)}, u32[]{:S(2)}) collective-permute-start(bf16[4,224,128]{2,1,0:T(8,128)(2,1)S(1)} %get-tuple-element.78), channel_id=1, source_target_pairs={{0,2},{2,0},{4,6},{6,4},{8,10},{10,8},{12,14},{14,12},{16,18},{18,... | collective-permute-start | bytes 688136 | tf_op jit(solution)/shard_map/ppermute | solution.py:23
  58.2 5.6 %collective-permute-start.12 = (bf16[2,224,128]{2,1,0:T(8,128)(2,1)S(1)}, bf16[2,224,128]{2,1,0:T(8,128)(2,1)S(1)}, u32[]{:S(2)}, u32[]{:S(2)}) collective-permute-start(bf16[2,224,128]{2,1,0:T(8,128)(2,1)S(1)} %get-tuple-element.79), channel_id=1, source_target_pairs={{0,4},{2,6},{4,0},{6,2},{8,12},{10,14},{12,8},{14,10},{16,20},{18,... | collective-permute-start | bytes 344072 | tf_op jit(solution)/shard_map/ppermute | solution.py:23
  58.7 6.0 %collective-permute-start.13 = (bf16[2,224,128]{2,1,0:T(8,128)(2,1)S(1)}, bf16[2,224,128]{2,1,0:T(8,128)(2,1)S(1)}, u32[]{:S(2)}, u32[]{:S(2)}) collective-permute-start(bf16[2,224,128]{2,1,0:T(8,128)(2,1)S(1)} %get-tuple-element.80), channel_id=1, source_target_pairs={{0,8},{2,10},{4,12},{6,14},{8,0},{10,2},{12,4},{14,6},{16,24},{18,... | collective-permute-start | bytes 344072 | tf_op jit(solution)/shard_map/ppermute | solution.py:23
  59.1 8.0 %collective-permute-start.14 = (bf16[2,224,128]{2,1,0:T(8,128)(2,1)S(1)}, bf16[2,224,128]{2,1,0:T(8,128)(2,1)S(1)}, u32[]{:S(2)}, u32[]{:S(2)}) collective-permute-start(bf16[2,224,128]{2,1,0:T(8,128)(2,1)S(1)} %get-tuple-element.81), channel_id=1, source_target_pairs={{0,12},{2,14},{4,8},{6,10},{8,4},{10,6},{12,0},{14,2},{16,28},{18,... | collective-permute-start | bytes 344072 | tf_op jit(solution)/shard_map/ppermute | solution.py:23
  67.2 4.2 %collective-permute-start.15 = (bf16[224,128]{1,0:T(8,128)(2,1)S(1)}, bf16[224,128]{1,0:T(8,128)(2,1)S(1)}, u32[]{:S(2)}, u32[]{:S(2)}) collective-permute-start(bf16[224,128]{1,0:T(8,128)(2,1)S(1)} %fusion.19), channel_id=1, source_target_pairs={{0,1},{1,0},{2,3},{3,2},{4,5},{5,4},{6,7},{7,6},{8,9},{9,8},{10,11... | collective-permute-start | bytes 172040 | tf_op jit(solution)/shard_map/ppermute | solution.py:19
  71.5 5.6 %collective-permute-start.16 = (bf16[224,128]{1,0:T(8,128)(2,1)S(1)}, bf16[224,128]{1,0:T(8,128)(2,1)S(1)}, u32[]{:S(2)}, u32[]{:S(2)}) collective-permute-start(bf16[224,128]{1,0:T(8,128)(2,1)S(1)} %fusion.15), channel_id=1, source_target_pairs={{0,16},{2,18},{4,20},{6,22},{8,24},{10,26},{12,28},{14,30},{16,0},... | collective-permute-start | bytes 172040 | tf_op jit(solution)/shard_map/ppermute | solution.py:369

commit v10 on v9

--- a/solution.py
+++ b/solution.py
@@ -186,15 +186,33 @@
         write_pieces(k, head_rows, delta_ref, upper, send_ref, keep_ref)
 
 
+def own_gradient_kernel(head_ref, delta_ref, out_ref):
+    pairs, _, rows, _ = out_ref.shape
+    for k in range(pairs):
+        block = lax.dot_general(
+            head_ref[2 * k * rows : 2 * (k + 1) * rows, :],
+            delta_ref[...],
+            (((1,), (1,)), ((), ())),
+            preferred_element_type=jnp.float32,
+        )
+        out_ref[k, 0] = block[:rows]
+        out_ref[k, 1] = block[rows:]
+
+
 def gradient(core, head, delta, run):
     rows = head.shape[0] // run
     shape = (run // 2, rows, delta.shape[0])
     in_vmem = pl.BlockSpec(memory_space=pltpu.VMEM)
+    if core is None:
+        outs = pltpu.VMEM((run // 2, 2, *shape[1:]), jnp.float32)
+    else:
+        outs = (pltpu.VMEM(shape, jnp.bfloat16), pltpu.VMEM(shape, jnp.float32))
+    arrays = [pltpu.with_memory_space_constraint(x, pltpu.VMEM) for x in (head, delta)]
     return pl.pallas_call(
-        gradient_kernel,
-        out_shape=(pltpu.VMEM(shape, jnp.bfloat16), pltpu.VMEM(shape, jnp.float32)),
-        in_specs=[pl.BlockSpec(memory_space=pltpu.SMEM), in_vmem, in_vmem],
-        out_specs=(in_vmem, in_vmem),
+        own_gradient_kernel if core is None else gradient_kernel,
+        out_shape=outs,
+        in_specs=([] if core is None else [pl.BlockSpec(memory_space=pltpu.SMEM)]) + [in_vmem] * 2,
+        out_specs=in_vmem if core is None else (in_vmem, in_vmem),
         compiler_params=pltpu.CompilerParams(vmem_limit_bytes=VMEM_LIMIT),
         cost_estimate=pl.CostEstimate(
             flops=2 * head.size * delta.shape[0],
@@ -202,11 +220,7 @@
             transcendentals=0,
         ),
         name="partial_gradient",
-    )(
-        core,
-        pltpu.with_memory_space_constraint(head, pltpu.VMEM),
-        pltpu.with_memory_space_constraint(delta, pltpu.VMEM),
-    )
+    )(*([] if core is None else [core]), *arrays)
 
 
 def head_gradient_kernel(steps, start, width, *refs):
@@ -322,23 +336,28 @@
     delta, lse, kl = finish(gather_vocab(stats, upper, places, vocab_size), logits, kept)
 
     deltas = [delta] + [shift_tok(delta, d, tok_size) for d in range(1, tok_size)]
-    send, keep = gradient(core_word, head_here, delta, run)
-    other = swap_vocab(send, 1, vocab_size)
-    state = [(keep, other)]
+    flags = [upper[i] for i in places]
+
+    def direct(pieces):
+        count = len(pieces)
+        return [select([pieces[j ^ i] for j in range(count)], flags) for i in range(count)]
+
+    own_pieces = direct(list(gradient(None, head_here, delta, run)))
+    own_others = [
+        swap_vocab(x.astype(jnp.bfloat16), 2 * i, vocab_size)
+        for i, x in enumerate(own_pieces[1:], 1)
+    ]
+    state = []
     for x in deltas[1:]:
         send, keep = gradient(core_word, head_here, x, run)
-        state[0], send = lax.optimization_barrier((state[0], send))
+        own_others, send = lax.optimization_barrier((own_others, send))
         state.append((keep, swap_vocab(send, 1, vocab_size)))
     all_delta = jnp.concatenate(deltas, axis=0)
 
     width = 256 if rows % 256 == 0 else rows
     chunks = rows // width
     held = jnp.stack([keep + other.astype(jnp.float32) for keep, other in state], axis=1)
-    pieces = held.shape[0]
-    flags = [upper[i] for i in places]
-    taken = [
-        select([held[j ^ offset] for j in range(pieces)], flags) for offset in range(pieces)
-    ]
+    taken = direct(list(held))
     sends = [x.astype(jnp.bfloat16) for x in taken[1:]]
     sends, all_delta = lax.optimization_barrier((sends, all_delta))
     others = [swap_vocab(x, 2 * (i + 1), vocab_size) for i, x in enumerate(sends)]
@@ -348,7 +367,13 @@
     sums = taken[0]
     for other in others:
         sums = sums + other.astype(jnp.float32)
-    sends = [x.astype(jnp.bfloat16) for x in (sums[d] for d in range(1, tok_size))]
+    own_sum = own_pieces[0]
+    for other in own_others:
+        own_sum = own_sum + other.astype(jnp.float32)
+    send = jnp.where(upper[0], own_sum[0], own_sum[1]).astype(jnp.bfloat16)
+    own_sum = jnp.where(upper[0], own_sum[1], own_sum[0])
+    own_sum = own_sum + swap_vocab(send, 1, vocab_size).astype(jnp.float32)
+    sends = [x.astype(jnp.bfloat16) for x in sums]
     sends, all_delta = lax.optimization_barrier((sends, all_delta))
     others = [shift_tok(x, -d, tok_size) for d, x in enumerate(sends, 1)]
     if done < chunks:
@@ -356,7 +381,7 @@
             all_features, all_delta, grad_head, done * width, chunks - done, width
         )
         others, grad_head = lax.optimization_barrier((others, grad_head))
-    sums = [sums[0]] + [x.astype(jnp.float32) for x in others]
+    sums = [own_sum] + [x.astype(jnp.float32) for x in others]
     blocks = []
     for k in range(tok_size):
         block = sums[k]

time: 77.9 us -> 75.5 us (0.969)
  waiting for transfers between devices: 37.7 us -> 32.3 us
  starting transfers between devices: 20.8 us -> 23.8 us
    ppermute x11 -> x14, starting transfers between devices: 9.94 us -> 13.4 us  [swap_vocab(): return lax.ppermute(x, 'vocab', [(i, i ^ bit) for i in range(size)])]
    ppermute x5, waiting for transfers between devices: 22.5 us -> 19.5 us  [shift_tok(): lax.ppermute(x, 'tok', [(i, (i + offset) % size) for i in range(size)])]
    ppermute x11 -> x14, waiting for transfers between devices: 12.2 us -> 10.4 us  [swap_vocab(): return lax.ppermute(x, 'vocab', [(i, i ^ bit) for i in range(size)])]
  transfers between devices with their start and end apart: 17 -> 20, of which waited for: 14 -> 15; matrix products, arithmetic and copies ran while one was open for 6% -> 6% of each run, Pallas kernels for 12% -> 13%
where the time goes in v10:
time: 75.5 us; the launch traced here: 75.3 us
  waiting for transfers between devices  32.3 us (43%)
  starting transfers between devices  23.8 us (32%)
  Pallas kernels  11 us (15%)
  matrix products  3.01 us (4%)
  local copies, waits for them, and re-layouts  2.03 us (3%)
  other arithmetic  1.67 us (2%)
  between operations  1.52 us (2%)
    ppermute x5, waiting for transfers between devices, shift_tok(): lax.ppermute(x, 'tok', [(i, (i + offset) % size) for i in range(size)])  19.5 us
    ppermute x14, starting transfers between devices, swap_vocab(): return lax.ppermute(x, 'vocab', [(i, i ^ bit) for i in range(size)])  13.4 us
    ppermute x14, waiting for transfers between devices, swap_vocab(): return lax.ppermute(x, 'vocab', [(i, i ^ bit) for i in range(size)])  10.4 us
    ppermute x5, starting transfers between devices, shift_tok(): lax.ppermute(x, 'tok', [(i, (i + offset) % size) for i in range(size)])  7.67 us
    pallas_call x2, Pallas kernels, head_gradient(): pl.pallas_call(functools.partial(head_gradient_kernel, steps, start, widt...  3.9 us
    pallas_call x2, Pallas kernels, gradient(): pl.pallas_call(own_gradient_kernel if core is None else gradient_kernel,...  3.15 us
    ppermute x1, starting transfers between devices, per_device(): lax.ppermute(blocks[k].astype(jnp.bfloat16), 'vocab', pairs)  2.66 us
    pallas_call x1, Pallas kernels, load(): pl.pallas_call(load_kernel, out_shape=pltpu.VMEM(head.shape, head.dtype),...  2.62 us
  transfers between devices with their start and end apart: 20, of which 15 were waited for; matrix products, arithmetic and copies ran while one was open for 6% of the time, Pallas kernels for 13%

profile of v10, /device:TPU:0, one launch (start us, length us, event | category | flops | bytes accessed | tf_op | source)
XLA Modules:
  0.0 75.3 jit_solution(9444737970721598979)
XLA Ops:
  0.6 1.0 %dynamic_slice.7 = bf16[64,1792]{1,0:T(8,128)(2,1)S(1)} dynamic-slice(bf16[128,3584]{1,0:T(8,128)(2,1)} %param.5, s32[]{:T(128)S(6)} %select_n.237, s32[]{:T(128)S(6)} %select_n.238), dynamic_slice_sizes={64,1792} | dynamic-slice | bytes 458756 | tf_op jit(solution)/shard_map/dynamic_slice | solution.py:282
  1.6 3.0 %collective-permute-start = (bf16[64,1792]{1,0:T(8,128)(2,1)S(1)}, bf16[64,1792]{1,0:T(8,128)(2,1)S(1)}, u32[]{:S(2)}, u32[]{:S(2)}) collective-permute-start(bf16[64,1792]{1,0:T(8,128)(2,1)S(1)} %dynamic_slice.7), channel_id=1, source_target_pairs={{0,1},{1,0},{2,3},{3,2},{4,5},{5,4},{6,7},{7,6},{8,9},{9,8},{10,11... | collective-permute-start | bytes 688136 | tf_op jit(solution)/shard_map/ppermute | solution.py:19
  5.3 1.1 %constant_dynamic-slice_fusion = bf16[128,1792]{1,0:T(8,128)(2,1)S(1)} fusion(bf16[128,3584]{1,0:T(8,128)(2,1)} %param.5, s32[]{:T(128)S(6)} %select_n.231), kind=kLoop, calls=%fused_computation.68 | loop fusion | bytes 917508 | tf_op jit(solution)/shard_map/dynamic_slice | solution.py:282
  6.4 2.6 %load_head.1.head_ref = bf16[1792,1536]{1,0:T(8,128)(2,1)S(1)} custom-call(bf16[1792,1536]{1,0:T(8,128)(2,1)} %head_ref), custom_call_target="tpu_custom_call" | custom-call | bytes 11010048 | tf_op jit(solution)/shard_map/load_head/pallas_call | solution.py:67
  9.0 0.0 copy-start.1
  9.0 0.0 copy-start
  9.0 1.2 %collective-permute-done = bf16[64,1792]{1,0:T(8,128)(2,1)S(1)} collective-permute-done((bf16[64,1792]{1,0:T(8,128)(2,1)S(1)}, bf16[64,1792]{1,0:T(8,128)(2,1)S(1)}, u32[]{:S(2)}, u32[]{:S(2)}) %collective-permute-start) | collective-permute-done | bytes 229408 | tf_op jit(solution)/shard_map/ppermute | solution.py:19
  10.2 0.0 collective-permute-start.2
  10.3 1.1 %fusion.17 = f32[64,1536]{1,0:T(8,128)S(1)} fusion(bf16[64,1792]{1,0:T(8,128)(2,1)S(1)} %collective-permute-done, bf16[1792,1536]{1,0:T(8,128)(2,1)S(1)} %load_head.1.head_ref), kind=kOutput, calls=%fused_computation.69 | convolution fusion | flops 352321536 | bytes 6127616 | tf_op jit(solution)/shard_map/dot_general | solution.py:310
  11.3 1.8 %collective-permute-start.1 = (f32[64,1536]{1,0:T(8,128)S(1)}, f32[64,1536]{1,0:T(8,128)S(1)}, u32[]{:S(2)}, u32[]{:S(2)}) collective-permute-start(f32[64,1536]{1,0:T(8,128)S(1)} %fusion.17), channel_id=1, source_target_pairs={{0,1},{1,0},{2,3},{3,2},{4,5},{5,4},{6,7},{7,6},{8,9},{9,8},{10,11... | collective-permute-start | bytes 1179656 | tf_op jit(solution)/shard_map/ppermute | solution.py:19
  13.1 0.9 %fusion.19.own_ref = f32[128,1536]{1,0:T(8,128)S(1)} fusion(bf16[128,1792]{1,0:T(8,128)(2,1)S(1)} %constant_dynamic-slice_fusion, bf16[1792,1536]{1,0:T(8,128)(2,1)S(1)} %load_head.1.head_ref), kind=kOutput, calls=%fused_computation.71 | convolution fusion | flops 704643072 | bytes 6750208 | tf_op jit(solution)/shard_map/dot_general | solution.py:316
  14.0 0.0 copy-done.1
  14.0 0.1 and_reduce_fusion
  14.1 0.3 fusion
  14.5 0.0 collective-permute-done.2
  14.5 1.1 %fusion.18 = f32[64,1536]{1,0:T(8,128)S(1)} fusion(bf16[64,1792]{1,0:T(8,128)(2,1)S(1)} %collective-permute-done.2, bf16[1792,1536]{1,0:T(8,128)(2,1)S(1)} %load_head.1.head_ref), kind=kOutput, calls=%fused_computation.70 | convolution fusion | flops 352321536 | bytes 6127616 | tf_op jit(solution)/shard_map/dot_general | solution.py:313
  15.5 0.3 collective-permute-start.3
  15.9 0.1 broadcast_select_fusion.1
  15.9 0.1 pad_maximum_fusion.refs_0_
  16.0 7.3 %collective-permute-done.1.refs_0_ = f32[64,1536]{1,0:T(8,128)S(1)} collective-permute-done((f32[64,1536]{1,0:T(8,128)S(1)}, f32[64,1536]{1,0:T(8,128)S(1)}, u32[]{:S(2)}, u32[]{:S(2)}) %collective-permute-start.1) | collective-permute-done | bytes 393248 | tf_op jit(solution)/shard_map/ppermute | solution.py:19
  23.3 8.0 %collective-permute-done.3.refs_1_ = f32[64,1536]{1,0:T(8,128)S(1)} collective-permute-done((f32[64,1536]{1,0:T(8,128)S(1)}, f32[64,1536]{1,0:T(8,128)S(1)}, u32[]{:S(2)}, u32[]{:S(2)}) %collective-permute-start.3) | collective-permute-done | bytes 393248 | tf_op jit(solution)/shard_map/ppermute | solution.py:19
  31.3 0.4 local_stats.1
  31.8 0.0 collective-permute-start.4
  31.8 1.1 %collective-permute-done.4 = f32[1,4,128]{2,1,0:T(4,128)S(1)} collective-permute-done((f32[1,4,128]{2,1,0:T(4,128)S(1)}, f32[1,4,128]{2,1,0:T(4,128)S(1)}, u32[]{:S(2)}, u32[]{:S(2)}) %collective-permute-start.4) | collective-permute-done | bytes 2080 | tf_op jit(solution)/shard_map/ppermute | solution.py:23
  33.0 1.8 %collective-permute-start.7 = (f32[2,4,128]{2,1,0:T(4,128)S(1)}, f32[2,4,128]{2,1,0:T(4,128)S(1)}, u32[]{:S(2)}, u32[]{:S(2)}) collective-permute-start(f32[2,4,128]{2,1,0:T(4,128)S(1)} %pad_maximum_fusion.4), channel_id=1, source_target_pairs={{0,4},{2,6},{4,0},{6,2},{8,12},{10,14},{12,8},{14,10},{16,20},{18,... | collective-permute-start | bytes 12296 | tf_op jit(solution)/shard_map/ppermute | solution.py:23
  34.7 1.6 %collective-permute-start.6 = (f32[2,4,128]{2,1,0:T(4,128)S(1)}, f32[2,4,128]{2,1,0:T(4,128)S(1)}, u32[]{:S(2)}, u32[]{:S(2)}) collective-permute-start(f32[2,4,128]{2,1,0:T(4,128)S(1)} %pad_maximum_fusion.4), channel_id=1, source_target_pairs={{0,8},{2,10},{4,12},{6,14},{8,0},{10,2},{12,4},{14,6},{16,24},{18,... | collective-permute-start | bytes 12296 | tf_op jit(solution)/shard_map/ppermute | solution.py:23
  36.3 0.2 collective-permute-start.5
  36.5 0.1 collective-permute-done.7
  36.6 1.7 %collective-permute-done.6 = f32[2,4,128]{2,1,0:T(4,128)S(1)} collective-permute-done((f32[2,4,128]{2,1,0:T(4,128)S(1)}, f32[2,4,128]{2,1,0:T(4,128)S(1)}, u32[]{:S(2)}, u32[]{:S(2)}) %collective-permute-start.6) | collective-permute-done | bytes 4128 | tf_op jit(solution)/shard_map/ppermute | solution.py:23
  38.3 2.5 %collective-permute-done.5 = f32[2,4,128]{2,1,0:T(4,128)S(1)} collective-permute-done((f32[2,4,128]{2,1,0:T(4,128)S(1)}, f32[2,4,128]{2,1,0:T(4,128)S(1)}, u32[]{:S(2)}, u32[]{:S(2)}) %collective-permute-start.5) | collective-permute-done | bytes 4128 | tf_op jit(solution)/shard_map/ppermute | solution.py:23
  40.8 2.7 %collective-permute-start.8 = (f32[8,4,128]{2,1,0:T(4,128)S(1)}, f32[8,4,128]{2,1,0:T(4,128)S(1)}, u32[]{:S(2)}, u32[]{:S(2)}) collective-permute-start(f32[8,4,128]{2,1,0:T(4,128)S(1)} %pad_maximum_fusion.3), channel_id=1, source_target_pairs={{0,16},{2,18},{4,20},{6,22},{8,24},{10,26},{12,28},{14,30},{16,0},... | collective-permute-start | bytes 49160 | tf_op jit(solution)/shard_map/ppermute | solution.py:23
  43.5 2.1 %collective-permute-done.8 = f32[8,4,128]{2,1,0:T(4,128)S(1)} collective-permute-done((f32[8,4,128]{2,1,0:T(4,128)S(1)}, f32[8,4,128]{2,1,0:T(4,128)S(1)}, u32[]{:S(2)}, u32[]{:S(2)}) %collective-permute-start.8) | collective-permute-done | bytes 16416 | tf_op jit(solution)/shard_map/ppermute | solution.py:23
  45.6 0.9 %delta.1 = (bf16[128,1536]{1,0:T(8,128)(2,1)S(1)}, f32[1,128]{1,0:T(1,128)}, f32[1,128]{1,0:T(1,128)}) custom-call(f32[16,4,128]{2,1,0:T(4,128)S(1)} %pad_maximum_fusion.2.gathered_ref, f32[128,1536]{1,0:T(8,128)S(1)} %get-tuple-element.66.logits_ref, bf16[128,1536]{1,0:T(8,128)(2,1)S(1)} %get-tuple-element.61.kept_ref), custom_call_target="tpu_custom_call" | custom-call | flops 1572864 | bytes 1572864 | tf_op jit(solution)/shard_map/delta/pallas_call | solution.py:153
  46.5 1.5 %collective-permute-start.9 = (bf16[128,1536]{1,0:T(8,128)(2,1)S(1)}, bf16[128,1536]{1,0:T(8,128)(2,1)S(1)}, u32[]{:S(2)}, u32[]{:S(2)}) collective-permute-start(bf16[128,1536]{1,0:T(8,128)(2,1)S(1)} %get-tuple-element.70.delta_ref), channel_id=1, source_target_pairs={{0,1},{1,0},{2,3},{3,2},{4,5},{5,4},{6,7},{7,6},{8,9},{9,8},{10,11... | collective-permute-start | bytes 1179656 | tf_op jit(solution)/shard_map/ppermute | solution.py:19
  48.1 1.6 %partial_gradient.3 = f32[4,2,224,128]{3,2,1,0:T(8,128)S(1)} custom-call(bf16[1792,1536]{1,0:T(8,128)(2,1)S(1)} %load_head.1.head_ref, bf16[128,1536]{1,0:T(8,128)(2,1)S(1)} %get-tuple-element.70.delta_ref), custom_call_target="tpu_custom_call" | custom-call | flops 704643072 | bytes 5898240 | tf_op jit(solution)/shard_map/partial_gradient/pallas_call | solution.py:211
  49.6 0.1 fusion.11
  49.7 0.4 collective-permute-start.12
  50.1 1.6 %collective-permute-start.11 = (bf16[2,224,128]{2,1,0:T(8,128)(2,1)S(1)}, bf16[2,224,128]{2,1,0:T(8,128)(2,1)S(1)}, u32[]{:S(2)}, u32[]{:S(2)}) collective-permute-start(bf16[2,224,128]{2,1,0:T(8,128)(2,1)S(1)} %get-tuple-element.93), channel_id=1, source_target_pairs={{0,8},{2,10},{4,12},{6,14},{8,0},{10,2},{12,4},{14,6},{16,24},{18,... | collective-permute-start | bytes 344072 | tf_op jit(solution)/shard_map/ppermute | solution.py:23
  51.8 1.5 %collective-permute-start.10 = (bf16[2,224,128]{2,1,0:T(8,128)(2,1)S(1)}, bf16[2,224,128]{2,1,0:T(8,128)(2,1)S(1)}, u32[]{:S(2)}, u32[]{:S(2)}) collective-permute-start(bf16[2,224,128]{2,1,0:T(8,128)(2,1)S(1)} %get-tuple-element.94), channel_id=1, source_target_pairs={{0,4},{2,6},{4,0},{6,2},{8,12},{10,14},{12,8},{14,10},{16,20},{18,... | collective-permute-start | bytes 344072 | tf_op jit(solution)/shard_map/ppermute | solution.py:23
  53.2 1.6 %collective-permute-done.9.delta_ref = bf16[128,1536]{1,0:T(8,128)(2,1)S(1)} collective-permute-done((bf16[128,1536]{1,0:T(8,128)(2,1)S(1)}, bf16[128,1536]{1,0:T(8,128)(2,1)S(1)}, u32[]{:S(2)}, u32[]{:S(2)}) %collective-permute-start.9) | collective-permute-done | bytes 393248 | tf_op jit(solution)/shard_map/ppermute | solution.py:19
  54.8 1.6 %partial_gradient.2 = (bf16[4,224,128]{2,1,0:T(8,128)(2,1)S(1)}, f32[4,224,128]{2,1,0:T(8,128)S(1)}) custom-call(s32[1]{0:T(128)} %bitcast.1.core_ref, bf16[1792,1536]{1,0:T(8,128)(2,1)S(1)} %load_head.1.head_ref, bf16[128,1536]{1,0:T(8,128)(2,1)S(1)} %collective-permute-done.9.delta_ref), custom_call_target="tpu_custom_call" | custom-call | flops 704643072 | bytes 5898240 | tf_op jit(solution)/shard_map/partial_gradient/pallas_call | solution.py:211
  56.4 0.0 collective-permute-done.12
  56.4 0.0 collective-permute-done.11
  56.4 0.2 collective-permute-done.10
  56.7 0.0 collective-permute-start.13
  56.7 0.1 pad_maximum_fusion.1.refs_1_
  56.7 0.1 fusion.5
  56.8 1.3 %collective-permute-done.13 = bf16[4,224,128]{2,1,0:T(8,128)(2,1)S(1)} collective-permute-done((bf16[4,224,128]{2,1,0:T(8,128)(2,1)S(1)}, bf16[4,224,128]{2,1,0:T(8,128)(2,1)S(1)}, u32[]{:S(2)}, u32[]{:S(2)}) %collective-permute-start.13) | collective-permute-done | bytes 229408 | tf_op jit(solution)/shard_map/ppermute | solution.py:23
  58.3 1.4 %collective-permute-start.14 = (bf16[1,224,128]{2,1,0:T(8,128)(2,1)S(1)}, bf16[1,224,128]{2,1,0:T(8,128)(2,1)S(1)}, u32[]{:S(2)}, u32[]{:S(2)}) collective-permute-start(bf16[1,224,128]{2,1,0:T(8,128)(2,1)S(1)} %get-tuple-element.74), channel_id=1, source_target_pairs={{0,4},{2,6},{4,0},{6,2},{8,12},{10,14},{12,8},{14,10},{16,20},{18,... | collective-permute-start | bytes 172040 | tf_op jit(solution)/shard_map/ppermute | solution.py:23
  59.7 0.4 collective-permute-start.15
  60.1 1.7 %collective-permute-start.16 = (bf16[1,224,128]{2,1,0:T(8,128)(2,1)S(1)}, bf16[1,224,128]{2,1,0:T(8,128)(2,1)S(1)}, u32[]{:S(2)}, u32[]{:S(2)}) collective-permute-start(bf16[1,224,128]{2,1,0:T(8,128)(2,1)S(1)} %get-tuple-element.76), channel_id=1, source_target_pairs={{0,12},{2,14},{4,8},{6,10},{8,4},{10,6},{12,0},{14,2},{16,28},{18,... | collective-permute-start | bytes 172040 | tf_op jit(solution)/shard_map/ppermute | solution.py:23
  61.8 2.1 %head_gradient.2.refs_2_ = bf16[1792,1536]{1,0:T(8,128)(2,1)} custom-call(bf16[256,1792]{1,0:T(8,128)(2,1)S(1)} %pad_maximum_fusion.refs_0_, bf16[256,1536]{1,0:T(8,128)(2,1)S(1)} %pad_maximum_fusion.1.refs_1_), custom_call_target="tpu_custom_call" | custom-call | flops 805306368 | bytes 4849664 | tf_op jit(solution)/shard_map/head_gradient/pallas_call | solution.py:250
  63.9 0.0 collective-permute-done.14
  63.9 0.1 collective-permute-done.15
  64.0 1.2 %collective-permute-done.16 = bf16[1,224,128]{2,1,0:T(8,128)(2,1)S(1)} collective-permute-done((bf16[1,224,128]{2,1,0:T(8,128)(2,1)S(1)}, bf16[1,224,128]{2,1,0:T(8,128)(2,1)S(1)}, u32[]{:S(2)}, u32[]{:S(2)}) %collective-permute-start.16) | collective-permute-done | bytes 57376 | tf_op jit(solution)/shard_map/ppermute | solution.py:23
  65.2 0.1 fusion.12
  65.2 1.0 %collective-permute-start.17 = (bf16[224,128]{1,0:T(8,128)(2,1)S(1)}, bf16[224,128]{1,0:T(8,128)(2,1)S(1)}, u32[]{:S(2)}, u32[]{:S(2)}) collective-permute-start(bf16[224,128]{1,0:T(8,128)(2,1)S(1)} %fusion.12), channel_id=1, source_target_pairs={{0,1},{1,0},{2,3},{3,2},{4,5},{5,4},{6,7},{7,6},{8,9},{9,8},{10,11... | collective-permute-start | bytes 172040 | tf_op jit(solution)/shard_map/ppermute | solution.py:19
  66.2 0.1 collective-permute-start.18
  66.3 1.8 %head_gradient.3 = bf16[1792,1536]{1,0:T(8,128)(2,1)} custom-call(bf16[256,1792]{1,0:T(8,128)(2,1)S(1)} %pad_maximum_fusion.refs_0_, bf16[256,1536]{1,0:T(8,128)(2,1)S(1)} %pad_maximum_fusion.1.refs_1_, bf16[1792,1536]{1,0:T(8,128)(2,1)} %head_gradient.2.refs_2_), custom_call_target="tpu_custom_call", output_to_operand_aliasing={{}: (2, {})} | custom-call | flops 603979776 | bytes 4063232 | tf_op jit(solution)/shard_map/head_gradient/pallas_call | solution.py:250
  68.1 1.4 %collective-permute-done.17 = bf16[224,128]{1,0:T(8,128)(2,1)S(1)} collective-permute-done((bf16[224,128]{1,0:T(8,128)(2,1)S(1)}, bf16[224,128]{1,0:T(8,128)(2,1)S(1)}, u32[]{:S(2)}, u32[]{:S(2)}) %collective-permute-start.17) | collective-permute-done | bytes 57376 | tf_op jit(solution)/shard_map/ppermute | solution.py:19
  69.5 0.0 collective-permute-done.18
  69.5 2.7 %collective-permute-start.19 = (bf16[224,128]{1,0:T(8,128)(2,1)S(1)}, bf16[224,128]{1,0:T(8,128)(2,1)S(1)}, u32[]{:S(2)}, u32[]{:S(2)}) collective-permute-start(bf16[224,128]{1,0:T(8,128)(2,1)S(1)} %fusion.8), channel_id=1, source_target_pairs={{0,16},{2,18},{4,20},{6,22},{8,24},{10,26},{12,28},{14,30},{16,0},... | collective-permute-start | bytes 172040 | tf_op jit(solution)/shard_map/ppermute | solution.py:394
  72.2 2.5 %collective-permute-done.19 = bf16[224,128]{1,0:T(8,128)(2,1)S(1)} collective-permute-done((bf16[224,128]{1,0:T(8,128)(2,1)S(1)}, bf16[224,128]{1,0:T(8,128)(2,1)S(1)}, u32[]{:S(2)}, u32[]{:S(2)}) %collective-permute-start.19) | collective-permute-done | bytes 57376 | tf_op jit(solution)/shard_map/ppermute | solution.py:394
  74.6 0.7 fusion.7
  (14 shorter events, 0.2 us)
Async XLA Ops:
  1.6 8.6 %collective-permute-start = (bf16[64,1792]{1,0:T(8,128)(2,1)S(1)}, bf16[64,1792]{1,0:T(8,128)(2,1)S(1)}, u32[]{:S(2)}, u32[]{:S(2)}) collective-permute-start(bf16[64,1792]{1,0:T(8,128)(2,1)S(1)} %dynamic_slice.7), channel_id=1, source_target_pairs={{0,1},{1,0},{2,3},{3,2},{4,5},{5,4},{6,7},{7,6},{8,9},{9,8},{10,11... | collective-permute-start | bytes 688136 | tf_op jit(solution)/shard_map/ppermute | solution.py:19
  9.0 5.0 %copy-start.1 = (s32[1,16]{1,0:T(1,128)S(1)}, s32[1,16]{1,0:T(1,128)}, u32[]{:S(2)}) copy-start(s32[1,16]{1,0:T(1,128)} %param.8) | copy-start | bytes 196
  9.0 5.1 %copy-start = (bf16[128,1536]{1,0:T(8,128)(2,1)S(1)}, bf16[128,1536]{1,0:T(8,128)(2,1)}, u32[]{:S(2)}) copy-start(bf16[128,1536]{1,0:T(8,128)(2,1)} %param.7) | copy-start | bytes 1179652
  10.2 4.2 %collective-permute-start.2 = (bf16[64,1792]{1,0:T(8,128)(2,1)S(1)}, bf16[64,1792]{1,0:T(8,128)(2,1)S(1)}, u32[]{:S(2)}, u32[]{:S(2)}) collective-permute-start(bf16[64,1792]{1,0:T(8,128)(2,1)S(1)} %collective-permute-done), channel_id=1, source_target_pairs={{0,2},{2,0},{4,6},{6,4},{8,10},{10,8},{12,14},{14,12},{16,18},{18,... | collective-permute-start | bytes 688136 | tf_op jit(solution)/shard_map/ppermute | solution.py:23
  11.3 12.0 %collective-permute-start.1 = (f32[64,1536]{1,0:T(8,128)S(1)}, f32[64,1536]{1,0:T(8,128)S(1)}, u32[]{:S(2)}, u32[]{:S(2)}) collective-permute-start(f32[64,1536]{1,0:T(8,128)S(1)} %fusion.17), channel_id=1, source_target_pairs={{0,1},{1,0},{2,3},{3,2},{4,5},{5,4},{6,7},{7,6},{8,9},{9,8},{10,11... | collective-permute-start | bytes 1179656 | tf_op jit(solution)/shard_map/ppermute | solution.py:19
  15.5 15.8 %collective-permute-start.3 = (f32[64,1536]{1,0:T(8,128)S(1)}, f32[64,1536]{1,0:T(8,128)S(1)}, u32[]{:S(2)}, u32[]{:S(2)}) collective-permute-start(f32[64,1536]{1,0:T(8,128)S(1)} %fusion.18), channel_id=1, source_target_pairs={{0,1},{1,0},{2,3},{3,2},{4,5},{5,4},{6,7},{7,6},{8,9},{9,8},{10,11... | collective-permute-start | bytes 1179656 | tf_op jit(solution)/shard_map/ppermute | solution.py:19
  31.8 1.2 %collective-permute-start.4 = (f32[1,4,128]{2,1,0:T(4,128)S(1)}, f32[1,4,128]{2,1,0:T(4,128)S(1)}, u32[]{:S(2)}, u32[]{:S(2)}) collective-permute-start(f32[1,4,128]{2,1,0:T(4,128)S(1)} %bitcast.42), channel_id=1, source_target_pairs={{0,2},{2,0},{4,6},{6,4},{8,10},{10,8},{12,14},{14,12},{16,18},{18,... | collective-permute-start | bytes 6152 | tf_op jit(solution)/shard_map/ppermute | solution.py:23
  33.0 3.7 %collective-permute-start.7 = (f32[2,4,128]{2,1,0:T(4,128)S(1)}, f32[2,4,128]{2,1,0:T(4,128)S(1)}, u32[]{:S(2)}, u32[]{:S(2)}) collective-permute-start(f32[2,4,128]{2,1,0:T(4,128)S(1)} %pad_maximum_fusion.4), channel_id=1, source_target_pairs={{0,4},{2,6},{4,0},{6,2},{8,12},{10,14},{12,8},{14,10},{16,20},{18,... | collective-permute-start | bytes 12296 | tf_op jit(solution)/shard_map/ppermute | solution.py:23
  34.7 3.6 %collective-permute-start.6 = (f32[2,4,128]{2,1,0:T(4,128)S(1)}, f32[2,4,128]{2,1,0:T(4,128)S(1)}, u32[]{:S(2)}, u32[]{:S(2)}) collective-permute-start(f32[2,4,128]{2,1,0:T(4,128)S(1)} %pad_maximum_fusion.4), channel_id=1, source_target_pairs={{0,8},{2,10},{4,12},{6,14},{8,0},{10,2},{12,4},{14,6},{16,24},{18,... | collective-permute-start | bytes 12296 | tf_op jit(solution)/shard_map/ppermute | solution.py:23
  36.3 4.5 %collective-permute-start.5 = (f32[2,4,128]{2,1,0:T(4,128)S(1)}, f32[2,4,128]{2,1,0:T(4,128)S(1)}, u32[]{:S(2)}, u32[]{:S(2)}) collective-permute-start(f32[2,4,128]{2,1,0:T(4,128)S(1)} %pad_maximum_fusion.4), channel_id=1, source_target_pairs={{0,12},{2,14},{4,8},{6,10},{8,4},{10,6},{12,0},{14,2},{16,28},{18,... | collective-permute-start | bytes 12296 | tf_op jit(solution)/shard_map/ppermute | solution.py:23
  40.8 4.8 %collective-permute-start.8 = (f32[8,4,128]{2,1,0:T(4,128)S(1)}, f32[8,4,128]{2,1,0:T(4,128)S(1)}, u32[]{:S(2)}, u32[]{:S(2)}) collective-permute-start(f32[8,4,128]{2,1,0:T(4,128)S(1)} %pad_maximum_fusion.3), channel_id=1, source_target_pairs={{0,16},{2,18},{4,20},{6,22},{8,24},{10,26},{12,28},{14,30},{16,0},... | collective-permute-start | bytes 49160 | tf_op jit(solution)/shard_map/ppermute | solution.py:23
  46.5 8.3 %collective-permute-start.9 = (bf16[128,1536]{1,0:T(8,128)(2,1)S(1)}, bf16[128,1536]{1,0:T(8,128)(2,1)S(1)}, u32[]{:S(2)}, u32[]{:S(2)}) collective-permute-start(bf16[128,1536]{1,0:T(8,128)(2,1)S(1)} %get-tuple-element.70.delta_ref), channel_id=1, source_target_pairs={{0,1},{1,0},{2,3},{3,2},{4,5},{5,4},{6,7},{7,6},{8,9},{9,8},{10,11... | collective-permute-start | bytes 1179656 | tf_op jit(solution)/shard_map/ppermute | solution.py:19
  49.7 6.7 %collective-permute-start.12 = (bf16[2,224,128]{2,1,0:T(8,128)(2,1)S(1)}, bf16[2,224,128]{2,1,0:T(8,128)(2,1)S(1)}, u32[]{:S(2)}, u32[]{:S(2)}) collective-permute-start(bf16[2,224,128]{2,1,0:T(8,128)(2,1)S(1)} %get-tuple-element.92), channel_id=1, source_target_pairs={{0,12},{2,14},{4,8},{6,10},{8,4},{10,6},{12,0},{14,2},{16,28},{18,... | collective-permute-start | bytes 344072 | tf_op jit(solution)/shard_map/ppermute | solution.py:23
  50.1 6.3 %collective-permute-start.11 = (bf16[2,224,128]{2,1,0:T(8,128)(2,1)S(1)}, bf16[2,224,128]{2,1,0:T(8,128)(2,1)S(1)}, u32[]{:S(2)}, u32[]{:S(2)}) collective-permute-start(bf16[2,224,128]{2,1,0:T(8,128)(2,1)S(1)} %get-tuple-element.93), channel_id=1, source_target_pairs={{0,8},{2,10},{4,12},{6,14},{8,0},{10,2},{12,4},{14,6},{16,24},{18,... | collective-permute-start | bytes 344072 | tf_op jit(solution)/shard_map/ppermute | solution.py:23
  51.8 4.9 %collective-permute-start.10 = (bf16[2,224,128]{2,1,0:T(8,128)(2,1)S(1)}, bf16[2,224,128]{2,1,0:T(8,128)(2,1)S(1)}, u32[]{:S(2)}, u32[]{:S(2)}) collective-permute-start(bf16[2,224,128]{2,1,0:T(8,128)(2,1)S(1)} %get-tuple-element.94), channel_id=1, source_target_pairs={{0,4},{2,6},{4,0},{6,2},{8,12},{10,14},{12,8},{14,10},{16,20},{18,... | collective-permute-start | bytes 344072 | tf_op jit(solution)/shard_map/ppermute | solution.py:23
  56.7 1.5 %collective-permute-start.13 = (bf16[4,224,128]{2,1,0:T(8,128)(2,1)S(1)}, bf16[4,224,128]{2,1,0:T(8,128)(2,1)S(1)}, u32[]{:S(2)}, u32[]{:S(2)}) collective-permute-start(bf16[4,224,128]{2,1,0:T(8,128)(2,1)S(1)} %get-tuple-element.73), channel_id=1, source_target_pairs={{0,2},{2,0},{4,6},{6,4},{8,10},{10,8},{12,14},{14,12},{16,18},{18,... | collective-permute-start | bytes 688136 | tf_op jit(solution)/shard_map/ppermute | solution.py:23
  58.3 5.6 %collective-permute-start.14 = (bf16[1,224,128]{2,1,0:T(8,128)(2,1)S(1)}, bf16[1,224,128]{2,1,0:T(8,128)(2,1)S(1)}, u32[]{:S(2)}, u32[]{:S(2)}) collective-permute-start(bf16[1,224,128]{2,1,0:T(8,128)(2,1)S(1)} %get-tuple-element.74), channel_id=1, source_target_pairs={{0,4},{2,6},{4,0},{6,2},{8,12},{10,14},{12,8},{14,10},{16,20},{18,... | collective-permute-start | bytes 172040 | tf_op jit(solution)/shard_map/ppermute | solution.py:23
  59.7 4.3 %collective-permute-start.15 = (bf16[1,224,128]{2,1,0:T(8,128)(2,1)S(1)}, bf16[1,224,128]{2,1,0:T(8,128)(2,1)S(1)}, u32[]{:S(2)}, u32[]{:S(2)}) collective-permute-start(bf16[1,224,128]{2,1,0:T(8,128)(2,1)S(1)} %get-tuple-element.75), channel_id=1, source_target_pairs={{0,8},{2,10},{4,12},{6,14},{8,0},{10,2},{12,4},{14,6},{16,24},{18,... | collective-permute-start | bytes 172040 | tf_op jit(solution)/shard_map/ppermute | solution.py:23
  60.1 5.1 %collective-permute-start.16 = (bf16[1,224,128]{2,1,0:T(8,128)(2,1)S(1)}, bf16[1,224,128]{2,1,0:T(8,128)(2,1)S(1)}, u32[]{:S(2)}, u32[]{:S(2)}) collective-permute-start(bf16[1,224,128]{2,1,0:T(8,128)(2,1)S(1)} %get-tuple-element.76), channel_id=1, source_target_pairs={{0,12},{2,14},{4,8},{6,10},{8,4},{10,6},{12,0},{14,2},{16,28},{18,... | collective-permute-start | bytes 172040 | tf_op jit(solution)/shard_map/ppermute | solution.py:23
  65.2 4.2 %collective-permute-start.17 = (bf16[224,128]{1,0:T(8,128)(2,1)S(1)}, bf16[224,128]{1,0:T(8,128)(2,1)S(1)}, u32[]{:S(2)}, u32[]{:S(2)}) collective-permute-start(bf16[224,128]{1,0:T(8,128)(2,1)S(1)} %fusion.12), channel_id=1, source_target_pairs={{0,1},{1,0},{2,3},{3,2},{4,5},{5,4},{6,7},{7,6},{8,9},{9,8},{10,11... | collective-permute-start | bytes 172040 | tf_op jit(solution)/shard_map/ppermute | solution.py:19
  66.2 3.3 %collective-permute-start.18 = (bf16[224,128]{1,0:T(8,128)(2,1)S(1)}, bf16[224,128]{1,0:T(8,128)(2,1)S(1)}, u32[]{:S(2)}, u32[]{:S(2)}) collective-permute-start(bf16[224,128]{1,0:T(8,128)(2,1)S(1)} %fusion.13), channel_id=1, source_target_pairs={{0,2},{2,0},{4,6},{6,4},{8,10},{10,8},{12,14},{14,12},{16,18},{18,... | collective-permute-start | bytes 172040 | tf_op jit(solution)/shard_map/ppermute | solution.py:23
  69.5 5.1 %collective-permute-start.19 = (bf16[224,128]{1,0:T(8,128)(2,1)S(1)}, bf16[224,128]{1,0:T(8,128)(2,1)S(1)}, u32[]{:S(2)}, u32[]{:S(2)}) collective-permute-start(bf16[224,128]{1,0:T(8,128)(2,1)S(1)} %fusion.8), channel_id=1, source_target_pairs={{0,16},{2,18},{4,20},{6,22},{8,24},{10,26},{12,28},{14,30},{16,0},... | collective-permute-start | bytes 172040 | tf_op jit(solution)/shard_map/ppermute | solution.py:394

commit v11 on v10

--- a/solution.py
+++ b/solution.py
@@ -82,12 +82,14 @@
     parts, (logits_ref, stats_ref, turned_ref) = refs[:-3], refs[-3:]
     half = own_ref.shape[0] // 2
     lane = lax.broadcasted_iota(jnp.int32, (STEP, 128), 1)
-    for place in range(2):
-        start = (core_ref[0] if place == 0 else 1 - core_ref[0]) * half
-        for r in range(0, half, STEP):
+    groups = [(core_ref[0], 0, half // 2), (core_ref[0], half // 2, half // 2)]
+    groups.append((1 - core_ref[0], 0, half))
+    for place, (side, first, count) in enumerate(groups):
+        start = side * half + first
+        for r in range(0, count, STEP):
             rows = pl.ds(pl.multiple_of(start + r, STEP), STEP)
             logits = own_ref[rows, :]
-            for part in parts[place::2]:
+            for part in parts[place::3]:
                 logits = logits + part[r : r + STEP, :]
             logits_ref[rows, :] = logits
             top = jnp.max(logits, axis=1, keepdims=True)
@@ -281,9 +283,17 @@
     def columns_of(index, first, count):
         return lax.dynamic_slice(hidden, (first, index * rows), (count, rows))
 
-    near = [
-        shift_tok(columns_of(lax.rem(tok_index + d, tok_size), core * half, half), d, tok_size)
-        for d in range(1, tok_size)
+    quarter = half // 2
+    near, later = [
+        [
+            shift_tok(
+                columns_of(lax.rem(tok_index + d, tok_size), core * half + first, quarter),
+                d,
+                tok_size,
+            )
+            for d in range(1, tok_size)
+        ]
+        for first in (0, quarter)
     ]
     upper = []
     while 1 << len(upper) < vocab_size:
@@ -295,24 +305,29 @@
     column_block = (first_column + jnp.arange(column_count, dtype=jnp.int32)) // BLK
     live_slot = jnp.arange(block_ids.shape[1], dtype=jnp.int32)[None, :] < counts[:, None]
     core_word = core.reshape(1)
-    own = columns_of(tok_index, 0, token_count)
-    own, head, upper, apart_is, column_block, live_slot, core_word = lax.optimization_barrier(
-        (own, head, upper, apart_is, column_block, live_slot, core_word)
+    tok_is = [tok_index == d for d in range(tok_size)]
+    head, upper, apart_is, tok_is, column_block, live_slot, core_word = lax.optimization_barrier(
+        (head, upper, apart_is, tok_is, column_block, live_slot, core_word)
     )
     head_here = load(head)
-    near, head_here, column_block, teacher = lax.optimization_barrier(
-        (near, head_here, column_block, teacher)
-    )
+    near, head_here, column_block, teacher, hidden = lax.optimization_barrier(
+        (near, head_here, column_block, teacher, hidden)
+    )
+    products = [jnp.dot(x, head_here, preferred_element_type=jnp.float32) for x in near]
+    returned = [[shift_tok(x, -d, tok_size)] for d, x in enumerate(products, 1)]
+    later, _ = lax.optimization_barrier((later, products))
+    near = [jnp.concatenate(pair, axis=0) for pair in zip(near, later)]
     far = [swap_vocab(x, 1, vocab_size) for x in near]
-    returned = []
     for d in range(1, tok_size):
-        first = shift_tok(
-            jnp.dot(near[d - 1], head_here, preferred_element_type=jnp.float32), -d, tok_size
-        )
-        second = shift_tok(
-            jnp.dot(far[d - 1], head_here, preferred_element_type=jnp.float32), -d, tok_size
-        )
-        returned.append((first, second))
+        for x in (later[d - 1], far[d - 1]):
+            returned[d - 1].append(
+                shift_tok(
+                    jnp.dot(x, head_here, preferred_element_type=jnp.float32), -d, tok_size
+                )
+            )
+    own = hidden[:, :rows]
+    for d in range(1, tok_size):
+        own = jnp.where(tok_is[d], hidden[:, d * rows : (d + 1) * rows], own)
     logits = jnp.dot(own, head_here, preferred_element_type=jnp.float32)
     block_hit = jnp.any(
         (block_ids[:, :, None] == column_block[None, None, :]) & live_slot[:, :, None], axis=1

time: 75.5 us -> 73.8 us (0.977)
  waiting for transfers between devices: 32.3 us -> 28.8 us
  starting transfers between devices: 23.8 us -> 25.6 us
  local copies, waits for them, and re-layouts: 2.03 us -> 1.01 us
  matrix products: 3.01 us -> 4.01 us
    ppermute x5 -> x7, waiting for transfers between devices: 19.5 us -> 16.2 us  [shift_tok(): lax.ppermute(x, 'tok', [(i, (i + offset) % size) for i in range(size)])]
    ppermute x5 -> x7, starting transfers between devices: 7.67 us -> 9.51 us  [shift_tok(): lax.ppermute(x, 'tok', [(i, (i + offset) % size) for i in range(size)])]
    dynamic_slice x2 -> x1, local copies, waits for them, and re-layouts: 2.02 us -> 0.98 us  [columns_of(): return lax.dynamic_slice(hidden, (first, index * rows), (count, rows))]
    dot_general x2 -> x3, matrix products: 2.13 us -> 3.13 us  [per_device(): jnp.dot(x, head_here, preferred_element_type=jnp.float32)]
  transfers between devices with their start and end apart: 20 -> 22, of which waited for: 15 -> 16; matrix products, arithmetic and copies ran while one was open for 6% -> 7% of each run, Pallas kernels for 13% -> 13%
where the time goes in v11:
time: 73.8 us; the launch traced here: 73.7 us
  waiting for transfers between devices  28.8 us (39%)
  starting transfers between devices  25.6 us (35%)
  Pallas kernels  11 us (15%)
  matrix products  4.01 us (5%)
  other arithmetic  1.69 us (2%)
  between operations  1.56 us (2%)
  local copies, waits for them, and re-layouts  1.01 us (1%)
    ppermute x7, waiting for transfers between devices, shift_tok(): lax.ppermute(x, 'tok', [(i, (i + offset) % size) for i in range(size)])  16.2 us
    ppermute x14, starting transfers between devices, swap_vocab(): return lax.ppermute(x, 'vocab', [(i, i ^ bit) for i in range(size)])  13.5 us
    ppermute x14, waiting for transfers between devices, swap_vocab(): return lax.ppermute(x, 'vocab', [(i, i ^ bit) for i in range(size)])  10.1 us
    ppermute x7, starting transfers between devices, shift_tok(): lax.ppermute(x, 'tok', [(i, (i + offset) % size) for i in range(size)])  9.51 us
    pallas_call x2, Pallas kernels, head_gradient(): pl.pallas_call(functools.partial(head_gradient_kernel, steps, start, widt...  3.9 us
    pallas_call x2, Pallas kernels, gradient(): pl.pallas_call(own_gradient_kernel if core is None else gradient_kernel,...  3.15 us
    dot_general x3, matrix products, per_device(): jnp.dot(x, head_here, preferred_element_type=jnp.float32)  3.13 us
    ppermute x1, starting transfers between devices, per_device(): lax.ppermute(blocks[k].astype(jnp.bfloat16), 'vocab', pairs)  2.65 us
  transfers between devices with their start and end apart: 22, of which 16 were waited for; matrix products, arithmetic and copies ran while one was open for 7% of the time, Pallas kernels for 13%

profile of v11, /device:TPU:0, one launch (start us, length us, event | category | flops | bytes accessed | tf_op | source)
XLA Modules:
  0.0 73.7 jit_solution(17987512886682389122)
XLA Ops:
  0.6 1.0 %fusion.17 = (bf16[32,1792]{1,0:T(8,128)(2,1)S(1)}, bf16[32,1792]{1,0:T(8,128)(2,1)S(1)}) fusion(bf16[128,3584]{1,0:T(8,128)(2,1)} %param.5, s32[]{:T(128)S(6)} %select_n.247, s32[]{:T(128)S(6)} %select_n.246, s32[]{:T(128)S(6)} %select_n.245), kind=kLoop, calls=%fused_computation.71 | loop fusion | bytes 458764 | tf_op jit(solution)/shard_map/dynamic_slice | solution.py:284
  1.6 3.0 %collective-permute-start.2 = (bf16[32,1792]{1,0:T(8,128)(2,1)S(1)}, bf16[32,1792]{1,0:T(8,128)(2,1)S(1)}, u32[]{:S(2)}, u32[]{:S(2)}) collective-permute-start(bf16[32,1792]{1,0:T(8,128)(2,1)S(1)} %get-tuple-element.101), channel_id=1, source_target_pairs={{0,1},{1,0},{2,3},{3,2},{4,5},{5,4},{6,7},{7,6},{8,9},{9,8},{10,11... | collective-permute-start | bytes 344072 | tf_op jit(solution)/shard_map/ppermute | solution.py:19
  4.7 0.1 collective-permute-start
  5.4 2.6 %load_head.1.head_ref = bf16[1792,1536]{1,0:T(8,128)(2,1)S(1)} custom-call(bf16[1792,1536]{1,0:T(8,128)(2,1)} %head_ref), custom_call_target="tpu_custom_call" | custom-call | bytes 11010048 | tf_op jit(solution)/shard_map/load_head/pallas_call | solution.py:67
  8.1 0.0 copy-start
  8.1 2.2 %collective-permute-done = bf16[32,1792]{1,0:T(8,128)(2,1)S(1)} collective-permute-done((bf16[32,1792]{1,0:T(8,128)(2,1)S(1)}, bf16[32,1792]{1,0:T(8,128)(2,1)S(1)}, u32[]{:S(2)}, u32[]{:S(2)}) %collective-permute-start) | collective-permute-done | bytes 114720 | tf_op jit(solution)/shard_map/ppermute | solution.py:19
  10.3 1.0 %fusion.18 = f32[32,1536]{1,0:T(8,128)S(1)} fusion(bf16[32,1792]{1,0:T(8,128)(2,1)S(1)} %collective-permute-done, bf16[1792,1536]{1,0:T(8,128)(2,1)S(1)} %load_head.1.head_ref), kind=kOutput, calls=%fused_computation.72 | convolution fusion | flops 176160768 | bytes 5816320 | tf_op jit(solution)/shard_map/dot_general | solution.py:316
  11.3 1.8 %collective-permute-start.1 = (f32[32,1536]{1,0:T(8,128)S(1)}, f32[32,1536]{1,0:T(8,128)S(1)}, u32[]{:S(2)}, u32[]{:S(2)}) collective-permute-start(f32[32,1536]{1,0:T(8,128)S(1)} %fusion.18), channel_id=1, source_target_pairs={{0,1},{1,0},{2,3},{3,2},{4,5},{5,4},{6,7},{7,6},{8,9},{9,8},{10,11... | collective-permute-start | bytes 589832 | tf_op jit(solution)/shard_map/ppermute | solution.py:19
  13.1 0.0 collective-permute-done.2
  13.1 1.0 %fusion.19 = f32[32,1536]{1,0:T(8,128)S(1)} fusion(bf16[32,1792]{1,0:T(8,128)(2,1)S(1)} %collective-permute-done.2, bf16[1792,1536]{1,0:T(8,128)(2,1)S(1)} %load_head.1.head_ref), kind=kOutput, calls=%fused_computation.73 | convolution fusion | flops 176160768 | bytes 5816320 | tf_op jit(solution)/shard_map/dot_general | solution.py:325
  14.1 0.4 collective-permute-start.3
  14.5 0.0 collective-permute-start.4
  14.5 0.9 %fusion.21.own_ref = f32[128,1536]{1,0:T(8,128)S(1)} fusion(bf16[128,1792]{1,0:T(8,128)(2,1)S(1)} %slice_select_fusion, bf16[1792,1536]{1,0:T(8,128)(2,1)S(1)} %load_head.1.head_ref), kind=kOutput, calls=%fused_computation.75 | convolution fusion | flops 704643072 | bytes 6750208 | tf_op jit(solution)/shard_map/dot_general | solution.py:331
  15.4 0.1 and_reduce_fusion
  15.6 0.3 fusion
  15.9 0.1 collective-permute-done.4
  16.0 1.1 %fusion.20 = f32[64,1536]{1,0:T(8,128)S(1)} fusion(bf16[64,1792]{1,0:T(8,128)(2,1)S(1)} %collective-permute-done.4, bf16[1792,1536]{1,0:T(8,128)(2,1)S(1)} %load_head.1.head_ref), kind=kOutput, calls=%fused_computation.74 | convolution fusion | flops 352321536 | bytes 6127616 | tf_op jit(solution)/shard_map/dot_general | solution.py:325
  17.0 1.8 %collective-permute-start.5 = (f32[64,1536]{1,0:T(8,128)S(1)}, f32[64,1536]{1,0:T(8,128)S(1)}, u32[]{:S(2)}, u32[]{:S(2)}) collective-permute-start(f32[64,1536]{1,0:T(8,128)S(1)} %fusion.20), channel_id=1, source_target_pairs={{0,1},{1,0},{2,3},{3,2},{4,5},{5,4},{6,7},{7,6},{8,9},{9,8},{10,11... | collective-permute-start | bytes 1179656 | tf_op jit(solution)/shard_map/ppermute | solution.py:19
  18.9 0.1 pad_maximum_fusion.refs_0_
  19.0 4.1 %collective-permute-done.3.refs_1_ = f32[32,1536]{1,0:T(8,128)S(1)} collective-permute-done((f32[32,1536]{1,0:T(8,128)S(1)}, f32[32,1536]{1,0:T(8,128)S(1)}, u32[]{:S(2)}, u32[]{:S(2)}) %collective-permute-start.3) | collective-permute-done | bytes 196640 | tf_op jit(solution)/shard_map/ppermute | solution.py:19
  23.0 0.0 collective-permute-done.1.refs_0_
  23.0 7.0 %collective-permute-done.5.refs_2_ = f32[64,1536]{1,0:T(8,128)S(1)} collective-permute-done((f32[64,1536]{1,0:T(8,128)S(1)}, f32[64,1536]{1,0:T(8,128)S(1)}, u32[]{:S(2)}, u32[]{:S(2)}) %collective-permute-start.5) | collective-permute-done | bytes 393248 | tf_op jit(solution)/shard_map/ppermute | solution.py:19
  30.0 0.4 local_stats.1
  30.4 0.0 collective-permute-start.6
  30.5 1.1 %collective-permute-done.6 = f32[1,4,128]{2,1,0:T(4,128)S(1)} collective-permute-done((f32[1,4,128]{2,1,0:T(4,128)S(1)}, f32[1,4,128]{2,1,0:T(4,128)S(1)}, u32[]{:S(2)}, u32[]{:S(2)}) %collective-permute-start.6) | collective-permute-done | bytes 2080 | tf_op jit(solution)/shard_map/ppermute | solution.py:23
  31.7 1.5 %collective-permute-start.9 = (f32[2,4,128]{2,1,0:T(4,128)S(1)}, f32[2,4,128]{2,1,0:T(4,128)S(1)}, u32[]{:S(2)}, u32[]{:S(2)}) collective-permute-start(f32[2,4,128]{2,1,0:T(4,128)S(1)} %pad_maximum_fusion.4), channel_id=1, source_target_pairs={{0,4},{2,6},{4,0},{6,2},{8,12},{10,14},{12,8},{14,10},{16,20},{18,... | collective-permute-start | bytes 12296 | tf_op jit(solution)/shard_map/ppermute | solution.py:23
  33.1 1.6 %collective-permute-start.8 = (f32[2,4,128]{2,1,0:T(4,128)S(1)}, f32[2,4,128]{2,1,0:T(4,128)S(1)}, u32[]{:S(2)}, u32[]{:S(2)}) collective-permute-start(f32[2,4,128]{2,1,0:T(4,128)S(1)} %pad_maximum_fusion.4), channel_id=1, source_target_pairs={{0,8},{2,10},{4,12},{6,14},{8,0},{10,2},{12,4},{14,6},{16,24},{18,... | collective-permute-start | bytes 12296 | tf_op jit(solution)/shard_map/ppermute | solution.py:23
  34.7 0.5 collective-permute-start.7
  35.2 0.1 collective-permute-done.9
  35.3 1.4 %collective-permute-done.8 = f32[2,4,128]{2,1,0:T(4,128)S(1)} collective-permute-done((f32[2,4,128]{2,1,0:T(4,128)S(1)}, f32[2,4,128]{2,1,0:T(4,128)S(1)}, u32[]{:S(2)}, u32[]{:S(2)}) %collective-permute-start.8) | collective-permute-done | bytes 4128 | tf_op jit(solution)/shard_map/ppermute | solution.py:23
  36.7 2.5 %collective-permute-done.7 = f32[2,4,128]{2,1,0:T(4,128)S(1)} collective-permute-done((f32[2,4,128]{2,1,0:T(4,128)S(1)}, f32[2,4,128]{2,1,0:T(4,128)S(1)}, u32[]{:S(2)}, u32[]{:S(2)}) %collective-permute-start.7) | collective-permute-done | bytes 4128 | tf_op jit(solution)/shard_map/ppermute | solution.py:23
  39.2 2.7 %collective-permute-start.10 = (f32[8,4,128]{2,1,0:T(4,128)S(1)}, f32[8,4,128]{2,1,0:T(4,128)S(1)}, u32[]{:S(2)}, u32[]{:S(2)}) collective-permute-start(f32[8,4,128]{2,1,0:T(4,128)S(1)} %pad_maximum_fusion.3), channel_id=1, source_target_pairs={{0,16},{2,18},{4,20},{6,22},{8,24},{10,26},{12,28},{14,30},{16,0},... | collective-permute-start | bytes 49160 | tf_op jit(solution)/shard_map/ppermute | solution.py:23
  41.9 2.1 %collective-permute-done.10 = f32[8,4,128]{2,1,0:T(4,128)S(1)} collective-permute-done((f32[8,4,128]{2,1,0:T(4,128)S(1)}, f32[8,4,128]{2,1,0:T(4,128)S(1)}, u32[]{:S(2)}, u32[]{:S(2)}) %collective-permute-start.10) | collective-permute-done | bytes 16416 | tf_op jit(solution)/shard_map/ppermute | solution.py:23
  44.0 0.9 %delta.1 = (bf16[128,1536]{1,0:T(8,128)(2,1)S(1)}, f32[1,128]{1,0:T(1,128)}, f32[1,128]{1,0:T(1,128)}) custom-call(f32[16,4,128]{2,1,0:T(4,128)S(1)} %pad_maximum_fusion.2.gathered_ref, f32[128,1536]{1,0:T(8,128)S(1)} %get-tuple-element.72.logits_ref, bf16[128,1536]{1,0:T(8,128)(2,1)S(1)} %get-tuple-element.66.kept_ref), custom_call_target="tpu_custom_call" | custom-call | flops 1572864 | bytes 1572864 | tf_op jit(solution)/shard_map/delta/pallas_call | solution.py:155
  44.9 1.5 %collective-permute-start.11 = (bf16[128,1536]{1,0:T(8,128)(2,1)S(1)}, bf16[128,1536]{1,0:T(8,128)(2,1)S(1)}, u32[]{:S(2)}, u32[]{:S(2)}) collective-permute-start(bf16[128,1536]{1,0:T(8,128)(2,1)S(1)} %get-tuple-element.76.delta_ref), channel_id=1, source_target_pairs={{0,1},{1,0},{2,3},{3,2},{4,5},{5,4},{6,7},{7,6},{8,9},{9,8},{10,11... | collective-permute-start | bytes 1179656 | tf_op jit(solution)/shard_map/ppermute | solution.py:19
  46.4 1.6 %partial_gradient.3 = f32[4,2,224,128]{3,2,1,0:T(8,128)S(1)} custom-call(bf16[1792,1536]{1,0:T(8,128)(2,1)S(1)} %load_head.1.head_ref, bf16[128,1536]{1,0:T(8,128)(2,1)S(1)} %get-tuple-element.76.delta_ref), custom_call_target="tpu_custom_call" | custom-call | flops 704643072 | bytes 5898240 | tf_op jit(solution)/shard_map/partial_gradient/pallas_call | solution.py:213
  48.0 0.1 fusion.11
  48.1 0.4 collective-permute-start.14
  48.5 1.6 %collective-permute-start.13 = (bf16[2,224,128]{2,1,0:T(8,128)(2,1)S(1)}, bf16[2,224,128]{2,1,0:T(8,128)(2,1)S(1)}, u32[]{:S(2)}, u32[]{:S(2)}) collective-permute-start(bf16[2,224,128]{2,1,0:T(8,128)(2,1)S(1)} %get-tuple-element.99), channel_id=1, source_target_pairs={{0,8},{2,10},{4,12},{6,14},{8,0},{10,2},{12,4},{14,6},{16,24},{18,... | collective-permute-start | bytes 344072 | tf_op jit(solution)/shard_map/ppermute | solution.py:23
  50.1 1.5 %collective-permute-start.12 = (bf16[2,224,128]{2,1,0:T(8,128)(2,1)S(1)}, bf16[2,224,128]{2,1,0:T(8,128)(2,1)S(1)}, u32[]{:S(2)}, u32[]{:S(2)}) collective-permute-start(bf16[2,224,128]{2,1,0:T(8,128)(2,1)S(1)} %get-tuple-element.100), channel_id=1, source_target_pairs={{0,4},{2,6},{4,0},{6,2},{8,12},{10,14},{12,8},{14,10},{16,20},{18,... | collective-permute-start | bytes 344072 | tf_op jit(solution)/shard_map/ppermute | solution.py:23
  51.6 1.6 %collective-permute-done.11.delta_ref = bf16[128,1536]{1,0:T(8,128)(2,1)S(1)} collective-permute-done((bf16[128,1536]{1,0:T(8,128)(2,1)S(1)}, bf16[128,1536]{1,0:T(8,128)(2,1)S(1)}, u32[]{:S(2)}, u32[]{:S(2)}) %collective-permute-start.11) | collective-permute-done | bytes 393248 | tf_op jit(solution)/shard_map/ppermute | solution.py:19
  53.2 1.6 %partial_gradient.2 = (bf16[4,224,128]{2,1,0:T(8,128)(2,1)S(1)}, f32[4,224,128]{2,1,0:T(8,128)S(1)}) custom-call(s32[1]{0:T(128)} %bitcast.1.core_ref, bf16[1792,1536]{1,0:T(8,128)(2,1)S(1)} %load_head.1.head_ref, bf16[128,1536]{1,0:T(8,128)(2,1)S(1)} %collective-permute-done.11.delta_ref), custom_call_target="tpu_custom_call" | custom-call | flops 704643072 | bytes 5898240 | tf_op jit(solution)/shard_map/partial_gradient/pallas_call | solution.py:213
  54.8 0.0 collective-permute-done.14
  54.8 0.0 collective-permute-done.13
  54.8 0.2 collective-permute-done.12
  55.1 0.0 collective-permute-start.15
  55.1 0.1 pad_maximum_fusion.1.refs_1_
  55.1 0.1 fusion.5
  55.2 1.3 %collective-permute-done.15 = bf16[4,224,128]{2,1,0:T(8,128)(2,1)S(1)} collective-permute-done((bf16[4,224,128]{2,1,0:T(8,128)(2,1)S(1)}, bf16[4,224,128]{2,1,0:T(8,128)(2,1)S(1)}, u32[]{:S(2)}, u32[]{:S(2)}) %collective-permute-start.15) | collective-permute-done | bytes 229408 | tf_op jit(solution)/shard_map/ppermute | solution.py:23
  56.6 1.4 %collective-permute-start.16 = (bf16[1,224,128]{2,1,0:T(8,128)(2,1)S(1)}, bf16[1,224,128]{2,1,0:T(8,128)(2,1)S(1)}, u32[]{:S(2)}, u32[]{:S(2)}) collective-permute-start(bf16[1,224,128]{2,1,0:T(8,128)(2,1)S(1)} %get-tuple-element.80), channel_id=1, source_target_pairs={{0,4},{2,6},{4,0},{6,2},{8,12},{10,14},{12,8},{14,10},{16,20},{18,... | collective-permute-start | bytes 172040 | tf_op jit(solution)/shard_map/ppermute | solution.py:23
  58.1 0.4 collective-permute-start.17
  58.5 1.7 %collective-permute-start.18 = (bf16[1,224,128]{2,1,0:T(8,128)(2,1)S(1)}, bf16[1,224,128]{2,1,0:T(8,128)(2,1)S(1)}, u32[]{:S(2)}, u32[]{:S(2)}) collective-permute-start(bf16[1,224,128]{2,1,0:T(8,128)(2,1)S(1)} %get-tuple-element.82), channel_id=1, source_target_pairs={{0,12},{2,14},{4,8},{6,10},{8,4},{10,6},{12,0},{14,2},{16,28},{18,... | collective-permute-start | bytes 172040 | tf_op jit(solution)/shard_map/ppermute | solution.py:23
  60.2 2.1 %head_gradient.2.refs_2_ = bf16[1792,1536]{1,0:T(8,128)(2,1)} custom-call(bf16[256,1792]{1,0:T(8,128)(2,1)S(1)} %pad_maximum_fusion.refs_0_, bf16[256,1536]{1,0:T(8,128)(2,1)S(1)} %pad_maximum_fusion.1.refs_1_), custom_call_target="tpu_custom_call" | custom-call | flops 805306368 | bytes 4849664 | tf_op jit(solution)/shard_map/head_gradient/pallas_call | solution.py:252
  62.3 0.0 collective-permute-done.16
  62.3 0.1 collective-permute-done.17
  62.4 1.2 %collective-permute-done.18 = bf16[1,224,128]{2,1,0:T(8,128)(2,1)S(1)} collective-permute-done((bf16[1,224,128]{2,1,0:T(8,128)(2,1)S(1)}, bf16[1,224,128]{2,1,0:T(8,128)(2,1)S(1)}, u32[]{:S(2)}, u32[]{:S(2)}) %collective-permute-start.18) | collective-permute-done | bytes 57376 | tf_op jit(solution)/shard_map/ppermute | solution.py:23
  63.5 0.1 fusion.12
  63.6 1.0 %collective-permute-start.19 = (bf16[224,128]{1,0:T(8,128)(2,1)S(1)}, bf16[224,128]{1,0:T(8,128)(2,1)S(1)}, u32[]{:S(2)}, u32[]{:S(2)}) collective-permute-start(bf16[224,128]{1,0:T(8,128)(2,1)S(1)} %fusion.12), channel_id=1, source_target_pairs={{0,1},{1,0},{2,3},{3,2},{4,5},{5,4},{6,7},{7,6},{8,9},{9,8},{10,11... | collective-permute-start | bytes 172040 | tf_op jit(solution)/shard_map/ppermute | solution.py:19
  64.6 0.1 collective-permute-start.20
  64.7 1.8 %head_gradient.3 = bf16[1792,1536]{1,0:T(8,128)(2,1)} custom-call(bf16[256,1792]{1,0:T(8,128)(2,1)S(1)} %pad_maximum_fusion.refs_0_, bf16[256,1536]{1,0:T(8,128)(2,1)S(1)} %pad_maximum_fusion.1.refs_1_, bf16[1792,1536]{1,0:T(8,128)(2,1)} %head_gradient.2.refs_2_), custom_call_target="tpu_custom_call", output_to_operand_aliasing={{}: (2, {})} | custom-call | flops 603979776 | bytes 4063232 | tf_op jit(solution)/shard_map/head_gradient/pallas_call | solution.py:252
  66.5 1.4 %collective-permute-done.19 = bf16[224,128]{1,0:T(8,128)(2,1)S(1)} collective-permute-done((bf16[224,128]{1,0:T(8,128)(2,1)S(1)}, bf16[224,128]{1,0:T(8,128)(2,1)S(1)}, u32[]{:S(2)}, u32[]{:S(2)}) %collective-permute-start.19) | collective-permute-done | bytes 57376 | tf_op jit(solution)/shard_map/ppermute | solution.py:19
  67.9 2.7 %collective-permute-start.21 = (bf16[224,128]{1,0:T(8,128)(2,1)S(1)}, bf16[224,128]{1,0:T(8,128)(2,1)S(1)}, u32[]{:S(2)}, u32[]{:S(2)}) collective-permute-start(bf16[224,128]{1,0:T(8,128)(2,1)S(1)} %fusion.8), channel_id=1, source_target_pairs={{0,16},{2,18},{4,20},{6,22},{8,24},{10,26},{12,28},{14,30},{16,0},... | collective-permute-start | bytes 172040 | tf_op jit(solution)/shard_map/ppermute | solution.py:409
  70.5 2.5 %collective-permute-done.21 = bf16[224,128]{1,0:T(8,128)(2,1)S(1)} collective-permute-done((bf16[224,128]{1,0:T(8,128)(2,1)S(1)}, bf16[224,128]{1,0:T(8,128)(2,1)S(1)}, u32[]{:S(2)}, u32[]{:S(2)}) %collective-permute-start.21) | collective-permute-done | bytes 57376 | tf_op jit(solution)/shard_map/ppermute | solution.py:409
  73.0 0.7 fusion.7
  (23 shorter events, 0.3 us)
Async XLA Ops:
  1.6 11.4 %collective-permute-start.2 = (bf16[32,1792]{1,0:T(8,128)(2,1)S(1)}, bf16[32,1792]{1,0:T(8,128)(2,1)S(1)}, u32[]{:S(2)}, u32[]{:S(2)}) collective-permute-start(bf16[32,1792]{1,0:T(8,128)(2,1)S(1)} %get-tuple-element.101), channel_id=1, source_target_pairs={{0,1},{1,0},{2,3},{3,2},{4,5},{5,4},{6,7},{7,6},{8,9},{9,8},{10,11... | collective-permute-start | bytes 344072 | tf_op jit(solution)/shard_map/ppermute | solution.py:19
  4.7 5.6 %collective-permute-start = (bf16[32,1792]{1,0:T(8,128)(2,1)S(1)}, bf16[32,1792]{1,0:T(8,128)(2,1)S(1)}, u32[]{:S(2)}, u32[]{:S(2)}) collective-permute-start(bf16[32,1792]{1,0:T(8,128)(2,1)S(1)} %get-tuple-element.102), channel_id=1, source_target_pairs={{0,1},{1,0},{2,3},{3,2},{4,5},{5,4},{6,7},{7,6},{8,9},{9,8},{10,11... | collective-permute-start | bytes 344072 | tf_op jit(solution)/shard_map/ppermute | solution.py:19
  8.1 6.4 %copy-start = (bf16[128,3584]{1,0:T(8,128)(2,1)S(1)}, bf16[128,3584]{1,0:T(8,128)(2,1)}, u32[]{:S(2)}) copy-start(bf16[128,3584]{1,0:T(8,128)(2,1)} %param.5) | copy-start | bytes 2752516
  11.3 11.7 %collective-permute-start.1 = (f32[32,1536]{1,0:T(8,128)S(1)}, f32[32,1536]{1,0:T(8,128)S(1)}, u32[]{:S(2)}, u32[]{:S(2)}) collective-permute-start(f32[32,1536]{1,0:T(8,128)S(1)} %fusion.18), channel_id=1, source_target_pairs={{0,1},{1,0},{2,3},{3,2},{4,5},{5,4},{6,7},{7,6},{8,9},{9,8},{10,11... | collective-permute-start | bytes 589832 | tf_op jit(solution)/shard_map/ppermute | solution.py:19
  14.1 1.3 %copy-start.2 = (s32[1,16]{1,0:T(1,128)S(1)}, s32[1,16]{1,0:T(1,128)}, u32[]{:S(2)}) copy-start(s32[1,16]{1,0:T(1,128)} %param.8) | copy-start | bytes 196
  14.1 1.5 %copy-start.1 = (bf16[128,1536]{1,0:T(8,128)(2,1)S(1)}, bf16[128,1536]{1,0:T(8,128)(2,1)}, u32[]{:S(2)}) copy-start(bf16[128,1536]{1,0:T(8,128)(2,1)} %param.7) | copy-start | bytes 1179652
  14.1 8.9 %collective-permute-start.3 = (f32[32,1536]{1,0:T(8,128)S(1)}, f32[32,1536]{1,0:T(8,128)S(1)}, u32[]{:S(2)}, u32[]{:S(2)}) collective-permute-start(f32[32,1536]{1,0:T(8,128)S(1)} %fusion.19), channel_id=1, source_target_pairs={{0,1},{1,0},{2,3},{3,2},{4,5},{5,4},{6,7},{7,6},{8,9},{9,8},{10,11... | collective-permute-start | bytes 589832 | tf_op jit(solution)/shard_map/ppermute | solution.py:19
  14.5 1.5 %collective-permute-start.4 = (bf16[64,1792]{1,0:T(8,128)(2,1)S(1)}, bf16[64,1792]{1,0:T(8,128)(2,1)S(1)}, u32[]{:S(2)}, u32[]{:S(2)}) collective-permute-start(bf16[64,1792]{1,0:T(8,128)(2,1)S(1)} %constant_dynamic-update-slice_fusion), channel_id=1, source_target_pairs={{0,2},{2,0},{4,6},{6,4},{8,10},{10,8},{12,14},{14,12},{16,18},{18,... | collective-permute-start | bytes 688136 | tf_op jit(solution)/shard_map/ppermute | solution.py:23
  17.0 13.0 %collective-permute-start.5 = (f32[64,1536]{1,0:T(8,128)S(1)}, f32[64,1536]{1,0:T(8,128)S(1)}, u32[]{:S(2)}, u32[]{:S(2)}) collective-permute-start(f32[64,1536]{1,0:T(8,128)S(1)} %fusion.20), channel_id=1, source_target_pairs={{0,1},{1,0},{2,3},{3,2},{4,5},{5,4},{6,7},{7,6},{8,9},{9,8},{10,11... | collective-permute-start | bytes 1179656 | tf_op jit(solution)/shard_map/ppermute | solution.py:19
  30.4 1.2 %collective-permute-start.6 = (f32[1,4,128]{2,1,0:T(4,128)S(1)}, f32[1,4,128]{2,1,0:T(4,128)S(1)}, u32[]{:S(2)}, u32[]{:S(2)}) collective-permute-start(f32[1,4,128]{2,1,0:T(4,128)S(1)} %bitcast.44), channel_id=1, source_target_pairs={{0,2},{2,0},{4,6},{6,4},{8,10},{10,8},{12,14},{14,12},{16,18},{18,... | collective-permute-start | bytes 6152 | tf_op jit(solution)/shard_map/ppermute | solution.py:23
  31.7 3.7 %collective-permute-start.9 = (f32[2,4,128]{2,1,0:T(4,128)S(1)}, f32[2,4,128]{2,1,0:T(4,128)S(1)}, u32[]{:S(2)}, u32[]{:S(2)}) collective-permute-start(f32[2,4,128]{2,1,0:T(4,128)S(1)} %pad_maximum_fusion.4), channel_id=1, source_target_pairs={{0,4},{2,6},{4,0},{6,2},{8,12},{10,14},{12,8},{14,10},{16,20},{18,... | collective-permute-start | bytes 12296 | tf_op jit(solution)/shard_map/ppermute | solution.py:23
  33.1 3.6 %collective-permute-start.8 = (f32[2,4,128]{2,1,0:T(4,128)S(1)}, f32[2,4,128]{2,1,0:T(4,128)S(1)}, u32[]{:S(2)}, u32[]{:S(2)}) collective-permute-start(f32[2,4,128]{2,1,0:T(4,128)S(1)} %pad_maximum_fusion.4), channel_id=1, source_target_pairs={{0,8},{2,10},{4,12},{6,14},{8,0},{10,2},{12,4},{14,6},{16,24},{18,... | collective-permute-start | bytes 12296 | tf_op jit(solution)/shard_map/ppermute | solution.py:23
  34.7 4.5 %collective-permute-start.7 = (f32[2,4,128]{2,1,0:T(4,128)S(1)}, f32[2,4,128]{2,1,0:T(4,128)S(1)}, u32[]{:S(2)}, u32[]{:S(2)}) collective-permute-start(f32[2,4,128]{2,1,0:T(4,128)S(1)} %pad_maximum_fusion.4), channel_id=1, source_target_pairs={{0,12},{2,14},{4,8},{6,10},{8,4},{10,6},{12,0},{14,2},{16,28},{18,... | collective-permute-start | bytes 12296 | tf_op jit(solution)/shard_map/ppermute | solution.py:23
  39.2 4.8 %collective-permute-start.10 = (f32[8,4,128]{2,1,0:T(4,128)S(1)}, f32[8,4,128]{2,1,0:T(4,128)S(1)}, u32[]{:S(2)}, u32[]{:S(2)}) collective-permute-start(f32[8,4,128]{2,1,0:T(4,128)S(1)} %pad_maximum_fusion.3), channel_id=1, source_target_pairs={{0,16},{2,18},{4,20},{6,22},{8,24},{10,26},{12,28},{14,30},{16,0},... | collective-permute-start | bytes 49160 | tf_op jit(solution)/shard_map/ppermute | solution.py:23
  44.9 8.3 %collective-permute-start.11 = (bf16[128,1536]{1,0:T(8,128)(2,1)S(1)}, bf16[128,1536]{1,0:T(8,128)(2,1)S(1)}, u32[]{:S(2)}, u32[]{:S(2)}) collective-permute-start(bf16[128,1536]{1,0:T(8,128)(2,1)S(1)} %get-tuple-element.76.delta_ref), channel_id=1, source_target_pairs={{0,1},{1,0},{2,3},{3,2},{4,5},{5,4},{6,7},{7,6},{8,9},{9,8},{10,11... | collective-permute-start | bytes 1179656 | tf_op jit(solution)/shard_map/ppermute | solution.py:19
  48.1 6.7 %collective-permute-start.14 = (bf16[2,224,128]{2,1,0:T(8,128)(2,1)S(1)}, bf16[2,224,128]{2,1,0:T(8,128)(2,1)S(1)}, u32[]{:S(2)}, u32[]{:S(2)}) collective-permute-start(bf16[2,224,128]{2,1,0:T(8,128)(2,1)S(1)} %get-tuple-element.98), channel_id=1, source_target_pairs={{0,12},{2,14},{4,8},{6,10},{8,4},{10,6},{12,0},{14,2},{16,28},{18,... | collective-permute-start | bytes 344072 | tf_op jit(solution)/shard_map/ppermute | solution.py:23
  48.5 6.3 %collective-permute-start.13 = (bf16[2,224,128]{2,1,0:T(8,128)(2,1)S(1)}, bf16[2,224,128]{2,1,0:T(8,128)(2,1)S(1)}, u32[]{:S(2)}, u32[]{:S(2)}) collective-permute-start(bf16[2,224,128]{2,1,0:T(8,128)(2,1)S(1)} %get-tuple-element.99), channel_id=1, source_target_pairs={{0,8},{2,10},{4,12},{6,14},{8,0},{10,2},{12,4},{14,6},{16,24},{18,... | collective-permute-start | bytes 344072 | tf_op jit(solution)/shard_map/ppermute | solution.py:23
  50.1 4.9 %collective-permute-start.12 = (bf16[2,224,128]{2,1,0:T(8,128)(2,1)S(1)}, bf16[2,224,128]{2,1,0:T(8,128)(2,1)S(1)}, u32[]{:S(2)}, u32[]{:S(2)}) collective-permute-start(bf16[2,224,128]{2,1,0:T(8,128)(2,1)S(1)} %get-tuple-element.100), channel_id=1, source_target_pairs={{0,4},{2,6},{4,0},{6,2},{8,12},{10,14},{12,8},{14,10},{16,20},{18,... | collective-permute-start | bytes 344072 | tf_op jit(solution)/shard_map/ppermute | solution.py:23
  55.1 1.5 %collective-permute-start.15 = (bf16[4,224,128]{2,1,0:T(8,128)(2,1)S(1)}, bf16[4,224,128]{2,1,0:T(8,128)(2,1)S(1)}, u32[]{:S(2)}, u32[]{:S(2)}) collective-permute-start(bf16[4,224,128]{2,1,0:T(8,128)(2,1)S(1)} %get-tuple-element.79), channel_id=1, source_target_pairs={{0,2},{2,0},{4,6},{6,4},{8,10},{10,8},{12,14},{14,12},{16,18},{18,... | collective-permute-start | bytes 688136 | tf_op jit(solution)/shard_map/ppermute | solution.py:23
  56.6 5.6 %collective-permute-start.16 = (bf16[1,224,128]{2,1,0:T(8,128)(2,1)S(1)}, bf16[1,224,128]{2,1,0:T(8,128)(2,1)S(1)}, u32[]{:S(2)}, u32[]{:S(2)}) collective-permute-start(bf16[1,224,128]{2,1,0:T(8,128)(2,1)S(1)} %get-tuple-element.80), channel_id=1, source_target_pairs={{0,4},{2,6},{4,0},{6,2},{8,12},{10,14},{12,8},{14,10},{16,20},{18,... | collective-permute-start | bytes 172040 | tf_op jit(solution)/shard_map/ppermute | solution.py:23
  58.1 4.3 %collective-permute-start.17 = (bf16[1,224,128]{2,1,0:T(8,128)(2,1)S(1)}, bf16[1,224,128]{2,1,0:T(8,128)(2,1)S(1)}, u32[]{:S(2)}, u32[]{:S(2)}) collective-permute-start(bf16[1,224,128]{2,1,0:T(8,128)(2,1)S(1)} %get-tuple-element.81), channel_id=1, source_target_pairs={{0,8},{2,10},{4,12},{6,14},{8,0},{10,2},{12,4},{14,6},{16,24},{18,... | collective-permute-start | bytes 172040 | tf_op jit(solution)/shard_map/ppermute | solution.py:23
  58.5 5.1 %collective-permute-start.18 = (bf16[1,224,128]{2,1,0:T(8,128)(2,1)S(1)}, bf16[1,224,128]{2,1,0:T(8,128)(2,1)S(1)}, u32[]{:S(2)}, u32[]{:S(2)}) collective-permute-start(bf16[1,224,128]{2,1,0:T(8,128)(2,1)S(1)} %get-tuple-element.82), channel_id=1, source_target_pairs={{0,12},{2,14},{4,8},{6,10},{8,4},{10,6},{12,0},{14,2},{16,28},{18,... | collective-permute-start | bytes 172040 | tf_op jit(solution)/shard_map/ppermute | solution.py:23
  63.6 4.2 %collective-permute-start.19 = (bf16[224,128]{1,0:T(8,128)(2,1)S(1)}, bf16[224,128]{1,0:T(8,128)(2,1)S(1)}, u32[]{:S(2)}, u32[]{:S(2)}) collective-permute-start(bf16[224,128]{1,0:T(8,128)(2,1)S(1)} %fusion.12), channel_id=1, source_target_pairs={{0,1},{1,0},{2,3},{3,2},{4,5},{5,4},{6,7},{7,6},{8,9},{9,8},{10,11... | collective-permute-start | bytes 172040 | tf_op jit(solution)/shard_map/ppermute | solution.py:19
  64.6 3.3 %collective-permute-start.20 = (bf16[224,128]{1,0:T(8,128)(2,1)S(1)}, bf16[224,128]{1,0:T(8,128)(2,1)S(1)}, u32[]{:S(2)}, u32[]{:S(2)}) collective-permute-start(bf16[224,128]{1,0:T(8,128)(2,1)S(1)} %fusion.13), channel_id=1, source_target_pairs={{0,2},{2,0},{4,6},{6,4},{8,10},{10,8},{12,14},{14,12},{16,18},{18,... | collective-permute-start | bytes 172040 | tf_op jit(solution)/shard_map/ppermute | solution.py:23
  67.9 5.1 %collective-permute-start.21 = (bf16[224,128]{1,0:T(8,128)(2,1)S(1)}, bf16[224,128]{1,0:T(8,128)(2,1)S(1)}, u32[]{:S(2)}, u32[]{:S(2)}) collective-permute-start(bf16[224,128]{1,0:T(8,128)(2,1)S(1)} %fusion.8), channel_id=1, source_target_pairs={{0,16},{2,18},{4,20},{6,22},{8,24},{10,26},{12,28},{14,30},{16,0},... | collective-permute-start | bytes 172040 | tf_op jit(solution)/shard_map/ppermute | solution.py:409

commit v12 on v11

--- a/solution.py
+++ b/solution.py
@@ -170,22 +170,21 @@
     return delta, lse.reshape(tokens), kl.reshape(tokens)
 
 
-def write_pieces(k, head_rows, delta_ref, upper, send_ref, keep_ref):
-    rows = send_ref.shape[1]
-    block = lax.dot_general(
-        head_rows, delta_ref[...], (((1,), (1,)), ((), ())), preferred_element_type=jnp.float32
-    )
-    low, high = block[:rows], block[rows:]
-    send_ref[k] = jnp.where(upper, low, high).astype(jnp.bfloat16)
-    keep_ref[k] = jnp.where(upper, high, low)
-
-
-def gradient_kernel(core_ref, head_ref, delta_ref, send_ref, keep_ref):
-    upper = core_ref[0] == 1
-    pairs, rows, _ = send_ref.shape
+def gradient_kernel(other, core_ref, head_ref, delta_ref, out_ref):
+    side = 1 - core_ref[0] if other else core_ref[0]
+    pairs, rows, _ = out_ref.shape
     for k in range(pairs):
-        head_rows = head_ref[2 * k * rows : 2 * (k + 1) * rows, :]
-        write_pieces(k, head_rows, delta_ref, upper, send_ref, keep_ref)
+        if rows % 16 == 0:
+            start = pl.multiple_of((2 * k + side) * rows, 16)
+            head_rows = head_ref[pl.ds(start, rows), :]
+        else:
+            head_rows = head_ref[2 * k * rows : 2 * (k + 1) * rows, :]
+        block = lax.dot_general(
+            head_rows, delta_ref[...], (((1,), (1,)), ((), ())), preferred_element_type=jnp.float32
+        )
+        if rows % 16:
+            block = jnp.where(side == 0, block[:rows], block[rows:])
+        out_ref[k] = block.astype(out_ref.dtype)
 
 
 def own_gradient_kernel(head_ref, delta_ref, out_ref):
@@ -201,20 +200,22 @@
         out_ref[k, 1] = block[rows:]
 
 
-def gradient(core, head, delta, run):
+def gradient(core, head, delta, run, other=False):
     rows = head.shape[0] // run
     shape = (run // 2, rows, delta.shape[0])
     in_vmem = pl.BlockSpec(memory_space=pltpu.VMEM)
     if core is None:
-        outs = pltpu.VMEM((run // 2, 2, *shape[1:]), jnp.float32)
+        out = pltpu.VMEM((run // 2, 2, *shape[1:]), jnp.float32)
+        kernel = own_gradient_kernel
     else:
-        outs = (pltpu.VMEM(shape, jnp.bfloat16), pltpu.VMEM(shape, jnp.float32))
+        out = pltpu.VMEM(shape, jnp.bfloat16 if other else jnp.float32)
+        kernel = functools.partial(gradient_kernel, other)
     arrays = [pltpu.with_memory_space_constraint(x, pltpu.VMEM) for x in (head, delta)]
     return pl.pallas_call(
-        own_gradient_kernel if core is None else gradient_kernel,
-        out_shape=outs,
+        kernel,
+        out_shape=out,
         in_specs=([] if core is None else [pl.BlockSpec(memory_space=pltpu.SMEM)]) + [in_vmem] * 2,
-        out_specs=in_vmem if core is None else (in_vmem, in_vmem),
+        out_specs=in_vmem,
         compiler_params=pltpu.CompilerParams(vmem_limit_bytes=VMEM_LIMIT),
         cost_estimate=pl.CostEstimate(
             flops=2 * head.size * delta.shape[0],
@@ -284,17 +285,19 @@
         return lax.dynamic_slice(hidden, (first, index * rows), (count, rows))
 
     quarter = half // 2
-    near, later = [
-        [
-            shift_tok(
-                columns_of(lax.rem(tok_index + d, tok_size), core * half + first, quarter),
-                d,
-                tok_size,
-            )
+
+    def fetched(first):
+        return [
+            columns_of(lax.rem(tok_index + d, tok_size), core * half + first, quarter)
             for d in range(1, tok_size)
         ]
-        for first in (0, quarter)
-    ]
+
+    def fetch(slices):
+        return [shift_tok(x, d, tok_size) for d, x in enumerate(slices, 1)]
+
+    wanted = fetched(0)
+    hidden, wanted = lax.optimization_barrier((hidden, wanted))
+    near, later = fetch(wanted), fetched(quarter)
     upper = []
     while 1 << len(upper) < vocab_size:
         upper.append((vocab_index & (1 << len(upper))) != 0)
@@ -306,10 +309,12 @@
     live_slot = jnp.arange(block_ids.shape[1], dtype=jnp.int32)[None, :] < counts[:, None]
     core_word = core.reshape(1)
     tok_is = [tok_index == d for d in range(tok_size)]
-    head, upper, apart_is, tok_is, column_block, live_slot, core_word = lax.optimization_barrier(
-        (head, upper, apart_is, tok_is, column_block, live_slot, core_word)
+    later, head, upper, apart_is, tok_is, column_block, live_slot, core_word = lax.optimization_barrier(
+        (later, head, upper, apart_is, tok_is, column_block, live_slot, core_word)
     )
     head_here = load(head)
+    later, head_here = lax.optimization_barrier((later, head_here))
+    later = fetch(later)
     near, head_here, column_block, teacher, hidden = lax.optimization_barrier(
         (near, head_here, column_block, teacher, hidden)
     )
@@ -364,8 +369,10 @@
     ]
     state = []
     for x in deltas[1:]:
-        send, keep = gradient(core_word, head_here, x, run)
-        own_others, send = lax.optimization_barrier((own_others, send))
+        send = gradient(core_word, head_here, x, run, other=True)
+        own_others, _ = lax.optimization_barrier((own_others, send))
+        x, _ = lax.optimization_barrier((x, send))
+        keep = gradient(core_word, head_here, x, run)
         state.append((keep, swap_vocab(send, 1, vocab_size)))
     all_delta = jnp.concatenate(deltas, axis=0)
 

time: 73.8 us -> 74 us (level)
  waiting for transfers between devices: 28.8 us -> 27.1 us
  local copies, waits for them, and re-layouts: 1.01 us -> 1.86 us
  starting transfers between devices: 25.6 us -> 26.4 us
    ppermute x7, waiting for transfers between devices: 16.2 us -> 14.9 us  [shift_tok(): lax.ppermute(x, 'tok', [(i, (i + offset) % size) for i in range(size)])]
    ppermute x14, waiting for transfers between devices: 10.1 us -> 8.97 us  [swap_vocab(): return lax.ppermute(x, 'vocab', [(i, i ^ bit) for i in range(size)])]
    dynamic_slice x1 -> x2, local copies, waits for them, and re-layouts: 0.98 us -> 1.83 us  [columns_of(): return lax.dynamic_slice(hidden, (first, index * rows), (count, rows))]
    pallas_call x2 -> x3, Pallas kernels: 3.15 us -> 3.32 us  [gradient(): pl.pallas_call(kernel, out_shape=out, in_specs=([] if core is None else [...]
  transfers between devices with their start and end apart: 22 -> 22, of which waited for: 16 -> 14; matrix products, arithmetic and copies ran while one was open for 7% -> 8% of each run, Pallas kernels for 13% -> 13%
where the time goes in v12:
time: 74 us; the launch traced here: 73.8 us
  waiting for transfers between devices  27.1 us (37%)
  starting transfers between devices  26.4 us (36%)
  Pallas kernels  11.1 us (15%)
  matrix products  4.01 us (5%)
  local copies, waits for them, and re-layouts  1.86 us (3%)
  other arithmetic  1.7 us (2%)
  between operations  1.62 us (2%)
    ppermute x7, waiting for transfers between devices, shift_tok(): lax.ppermute(x, 'tok', [(i, (i + offset) % size) for i in range(size)])  14.9 us
    ppermute x14, starting transfers between devices, swap_vocab(): return lax.ppermute(x, 'vocab', [(i, i ^ bit) for i in range(size)])  13.6 us
    ppermute x7, starting transfers between devices, shift_tok(): lax.ppermute(x, 'tok', [(i, (i + offset) % size) for i in range(size)])  10.2 us
    ppermute x14, waiting for transfers between devices, swap_vocab(): return lax.ppermute(x, 'vocab', [(i, i ^ bit) for i in range(size)])  8.97 us
    pallas_call x2, Pallas kernels, head_gradient(): pl.pallas_call(functools.partial(head_gradient_kernel, steps, start, widt...  3.9 us
    pallas_call x3, Pallas kernels, gradient(): pl.pallas_call(kernel, out_shape=out, in_specs=([] if core is None else [...  3.32 us
    ppermute x1, waiting for transfers between devices, per_device(): lax.ppermute(blocks[k].astype(jnp.bfloat16), 'vocab', pairs)  3.23 us
    dot_general x3, matrix products, per_device(): jnp.dot(x, head_here, preferred_element_type=jnp.float32)  3.12 us
  transfers between devices with their start and end apart: 22, of which 14 were waited for; matrix products, arithmetic and copies ran while one was open for 8% of the time, Pallas kernels for 13%

profile of v12, /device:TPU:0, one launch (start us, length us, event | category | flops | bytes accessed | tf_op | source)
XLA Modules:
  0.0 73.8 jit_solution(1131193603391416193)
XLA Ops:
  0.6 0.9 %dynamic_slice.6 = bf16[32,1792]{1,0:T(8,128)(2,1)S(1)} dynamic-slice(bf16[128,3584]{1,0:T(8,128)(2,1)} %param.5, s32[]{:T(128)S(6)} %select_n.240, s32[]{:T(128)S(6)} %select_n.241), dynamic_slice_sizes={32,1792} | dynamic-slice | bytes 229380 | tf_op jit(solution)/shard_map/dynamic_slice | solution.py:285
  1.6 3.0 %collective-permute-start = (bf16[32,1792]{1,0:T(8,128)(2,1)S(1)}, bf16[32,1792]{1,0:T(8,128)(2,1)S(1)}, u32[]{:S(2)}, u32[]{:S(2)}) collective-permute-start(bf16[32,1792]{1,0:T(8,128)(2,1)S(1)} %dynamic_slice.6), channel_id=1, source_target_pairs={{0,1},{1,0},{2,3},{3,2},{4,5},{5,4},{6,7},{7,6},{8,9},{9,8},{10,11... | collective-permute-start | bytes 344072 | tf_op jit(solution)/shard_map/ppermute | solution.py:19
  5.2 0.9 %dynamic_slice.7 = bf16[32,1792]{1,0:T(8,128)(2,1)S(1)} dynamic-slice(bf16[128,3584]{1,0:T(8,128)(2,1)} %param.5, s32[]{:T(128)S(6)} %select_n.242, s32[]{:T(128)S(6)} %select_n.241), dynamic_slice_sizes={32,1792} | dynamic-slice | bytes 229380 | tf_op jit(solution)/shard_map/dynamic_slice | solution.py:285
  6.1 2.6 %load_head.1.head_ref = bf16[1792,1536]{1,0:T(8,128)(2,1)S(1)} custom-call(bf16[1792,1536]{1,0:T(8,128)(2,1)} %head_ref), custom_call_target="tpu_custom_call" | custom-call | bytes 11010048 | tf_op jit(solution)/shard_map/load_head/pallas_call | solution.py:67
  8.8 0.0 copy-start
  8.8 0.1 collective-permute-start.2
  8.9 1.0 %fusion.17 = f32[32,1536]{1,0:T(8,128)S(1)} fusion(bf16[32,1792]{1,0:T(8,128)(2,1)S(1)} %collective-permute-done, bf16[1792,1536]{1,0:T(8,128)(2,1)S(1)} %load_head.1.head_ref), kind=kOutput, calls=%fused_computation.71 | convolution fusion | flops 176160768 | bytes 5816320 | tf_op jit(solution)/shard_map/dot_general | solution.py:321
  9.9 2.0 %collective-permute-start.1 = (f32[32,1536]{1,0:T(8,128)S(1)}, f32[32,1536]{1,0:T(8,128)S(1)}, u32[]{:S(2)}, u32[]{:S(2)}) collective-permute-start(f32[32,1536]{1,0:T(8,128)S(1)} %fusion.17), channel_id=1, source_target_pairs={{0,1},{1,0},{2,3},{3,2},{4,5},{5,4},{6,7},{7,6},{8,9},{9,8},{10,11... | collective-permute-start | bytes 589832 | tf_op jit(solution)/shard_map/ppermute | solution.py:19
  11.9 3.0 %collective-permute-done.2 = bf16[32,1792]{1,0:T(8,128)(2,1)S(1)} collective-permute-done((bf16[32,1792]{1,0:T(8,128)(2,1)S(1)}, bf16[32,1792]{1,0:T(8,128)(2,1)S(1)}, u32[]{:S(2)}, u32[]{:S(2)}) %collective-permute-start.2) | collective-permute-done | bytes 114720 | tf_op jit(solution)/shard_map/ppermute | solution.py:19
  14.9 1.0 %fusion.18 = f32[32,1536]{1,0:T(8,128)S(1)} fusion(bf16[32,1792]{1,0:T(8,128)(2,1)S(1)} %collective-permute-done.2, bf16[1792,1536]{1,0:T(8,128)(2,1)S(1)} %load_head.1.head_ref), kind=kOutput, calls=%fused_computation.72 | convolution fusion | flops 176160768 | bytes 5816320 | tf_op jit(solution)/shard_map/dot_general | solution.py:330
  16.0 0.1 collective-permute-start.3
  16.1 0.1 collective-permute-start.4
  16.2 0.9 %fusion.20.own_ref = f32[128,1536]{1,0:T(8,128)S(1)} fusion(bf16[128,1792]{1,0:T(8,128)(2,1)S(1)} %slice_select_fusion, bf16[1792,1536]{1,0:T(8,128)(2,1)S(1)} %load_head.1.head_ref), kind=kOutput, calls=%fused_computation.74 | convolution fusion | flops 704643072 | bytes 6750208 | tf_op jit(solution)/shard_map/dot_general | solution.py:336
  17.1 0.1 and_reduce_fusion
  17.2 0.3 fusion
  17.6 0.1 collective-permute-done.4
  17.6 1.1 %fusion.19 = f32[64,1536]{1,0:T(8,128)S(1)} fusion(bf16[64,1792]{1,0:T(8,128)(2,1)S(1)} %collective-permute-done.4, bf16[1792,1536]{1,0:T(8,128)(2,1)S(1)} %load_head.1.head_ref), kind=kOutput, calls=%fused_computation.73 | convolution fusion | flops 352321536 | bytes 6127616 | tf_op jit(solution)/shard_map/dot_general | solution.py:330
  18.7 2.0 %collective-permute-start.5 = (f32[64,1536]{1,0:T(8,128)S(1)}, f32[64,1536]{1,0:T(8,128)S(1)}, u32[]{:S(2)}, u32[]{:S(2)}) collective-permute-start(f32[64,1536]{1,0:T(8,128)S(1)} %fusion.19), channel_id=1, source_target_pairs={{0,1},{1,0},{2,3},{3,2},{4,5},{5,4},{6,7},{7,6},{8,9},{9,8},{10,11... | collective-permute-start | bytes 1179656 | tf_op jit(solution)/shard_map/ppermute | solution.py:19
  20.7 0.1 pad_maximum_fusion.refs_0_
  20.8 1.1 %collective-permute-done.3.refs_1_ = f32[32,1536]{1,0:T(8,128)S(1)} collective-permute-done((f32[32,1536]{1,0:T(8,128)S(1)}, f32[32,1536]{1,0:T(8,128)S(1)}, u32[]{:S(2)}, u32[]{:S(2)}) %collective-permute-start.3) | collective-permute-done | bytes 196640 | tf_op jit(solution)/shard_map/ppermute | solution.py:19
  21.9 8.5 %collective-permute-done.5.refs_2_ = f32[64,1536]{1,0:T(8,128)S(1)} collective-permute-done((f32[64,1536]{1,0:T(8,128)S(1)}, f32[64,1536]{1,0:T(8,128)S(1)}, u32[]{:S(2)}, u32[]{:S(2)}) %collective-permute-start.5) | collective-permute-done | bytes 393248 | tf_op jit(solution)/shard_map/ppermute | solution.py:19
  30.4 0.4 local_stats.1
  30.8 0.0 collective-permute-start.6
  30.9 1.1 %collective-permute-done.6 = f32[1,4,128]{2,1,0:T(4,128)S(1)} collective-permute-done((f32[1,4,128]{2,1,0:T(4,128)S(1)}, f32[1,4,128]{2,1,0:T(4,128)S(1)}, u32[]{:S(2)}, u32[]{:S(2)}) %collective-permute-start.6) | collective-permute-done | bytes 2080 | tf_op jit(solution)/shard_map/ppermute | solution.py:23
  32.0 1.5 %collective-permute-start.9 = (f32[2,4,128]{2,1,0:T(4,128)S(1)}, f32[2,4,128]{2,1,0:T(4,128)S(1)}, u32[]{:S(2)}, u32[]{:S(2)}) collective-permute-start(f32[2,4,128]{2,1,0:T(4,128)S(1)} %pad_maximum_fusion.4), channel_id=1, source_target_pairs={{0,4},{2,6},{4,0},{6,2},{8,12},{10,14},{12,8},{14,10},{16,20},{18,... | collective-permute-start | bytes 12296 | tf_op jit(solution)/shard_map/ppermute | solution.py:23
  33.5 1.6 %collective-permute-start.8 = (f32[2,4,128]{2,1,0:T(4,128)S(1)}, f32[2,4,128]{2,1,0:T(4,128)S(1)}, u32[]{:S(2)}, u32[]{:S(2)}) collective-permute-start(f32[2,4,128]{2,1,0:T(4,128)S(1)} %pad_maximum_fusion.4), channel_id=1, source_target_pairs={{0,8},{2,10},{4,12},{6,14},{8,0},{10,2},{12,4},{14,6},{16,24},{18,... | collective-permute-start | bytes 12296 | tf_op jit(solution)/shard_map/ppermute | solution.py:23
  35.1 0.5 collective-permute-start.7
  35.6 0.1 collective-permute-done.9
  35.7 1.5 %collective-permute-done.8 = f32[2,4,128]{2,1,0:T(4,128)S(1)} collective-permute-done((f32[2,4,128]{2,1,0:T(4,128)S(1)}, f32[2,4,128]{2,1,0:T(4,128)S(1)}, u32[]{:S(2)}, u32[]{:S(2)}) %collective-permute-start.8) | collective-permute-done | bytes 4128 | tf_op jit(solution)/shard_map/ppermute | solution.py:23
  37.1 2.5 %collective-permute-done.7 = f32[2,4,128]{2,1,0:T(4,128)S(1)} collective-permute-done((f32[2,4,128]{2,1,0:T(4,128)S(1)}, f32[2,4,128]{2,1,0:T(4,128)S(1)}, u32[]{:S(2)}, u32[]{:S(2)}) %collective-permute-start.7) | collective-permute-done | bytes 4128 | tf_op jit(solution)/shard_map/ppermute | solution.py:23
  39.6 2.7 %collective-permute-start.10 = (f32[8,4,128]{2,1,0:T(4,128)S(1)}, f32[8,4,128]{2,1,0:T(4,128)S(1)}, u32[]{:S(2)}, u32[]{:S(2)}) collective-permute-start(f32[8,4,128]{2,1,0:T(4,128)S(1)} %pad_maximum_fusion.3), channel_id=1, source_target_pairs={{0,16},{2,18},{4,20},{6,22},{8,24},{10,26},{12,28},{14,30},{16,0},... | collective-permute-start | bytes 49160 | tf_op jit(solution)/shard_map/ppermute | solution.py:23
  42.3 2.1 %collective-permute-done.10 = f32[8,4,128]{2,1,0:T(4,128)S(1)} collective-permute-done((f32[8,4,128]{2,1,0:T(4,128)S(1)}, f32[8,4,128]{2,1,0:T(4,128)S(1)}, u32[]{:S(2)}, u32[]{:S(2)}) %collective-permute-start.10) | collective-permute-done | bytes 16416 | tf_op jit(solution)/shard_map/ppermute | solution.py:23
  44.4 0.9 %delta.1 = (bf16[128,1536]{1,0:T(8,128)(2,1)S(1)}, f32[1,128]{1,0:T(1,128)}, f32[1,128]{1,0:T(1,128)}) custom-call(f32[16,4,128]{2,1,0:T(4,128)S(1)} %pad_maximum_fusion.2.gathered_ref, f32[128,1536]{1,0:T(8,128)S(1)} %get-tuple-element.80.logits_ref, bf16[128,1536]{1,0:T(8,128)(2,1)S(1)} %get-tuple-element.74.kept_ref), custom_call_target="tpu_custom_call" | custom-call | flops 1572864 | bytes 1572864 | tf_op jit(solution)/shard_map/delta/pallas_call | solution.py:155
  45.3 1.7 %collective-permute-start.11 = (bf16[128,1536]{1,0:T(8,128)(2,1)S(1)}, bf16[128,1536]{1,0:T(8,128)(2,1)S(1)}, u32[]{:S(2)}, u32[]{:S(2)}) collective-permute-start(bf16[128,1536]{1,0:T(8,128)(2,1)S(1)} %get-tuple-element.84.delta_ref), channel_id=1, source_target_pairs={{0,1},{1,0},{2,3},{3,2},{4,5},{5,4},{6,7},{7,6},{8,9},{9,8},{10,11... | collective-permute-start | bytes 1179656 | tf_op jit(solution)/shard_map/ppermute | solution.py:19
  47.1 1.6 %partial_gradient.5 = f32[4,2,224,128]{3,2,1,0:T(8,128)S(1)} custom-call(bf16[1792,1536]{1,0:T(8,128)(2,1)S(1)} %load_head.1.head_ref, bf16[128,1536]{1,0:T(8,128)(2,1)S(1)} %get-tuple-element.84.delta_ref), custom_call_target="tpu_custom_call" | custom-call | flops 704643072 | bytes 5898240 | tf_op jit(solution)/shard_map/partial_gradient/pallas_call | solution.py:214
  48.6 0.1 fusion.11
  48.7 0.5 collective-permute-start.19
  49.2 1.4 %collective-permute-start.17 = (bf16[2,224,128]{2,1,0:T(8,128)(2,1)S(1)}, bf16[2,224,128]{2,1,0:T(8,128)(2,1)S(1)}, u32[]{:S(2)}, u32[]{:S(2)}) collective-permute-start(bf16[2,224,128]{2,1,0:T(8,128)(2,1)S(1)} %get-tuple-element.105), channel_id=1, source_target_pairs={{0,4},{2,6},{4,0},{6,2},{8,12},{10,14},{12,8},{14,10},{16,20},{18,... | collective-permute-start | bytes 344072 | tf_op jit(solution)/shard_map/ppermute | solution.py:23
  50.6 1.6 %collective-permute-start.18 = (bf16[2,224,128]{2,1,0:T(8,128)(2,1)S(1)}, bf16[2,224,128]{2,1,0:T(8,128)(2,1)S(1)}, u32[]{:S(2)}, u32[]{:S(2)}) collective-permute-start(bf16[2,224,128]{2,1,0:T(8,128)(2,1)S(1)} %get-tuple-element.106), channel_id=1, source_target_pairs={{0,8},{2,10},{4,12},{6,14},{8,0},{10,2},{12,4},{14,6},{16,24},{18,... | collective-permute-start | bytes 344072 | tf_op jit(solution)/shard_map/ppermute | solution.py:23
  52.3 1.4 %collective-permute-done.11.delta_ref = bf16[128,1536]{1,0:T(8,128)(2,1)S(1)} collective-permute-done((bf16[128,1536]{1,0:T(8,128)(2,1)S(1)}, bf16[128,1536]{1,0:T(8,128)(2,1)S(1)}, u32[]{:S(2)}, u32[]{:S(2)}) %collective-permute-start.11) | collective-permute-done | bytes 393248 | tf_op jit(solution)/shard_map/ppermute | solution.py:19
  53.6 0.9 %partial_gradient.3 = bf16[4,224,128]{2,1,0:T(8,128)(2,1)S(1)} custom-call(s32[1]{0:T(128)} %bitcast.1.core_ref, bf16[1792,1536]{1,0:T(8,128)(2,1)S(1)} %load_head.1.head_ref, bf16[128,1536]{1,0:T(8,128)(2,1)S(1)} %collective-permute-done.11.delta_ref), custom_call_target="tpu_custom_call" | custom-call | flops 704643072 | bytes 5898240 | tf_op jit(solution)/shard_map/partial_gradient/pallas_call | solution.py:214
  54.5 0.1 collective-permute-start.12
  54.6 0.9 %partial_gradient.4 = f32[4,224,128]{2,1,0:T(8,128)S(1)} custom-call(s32[1]{0:T(128)} %bitcast.1.core_ref, bf16[1792,1536]{1,0:T(8,128)(2,1)S(1)} %load_head.1.head_ref, bf16[128,1536]{1,0:T(8,128)(2,1)S(1)} %collective-permute-done.11.delta_ref), custom_call_target="tpu_custom_call" | custom-call | flops 704643072 | bytes 5898240 | tf_op jit(solution)/shard_map/partial_gradient/pallas_call | solution.py:214
  55.5 0.0 collective-permute-done.17
  55.5 0.1 pad_maximum_fusion.1.refs_1_
  55.6 0.1 fusion.5
  55.7 0.4 collective-permute-done.12
  56.1 0.1 convert_add_fusion
  56.2 0.6 collective-permute-start.13
  56.8 1.2 %collective-permute-start.14 = (bf16[1,224,128]{2,1,0:T(8,128)(2,1)S(1)}, bf16[1,224,128]{2,1,0:T(8,128)(2,1)S(1)}, u32[]{:S(2)}, u32[]{:S(2)}) collective-permute-start(bf16[1,224,128]{2,1,0:T(8,128)(2,1)S(1)} %get-tuple-element.87), channel_id=1, source_target_pairs={{0,8},{2,10},{4,12},{6,14},{8,0},{10,2},{12,4},{14,6},{16,24},{18,... | collective-permute-start | bytes 172040 | tf_op jit(solution)/shard_map/ppermute | solution.py:23
  58.0 1.7 %collective-permute-start.15 = (bf16[1,224,128]{2,1,0:T(8,128)(2,1)S(1)}, bf16[1,224,128]{2,1,0:T(8,128)(2,1)S(1)}, u32[]{:S(2)}, u32[]{:S(2)}) collective-permute-start(bf16[1,224,128]{2,1,0:T(8,128)(2,1)S(1)} %get-tuple-element.88), channel_id=1, source_target_pairs={{0,12},{2,14},{4,8},{6,10},{8,4},{10,6},{12,0},{14,2},{16,28},{18,... | collective-permute-start | bytes 172040 | tf_op jit(solution)/shard_map/ppermute | solution.py:23
  59.7 2.1 %head_gradient.2.refs_2_ = bf16[1792,1536]{1,0:T(8,128)(2,1)} custom-call(bf16[256,1792]{1,0:T(8,128)(2,1)S(1)} %pad_maximum_fusion.refs_0_, bf16[256,1536]{1,0:T(8,128)(2,1)S(1)} %pad_maximum_fusion.1.refs_1_), custom_call_target="tpu_custom_call" | custom-call | flops 805306368 | bytes 4849664 | tf_op jit(solution)/shard_map/head_gradient/pallas_call | solution.py:253
  61.8 0.0 collective-permute-done.13
  61.8 0.0 collective-permute-done.14
  61.8 1.2 %collective-permute-done.15 = bf16[1,224,128]{2,1,0:T(8,128)(2,1)S(1)} collective-permute-done((bf16[1,224,128]{2,1,0:T(8,128)(2,1)S(1)}, bf16[1,224,128]{2,1,0:T(8,128)(2,1)S(1)}, u32[]{:S(2)}, u32[]{:S(2)}) %collective-permute-start.15) | collective-permute-done | bytes 57376 | tf_op jit(solution)/shard_map/ppermute | solution.py:23
  63.0 0.1 fusion.12
  63.1 1.3 %collective-permute-start.16 = (bf16[224,128]{1,0:T(8,128)(2,1)S(1)}, bf16[224,128]{1,0:T(8,128)(2,1)S(1)}, u32[]{:S(2)}, u32[]{:S(2)}) collective-permute-start(bf16[224,128]{1,0:T(8,128)(2,1)S(1)} %fusion.12), channel_id=1, source_target_pairs={{0,1},{1,0},{2,3},{3,2},{4,5},{5,4},{6,7},{7,6},{8,9},{9,8},{10,11... | collective-permute-start | bytes 172040 | tf_op jit(solution)/shard_map/ppermute | solution.py:19
  64.5 0.1 collective-permute-start.20
  64.5 1.8 %head_gradient.3 = bf16[1792,1536]{1,0:T(8,128)(2,1)} custom-call(bf16[256,1792]{1,0:T(8,128)(2,1)S(1)} %pad_maximum_fusion.refs_0_, bf16[256,1536]{1,0:T(8,128)(2,1)S(1)} %pad_maximum_fusion.1.refs_1_, bf16[1792,1536]{1,0:T(8,128)(2,1)} %head_gradient.2.refs_2_), custom_call_target="tpu_custom_call", output_to_operand_aliasing={{}: (2, {})} | custom-call | flops 603979776 | bytes 4063232 | tf_op jit(solution)/shard_map/head_gradient/pallas_call | solution.py:253
  66.4 1.0 %collective-permute-done.16 = bf16[224,128]{1,0:T(8,128)(2,1)S(1)} collective-permute-done((bf16[224,128]{1,0:T(8,128)(2,1)S(1)}, bf16[224,128]{1,0:T(8,128)(2,1)S(1)}, u32[]{:S(2)}, u32[]{:S(2)}) %collective-permute-start.16) | collective-permute-done | bytes 57376 | tf_op jit(solution)/shard_map/ppermute | solution.py:19
  67.3 0.0 collective-permute-done.20
  67.4 2.5 %collective-permute-start.21 = (bf16[224,128]{1,0:T(8,128)(2,1)S(1)}, bf16[224,128]{1,0:T(8,128)(2,1)S(1)}, u32[]{:S(2)}, u32[]{:S(2)}) collective-permute-start(bf16[224,128]{1,0:T(8,128)(2,1)S(1)} %fusion.8), channel_id=1, source_target_pairs={{0,16},{2,18},{4,20},{6,22},{8,24},{10,26},{12,28},{14,30},{16,0},... | collective-permute-start | bytes 172040 | tf_op jit(solution)/shard_map/ppermute | solution.py:416
  69.9 3.2 %collective-permute-done.21 = bf16[224,128]{1,0:T(8,128)(2,1)S(1)} collective-permute-done((bf16[224,128]{1,0:T(8,128)(2,1)S(1)}, bf16[224,128]{1,0:T(8,128)(2,1)S(1)}, u32[]{:S(2)}, u32[]{:S(2)}) %collective-permute-start.21) | collective-permute-done | bytes 57376 | tf_op jit(solution)/shard_map/ppermute | solution.py:416
  73.1 0.7 fusion.7
  (25 shorter events, 0.3 us)
Async XLA Ops:
  1.6 7.3 %collective-permute-start = (bf16[32,1792]{1,0:T(8,128)(2,1)S(1)}, bf16[32,1792]{1,0:T(8,128)(2,1)S(1)}, u32[]{:S(2)}, u32[]{:S(2)}) collective-permute-start(bf16[32,1792]{1,0:T(8,128)(2,1)S(1)} %dynamic_slice.6), channel_id=1, source_target_pairs={{0,1},{1,0},{2,3},{3,2},{4,5},{5,4},{6,7},{7,6},{8,9},{9,8},{10,11... | collective-permute-start | bytes 344072 | tf_op jit(solution)/shard_map/ppermute | solution.py:19
  8.8 7.4 %copy-start = (bf16[128,3584]{1,0:T(8,128)(2,1)S(1)}, bf16[128,3584]{1,0:T(8,128)(2,1)}, u32[]{:S(2)}) copy-start(bf16[128,3584]{1,0:T(8,128)(2,1)} %param.5) | copy-start | bytes 2752516
  8.8 6.1 %collective-permute-start.2 = (bf16[32,1792]{1,0:T(8,128)(2,1)S(1)}, bf16[32,1792]{1,0:T(8,128)(2,1)S(1)}, u32[]{:S(2)}, u32[]{:S(2)}) collective-permute-start(bf16[32,1792]{1,0:T(8,128)(2,1)S(1)} %dynamic_slice.7), channel_id=1, source_target_pairs={{0,1},{1,0},{2,3},{3,2},{4,5},{5,4},{6,7},{7,6},{8,9},{9,8},{10,11... | collective-permute-start | bytes 344072 | tf_op jit(solution)/shard_map/ppermute | solution.py:19
  9.9 12.0 %collective-permute-start.1 = (f32[32,1536]{1,0:T(8,128)S(1)}, f32[32,1536]{1,0:T(8,128)S(1)}, u32[]{:S(2)}, u32[]{:S(2)}) collective-permute-start(f32[32,1536]{1,0:T(8,128)S(1)} %fusion.17), channel_id=1, source_target_pairs={{0,1},{1,0},{2,3},{3,2},{4,5},{5,4},{6,7},{7,6},{8,9},{9,8},{10,11... | collective-permute-start | bytes 589832 | tf_op jit(solution)/shard_map/ppermute | solution.py:19
  16.0 1.2 %copy-start.2 = (s32[1,16]{1,0:T(1,128)S(1)}, s32[1,16]{1,0:T(1,128)}, u32[]{:S(2)}) copy-start(s32[1,16]{1,0:T(1,128)} %param.8) | copy-start | bytes 196
  16.0 1.3 %copy-start.1 = (bf16[128,1536]{1,0:T(8,128)(2,1)S(1)}, bf16[128,1536]{1,0:T(8,128)(2,1)}, u32[]{:S(2)}) copy-start(bf16[128,1536]{1,0:T(8,128)(2,1)} %param.7) | copy-start | bytes 1179652
  16.0 5.9 %collective-permute-start.3 = (f32[32,1536]{1,0:T(8,128)S(1)}, f32[32,1536]{1,0:T(8,128)S(1)}, u32[]{:S(2)}, u32[]{:S(2)}) collective-permute-start(f32[32,1536]{1,0:T(8,128)S(1)} %fusion.18), channel_id=1, source_target_pairs={{0,1},{1,0},{2,3},{3,2},{4,5},{5,4},{6,7},{7,6},{8,9},{9,8},{10,11... | collective-permute-start | bytes 589832 | tf_op jit(solution)/shard_map/ppermute | solution.py:19
  16.1 1.6 %collective-permute-start.4 = (bf16[64,1792]{1,0:T(8,128)(2,1)S(1)}, bf16[64,1792]{1,0:T(8,128)(2,1)S(1)}, u32[]{:S(2)}, u32[]{:S(2)}) collective-permute-start(bf16[64,1792]{1,0:T(8,128)(2,1)S(1)} %constant_dynamic-update-slice_fusion), channel_id=1, source_target_pairs={{0,2},{2,0},{4,6},{6,4},{8,10},{10,8},{12,14},{14,12},{16,18},{18,... | collective-permute-start | bytes 688136 | tf_op jit(solution)/shard_map/ppermute | solution.py:23
  18.7 11.7 %collective-permute-start.5 = (f32[64,1536]{1,0:T(8,128)S(1)}, f32[64,1536]{1,0:T(8,128)S(1)}, u32[]{:S(2)}, u32[]{:S(2)}) collective-permute-start(f32[64,1536]{1,0:T(8,128)S(1)} %fusion.19), channel_id=1, source_target_pairs={{0,1},{1,0},{2,3},{3,2},{4,5},{5,4},{6,7},{7,6},{8,9},{9,8},{10,11... | collective-permute-start | bytes 1179656 | tf_op jit(solution)/shard_map/ppermute | solution.py:19
  30.8 1.2 %collective-permute-start.6 = (f32[1,4,128]{2,1,0:T(4,128)S(1)}, f32[1,4,128]{2,1,0:T(4,128)S(1)}, u32[]{:S(2)}, u32[]{:S(2)}) collective-permute-start(f32[1,4,128]{2,1,0:T(4,128)S(1)} %bitcast.44), channel_id=1, source_target_pairs={{0,2},{2,0},{4,6},{6,4},{8,10},{10,8},{12,14},{14,12},{16,18},{18,... | collective-permute-start | bytes 6152 | tf_op jit(solution)/shard_map/ppermute | solution.py:23
  32.0 3.7 %collective-permute-start.9 = (f32[2,4,128]{2,1,0:T(4,128)S(1)}, f32[2,4,128]{2,1,0:T(4,128)S(1)}, u32[]{:S(2)}, u32[]{:S(2)}) collective-permute-start(f32[2,4,128]{2,1,0:T(4,128)S(1)} %pad_maximum_fusion.4), channel_id=1, source_target_pairs={{0,4},{2,6},{4,0},{6,2},{8,12},{10,14},{12,8},{14,10},{16,20},{18,... | collective-permute-start | bytes 12296 | tf_op jit(solution)/shard_map/ppermute | solution.py:23
  33.5 3.6 %collective-permute-start.8 = (f32[2,4,128]{2,1,0:T(4,128)S(1)}, f32[2,4,128]{2,1,0:T(4,128)S(1)}, u32[]{:S(2)}, u32[]{:S(2)}) collective-permute-start(f32[2,4,128]{2,1,0:T(4,128)S(1)} %pad_maximum_fusion.4), channel_id=1, source_target_pairs={{0,8},{2,10},{4,12},{6,14},{8,0},{10,2},{12,4},{14,6},{16,24},{18,... | collective-permute-start | bytes 12296 | tf_op jit(solution)/shard_map/ppermute | solution.py:23
  35.1 4.5 %collective-permute-start.7 = (f32[2,4,128]{2,1,0:T(4,128)S(1)}, f32[2,4,128]{2,1,0:T(4,128)S(1)}, u32[]{:S(2)}, u32[]{:S(2)}) collective-permute-start(f32[2,4,128]{2,1,0:T(4,128)S(1)} %pad_maximum_fusion.4), channel_id=1, source_target_pairs={{0,12},{2,14},{4,8},{6,10},{8,4},{10,6},{12,0},{14,2},{16,28},{18,... | collective-permute-start | bytes 12296 | tf_op jit(solution)/shard_map/ppermute | solution.py:23
  39.6 4.8 %collective-permute-start.10 = (f32[8,4,128]{2,1,0:T(4,128)S(1)}, f32[8,4,128]{2,1,0:T(4,128)S(1)}, u32[]{:S(2)}, u32[]{:S(2)}) collective-permute-start(f32[8,4,128]{2,1,0:T(4,128)S(1)} %pad_maximum_fusion.3), channel_id=1, source_target_pairs={{0,16},{2,18},{4,20},{6,22},{8,24},{10,26},{12,28},{14,30},{16,0},... | collective-permute-start | bytes 49160 | tf_op jit(solution)/shard_map/ppermute | solution.py:23
  45.3 8.3 %collective-permute-start.11 = (bf16[128,1536]{1,0:T(8,128)(2,1)S(1)}, bf16[128,1536]{1,0:T(8,128)(2,1)S(1)}, u32[]{:S(2)}, u32[]{:S(2)}) collective-permute-start(bf16[128,1536]{1,0:T(8,128)(2,1)S(1)} %get-tuple-element.84.delta_ref), channel_id=1, source_target_pairs={{0,1},{1,0},{2,3},{3,2},{4,5},{5,4},{6,7},{7,6},{8,9},{9,8},{10,11... | collective-permute-start | bytes 1179656 | tf_op jit(solution)/shard_map/ppermute | solution.py:19
  48.7 6.8 %collective-permute-start.19 = (bf16[2,224,128]{2,1,0:T(8,128)(2,1)S(1)}, bf16[2,224,128]{2,1,0:T(8,128)(2,1)S(1)}, u32[]{:S(2)}, u32[]{:S(2)}) collective-permute-start(bf16[2,224,128]{2,1,0:T(8,128)(2,1)S(1)} %get-tuple-element.104), channel_id=1, source_target_pairs={{0,12},{2,14},{4,8},{6,10},{8,4},{10,6},{12,0},{14,2},{16,28},{18,... | collective-permute-start | bytes 344072 | tf_op jit(solution)/shard_map/ppermute | solution.py:23
  49.2 6.3 %collective-permute-start.17 = (bf16[2,224,128]{2,1,0:T(8,128)(2,1)S(1)}, bf16[2,224,128]{2,1,0:T(8,128)(2,1)S(1)}, u32[]{:S(2)}, u32[]{:S(2)}) collective-permute-start(bf16[2,224,128]{2,1,0:T(8,128)(2,1)S(1)} %get-tuple-element.105), channel_id=1, source_target_pairs={{0,4},{2,6},{4,0},{6,2},{8,12},{10,14},{12,8},{14,10},{16,20},{18,... | collective-permute-start | bytes 344072 | tf_op jit(solution)/shard_map/ppermute | solution.py:23
  50.6 4.9 %collective-permute-start.18 = (bf16[2,224,128]{2,1,0:T(8,128)(2,1)S(1)}, bf16[2,224,128]{2,1,0:T(8,128)(2,1)S(1)}, u32[]{:S(2)}, u32[]{:S(2)}) collective-permute-start(bf16[2,224,128]{2,1,0:T(8,128)(2,1)S(1)} %get-tuple-element.106), channel_id=1, source_target_pairs={{0,8},{2,10},{4,12},{6,14},{8,0},{10,2},{12,4},{14,6},{16,24},{18,... | collective-permute-start | bytes 344072 | tf_op jit(solution)/shard_map/ppermute | solution.py:23
  54.5 1.6 %collective-permute-start.12 = (bf16[4,224,128]{2,1,0:T(8,128)(2,1)S(1)}, bf16[4,224,128]{2,1,0:T(8,128)(2,1)S(1)}, u32[]{:S(2)}, u32[]{:S(2)}) collective-permute-start(bf16[4,224,128]{2,1,0:T(8,128)(2,1)S(1)} %partial_gradient.3), channel_id=1, source_target_pairs={{0,2},{2,0},{4,6},{6,4},{8,10},{10,8},{12,14},{14,12},{16,18},{18,... | collective-permute-start | bytes 688136 | tf_op jit(solution)/shard_map/ppermute | solution.py:23
  56.2 5.6 %collective-permute-start.13 = (bf16[1,224,128]{2,1,0:T(8,128)(2,1)S(1)}, bf16[1,224,128]{2,1,0:T(8,128)(2,1)S(1)}, u32[]{:S(2)}, u32[]{:S(2)}) collective-permute-start(bf16[1,224,128]{2,1,0:T(8,128)(2,1)S(1)} %get-tuple-element.86), channel_id=1, source_target_pairs={{0,4},{2,6},{4,0},{6,2},{8,12},{10,14},{12,8},{14,10},{16,20},{18,... | collective-permute-start | bytes 172040 | tf_op jit(solution)/shard_map/ppermute | solution.py:23
  56.8 5.0 %collective-permute-start.14 = (bf16[1,224,128]{2,1,0:T(8,128)(2,1)S(1)}, bf16[1,224,128]{2,1,0:T(8,128)(2,1)S(1)}, u32[]{:S(2)}, u32[]{:S(2)}) collective-permute-start(bf16[1,224,128]{2,1,0:T(8,128)(2,1)S(1)} %get-tuple-element.87), channel_id=1, source_target_pairs={{0,8},{2,10},{4,12},{6,14},{8,0},{10,2},{12,4},{14,6},{16,24},{18,... | collective-permute-start | bytes 172040 | tf_op jit(solution)/shard_map/ppermute | solution.py:23
  58.0 5.1 %collective-permute-start.15 = (bf16[1,224,128]{2,1,0:T(8,128)(2,1)S(1)}, bf16[1,224,128]{2,1,0:T(8,128)(2,1)S(1)}, u32[]{:S(2)}, u32[]{:S(2)}) collective-permute-start(bf16[1,224,128]{2,1,0:T(8,128)(2,1)S(1)} %get-tuple-element.88), channel_id=1, source_target_pairs={{0,12},{2,14},{4,8},{6,10},{8,4},{10,6},{12,0},{14,2},{16,28},{18,... | collective-permute-start | bytes 172040 | tf_op jit(solution)/shard_map/ppermute | solution.py:23
  63.1 4.2 %collective-permute-start.16 = (bf16[224,128]{1,0:T(8,128)(2,1)S(1)}, bf16[224,128]{1,0:T(8,128)(2,1)S(1)}, u32[]{:S(2)}, u32[]{:S(2)}) collective-permute-start(bf16[224,128]{1,0:T(8,128)(2,1)S(1)} %fusion.12), channel_id=1, source_target_pairs={{0,1},{1,0},{2,3},{3,2},{4,5},{5,4},{6,7},{7,6},{8,9},{9,8},{10,11... | collective-permute-start | bytes 172040 | tf_op jit(solution)/shard_map/ppermute | solution.py:19
  64.5 2.9 %collective-permute-start.20 = (bf16[224,128]{1,0:T(8,128)(2,1)S(1)}, bf16[224,128]{1,0:T(8,128)(2,1)S(1)}, u32[]{:S(2)}, u32[]{:S(2)}) collective-permute-start(bf16[224,128]{1,0:T(8,128)(2,1)S(1)} %fusion.13), channel_id=1, source_target_pairs={{0,2},{2,0},{4,6},{6,4},{8,10},{10,8},{12,14},{14,12},{16,18},{18,... | collective-permute-start | bytes 172040 | tf_op jit(solution)/shard_map/ppermute | solution.py:23
  67.4 5.8 %collective-permute-start.21 = (bf16[224,128]{1,0:T(8,128)(2,1)S(1)}, bf16[224,128]{1,0:T(8,128)(2,1)S(1)}, u32[]{:S(2)}, u32[]{:S(2)}) collective-permute-start(bf16[224,128]{1,0:T(8,128)(2,1)S(1)} %fusion.8), channel_id=1, source_target_pairs={{0,16},{2,18},{4,20},{6,22},{8,24},{10,26},{12,28},{14,30},{16,0},... | collective-permute-start | bytes 172040 | tf_op jit(solution)/shard_map/ppermute | solution.py:416

commit v13 on v12

--- a/solution.py
+++ b/solution.py
@@ -285,19 +285,19 @@
         return lax.dynamic_slice(hidden, (first, index * rows), (count, rows))
 
     quarter = half // 2
-
-    def fetched(first):
-        return [
-            columns_of(lax.rem(tok_index + d, tok_size), core * half + first, quarter)
+    part = quarter // 2
+    second = lax.div(vocab_index, 2) & 1
+    near, later = [
+        [
+            shift_tok(
+                columns_of(lax.rem(tok_index + d, tok_size), core * half + first, count),
+                d,
+                tok_size,
+            )
             for d in range(1, tok_size)
         ]
-
-    def fetch(slices):
-        return [shift_tok(x, d, tok_size) for d, x in enumerate(slices, 1)]
-
-    wanted = fetched(0)
-    hidden, wanted = lax.optimization_barrier((hidden, wanted))
-    near, later = fetch(wanted), fetched(quarter)
+        for first, count in ((0, quarter), (quarter + second * part, part))
+    ]
     upper = []
     while 1 << len(upper) < vocab_size:
         upper.append((vocab_index & (1 << len(upper))) != 0)
@@ -309,18 +309,17 @@
     live_slot = jnp.arange(block_ids.shape[1], dtype=jnp.int32)[None, :] < counts[:, None]
     core_word = core.reshape(1)
     tok_is = [tok_index == d for d in range(tok_size)]
-    later, head, upper, apart_is, tok_is, column_block, live_slot, core_word = lax.optimization_barrier(
-        (later, head, upper, apart_is, tok_is, column_block, live_slot, core_word)
+    head, upper, apart_is, tok_is, column_block, live_slot, core_word = lax.optimization_barrier(
+        (head, upper, apart_is, tok_is, column_block, live_slot, core_word)
     )
     head_here = load(head)
-    later, head_here = lax.optimization_barrier((later, head_here))
-    later = fetch(later)
     near, head_here, column_block, teacher, hidden = lax.optimization_barrier(
         (near, head_here, column_block, teacher, hidden)
     )
     products = [jnp.dot(x, head_here, preferred_element_type=jnp.float32) for x in near]
     returned = [[shift_tok(x, -d, tok_size)] for d, x in enumerate(products, 1)]
     later, _ = lax.optimization_barrier((later, products))
+    later = [in_order(x, swap_vocab(x, 2, vocab_size), upper[1]) for x in later]
     near = [jnp.concatenate(pair, axis=0) for pair in zip(near, later)]
     far = [swap_vocab(x, 1, vocab_size) for x in near]
     for d in range(1, tok_size):

time: 74 us -> 75.9 us (1.026)
  waiting for transfers between devices: 27.1 us -> 29.4 us
    ppermute x7, starting transfers between devices: 10.2 us -> 8.1 us  [shift_tok(): lax.ppermute(x, 'tok', [(i, (i + offset) % size) for i in range(size)])]
    ppermute x7, waiting for transfers between devices: 14.9 us -> 17 us  [shift_tok(): lax.ppermute(x, 'tok', [(i, (i + offset) % size) for i in range(size)])]
    ppermute x14 -> x15, starting transfers between devices: 13.6 us -> 15.3 us  [swap_vocab(): return lax.ppermute(x, 'vocab', [(i, i ^ bit) for i in range(size)])]
    ppermute x14 -> x15, waiting for transfers between devices: 8.97 us -> 9.84 us  [swap_vocab(): return lax.ppermute(x, 'vocab', [(i, i ^ bit) for i in range(size)])]
  transfers between devices with their start and end apart: 22 -> 23, of which waited for: 14 -> 14; matrix products, arithmetic and copies ran while one was open for 8% -> 8% of each run, Pallas kernels for 13% -> 13%
where the time goes in v13:
time: 75.9 us; the launch traced here: 75.7 us
  waiting for transfers between devices  29.4 us (39%)
  starting transfers between devices  26 us (34%)
  Pallas kernels  11.1 us (15%)
  matrix products  4 us (5%)
  other arithmetic  1.77 us (2%)
  local copies, waits for them, and re-layouts  1.75 us (2%)
  between operations  1.6 us (2%)
    ppermute x7, waiting for transfers between devices, shift_tok(): lax.ppermute(x, 'tok', [(i, (i + offset) % size) for i in range(size)])  17 us
    ppermute x15, starting transfers between devices, swap_vocab(): return lax.ppermute(x, 'vocab', [(i, i ^ bit) for i in range(size)])  15.3 us
    ppermute x15, waiting for transfers between devices, swap_vocab(): return lax.ppermute(x, 'vocab', [(i, i ^ bit) for i in range(size)])  9.84 us
    ppermute x7, starting transfers between devices, shift_tok(): lax.ppermute(x, 'tok', [(i, (i + offset) % size) for i in range(size)])  8.1 us
    pallas_call x2, Pallas kernels, head_gradient(): pl.pallas_call(functools.partial(head_gradient_kernel, steps, start, widt...  3.9 us
    pallas_call x3, Pallas kernels, gradient(): pl.pallas_call(kernel, out_shape=out, in_specs=([] if core is None else [...  3.32 us
    dot_general x3, matrix products, per_device(): jnp.dot(x, head_here, preferred_element_type=jnp.float32)  3.12 us
    pallas_call x1, Pallas kernels, load(): pl.pallas_call(load_kernel, out_shape=pltpu.VMEM(head.shape, head.dtype),...  2.62 us
  transfers between devices with their start and end apart: 23, of which 14 were waited for; matrix products, arithmetic and copies ran while one was open for 8% of the time, Pallas kernels for 13%

profile of v13, /device:TPU:0, one launch (start us, length us, event | category | flops | bytes accessed | tf_op | source)
XLA Modules:
  0.0 75.7 jit_solution(11185343963576588862)
XLA Ops:
  0.6 0.8 %dynamic_slice.7 = bf16[16,1792]{1,0:T(8,128)(2,1)S(1)} dynamic-slice(bf16[128,3584]{1,0:T(8,128)(2,1)} %param.5, s32[]{:T(128)S(6)} %select_n.260, s32[]{:T(128)S(6)} %select_n.258), dynamic_slice_sizes={16,1792} | dynamic-slice | bytes 114692 | tf_op jit(solution)/shard_map/dynamic_slice | solution.py:285
  1.5 3.0 %collective-permute-start.2 = (bf16[16,1792]{1,0:T(8,128)(2,1)S(1)}, bf16[16,1792]{1,0:T(8,128)(2,1)S(1)}, u32[]{:S(2)}, u32[]{:S(2)}) collective-permute-start(bf16[16,1792]{1,0:T(8,128)(2,1)S(1)} %dynamic_slice.7), channel_id=1, source_target_pairs={{0,1},{1,0},{2,3},{3,2},{4,5},{5,4},{6,7},{7,6},{8,9},{9,8},{10,11... | collective-permute-start | bytes 172040 | tf_op jit(solution)/shard_map/ppermute | solution.py:19
  4.4 0.9 %dynamic_slice.6 = bf16[32,1792]{1,0:T(8,128)(2,1)S(1)} dynamic-slice(bf16[128,3584]{1,0:T(8,128)(2,1)} %param.5, s32[]{:T(128)S(6)} %select_n.257, s32[]{:T(128)S(6)} %select_n.258), dynamic_slice_sizes={32,1792} | dynamic-slice | bytes 229380 | tf_op jit(solution)/shard_map/dynamic_slice | solution.py:285
  5.4 0.0 collective-permute-start
  6.1 2.6 %load_head.1.head_ref = bf16[1792,1536]{1,0:T(8,128)(2,1)S(1)} custom-call(bf16[1792,1536]{1,0:T(8,128)(2,1)} %head_ref), custom_call_target="tpu_custom_call" | custom-call | bytes 11010048 | tf_op jit(solution)/shard_map/load_head/pallas_call | solution.py:67
  8.7 0.0 copy-start
  8.7 1.4 %collective-permute-done = bf16[32,1792]{1,0:T(8,128)(2,1)S(1)} collective-permute-done((bf16[32,1792]{1,0:T(8,128)(2,1)S(1)}, bf16[32,1792]{1,0:T(8,128)(2,1)S(1)}, u32[]{:S(2)}, u32[]{:S(2)}) %collective-permute-start) | collective-permute-done | bytes 114720 | tf_op jit(solution)/shard_map/ppermute | solution.py:19
  10.1 1.0 %fusion.22 = f32[32,1536]{1,0:T(8,128)S(1)} fusion(bf16[32,1792]{1,0:T(8,128)(2,1)S(1)} %collective-permute-done, bf16[1792,1536]{1,0:T(8,128)(2,1)S(1)} %load_head.1.head_ref), kind=kOutput, calls=%fused_computation.77 | convolution fusion | flops 176160768 | bytes 5816320 | tf_op jit(solution)/shard_map/dot_general | solution.py:319
  11.2 0.8 %collective-permute-start.1 = (f32[32,1536]{1,0:T(8,128)S(1)}, f32[32,1536]{1,0:T(8,128)S(1)}, u32[]{:S(2)}, u32[]{:S(2)}) collective-permute-start(f32[32,1536]{1,0:T(8,128)S(1)} %fusion.22), channel_id=1, source_target_pairs={{0,1},{1,0},{2,3},{3,2},{4,5},{5,4},{6,7},{7,6},{8,9},{9,8},{10,11... | collective-permute-start | bytes 589832 | tf_op jit(solution)/shard_map/ppermute | solution.py:19
  12.0 1.7 %collective-permute-start.3 = (bf16[16,1792]{1,0:T(8,128)(2,1)S(1)}, bf16[16,1792]{1,0:T(8,128)(2,1)S(1)}, u32[]{:S(2)}, u32[]{:S(2)}) collective-permute-start(bf16[16,1792]{1,0:T(8,128)(2,1)S(1)} %collective-permute-done.2), channel_id=1, source_target_pairs={{0,4},{2,6},{4,0},{6,2},{8,12},{10,14},{12,8},{14,10},{16,20},{18,... | collective-permute-start | bytes 172040 | tf_op jit(solution)/shard_map/ppermute | solution.py:23
  13.7 0.9 %fusion.24.own_ref = f32[128,1536]{1,0:T(8,128)S(1)} fusion(bf16[128,1792]{1,0:T(8,128)(2,1)S(1)} %slice_select_fusion, bf16[1792,1536]{1,0:T(8,128)(2,1)S(1)} %load_head.1.head_ref), kind=kOutput, calls=%fused_computation.79 | convolution fusion | flops 704643072 | bytes 6750208 | tf_op jit(solution)/shard_map/dot_general | solution.py:335
  14.6 0.1 and_reduce_fusion
  14.7 0.3 fusion
  15.1 1.1 %collective-permute-done.3 = bf16[16,1792]{1,0:T(8,128)(2,1)S(1)} collective-permute-done((bf16[16,1792]{1,0:T(8,128)(2,1)S(1)}, bf16[16,1792]{1,0:T(8,128)(2,1)S(1)}, u32[]{:S(2)}, u32[]{:S(2)}) %collective-permute-start.3) | collective-permute-done | bytes 57376 | tf_op jit(solution)/shard_map/ppermute | solution.py:23
  16.2 0.1 collective-permute-start.5
  16.3 1.0 %fusion.12 = f32[32,1536]{1,0:T(8,128)S(1)} fusion(bf16[1792,1536]{1,0:T(8,128)(2,1)S(1)} %load_head.1.head_ref, bf16[16,1792]{1,0:T(8,128)(2,1)S(1)} %get-tuple-element.104, bf16[16,1792]{1,0:T(8,128)(2,1)S(1)} %get-tuple-element.103), kind=kOutput, calls=%fused_computation.31 | convolution fusion | flops 176390144 | bytes 5816320 | tf_op jit(solution)/shard_map/dot_general | solution.py:329
  17.3 1.3 %collective-permute-start.4 = (f32[32,1536]{1,0:T(8,128)S(1)}, f32[32,1536]{1,0:T(8,128)S(1)}, u32[]{:S(2)}, u32[]{:S(2)}) collective-permute-start(f32[32,1536]{1,0:T(8,128)S(1)} %fusion.12), channel_id=1, source_target_pairs={{0,1},{1,0},{2,3},{3,2},{4,5},{5,4},{6,7},{7,6},{8,9},{9,8},{10,11... | collective-permute-start | bytes 589832 | tf_op jit(solution)/shard_map/ppermute | solution.py:19
  18.6 0.0 collective-permute-done.5
  18.6 1.1 %fusion.23 = f32[64,1536]{1,0:T(8,128)S(1)} fusion(bf16[64,1792]{1,0:T(8,128)(2,1)S(1)} %collective-permute-done.5, bf16[1792,1536]{1,0:T(8,128)(2,1)S(1)} %load_head.1.head_ref), kind=kOutput, calls=%fused_computation.78 | convolution fusion | flops 352321536 | bytes 6127616 | tf_op jit(solution)/shard_map/dot_general | solution.py:329
  19.7 0.8 %collective-permute-start.6 = (f32[64,1536]{1,0:T(8,128)S(1)}, f32[64,1536]{1,0:T(8,128)S(1)}, u32[]{:S(2)}, u32[]{:S(2)}) collective-permute-start(f32[64,1536]{1,0:T(8,128)S(1)} %fusion.23), channel_id=1, source_target_pairs={{0,1},{1,0},{2,3},{3,2},{4,5},{5,4},{6,7},{7,6},{8,9},{9,8},{10,11... | collective-permute-start | bytes 1179656 | tf_op jit(solution)/shard_map/ppermute | solution.py:19
  20.5 0.1 broadcast_select_fusion.1
  20.6 0.1 pad_maximum_fusion.refs_0_
  20.6 0.0 collective-permute-done.1.refs_0_
  20.6 4.4 %collective-permute-done.4.refs_1_ = f32[32,1536]{1,0:T(8,128)S(1)} collective-permute-done((f32[32,1536]{1,0:T(8,128)S(1)}, f32[32,1536]{1,0:T(8,128)S(1)}, u32[]{:S(2)}, u32[]{:S(2)}) %collective-permute-start.4) | collective-permute-done | bytes 196640 | tf_op jit(solution)/shard_map/ppermute | solution.py:19
  25.0 8.0 %collective-permute-done.6.refs_2_ = f32[64,1536]{1,0:T(8,128)S(1)} collective-permute-done((f32[64,1536]{1,0:T(8,128)S(1)}, f32[64,1536]{1,0:T(8,128)S(1)}, u32[]{:S(2)}, u32[]{:S(2)}) %collective-permute-start.6) | collective-permute-done | bytes 393248 | tf_op jit(solution)/shard_map/ppermute | solution.py:19
  33.0 0.4 local_stats.1
  33.5 0.0 collective-permute-start.7
  33.5 1.1 %collective-permute-done.7 = f32[1,4,128]{2,1,0:T(4,128)S(1)} collective-permute-done((f32[1,4,128]{2,1,0:T(4,128)S(1)}, f32[1,4,128]{2,1,0:T(4,128)S(1)}, u32[]{:S(2)}, u32[]{:S(2)}) %collective-permute-start.7) | collective-permute-done | bytes 2080 | tf_op jit(solution)/shard_map/ppermute | solution.py:23
  34.7 1.8 %collective-permute-start.10 = (f32[2,4,128]{2,1,0:T(4,128)S(1)}, f32[2,4,128]{2,1,0:T(4,128)S(1)}, u32[]{:S(2)}, u32[]{:S(2)}) collective-permute-start(f32[2,4,128]{2,1,0:T(4,128)S(1)} %pad_maximum_fusion.5), channel_id=1, source_target_pairs={{0,4},{2,6},{4,0},{6,2},{8,12},{10,14},{12,8},{14,10},{16,20},{18,... | collective-permute-start | bytes 12296 | tf_op jit(solution)/shard_map/ppermute | solution.py:23
  36.4 1.6 %collective-permute-start.9 = (f32[2,4,128]{2,1,0:T(4,128)S(1)}, f32[2,4,128]{2,1,0:T(4,128)S(1)}, u32[]{:S(2)}, u32[]{:S(2)}) collective-permute-start(f32[2,4,128]{2,1,0:T(4,128)S(1)} %pad_maximum_fusion.5), channel_id=1, source_target_pairs={{0,8},{2,10},{4,12},{6,14},{8,0},{10,2},{12,4},{14,6},{16,24},{18,... | collective-permute-start | bytes 12296 | tf_op jit(solution)/shard_map/ppermute | solution.py:23
  38.0 0.2 collective-permute-start.8
  38.2 0.1 collective-permute-done.10
  38.3 1.7 %collective-permute-done.9 = f32[2,4,128]{2,1,0:T(4,128)S(1)} collective-permute-done((f32[2,4,128]{2,1,0:T(4,128)S(1)}, f32[2,4,128]{2,1,0:T(4,128)S(1)}, u32[]{:S(2)}, u32[]{:S(2)}) %collective-permute-start.9) | collective-permute-done | bytes 4128 | tf_op jit(solution)/shard_map/ppermute | solution.py:23
  40.0 2.5 %collective-permute-done.8 = f32[2,4,128]{2,1,0:T(4,128)S(1)} collective-permute-done((f32[2,4,128]{2,1,0:T(4,128)S(1)}, f32[2,4,128]{2,1,0:T(4,128)S(1)}, u32[]{:S(2)}, u32[]{:S(2)}) %collective-permute-start.8) | collective-permute-done | bytes 4128 | tf_op jit(solution)/shard_map/ppermute | solution.py:23
  42.5 2.7 %collective-permute-start.11 = (f32[8,4,128]{2,1,0:T(4,128)S(1)}, f32[8,4,128]{2,1,0:T(4,128)S(1)}, u32[]{:S(2)}, u32[]{:S(2)}) collective-permute-start(f32[8,4,128]{2,1,0:T(4,128)S(1)} %pad_maximum_fusion.4), channel_id=1, source_target_pairs={{0,16},{2,18},{4,20},{6,22},{8,24},{10,26},{12,28},{14,30},{16,0},... | collective-permute-start | bytes 49160 | tf_op jit(solution)/shard_map/ppermute | solution.py:23
  45.2 2.1 %collective-permute-done.11 = f32[8,4,128]{2,1,0:T(4,128)S(1)} collective-permute-done((f32[8,4,128]{2,1,0:T(4,128)S(1)}, f32[8,4,128]{2,1,0:T(4,128)S(1)}, u32[]{:S(2)}, u32[]{:S(2)}) %collective-permute-start.11) | collective-permute-done | bytes 16416 | tf_op jit(solution)/shard_map/ppermute | solution.py:23
  47.3 0.9 %delta.1 = (bf16[128,1536]{1,0:T(8,128)(2,1)S(1)}, f32[1,128]{1,0:T(1,128)}, f32[1,128]{1,0:T(1,128)}) custom-call(f32[16,4,128]{2,1,0:T(4,128)S(1)} %pad_maximum_fusion.3.gathered_ref, f32[128,1536]{1,0:T(8,128)S(1)} %get-tuple-element.70.logits_ref, bf16[128,1536]{1,0:T(8,128)(2,1)S(1)} %get-tuple-element.64.kept_ref), custom_call_target="tpu_custom_call" | custom-call | flops 1572864 | bytes 1572864 | tf_op jit(solution)/shard_map/delta/pallas_call | solution.py:155
  48.2 1.1 %collective-permute-start.12 = (bf16[128,1536]{1,0:T(8,128)(2,1)S(1)}, bf16[128,1536]{1,0:T(8,128)(2,1)S(1)}, u32[]{:S(2)}, u32[]{:S(2)}) collective-permute-start(bf16[128,1536]{1,0:T(8,128)(2,1)S(1)} %get-tuple-element.74.delta_ref), channel_id=1, source_target_pairs={{0,1},{1,0},{2,3},{3,2},{4,5},{5,4},{6,7},{7,6},{8,9},{9,8},{10,11... | collective-permute-start | bytes 1179656 | tf_op jit(solution)/shard_map/ppermute | solution.py:19
  49.3 1.6 %partial_gradient.5 = f32[4,2,224,128]{3,2,1,0:T(8,128)S(1)} custom-call(bf16[1792,1536]{1,0:T(8,128)(2,1)S(1)} %load_head.1.head_ref, bf16[128,1536]{1,0:T(8,128)(2,1)S(1)} %get-tuple-element.74.delta_ref), custom_call_target="tpu_custom_call" | custom-call | flops 704643072 | bytes 5898240 | tf_op jit(solution)/shard_map/partial_gradient/pallas_call | solution.py:214
  50.9 0.1 fusion.11
  51.0 0.4 collective-permute-start.20
  51.4 1.5 %collective-permute-start.18 = (bf16[2,224,128]{2,1,0:T(8,128)(2,1)S(1)}, bf16[2,224,128]{2,1,0:T(8,128)(2,1)S(1)}, u32[]{:S(2)}, u32[]{:S(2)}) collective-permute-start(bf16[2,224,128]{2,1,0:T(8,128)(2,1)S(1)} %get-tuple-element.95), channel_id=1, source_target_pairs={{0,4},{2,6},{4,0},{6,2},{8,12},{10,14},{12,8},{14,10},{16,20},{18,... | collective-permute-start | bytes 344072 | tf_op jit(solution)/shard_map/ppermute | solution.py:23
  52.9 1.6 %collective-permute-start.19 = (bf16[2,224,128]{2,1,0:T(8,128)(2,1)S(1)}, bf16[2,224,128]{2,1,0:T(8,128)(2,1)S(1)}, u32[]{:S(2)}, u32[]{:S(2)}) collective-permute-start(bf16[2,224,128]{2,1,0:T(8,128)(2,1)S(1)} %get-tuple-element.96), channel_id=1, source_target_pairs={{0,8},{2,10},{4,12},{6,14},{8,0},{10,2},{12,4},{14,6},{16,24},{18,... | collective-permute-start | bytes 344072 | tf_op jit(solution)/shard_map/ppermute | solution.py:23
  54.5 2.0 %collective-permute-done.12.delta_ref = bf16[128,1536]{1,0:T(8,128)(2,1)S(1)} collective-permute-done((bf16[128,1536]{1,0:T(8,128)(2,1)S(1)}, bf16[128,1536]{1,0:T(8,128)(2,1)S(1)}, u32[]{:S(2)}, u32[]{:S(2)}) %collective-permute-start.12) | collective-permute-done | bytes 393248 | tf_op jit(solution)/shard_map/ppermute | solution.py:19
  56.5 0.9 %partial_gradient.3 = bf16[4,224,128]{2,1,0:T(8,128)(2,1)S(1)} custom-call(s32[1]{0:T(128)} %bitcast.1.core_ref, bf16[1792,1536]{1,0:T(8,128)(2,1)S(1)} %load_head.1.head_ref, bf16[128,1536]{1,0:T(8,128)(2,1)S(1)} %collective-permute-done.12.delta_ref), custom_call_target="tpu_custom_call" | custom-call | flops 704643072 | bytes 5898240 | tf_op jit(solution)/shard_map/partial_gradient/pallas_call | solution.py:214
  57.4 0.1 collective-permute-start.13
  57.5 0.9 %partial_gradient.4 = f32[4,224,128]{2,1,0:T(8,128)S(1)} custom-call(s32[1]{0:T(128)} %bitcast.1.core_ref, bf16[1792,1536]{1,0:T(8,128)(2,1)S(1)} %load_head.1.head_ref, bf16[128,1536]{1,0:T(8,128)(2,1)S(1)} %collective-permute-done.12.delta_ref), custom_call_target="tpu_custom_call" | custom-call | flops 704643072 | bytes 5898240 | tf_op jit(solution)/shard_map/partial_gradient/pallas_call | solution.py:214
  58.4 0.1 pad_maximum_fusion.1.refs_1_
  58.5 0.1 fusion.5
  58.6 0.4 collective-permute-done.13
  59.0 0.1 convert_add_fusion
  59.1 0.5 collective-permute-start.14
  59.6 0.6 collective-permute-start.15
  60.2 2.4 %collective-permute-start.16 = (bf16[1,224,128]{2,1,0:T(8,128)(2,1)S(1)}, bf16[1,224,128]{2,1,0:T(8,128)(2,1)S(1)}, u32[]{:S(2)}, u32[]{:S(2)}) collective-permute-start(bf16[1,224,128]{2,1,0:T(8,128)(2,1)S(1)} %get-tuple-element.78), channel_id=1, source_target_pairs={{0,12},{2,14},{4,8},{6,10},{8,4},{10,6},{12,0},{14,2},{16,28},{18,... | collective-permute-start | bytes 172040 | tf_op jit(solution)/shard_map/ppermute | solution.py:23
  62.6 2.1 %head_gradient.2.refs_2_ = bf16[1792,1536]{1,0:T(8,128)(2,1)} custom-call(bf16[256,1792]{1,0:T(8,128)(2,1)S(1)} %pad_maximum_fusion.refs_0_, bf16[256,1536]{1,0:T(8,128)(2,1)S(1)} %pad_maximum_fusion.1.refs_1_), custom_call_target="tpu_custom_call" | custom-call | flops 805306368 | bytes 4849664 | tf_op jit(solution)/shard_map/head_gradient/pallas_call | solution.py:253
  64.7 0.8 %collective-permute-done.16 = bf16[1,224,128]{2,1,0:T(8,128)(2,1)S(1)} collective-permute-done((bf16[1,224,128]{2,1,0:T(8,128)(2,1)S(1)}, bf16[1,224,128]{2,1,0:T(8,128)(2,1)S(1)}, u32[]{:S(2)}, u32[]{:S(2)}) %collective-permute-start.16) | collective-permute-done | bytes 57376 | tf_op jit(solution)/shard_map/ppermute | solution.py:23
  65.5 0.1 fusion.16
  65.6 1.2 %collective-permute-start.17 = (bf16[224,128]{1,0:T(8,128)(2,1)S(1)}, bf16[224,128]{1,0:T(8,128)(2,1)S(1)}, u32[]{:S(2)}, u32[]{:S(2)}) collective-permute-start(bf16[224,128]{1,0:T(8,128)(2,1)S(1)} %fusion.16), channel_id=1, source_target_pairs={{0,1},{1,0},{2,3},{3,2},{4,5},{5,4},{6,7},{7,6},{8,9},{9,8},{10,11... | collective-permute-start | bytes 172040 | tf_op jit(solution)/shard_map/ppermute | solution.py:19
  66.7 0.1 collective-permute-start.21
  66.8 1.8 %head_gradient.3 = bf16[1792,1536]{1,0:T(8,128)(2,1)} custom-call(bf16[256,1792]{1,0:T(8,128)(2,1)S(1)} %pad_maximum_fusion.refs_0_, bf16[256,1536]{1,0:T(8,128)(2,1)S(1)} %pad_maximum_fusion.1.refs_1_, bf16[1792,1536]{1,0:T(8,128)(2,1)} %head_gradient.2.refs_2_), custom_call_target="tpu_custom_call", output_to_operand_aliasing={{}: (2, {})} | custom-call | flops 603979776 | bytes 4063232 | tf_op jit(solution)/shard_map/head_gradient/pallas_call | solution.py:253
  68.6 1.2 %collective-permute-done.17 = bf16[224,128]{1,0:T(8,128)(2,1)S(1)} collective-permute-done((bf16[224,128]{1,0:T(8,128)(2,1)S(1)}, bf16[224,128]{1,0:T(8,128)(2,1)S(1)}, u32[]{:S(2)}, u32[]{:S(2)}) %collective-permute-start.17) | collective-permute-done | bytes 57376 | tf_op jit(solution)/shard_map/ppermute | solution.py:19
  69.8 2.6 %collective-permute-start.22 = (bf16[224,128]{1,0:T(8,128)(2,1)S(1)}, bf16[224,128]{1,0:T(8,128)(2,1)S(1)}, u32[]{:S(2)}, u32[]{:S(2)}) collective-permute-start(bf16[224,128]{1,0:T(8,128)(2,1)S(1)} %fusion.8), channel_id=1, source_target_pairs={{0,16},{2,18},{4,20},{6,22},{8,24},{10,26},{12,28},{14,30},{16,0},... | collective-permute-start | bytes 172040 | tf_op jit(solution)/shard_map/ppermute | solution.py:415
  72.4 2.6 %collective-permute-done.22 = bf16[224,128]{1,0:T(8,128)(2,1)S(1)} collective-permute-done((bf16[224,128]{1,0:T(8,128)(2,1)S(1)}, bf16[224,128]{1,0:T(8,128)(2,1)S(1)}, u32[]{:S(2)}, u32[]{:S(2)}) %collective-permute-start.22) | collective-permute-done | bytes 57376 | tf_op jit(solution)/shard_map/ppermute | solution.py:415
  75.0 0.7 fusion.7
  (27 shorter events, 0.3 us)
Async XLA Ops:
  1.5 10.5 %collective-permute-start.2 = (bf16[16,1792]{1,0:T(8,128)(2,1)S(1)}, bf16[16,1792]{1,0:T(8,128)(2,1)S(1)}, u32[]{:S(2)}, u32[]{:S(2)}) collective-permute-start(bf16[16,1792]{1,0:T(8,128)(2,1)S(1)} %dynamic_slice.7), channel_id=1, source_target_pairs={{0,1},{1,0},{2,3},{3,2},{4,5},{5,4},{6,7},{7,6},{8,9},{9,8},{10,11... | collective-permute-start | bytes 172040 | tf_op jit(solution)/shard_map/ppermute | solution.py:19
  5.4 4.8 %collective-permute-start = (bf16[32,1792]{1,0:T(8,128)(2,1)S(1)}, bf16[32,1792]{1,0:T(8,128)(2,1)S(1)}, u32[]{:S(2)}, u32[]{:S(2)}) collective-permute-start(bf16[32,1792]{1,0:T(8,128)(2,1)S(1)} %dynamic_slice.6), channel_id=1, source_target_pairs={{0,1},{1,0},{2,3},{3,2},{4,5},{5,4},{6,7},{7,6},{8,9},{9,8},{10,11... | collective-permute-start | bytes 344072 | tf_op jit(solution)/shard_map/ppermute | solution.py:19
  8.7 5.0 %copy-start = (bf16[128,3584]{1,0:T(8,128)(2,1)S(1)}, bf16[128,3584]{1,0:T(8,128)(2,1)}, u32[]{:S(2)}) copy-start(bf16[128,3584]{1,0:T(8,128)(2,1)} %param.5) | copy-start | bytes 2752516
  11.2 3.5 %copy-start.2 = (s32[1,16]{1,0:T(1,128)S(1)}, s32[1,16]{1,0:T(1,128)}, u32[]{:S(2)}) copy-start(s32[1,16]{1,0:T(1,128)} %param.8) | copy-start | bytes 196
  11.2 3.6 %copy-start.1 = (bf16[128,1536]{1,0:T(8,128)(2,1)S(1)}, bf16[128,1536]{1,0:T(8,128)(2,1)}, u32[]{:S(2)}) copy-start(bf16[128,1536]{1,0:T(8,128)(2,1)} %param.7) | copy-start | bytes 1179652
  11.2 9.4 %collective-permute-start.1 = (f32[32,1536]{1,0:T(8,128)S(1)}, f32[32,1536]{1,0:T(8,128)S(1)}, u32[]{:S(2)}, u32[]{:S(2)}) collective-permute-start(f32[32,1536]{1,0:T(8,128)S(1)} %fusion.22), channel_id=1, source_target_pairs={{0,1},{1,0},{2,3},{3,2},{4,5},{5,4},{6,7},{7,6},{8,9},{9,8},{10,11... | collective-permute-start | bytes 589832 | tf_op jit(solution)/shard_map/ppermute | solution.py:19
  12.0 4.2 %collective-permute-start.3 = (bf16[16,1792]{1,0:T(8,128)(2,1)S(1)}, bf16[16,1792]{1,0:T(8,128)(2,1)S(1)}, u32[]{:S(2)}, u32[]{:S(2)}) collective-permute-start(bf16[16,1792]{1,0:T(8,128)(2,1)S(1)} %collective-permute-done.2), channel_id=1, source_target_pairs={{0,4},{2,6},{4,0},{6,2},{8,12},{10,14},{12,8},{14,10},{16,20},{18,... | collective-permute-start | bytes 172040 | tf_op jit(solution)/shard_map/ppermute | solution.py:23
  16.2 2.4 %collective-permute-start.5 = (bf16[64,1792]{1,0:T(8,128)(2,1)S(1)}, bf16[64,1792]{1,0:T(8,128)(2,1)S(1)}, u32[]{:S(2)}, u32[]{:S(2)}) collective-permute-start(bf16[64,1792]{1,0:T(8,128)(2,1)S(1)} %pad_maximum_fusion.2), channel_id=1, source_target_pairs={{0,2},{2,0},{4,6},{6,4},{8,10},{10,8},{12,14},{14,12},{16,18},{18,... | collective-permute-start | bytes 688136 | tf_op jit(solution)/shard_map/ppermute | solution.py:23
  17.3 7.7 %collective-permute-start.4 = (f32[32,1536]{1,0:T(8,128)S(1)}, f32[32,1536]{1,0:T(8,128)S(1)}, u32[]{:S(2)}, u32[]{:S(2)}) collective-permute-start(f32[32,1536]{1,0:T(8,128)S(1)} %fusion.12), channel_id=1, source_target_pairs={{0,1},{1,0},{2,3},{3,2},{4,5},{5,4},{6,7},{7,6},{8,9},{9,8},{10,11... | collective-permute-start | bytes 589832 | tf_op jit(solution)/shard_map/ppermute | solution.py:19
  19.7 13.3 %collective-permute-start.6 = (f32[64,1536]{1,0:T(8,128)S(1)}, f32[64,1536]{1,0:T(8,128)S(1)}, u32[]{:S(2)}, u32[]{:S(2)}) collective-permute-start(f32[64,1536]{1,0:T(8,128)S(1)} %fusion.23), channel_id=1, source_target_pairs={{0,1},{1,0},{2,3},{3,2},{4,5},{5,4},{6,7},{7,6},{8,9},{9,8},{10,11... | collective-permute-start | bytes 1179656 | tf_op jit(solution)/shard_map/ppermute | solution.py:19
  33.5 1.2 %collective-permute-start.7 = (f32[1,4,128]{2,1,0:T(4,128)S(1)}, f32[1,4,128]{2,1,0:T(4,128)S(1)}, u32[]{:S(2)}, u32[]{:S(2)}) collective-permute-start(f32[1,4,128]{2,1,0:T(4,128)S(1)} %bitcast.43), channel_id=1, source_target_pairs={{0,2},{2,0},{4,6},{6,4},{8,10},{10,8},{12,14},{14,12},{16,18},{18,... | collective-permute-start | bytes 6152 | tf_op jit(solution)/shard_map/ppermute | solution.py:23
  34.7 3.7 %collective-permute-start.10 = (f32[2,4,128]{2,1,0:T(4,128)S(1)}, f32[2,4,128]{2,1,0:T(4,128)S(1)}, u32[]{:S(2)}, u32[]{:S(2)}) collective-permute-start(f32[2,4,128]{2,1,0:T(4,128)S(1)} %pad_maximum_fusion.5), channel_id=1, source_target_pairs={{0,4},{2,6},{4,0},{6,2},{8,12},{10,14},{12,8},{14,10},{16,20},{18,... | collective-permute-start | bytes 12296 | tf_op jit(solution)/shard_map/ppermute | solution.py:23
  36.4 3.6 %collective-permute-start.9 = (f32[2,4,128]{2,1,0:T(4,128)S(1)}, f32[2,4,128]{2,1,0:T(4,128)S(1)}, u32[]{:S(2)}, u32[]{:S(2)}) collective-permute-start(f32[2,4,128]{2,1,0:T(4,128)S(1)} %pad_maximum_fusion.5), channel_id=1, source_target_pairs={{0,8},{2,10},{4,12},{6,14},{8,0},{10,2},{12,4},{14,6},{16,24},{18,... | collective-permute-start | bytes 12296 | tf_op jit(solution)/shard_map/ppermute | solution.py:23
  38.0 4.5 %collective-permute-start.8 = (f32[2,4,128]{2,1,0:T(4,128)S(1)}, f32[2,4,128]{2,1,0:T(4,128)S(1)}, u32[]{:S(2)}, u32[]{:S(2)}) collective-permute-start(f32[2,4,128]{2,1,0:T(4,128)S(1)} %pad_maximum_fusion.5), channel_id=1, source_target_pairs={{0,12},{2,14},{4,8},{6,10},{8,4},{10,6},{12,0},{14,2},{16,28},{18,... | collective-permute-start | bytes 12296 | tf_op jit(solution)/shard_map/ppermute | solution.py:23
  42.5 4.8 %collective-permute-start.11 = (f32[8,4,128]{2,1,0:T(4,128)S(1)}, f32[8,4,128]{2,1,0:T(4,128)S(1)}, u32[]{:S(2)}, u32[]{:S(2)}) collective-permute-start(f32[8,4,128]{2,1,0:T(4,128)S(1)} %pad_maximum_fusion.4), channel_id=1, source_target_pairs={{0,16},{2,18},{4,20},{6,22},{8,24},{10,26},{12,28},{14,30},{16,0},... | collective-permute-start | bytes 49160 | tf_op jit(solution)/shard_map/ppermute | solution.py:23
  48.2 8.3 %collective-permute-start.12 = (bf16[128,1536]{1,0:T(8,128)(2,1)S(1)}, bf16[128,1536]{1,0:T(8,128)(2,1)S(1)}, u32[]{:S(2)}, u32[]{:S(2)}) collective-permute-start(bf16[128,1536]{1,0:T(8,128)(2,1)S(1)} %get-tuple-element.74.delta_ref), channel_id=1, source_target_pairs={{0,1},{1,0},{2,3},{3,2},{4,5},{5,4},{6,7},{7,6},{8,9},{9,8},{10,11... | collective-permute-start | bytes 1179656 | tf_op jit(solution)/shard_map/ppermute | solution.py:19
  51.0 7.4 %collective-permute-start.20 = (bf16[2,224,128]{2,1,0:T(8,128)(2,1)S(1)}, bf16[2,224,128]{2,1,0:T(8,128)(2,1)S(1)}, u32[]{:S(2)}, u32[]{:S(2)}) collective-permute-start(bf16[2,224,128]{2,1,0:T(8,128)(2,1)S(1)} %get-tuple-element.94), channel_id=1, source_target_pairs={{0,12},{2,14},{4,8},{6,10},{8,4},{10,6},{12,0},{14,2},{16,28},{18,... | collective-permute-start | bytes 344072 | tf_op jit(solution)/shard_map/ppermute | solution.py:23
  51.4 7.0 %collective-permute-start.18 = (bf16[2,224,128]{2,1,0:T(8,128)(2,1)S(1)}, bf16[2,224,128]{2,1,0:T(8,128)(2,1)S(1)}, u32[]{:S(2)}, u32[]{:S(2)}) collective-permute-start(bf16[2,224,128]{2,1,0:T(8,128)(2,1)S(1)} %get-tuple-element.95), channel_id=1, source_target_pairs={{0,4},{2,6},{4,0},{6,2},{8,12},{10,14},{12,8},{14,10},{16,20},{18,... | collective-permute-start | bytes 344072 | tf_op jit(solution)/shard_map/ppermute | solution.py:23
  52.9 5.5 %collective-permute-start.19 = (bf16[2,224,128]{2,1,0:T(8,128)(2,1)S(1)}, bf16[2,224,128]{2,1,0:T(8,128)(2,1)S(1)}, u32[]{:S(2)}, u32[]{:S(2)}) collective-permute-start(bf16[2,224,128]{2,1,0:T(8,128)(2,1)S(1)} %get-tuple-element.96), channel_id=1, source_target_pairs={{0,8},{2,10},{4,12},{6,14},{8,0},{10,2},{12,4},{14,6},{16,24},{18,... | collective-permute-start | bytes 344072 | tf_op jit(solution)/shard_map/ppermute | solution.py:23
  57.4 1.6 %collective-permute-start.13 = (bf16[4,224,128]{2,1,0:T(8,128)(2,1)S(1)}, bf16[4,224,128]{2,1,0:T(8,128)(2,1)S(1)}, u32[]{:S(2)}, u32[]{:S(2)}) collective-permute-start(bf16[4,224,128]{2,1,0:T(8,128)(2,1)S(1)} %partial_gradient.3), channel_id=1, source_target_pairs={{0,2},{2,0},{4,6},{6,4},{8,10},{10,8},{12,14},{14,12},{16,18},{18,... | collective-permute-start | bytes 688136 | tf_op jit(solution)/shard_map/ppermute | solution.py:23
  59.1 5.6 %collective-permute-start.14 = (bf16[1,224,128]{2,1,0:T(8,128)(2,1)S(1)}, bf16[1,224,128]{2,1,0:T(8,128)(2,1)S(1)}, u32[]{:S(2)}, u32[]{:S(2)}) collective-permute-start(bf16[1,224,128]{2,1,0:T(8,128)(2,1)S(1)} %get-tuple-element.76), channel_id=1, source_target_pairs={{0,4},{2,6},{4,0},{6,2},{8,12},{10,14},{12,8},{14,10},{16,20},{18,... | collective-permute-start | bytes 172040 | tf_op jit(solution)/shard_map/ppermute | solution.py:23
  59.6 5.1 %collective-permute-start.15 = (bf16[1,224,128]{2,1,0:T(8,128)(2,1)S(1)}, bf16[1,224,128]{2,1,0:T(8,128)(2,1)S(1)}, u32[]{:S(2)}, u32[]{:S(2)}) collective-permute-start(bf16[1,224,128]{2,1,0:T(8,128)(2,1)S(1)} %get-tuple-element.77), channel_id=1, source_target_pairs={{0,8},{2,10},{4,12},{6,14},{8,0},{10,2},{12,4},{14,6},{16,24},{18,... | collective-permute-start | bytes 172040 | tf_op jit(solution)/shard_map/ppermute | solution.py:23
  60.2 5.3 %collective-permute-start.16 = (bf16[1,224,128]{2,1,0:T(8,128)(2,1)S(1)}, bf16[1,224,128]{2,1,0:T(8,128)(2,1)S(1)}, u32[]{:S(2)}, u32[]{:S(2)}) collective-permute-start(bf16[1,224,128]{2,1,0:T(8,128)(2,1)S(1)} %get-tuple-element.78), channel_id=1, source_target_pairs={{0,12},{2,14},{4,8},{6,10},{8,4},{10,6},{12,0},{14,2},{16,28},{18,... | collective-permute-start | bytes 172040 | tf_op jit(solution)/shard_map/ppermute | solution.py:23
  65.6 4.2 %collective-permute-start.17 = (bf16[224,128]{1,0:T(8,128)(2,1)S(1)}, bf16[224,128]{1,0:T(8,128)(2,1)S(1)}, u32[]{:S(2)}, u32[]{:S(2)}) collective-permute-start(bf16[224,128]{1,0:T(8,128)(2,1)S(1)} %fusion.16), channel_id=1, source_target_pairs={{0,1},{1,0},{2,3},{3,2},{4,5},{5,4},{6,7},{7,6},{8,9},{9,8},{10,11... | collective-permute-start | bytes 172040 | tf_op jit(solution)/shard_map/ppermute | solution.py:19
  66.7 3.1 %collective-permute-start.21 = (bf16[224,128]{1,0:T(8,128)(2,1)S(1)}, bf16[224,128]{1,0:T(8,128)(2,1)S(1)}, u32[]{:S(2)}, u32[]{:S(2)}) collective-permute-start(bf16[224,128]{1,0:T(8,128)(2,1)S(1)} %fusion.17), channel_id=1, source_target_pairs={{0,2},{2,0},{4,6},{6,4},{8,10},{10,8},{12,14},{14,12},{16,18},{18,... | collective-permute-start | bytes 172040 | tf_op jit(solution)/shard_map/ppermute | solution.py:23
  69.8 5.1 %collective-permute-start.22 = (bf16[224,128]{1,0:T(8,128)(2,1)S(1)}, bf16[224,128]{1,0:T(8,128)(2,1)S(1)}, u32[]{:S(2)}, u32[]{:S(2)}) collective-permute-start(bf16[224,128]{1,0:T(8,128)(2,1)S(1)} %fusion.8), channel_id=1, source_target_pairs={{0,16},{2,18},{4,20},{6,22},{8,24},{10,26},{12,28},{14,30},{16,0},... | collective-permute-start | bytes 172040 | tf_op jit(solution)/shard_map/ppermute | solution.py:415

commit v14 on v13

--- a/solution.py
+++ b/solution.py
@@ -285,18 +285,16 @@
         return lax.dynamic_slice(hidden, (first, index * rows), (count, rows))
 
     quarter = half // 2
-    part = quarter // 2
-    second = lax.div(vocab_index, 2) & 1
     near, later = [
         [
             shift_tok(
-                columns_of(lax.rem(tok_index + d, tok_size), core * half + first, count),
+                columns_of(lax.rem(tok_index + d, tok_size), core * half + first, quarter),
                 d,
                 tok_size,
             )
             for d in range(1, tok_size)
         ]
-        for first, count in ((0, quarter), (quarter + second * part, part))
+        for first in (0, quarter)
     ]
     upper = []
     while 1 << len(upper) < vocab_size:
@@ -319,7 +317,6 @@
     products = [jnp.dot(x, head_here, preferred_element_type=jnp.float32) for x in near]
     returned = [[shift_tok(x, -d, tok_size)] for d, x in enumerate(products, 1)]
     later, _ = lax.optimization_barrier((later, products))
-    later = [in_order(x, swap_vocab(x, 2, vocab_size), upper[1]) for x in later]
     near = [jnp.concatenate(pair, axis=0) for pair in zip(near, later)]
     far = [swap_vocab(x, 1, vocab_size) for x in near]
     for d in range(1, tok_size):

time: 75.9 us -> 72.7 us (0.958)
  waiting for transfers between devices: 29.4 us -> 27 us
    ppermute x7, starting transfers between devices: 8.1 us -> 9.95 us  [shift_tok(): lax.ppermute(x, 'tok', [(i, (i + offset) % size) for i in range(size)])]
    ppermute x15 -> x14, starting transfers between devices: 15.3 us -> 13.5 us  [swap_vocab(): return lax.ppermute(x, 'vocab', [(i, i ^ bit) for i in range(size)])]
    ppermute x7, waiting for transfers between devices: 17 us -> 15.7 us  [shift_tok(): lax.ppermute(x, 'tok', [(i, (i + offset) % size) for i in range(size)])]
    ppermute x15 -> x14, waiting for transfers between devices: 9.84 us -> 8.67 us  [swap_vocab(): return lax.ppermute(x, 'vocab', [(i, i ^ bit) for i in range(size)])]
    dynamic_slice x2 -> x1, local copies, waits for them, and re-layouts: 1.74 us -> 0.98 us  [columns_of(): return lax.dynamic_slice(hidden, (first, index * rows), (count, rows))]
  transfers between devices with their start and end apart: 23 -> 22, of which waited for: 14 -> 14; matrix products, arithmetic and copies ran while one was open for 8% -> 7% of each run, Pallas kernels for 13% -> 14%
where the time goes in v14:
time: 72.7 us; the launch traced here: 72.5 us
  waiting for transfers between devices  27 us (37%)
  starting transfers between devices  26.1 us (36%)
  Pallas kernels  11.1 us (15%)
  matrix products  4.01 us (6%)
  other arithmetic  1.69 us (2%)
  between operations  1.59 us (2%)
  local copies, waits for them, and re-layouts  1.01 us (1%)
    ppermute x7, waiting for transfers between devices, shift_tok(): lax.ppermute(x, 'tok', [(i, (i + offset) % size) for i in range(size)])  15.7 us
    ppermute x14, starting transfers between devices, swap_vocab(): return lax.ppermute(x, 'vocab', [(i, i ^ bit) for i in range(size)])  13.5 us
    ppermute x7, starting transfers between devices, shift_tok(): lax.ppermute(x, 'tok', [(i, (i + offset) % size) for i in range(size)])  9.95 us
    ppermute x14, waiting for transfers between devices, swap_vocab(): return lax.ppermute(x, 'vocab', [(i, i ^ bit) for i in range(size)])  8.67 us
    pallas_call x2, Pallas kernels, head_gradient(): pl.pallas_call(functools.partial(head_gradient_kernel, steps, start, widt...  3.9 us
    pallas_call x3, Pallas kernels, gradient(): pl.pallas_call(kernel, out_shape=out, in_specs=([] if core is None else [...  3.32 us
    dot_general x3, matrix products, per_device(): jnp.dot(x, head_here, preferred_element_type=jnp.float32)  3.13 us
    pallas_call x1, Pallas kernels, load(): pl.pallas_call(load_kernel, out_shape=pltpu.VMEM(head.shape, head.dtype),...  2.62 us
  transfers between devices with their start and end apart: 22, of which 14 were waited for; matrix products, arithmetic and copies ran while one was open for 7% of the time, Pallas kernels for 14%

profile of v14, /device:TPU:0, one launch (start us, length us, event | category | flops | bytes accessed | tf_op | source)
XLA Modules:
  0.0 72.5 jit_solution(8963128100538346771)
XLA Ops:
  0.6 1.0 %fusion.17 = (bf16[32,1792]{1,0:T(8,128)(2,1)S(1)}, bf16[32,1792]{1,0:T(8,128)(2,1)S(1)}) fusion(bf16[128,3584]{1,0:T(8,128)(2,1)} %param.5, s32[]{:T(128)S(6)} %select_n.247, s32[]{:T(128)S(6)} %select_n.246, s32[]{:T(128)S(6)} %select_n.245), kind=kLoop, calls=%fused_computation.71 | loop fusion | bytes 458764 | tf_op jit(solution)/shard_map/dynamic_slice | solution.py:285
  1.6 3.0 %collective-permute-start.2 = (bf16[32,1792]{1,0:T(8,128)(2,1)S(1)}, bf16[32,1792]{1,0:T(8,128)(2,1)S(1)}, u32[]{:S(2)}, u32[]{:S(2)}) collective-permute-start(bf16[32,1792]{1,0:T(8,128)(2,1)S(1)} %get-tuple-element.97), channel_id=1, source_target_pairs={{0,1},{1,0},{2,3},{3,2},{4,5},{5,4},{6,7},{7,6},{8,9},{9,8},{10,11... | collective-permute-start | bytes 344072 | tf_op jit(solution)/shard_map/ppermute | solution.py:19
  4.7 0.1 collective-permute-start
  5.4 2.6 %load_head.1.head_ref = bf16[1792,1536]{1,0:T(8,128)(2,1)S(1)} custom-call(bf16[1792,1536]{1,0:T(8,128)(2,1)} %head_ref), custom_call_target="tpu_custom_call" | custom-call | bytes 11010048 | tf_op jit(solution)/shard_map/load_head/pallas_call | solution.py:67
  8.1 0.0 copy-start
  8.1 2.2 %collective-permute-done = bf16[32,1792]{1,0:T(8,128)(2,1)S(1)} collective-permute-done((bf16[32,1792]{1,0:T(8,128)(2,1)S(1)}, bf16[32,1792]{1,0:T(8,128)(2,1)S(1)}, u32[]{:S(2)}, u32[]{:S(2)}) %collective-permute-start) | collective-permute-done | bytes 114720 | tf_op jit(solution)/shard_map/ppermute | solution.py:19
  10.3 1.0 %fusion.18 = f32[32,1536]{1,0:T(8,128)S(1)} fusion(bf16[32,1792]{1,0:T(8,128)(2,1)S(1)} %collective-permute-done, bf16[1792,1536]{1,0:T(8,128)(2,1)S(1)} %load_head.1.head_ref), kind=kOutput, calls=%fused_computation.72 | convolution fusion | flops 176160768 | bytes 5816320 | tf_op jit(solution)/shard_map/dot_general | solution.py:317
  11.3 1.8 %collective-permute-start.1 = (f32[32,1536]{1,0:T(8,128)S(1)}, f32[32,1536]{1,0:T(8,128)S(1)}, u32[]{:S(2)}, u32[]{:S(2)}) collective-permute-start(f32[32,1536]{1,0:T(8,128)S(1)} %fusion.18), channel_id=1, source_target_pairs={{0,1},{1,0},{2,3},{3,2},{4,5},{5,4},{6,7},{7,6},{8,9},{9,8},{10,11... | collective-permute-start | bytes 589832 | tf_op jit(solution)/shard_map/ppermute | solution.py:19
  13.1 0.0 collective-permute-done.2
  13.1 1.0 %fusion.19 = f32[32,1536]{1,0:T(8,128)S(1)} fusion(bf16[32,1792]{1,0:T(8,128)(2,1)S(1)} %collective-permute-done.2, bf16[1792,1536]{1,0:T(8,128)(2,1)S(1)} %load_head.1.head_ref), kind=kOutput, calls=%fused_computation.73 | convolution fusion | flops 176160768 | bytes 5816320 | tf_op jit(solution)/shard_map/dot_general | solution.py:326
  14.1 0.4 collective-permute-start.3
  14.5 0.0 collective-permute-start.4
  14.5 0.9 %fusion.21.own_ref = f32[128,1536]{1,0:T(8,128)S(1)} fusion(bf16[128,1792]{1,0:T(8,128)(2,1)S(1)} %slice_select_fusion, bf16[1792,1536]{1,0:T(8,128)(2,1)S(1)} %load_head.1.head_ref), kind=kOutput, calls=%fused_computation.75 | convolution fusion | flops 704643072 | bytes 6750208 | tf_op jit(solution)/shard_map/dot_general | solution.py:332
  15.4 0.1 and_reduce_fusion
  15.6 0.3 fusion
  15.9 0.1 collective-permute-done.4
  16.0 1.1 %fusion.20 = f32[64,1536]{1,0:T(8,128)S(1)} fusion(bf16[64,1792]{1,0:T(8,128)(2,1)S(1)} %collective-permute-done.4, bf16[1792,1536]{1,0:T(8,128)(2,1)S(1)} %load_head.1.head_ref), kind=kOutput, calls=%fused_computation.74 | convolution fusion | flops 352321536 | bytes 6127616 | tf_op jit(solution)/shard_map/dot_general | solution.py:326
  17.0 1.8 %collective-permute-start.5 = (f32[64,1536]{1,0:T(8,128)S(1)}, f32[64,1536]{1,0:T(8,128)S(1)}, u32[]{:S(2)}, u32[]{:S(2)}) collective-permute-start(f32[64,1536]{1,0:T(8,128)S(1)} %fusion.20), channel_id=1, source_target_pairs={{0,1},{1,0},{2,3},{3,2},{4,5},{5,4},{6,7},{7,6},{8,9},{9,8},{10,11... | collective-permute-start | bytes 1179656 | tf_op jit(solution)/shard_map/ppermute | solution.py:19
  18.9 0.1 pad_maximum_fusion.refs_0_
  19.0 4.1 %collective-permute-done.3.refs_1_ = f32[32,1536]{1,0:T(8,128)S(1)} collective-permute-done((f32[32,1536]{1,0:T(8,128)S(1)}, f32[32,1536]{1,0:T(8,128)S(1)}, u32[]{:S(2)}, u32[]{:S(2)}) %collective-permute-start.3) | collective-permute-done | bytes 196640 | tf_op jit(solution)/shard_map/ppermute | solution.py:19
  23.0 7.0 %collective-permute-done.5.refs_2_ = f32[64,1536]{1,0:T(8,128)S(1)} collective-permute-done((f32[64,1536]{1,0:T(8,128)S(1)}, f32[64,1536]{1,0:T(8,128)S(1)}, u32[]{:S(2)}, u32[]{:S(2)}) %collective-permute-start.5) | collective-permute-done | bytes 393248 | tf_op jit(solution)/shard_map/ppermute | solution.py:19
  30.0 0.4 local_stats.1
  30.4 0.0 collective-permute-start.6
  30.5 1.1 %collective-permute-done.6 = f32[1,4,128]{2,1,0:T(4,128)S(1)} collective-permute-done((f32[1,4,128]{2,1,0:T(4,128)S(1)}, f32[1,4,128]{2,1,0:T(4,128)S(1)}, u32[]{:S(2)}, u32[]{:S(2)}) %collective-permute-start.6) | collective-permute-done | bytes 2080 | tf_op jit(solution)/shard_map/ppermute | solution.py:23
  31.7 1.5 %collective-permute-start.9 = (f32[2,4,128]{2,1,0:T(4,128)S(1)}, f32[2,4,128]{2,1,0:T(4,128)S(1)}, u32[]{:S(2)}, u32[]{:S(2)}) collective-permute-start(f32[2,4,128]{2,1,0:T(4,128)S(1)} %pad_maximum_fusion.4), channel_id=1, source_target_pairs={{0,4},{2,6},{4,0},{6,2},{8,12},{10,14},{12,8},{14,10},{16,20},{18,... | collective-permute-start | bytes 12296 | tf_op jit(solution)/shard_map/ppermute | solution.py:23
  33.1 1.6 %collective-permute-start.8 = (f32[2,4,128]{2,1,0:T(4,128)S(1)}, f32[2,4,128]{2,1,0:T(4,128)S(1)}, u32[]{:S(2)}, u32[]{:S(2)}) collective-permute-start(f32[2,4,128]{2,1,0:T(4,128)S(1)} %pad_maximum_fusion.4), channel_id=1, source_target_pairs={{0,8},{2,10},{4,12},{6,14},{8,0},{10,2},{12,4},{14,6},{16,24},{18,... | collective-permute-start | bytes 12296 | tf_op jit(solution)/shard_map/ppermute | solution.py:23
  34.7 0.5 collective-permute-start.7
  35.2 0.1 collective-permute-done.9
  35.3 1.4 %collective-permute-done.8 = f32[2,4,128]{2,1,0:T(4,128)S(1)} collective-permute-done((f32[2,4,128]{2,1,0:T(4,128)S(1)}, f32[2,4,128]{2,1,0:T(4,128)S(1)}, u32[]{:S(2)}, u32[]{:S(2)}) %collective-permute-start.8) | collective-permute-done | bytes 4128 | tf_op jit(solution)/shard_map/ppermute | solution.py:23
  36.7 2.5 %collective-permute-done.7 = f32[2,4,128]{2,1,0:T(4,128)S(1)} collective-permute-done((f32[2,4,128]{2,1,0:T(4,128)S(1)}, f32[2,4,128]{2,1,0:T(4,128)S(1)}, u32[]{:S(2)}, u32[]{:S(2)}) %collective-permute-start.7) | collective-permute-done | bytes 4128 | tf_op jit(solution)/shard_map/ppermute | solution.py:23
  39.2 2.7 %collective-permute-start.10 = (f32[8,4,128]{2,1,0:T(4,128)S(1)}, f32[8,4,128]{2,1,0:T(4,128)S(1)}, u32[]{:S(2)}, u32[]{:S(2)}) collective-permute-start(f32[8,4,128]{2,1,0:T(4,128)S(1)} %pad_maximum_fusion.3), channel_id=1, source_target_pairs={{0,16},{2,18},{4,20},{6,22},{8,24},{10,26},{12,28},{14,30},{16,0},... | collective-permute-start | bytes 49160 | tf_op jit(solution)/shard_map/ppermute | solution.py:23
  41.9 2.1 %collective-permute-done.10 = f32[8,4,128]{2,1,0:T(4,128)S(1)} collective-permute-done((f32[8,4,128]{2,1,0:T(4,128)S(1)}, f32[8,4,128]{2,1,0:T(4,128)S(1)}, u32[]{:S(2)}, u32[]{:S(2)}) %collective-permute-start.10) | collective-permute-done | bytes 16416 | tf_op jit(solution)/shard_map/ppermute | solution.py:23
  44.0 0.9 %delta.1 = (bf16[128,1536]{1,0:T(8,128)(2,1)S(1)}, f32[1,128]{1,0:T(1,128)}, f32[1,128]{1,0:T(1,128)}) custom-call(f32[16,4,128]{2,1,0:T(4,128)S(1)} %pad_maximum_fusion.2.gathered_ref, f32[128,1536]{1,0:T(8,128)S(1)} %get-tuple-element.70.logits_ref, bf16[128,1536]{1,0:T(8,128)(2,1)S(1)} %get-tuple-element.64.kept_ref), custom_call_target="tpu_custom_call" | custom-call | flops 1572864 | bytes 1572864 | tf_op jit(solution)/shard_map/delta/pallas_call | solution.py:155
  44.9 1.5 %collective-permute-start.11 = (bf16[128,1536]{1,0:T(8,128)(2,1)S(1)}, bf16[128,1536]{1,0:T(8,128)(2,1)S(1)}, u32[]{:S(2)}, u32[]{:S(2)}) collective-permute-start(bf16[128,1536]{1,0:T(8,128)(2,1)S(1)} %get-tuple-element.74.delta_ref), channel_id=1, source_target_pairs={{0,1},{1,0},{2,3},{3,2},{4,5},{5,4},{6,7},{7,6},{8,9},{9,8},{10,11... | collective-permute-start | bytes 1179656 | tf_op jit(solution)/shard_map/ppermute | solution.py:19
  46.4 1.6 %partial_gradient.5 = f32[4,2,224,128]{3,2,1,0:T(8,128)S(1)} custom-call(bf16[1792,1536]{1,0:T(8,128)(2,1)S(1)} %load_head.1.head_ref, bf16[128,1536]{1,0:T(8,128)(2,1)S(1)} %get-tuple-element.74.delta_ref), custom_call_target="tpu_custom_call" | custom-call | flops 704643072 | bytes 5898240 | tf_op jit(solution)/shard_map/partial_gradient/pallas_call | solution.py:214
  48.0 0.1 fusion.11
  48.1 0.4 collective-permute-start.19
  48.5 1.5 %collective-permute-start.17 = (bf16[2,224,128]{2,1,0:T(8,128)(2,1)S(1)}, bf16[2,224,128]{2,1,0:T(8,128)(2,1)S(1)}, u32[]{:S(2)}, u32[]{:S(2)}) collective-permute-start(bf16[2,224,128]{2,1,0:T(8,128)(2,1)S(1)} %get-tuple-element.95), channel_id=1, source_target_pairs={{0,4},{2,6},{4,0},{6,2},{8,12},{10,14},{12,8},{14,10},{16,20},{18,... | collective-permute-start | bytes 344072 | tf_op jit(solution)/shard_map/ppermute | solution.py:23
  50.0 1.6 %collective-permute-start.18 = (bf16[2,224,128]{2,1,0:T(8,128)(2,1)S(1)}, bf16[2,224,128]{2,1,0:T(8,128)(2,1)S(1)}, u32[]{:S(2)}, u32[]{:S(2)}) collective-permute-start(bf16[2,224,128]{2,1,0:T(8,128)(2,1)S(1)} %get-tuple-element.96), channel_id=1, source_target_pairs={{0,8},{2,10},{4,12},{6,14},{8,0},{10,2},{12,4},{14,6},{16,24},{18,... | collective-permute-start | bytes 344072 | tf_op jit(solution)/shard_map/ppermute | solution.py:23
  51.6 1.6 %collective-permute-done.11.delta_ref = bf16[128,1536]{1,0:T(8,128)(2,1)S(1)} collective-permute-done((bf16[128,1536]{1,0:T(8,128)(2,1)S(1)}, bf16[128,1536]{1,0:T(8,128)(2,1)S(1)}, u32[]{:S(2)}, u32[]{:S(2)}) %collective-permute-start.11) | collective-permute-done | bytes 393248 | tf_op jit(solution)/shard_map/ppermute | solution.py:19
  53.2 0.9 %partial_gradient.3 = bf16[4,224,128]{2,1,0:T(8,128)(2,1)S(1)} custom-call(s32[1]{0:T(128)} %bitcast.1.core_ref, bf16[1792,1536]{1,0:T(8,128)(2,1)S(1)} %load_head.1.head_ref, bf16[128,1536]{1,0:T(8,128)(2,1)S(1)} %collective-permute-done.11.delta_ref), custom_call_target="tpu_custom_call" | custom-call | flops 704643072 | bytes 5898240 | tf_op jit(solution)/shard_map/partial_gradient/pallas_call | solution.py:214
  54.1 0.1 collective-permute-start.12
  54.2 0.9 %partial_gradient.4 = f32[4,224,128]{2,1,0:T(8,128)S(1)} custom-call(s32[1]{0:T(128)} %bitcast.1.core_ref, bf16[1792,1536]{1,0:T(8,128)(2,1)S(1)} %load_head.1.head_ref, bf16[128,1536]{1,0:T(8,128)(2,1)S(1)} %collective-permute-done.11.delta_ref), custom_call_target="tpu_custom_call" | custom-call | flops 704643072 | bytes 5898240 | tf_op jit(solution)/shard_map/partial_gradient/pallas_call | solution.py:214
  55.0 0.0 collective-permute-done.19
  55.1 0.0 collective-permute-done.17
  55.1 0.1 pad_maximum_fusion.1.refs_1_
  55.1 0.1 fusion.5
  55.2 0.4 collective-permute-done.12
  55.6 0.1 convert_add_fusion
  55.7 0.7 collective-permute-start.13
  56.4 0.8 %collective-permute-start.14 = (bf16[1,224,128]{2,1,0:T(8,128)(2,1)S(1)}, bf16[1,224,128]{2,1,0:T(8,128)(2,1)S(1)}, u32[]{:S(2)}, u32[]{:S(2)}) collective-permute-start(bf16[1,224,128]{2,1,0:T(8,128)(2,1)S(1)} %get-tuple-element.77), channel_id=1, source_target_pairs={{0,8},{2,10},{4,12},{6,14},{8,0},{10,2},{12,4},{14,6},{16,24},{18,... | collective-permute-start | bytes 172040 | tf_op jit(solution)/shard_map/ppermute | solution.py:23
  57.3 2.0 %collective-permute-start.15 = (bf16[1,224,128]{2,1,0:T(8,128)(2,1)S(1)}, bf16[1,224,128]{2,1,0:T(8,128)(2,1)S(1)}, u32[]{:S(2)}, u32[]{:S(2)}) collective-permute-start(bf16[1,224,128]{2,1,0:T(8,128)(2,1)S(1)} %get-tuple-element.78), channel_id=1, source_target_pairs={{0,12},{2,14},{4,8},{6,10},{8,4},{10,6},{12,0},{14,2},{16,28},{18,... | collective-permute-start | bytes 172040 | tf_op jit(solution)/shard_map/ppermute | solution.py:23
  59.3 2.1 %head_gradient.2.refs_2_ = bf16[1792,1536]{1,0:T(8,128)(2,1)} custom-call(bf16[256,1792]{1,0:T(8,128)(2,1)S(1)} %pad_maximum_fusion.refs_0_, bf16[256,1536]{1,0:T(8,128)(2,1)S(1)} %pad_maximum_fusion.1.refs_1_), custom_call_target="tpu_custom_call" | custom-call | flops 805306368 | bytes 4849664 | tf_op jit(solution)/shard_map/head_gradient/pallas_call | solution.py:253
  61.4 0.0 collective-permute-done.13
  61.4 0.9 %collective-permute-done.15 = bf16[1,224,128]{2,1,0:T(8,128)(2,1)S(1)} collective-permute-done((bf16[1,224,128]{2,1,0:T(8,128)(2,1)S(1)}, bf16[1,224,128]{2,1,0:T(8,128)(2,1)S(1)}, u32[]{:S(2)}, u32[]{:S(2)}) %collective-permute-start.15) | collective-permute-done | bytes 57376 | tf_op jit(solution)/shard_map/ppermute | solution.py:23
  62.3 0.1 fusion.12
  62.4 1.4 %collective-permute-start.16 = (bf16[224,128]{1,0:T(8,128)(2,1)S(1)}, bf16[224,128]{1,0:T(8,128)(2,1)S(1)}, u32[]{:S(2)}, u32[]{:S(2)}) collective-permute-start(bf16[224,128]{1,0:T(8,128)(2,1)S(1)} %fusion.12), channel_id=1, source_target_pairs={{0,1},{1,0},{2,3},{3,2},{4,5},{5,4},{6,7},{7,6},{8,9},{9,8},{10,11... | collective-permute-start | bytes 172040 | tf_op jit(solution)/shard_map/ppermute | solution.py:19
  63.8 0.1 collective-permute-start.20
  63.9 1.8 %head_gradient.3 = bf16[1792,1536]{1,0:T(8,128)(2,1)} custom-call(bf16[256,1792]{1,0:T(8,128)(2,1)S(1)} %pad_maximum_fusion.refs_0_, bf16[256,1536]{1,0:T(8,128)(2,1)S(1)} %pad_maximum_fusion.1.refs_1_, bf16[1792,1536]{1,0:T(8,128)(2,1)} %head_gradient.2.refs_2_), custom_call_target="tpu_custom_call", output_to_operand_aliasing={{}: (2, {})} | custom-call | flops 603979776 | bytes 4063232 | tf_op jit(solution)/shard_map/head_gradient/pallas_call | solution.py:253
  65.7 0.9 %collective-permute-done.16 = bf16[224,128]{1,0:T(8,128)(2,1)S(1)} collective-permute-done((bf16[224,128]{1,0:T(8,128)(2,1)S(1)}, bf16[224,128]{1,0:T(8,128)(2,1)S(1)}, u32[]{:S(2)}, u32[]{:S(2)}) %collective-permute-start.16) | collective-permute-done | bytes 57376 | tf_op jit(solution)/shard_map/ppermute | solution.py:19
  66.6 0.0 collective-permute-done.20
  66.7 2.6 %collective-permute-start.21 = (bf16[224,128]{1,0:T(8,128)(2,1)S(1)}, bf16[224,128]{1,0:T(8,128)(2,1)S(1)}, u32[]{:S(2)}, u32[]{:S(2)}) collective-permute-start(bf16[224,128]{1,0:T(8,128)(2,1)S(1)} %fusion.8), channel_id=1, source_target_pairs={{0,16},{2,18},{4,20},{6,22},{8,24},{10,26},{12,28},{14,30},{16,0},... | collective-permute-start | bytes 172040 | tf_op jit(solution)/shard_map/ppermute | solution.py:412
  69.3 2.6 %collective-permute-done.21 = bf16[224,128]{1,0:T(8,128)(2,1)S(1)} collective-permute-done((bf16[224,128]{1,0:T(8,128)(2,1)S(1)}, bf16[224,128]{1,0:T(8,128)(2,1)S(1)}, u32[]{:S(2)}, u32[]{:S(2)}) %collective-permute-start.21) | collective-permute-done | bytes 57376 | tf_op jit(solution)/shard_map/ppermute | solution.py:412
  71.8 0.7 fusion.7
  (24 shorter events, 0.3 us)
Async XLA Ops:
  1.6 11.4 %collective-permute-start.2 = (bf16[32,1792]{1,0:T(8,128)(2,1)S(1)}, bf16[32,1792]{1,0:T(8,128)(2,1)S(1)}, u32[]{:S(2)}, u32[]{:S(2)}) collective-permute-start(bf16[32,1792]{1,0:T(8,128)(2,1)S(1)} %get-tuple-element.97), channel_id=1, source_target_pairs={{0,1},{1,0},{2,3},{3,2},{4,5},{5,4},{6,7},{7,6},{8,9},{9,8},{10,11... | collective-permute-start | bytes 344072 | tf_op jit(solution)/shard_map/ppermute | solution.py:19
  4.7 5.6 %collective-permute-start = (bf16[32,1792]{1,0:T(8,128)(2,1)S(1)}, bf16[32,1792]{1,0:T(8,128)(2,1)S(1)}, u32[]{:S(2)}, u32[]{:S(2)}) collective-permute-start(bf16[32,1792]{1,0:T(8,128)(2,1)S(1)} %get-tuple-element.98), channel_id=1, source_target_pairs={{0,1},{1,0},{2,3},{3,2},{4,5},{5,4},{6,7},{7,6},{8,9},{9,8},{10,11... | collective-permute-start | bytes 344072 | tf_op jit(solution)/shard_map/ppermute | solution.py:19
  8.1 6.4 %copy-start = (bf16[128,3584]{1,0:T(8,128)(2,1)S(1)}, bf16[128,3584]{1,0:T(8,128)(2,1)}, u32[]{:S(2)}) copy-start(bf16[128,3584]{1,0:T(8,128)(2,1)} %param.5) | copy-start | bytes 2752516
  11.3 11.7 %collective-permute-start.1 = (f32[32,1536]{1,0:T(8,128)S(1)}, f32[32,1536]{1,0:T(8,128)S(1)}, u32[]{:S(2)}, u32[]{:S(2)}) collective-permute-start(f32[32,1536]{1,0:T(8,128)S(1)} %fusion.18), channel_id=1, source_target_pairs={{0,1},{1,0},{2,3},{3,2},{4,5},{5,4},{6,7},{7,6},{8,9},{9,8},{10,11... | collective-permute-start | bytes 589832 | tf_op jit(solution)/shard_map/ppermute | solution.py:19
  14.1 1.3 %copy-start.2 = (s32[1,16]{1,0:T(1,128)S(1)}, s32[1,16]{1,0:T(1,128)}, u32[]{:S(2)}) copy-start(s32[1,16]{1,0:T(1,128)} %param.8) | copy-start | bytes 196
  14.1 1.5 %copy-start.1 = (bf16[128,1536]{1,0:T(8,128)(2,1)S(1)}, bf16[128,1536]{1,0:T(8,128)(2,1)}, u32[]{:S(2)}) copy-start(bf16[128,1536]{1,0:T(8,128)(2,1)} %param.7) | copy-start | bytes 1179652
  14.1 8.9 %collective-permute-start.3 = (f32[32,1536]{1,0:T(8,128)S(1)}, f32[32,1536]{1,0:T(8,128)S(1)}, u32[]{:S(2)}, u32[]{:S(2)}) collective-permute-start(f32[32,1536]{1,0:T(8,128)S(1)} %fusion.19), channel_id=1, source_target_pairs={{0,1},{1,0},{2,3},{3,2},{4,5},{5,4},{6,7},{7,6},{8,9},{9,8},{10,11... | collective-permute-start | bytes 589832 | tf_op jit(solution)/shard_map/ppermute | solution.py:19
  14.5 1.5 %collective-permute-start.4 = (bf16[64,1792]{1,0:T(8,128)(2,1)S(1)}, bf16[64,1792]{1,0:T(8,128)(2,1)S(1)}, u32[]{:S(2)}, u32[]{:S(2)}) collective-permute-start(bf16[64,1792]{1,0:T(8,128)(2,1)S(1)} %constant_dynamic-update-slice_fusion), channel_id=1, source_target_pairs={{0,2},{2,0},{4,6},{6,4},{8,10},{10,8},{12,14},{14,12},{16,18},{18,... | collective-permute-start | bytes 688136 | tf_op jit(solution)/shard_map/ppermute | solution.py:23
  17.0 13.0 %collective-permute-start.5 = (f32[64,1536]{1,0:T(8,128)S(1)}, f32[64,1536]{1,0:T(8,128)S(1)}, u32[]{:S(2)}, u32[]{:S(2)}) collective-permute-start(f32[64,1536]{1,0:T(8,128)S(1)} %fusion.20), channel_id=1, source_target_pairs={{0,1},{1,0},{2,3},{3,2},{4,5},{5,4},{6,7},{7,6},{8,9},{9,8},{10,11... | collective-permute-start | bytes 1179656 | tf_op jit(solution)/shard_map/ppermute | solution.py:19
  30.4 1.2 %collective-permute-start.6 = (f32[1,4,128]{2,1,0:T(4,128)S(1)}, f32[1,4,128]{2,1,0:T(4,128)S(1)}, u32[]{:S(2)}, u32[]{:S(2)}) collective-permute-start(f32[1,4,128]{2,1,0:T(4,128)S(1)} %bitcast.44), channel_id=1, source_target_pairs={{0,2},{2,0},{4,6},{6,4},{8,10},{10,8},{12,14},{14,12},{16,18},{18,... | collective-permute-start | bytes 6152 | tf_op jit(solution)/shard_map/ppermute | solution.py:23
  31.7 3.7 %collective-permute-start.9 = (f32[2,4,128]{2,1,0:T(4,128)S(1)}, f32[2,4,128]{2,1,0:T(4,128)S(1)}, u32[]{:S(2)}, u32[]{:S(2)}) collective-permute-start(f32[2,4,128]{2,1,0:T(4,128)S(1)} %pad_maximum_fusion.4), channel_id=1, source_target_pairs={{0,4},{2,6},{4,0},{6,2},{8,12},{10,14},{12,8},{14,10},{16,20},{18,... | collective-permute-start | bytes 12296 | tf_op jit(solution)/shard_map/ppermute | solution.py:23
  33.1 3.6 %collective-permute-start.8 = (f32[2,4,128]{2,1,0:T(4,128)S(1)}, f32[2,4,128]{2,1,0:T(4,128)S(1)}, u32[]{:S(2)}, u32[]{:S(2)}) collective-permute-start(f32[2,4,128]{2,1,0:T(4,128)S(1)} %pad_maximum_fusion.4), channel_id=1, source_target_pairs={{0,8},{2,10},{4,12},{6,14},{8,0},{10,2},{12,4},{14,6},{16,24},{18,... | collective-permute-start | bytes 12296 | tf_op jit(solution)/shard_map/ppermute | solution.py:23
  34.7 4.5 %collective-permute-start.7 = (f32[2,4,128]{2,1,0:T(4,128)S(1)}, f32[2,4,128]{2,1,0:T(4,128)S(1)}, u32[]{:S(2)}, u32[]{:S(2)}) collective-permute-start(f32[2,4,128]{2,1,0:T(4,128)S(1)} %pad_maximum_fusion.4), channel_id=1, source_target_pairs={{0,12},{2,14},{4,8},{6,10},{8,4},{10,6},{12,0},{14,2},{16,28},{18,... | collective-permute-start | bytes 12296 | tf_op jit(solution)/shard_map/ppermute | solution.py:23
  39.2 4.8 %collective-permute-start.10 = (f32[8,4,128]{2,1,0:T(4,128)S(1)}, f32[8,4,128]{2,1,0:T(4,128)S(1)}, u32[]{:S(2)}, u32[]{:S(2)}) collective-permute-start(f32[8,4,128]{2,1,0:T(4,128)S(1)} %pad_maximum_fusion.3), channel_id=1, source_target_pairs={{0,16},{2,18},{4,20},{6,22},{8,24},{10,26},{12,28},{14,30},{16,0},... | collective-permute-start | bytes 49160 | tf_op jit(solution)/shard_map/ppermute | solution.py:23
  44.9 8.3 %collective-permute-start.11 = (bf16[128,1536]{1,0:T(8,128)(2,1)S(1)}, bf16[128,1536]{1,0:T(8,128)(2,1)S(1)}, u32[]{:S(2)}, u32[]{:S(2)}) collective-permute-start(bf16[128,1536]{1,0:T(8,128)(2,1)S(1)} %get-tuple-element.74.delta_ref), channel_id=1, source_target_pairs={{0,1},{1,0},{2,3},{3,2},{4,5},{5,4},{6,7},{7,6},{8,9},{9,8},{10,11... | collective-permute-start | bytes 1179656 | tf_op jit(solution)/shard_map/ppermute | solution.py:19
  48.1 7.0 %collective-permute-start.19 = (bf16[2,224,128]{2,1,0:T(8,128)(2,1)S(1)}, bf16[2,224,128]{2,1,0:T(8,128)(2,1)S(1)}, u32[]{:S(2)}, u32[]{:S(2)}) collective-permute-start(bf16[2,224,128]{2,1,0:T(8,128)(2,1)S(1)} %get-tuple-element.94), channel_id=1, source_target_pairs={{0,12},{2,14},{4,8},{6,10},{8,4},{10,6},{12,0},{14,2},{16,28},{18,... | collective-permute-start | bytes 344072 | tf_op jit(solution)/shard_map/ppermute | solution.py:23
  48.5 6.6 %collective-permute-start.17 = (bf16[2,224,128]{2,1,0:T(8,128)(2,1)S(1)}, bf16[2,224,128]{2,1,0:T(8,128)(2,1)S(1)}, u32[]{:S(2)}, u32[]{:S(2)}) collective-permute-start(bf16[2,224,128]{2,1,0:T(8,128)(2,1)S(1)} %get-tuple-element.95), channel_id=1, source_target_pairs={{0,4},{2,6},{4,0},{6,2},{8,12},{10,14},{12,8},{14,10},{16,20},{18,... | collective-permute-start | bytes 344072 | tf_op jit(solution)/shard_map/ppermute | solution.py:23
  50.0 5.1 %collective-permute-start.18 = (bf16[2,224,128]{2,1,0:T(8,128)(2,1)S(1)}, bf16[2,224,128]{2,1,0:T(8,128)(2,1)S(1)}, u32[]{:S(2)}, u32[]{:S(2)}) collective-permute-start(bf16[2,224,128]{2,1,0:T(8,128)(2,1)S(1)} %get-tuple-element.96), channel_id=1, source_target_pairs={{0,8},{2,10},{4,12},{6,14},{8,0},{10,2},{12,4},{14,6},{16,24},{18,... | collective-permute-start | bytes 344072 | tf_op jit(solution)/shard_map/ppermute | solution.py:23
  54.1 1.6 %collective-permute-start.12 = (bf16[4,224,128]{2,1,0:T(8,128)(2,1)S(1)}, bf16[4,224,128]{2,1,0:T(8,128)(2,1)S(1)}, u32[]{:S(2)}, u32[]{:S(2)}) collective-permute-start(bf16[4,224,128]{2,1,0:T(8,128)(2,1)S(1)} %partial_gradient.3), channel_id=1, source_target_pairs={{0,2},{2,0},{4,6},{6,4},{8,10},{10,8},{12,14},{14,12},{16,18},{18,... | collective-permute-start | bytes 688136 | tf_op jit(solution)/shard_map/ppermute | solution.py:23
  55.7 5.6 %collective-permute-start.13 = (bf16[1,224,128]{2,1,0:T(8,128)(2,1)S(1)}, bf16[1,224,128]{2,1,0:T(8,128)(2,1)S(1)}, u32[]{:S(2)}, u32[]{:S(2)}) collective-permute-start(bf16[1,224,128]{2,1,0:T(8,128)(2,1)S(1)} %get-tuple-element.76), channel_id=1, source_target_pairs={{0,4},{2,6},{4,0},{6,2},{8,12},{10,14},{12,8},{14,10},{16,20},{18,... | collective-permute-start | bytes 172040 | tf_op jit(solution)/shard_map/ppermute | solution.py:23
  56.4 5.0 %collective-permute-start.14 = (bf16[1,224,128]{2,1,0:T(8,128)(2,1)S(1)}, bf16[1,224,128]{2,1,0:T(8,128)(2,1)S(1)}, u32[]{:S(2)}, u32[]{:S(2)}) collective-permute-start(bf16[1,224,128]{2,1,0:T(8,128)(2,1)S(1)} %get-tuple-element.77), channel_id=1, source_target_pairs={{0,8},{2,10},{4,12},{6,14},{8,0},{10,2},{12,4},{14,6},{16,24},{18,... | collective-permute-start | bytes 172040 | tf_op jit(solution)/shard_map/ppermute | solution.py:23
  57.3 5.1 %collective-permute-start.15 = (bf16[1,224,128]{2,1,0:T(8,128)(2,1)S(1)}, bf16[1,224,128]{2,1,0:T(8,128)(2,1)S(1)}, u32[]{:S(2)}, u32[]{:S(2)}) collective-permute-start(bf16[1,224,128]{2,1,0:T(8,128)(2,1)S(1)} %get-tuple-element.78), channel_id=1, source_target_pairs={{0,12},{2,14},{4,8},{6,10},{8,4},{10,6},{12,0},{14,2},{16,28},{18,... | collective-permute-start | bytes 172040 | tf_op jit(solution)/shard_map/ppermute | solution.py:23
  62.4 4.2 %collective-permute-start.16 = (bf16[224,128]{1,0:T(8,128)(2,1)S(1)}, bf16[224,128]{1,0:T(8,128)(2,1)S(1)}, u32[]{:S(2)}, u32[]{:S(2)}) collective-permute-start(bf16[224,128]{1,0:T(8,128)(2,1)S(1)} %fusion.12), channel_id=1, source_target_pairs={{0,1},{1,0},{2,3},{3,2},{4,5},{5,4},{6,7},{7,6},{8,9},{9,8},{10,11... | collective-permute-start | bytes 172040 | tf_op jit(solution)/shard_map/ppermute | solution.py:19
  63.8 2.8 %collective-permute-start.20 = (bf16[224,128]{1,0:T(8,128)(2,1)S(1)}, bf16[224,128]{1,0:T(8,128)(2,1)S(1)}, u32[]{:S(2)}, u32[]{:S(2)}) collective-permute-start(bf16[224,128]{1,0:T(8,128)(2,1)S(1)} %fusion.13), channel_id=1, source_target_pairs={{0,2},{2,0},{4,6},{6,4},{8,10},{10,8},{12,14},{14,12},{16,18},{18,... | collective-permute-start | bytes 172040 | tf_op jit(solution)/shard_map/ppermute | solution.py:23
  66.7 5.1 %collective-permute-start.21 = (bf16[224,128]{1,0:T(8,128)(2,1)S(1)}, bf16[224,128]{1,0:T(8,128)(2,1)S(1)}, u32[]{:S(2)}, u32[]{:S(2)}) collective-permute-start(bf16[224,128]{1,0:T(8,128)(2,1)S(1)} %fusion.8), channel_id=1, source_target_pairs={{0,16},{2,18},{4,20},{6,22},{8,24},{10,26},{12,28},{14,30},{16,0},... | collective-permute-start | bytes 172040 | tf_op jit(solution)/shard_map/ppermute | solution.py:412

commit v15 on v14

--- a/solution.py
+++ b/solution.py
@@ -374,32 +374,37 @@
 
     width = 256 if rows % 256 == 0 else rows
     chunks = rows // width
-    held = jnp.stack([keep + other.astype(jnp.float32) for keep, other in state], axis=1)
-    taken = direct(list(held))
-    sends = [x.astype(jnp.bfloat16) for x in taken[1:]]
-    sends, all_delta = lax.optimization_barrier((sends, all_delta))
-    others = [swap_vocab(x, 2 * (i + 1), vocab_size) for i, x in enumerate(sends)]
+    taken = [
+        direct(list(keep + other.astype(jnp.float32))) for keep, other in state
+    ]
+    taken = [[x.astype(jnp.bfloat16) for x in pieces] for pieces in taken]
+    taken, all_delta = lax.optimization_barrier((taken, all_delta))
+    arrived = []
+    for d, pieces in enumerate(taken, 1):
+        block = []
+        for offset, piece in enumerate(pieces):
+            pairs = [
+                (v * tok_size + t, (v ^ (2 * offset)) * tok_size + (t - d) % tok_size)
+                for v in range(vocab_size)
+                for t in range(tok_size)
+            ]
+            block.append(lax.ppermute(piece, ("vocab", "tok"), pairs))
+        arrived.append(block)
     done = (chunks + 1) // 2
     grad_head = head_gradient(all_features, all_delta, None, 0, done, width)
-    others, grad_head = lax.optimization_barrier((others, grad_head))
-    sums = taken[0]
-    for other in others:
-        sums = sums + other.astype(jnp.float32)
+    arrived, grad_head = lax.optimization_barrier((arrived, grad_head))
     own_sum = own_pieces[0]
     for other in own_others:
         own_sum = own_sum + other.astype(jnp.float32)
     send = jnp.where(upper[0], own_sum[0], own_sum[1]).astype(jnp.bfloat16)
     own_sum = jnp.where(upper[0], own_sum[1], own_sum[0])
     own_sum = own_sum + swap_vocab(send, 1, vocab_size).astype(jnp.float32)
-    sends = [x.astype(jnp.bfloat16) for x in sums]
-    sends, all_delta = lax.optimization_barrier((sends, all_delta))
-    others = [shift_tok(x, -d, tok_size) for d, x in enumerate(sends, 1)]
-    if done < chunks:
-        grad_head = head_gradient(
-            all_features, all_delta, grad_head, done * width, chunks - done, width
-        )
-        others, grad_head = lax.optimization_barrier((others, grad_head))
-    sums = [own_sum] + [x.astype(jnp.float32) for x in others]
+    sums = [own_sum]
+    for block in arrived:
+        total = block[0].astype(jnp.float32)
+        for x in block[1:]:
+            total = total + x.astype(jnp.float32)
+        sums.append(total)
     blocks = []
     for k in range(tok_size):
         block = sums[k]
@@ -407,6 +412,11 @@
             block = jnp.where(apart_is[d], sums[(k - d) % tok_size], block)
         blocks.append(block)
     total = blocks[0]
+    if done < chunks:
+        blocks[1:], all_delta = lax.optimization_barrier((blocks[1:], all_delta))
+        grad_head = head_gradient(
+            all_features, all_delta, grad_head, done * width, chunks - done, width
+        )
     for k in range(1, tok_size):
         pairs = [(v, (v + k * run) % vocab_size) for v in range(vocab_size)]
         total = total + lax.ppermute(

time: 72.7 us -> 71.4 us (0.982)
  waiting for transfers between devices: 27 us -> 24.2 us
  starting transfers between devices: 26.1 us -> 27.6 us
    ppermute x0 -> x4, starting transfers between devices: none -> 5.91 us  [per_device(): block.append(lax.ppermute(piece, ('vocab', 'tok'), pairs))]
    ppermute x14 -> x11, starting transfers between devices: 13.5 us -> 10.5 us  [swap_vocab(): return lax.ppermute(x, 'vocab', [(i, i ^ bit) for i in range(size)])]
    ppermute x1, waiting for transfers between devices: 2.55 us -> 0.7 us  [per_device(): lax.ppermute(blocks[k].astype(jnp.bfloat16), 'vocab', pairs)]
    ppermute x7 -> x6, starting transfers between devices: 9.95 us -> 8.54 us  [shift_tok(): lax.ppermute(x, 'tok', [(i, (i + offset) % size) for i in range(size)])]
    ppermute x0 -> x4, waiting for transfers between devices: none -> 1.38 us  [per_device(): block.append(lax.ppermute(piece, ('vocab', 'tok'), pairs))]
    ppermute x14 -> x11, waiting for transfers between devices: 8.67 us -> 7.3 us  [swap_vocab(): return lax.ppermute(x, 'vocab', [(i, i ^ bit) for i in range(size)])]
    ppermute x7 -> x6, waiting for transfers between devices: 15.7 us -> 14.8 us  [shift_tok(): lax.ppermute(x, 'tok', [(i, (i + offset) % size) for i in range(size)])]
  transfers between devices with their start and end apart: 22 -> 22, of which waited for: 14 -> 12; matrix products, arithmetic and copies ran while one was open for 7% -> 7% of each run, Pallas kernels for 14% -> 14%
where the time goes in v15:
time: 71.4 us; the launch traced here: 71.2 us
  starting transfers between devices  27.6 us (39%)
  waiting for transfers between devices  24.2 us (34%)
  Pallas kernels  11.1 us (16%)
  matrix products  4.01 us (6%)
  other arithmetic  1.69 us (2%)
  between operations  1.6 us (2%)
  local copies, waits for them, and re-layouts  1.01 us (1%)
    ppermute x6, waiting for transfers between devices, shift_tok(): lax.ppermute(x, 'tok', [(i, (i + offset) % size) for i in range(size)])  14.8 us
    ppermute x11, starting transfers between devices, swap_vocab(): return lax.ppermute(x, 'vocab', [(i, i ^ bit) for i in range(size)])  10.5 us
    ppermute x6, starting transfers between devices, shift_tok(): lax.ppermute(x, 'tok', [(i, (i + offset) % size) for i in range(size)])  8.54 us
    ppermute x11, waiting for transfers between devices, swap_vocab(): return lax.ppermute(x, 'vocab', [(i, i ^ bit) for i in range(size)])  7.3 us
    ppermute x4, starting transfers between devices, per_device(): block.append(lax.ppermute(piece, ('vocab', 'tok'), pairs))  5.91 us
    pallas_call x2, Pallas kernels, head_gradient(): pl.pallas_call(functools.partial(head_gradient_kernel, steps, start, widt...  3.89 us
    pallas_call x3, Pallas kernels, gradient(): pl.pallas_call(kernel, out_shape=out, in_specs=([] if core is None else [...  3.32 us
    dot_general x3, matrix products, per_device(): jnp.dot(x, head_here, preferred_element_type=jnp.float32)  3.13 us
  transfers between devices with their start and end apart: 22, of which 12 were waited for; matrix products, arithmetic and copies ran while one was open for 7% of the time, Pallas kernels for 14%

profile of v15, /device:TPU:0, one launch (start us, length us, event | category | flops | bytes accessed | tf_op | source)
XLA Modules:
  0.0 71.2 jit_solution(15218249444437683160)
XLA Ops:
  0.6 1.0 %fusion.17 = (bf16[32,1792]{1,0:T(8,128)(2,1)S(1)}, bf16[32,1792]{1,0:T(8,128)(2,1)S(1)}) fusion(bf16[128,3584]{1,0:T(8,128)(2,1)} %param.5, s32[]{:T(128)S(6)} %select_n.253, s32[]{:T(128)S(6)} %select_n.252, s32[]{:T(128)S(6)} %select_n.251), kind=kLoop, calls=%fused_computation.72 | loop fusion | bytes 458764 | tf_op jit(solution)/shard_map/dynamic_slice | solution.py:285
  1.6 3.0 %collective-permute-start.2 = (bf16[32,1792]{1,0:T(8,128)(2,1)S(1)}, bf16[32,1792]{1,0:T(8,128)(2,1)S(1)}, u32[]{:S(2)}, u32[]{:S(2)}) collective-permute-start(bf16[32,1792]{1,0:T(8,128)(2,1)S(1)} %get-tuple-element.97), channel_id=1, source_target_pairs={{0,1},{1,0},{2,3},{3,2},{4,5},{5,4},{6,7},{7,6},{8,9},{9,8},{10,11... | collective-permute-start | bytes 344072 | tf_op jit(solution)/shard_map/ppermute | solution.py:19
  4.7 0.1 collective-permute-start
  5.4 2.6 %load_head.1.head_ref = bf16[1792,1536]{1,0:T(8,128)(2,1)S(1)} custom-call(bf16[1792,1536]{1,0:T(8,128)(2,1)} %head_ref), custom_call_target="tpu_custom_call" | custom-call | bytes 11010048 | tf_op jit(solution)/shard_map/load_head/pallas_call | solution.py:67
  8.1 0.0 copy-start
  8.1 2.2 %collective-permute-done = bf16[32,1792]{1,0:T(8,128)(2,1)S(1)} collective-permute-done((bf16[32,1792]{1,0:T(8,128)(2,1)S(1)}, bf16[32,1792]{1,0:T(8,128)(2,1)S(1)}, u32[]{:S(2)}, u32[]{:S(2)}) %collective-permute-start) | collective-permute-done | bytes 114720 | tf_op jit(solution)/shard_map/ppermute | solution.py:19
  10.3 1.0 %fusion.18 = f32[32,1536]{1,0:T(8,128)S(1)} fusion(bf16[32,1792]{1,0:T(8,128)(2,1)S(1)} %collective-permute-done, bf16[1792,1536]{1,0:T(8,128)(2,1)S(1)} %load_head.1.head_ref), kind=kOutput, calls=%fused_computation.73 | convolution fusion | flops 176160768 | bytes 5816320 | tf_op jit(solution)/shard_map/dot_general | solution.py:317
  11.3 1.8 %collective-permute-start.1 = (f32[32,1536]{1,0:T(8,128)S(1)}, f32[32,1536]{1,0:T(8,128)S(1)}, u32[]{:S(2)}, u32[]{:S(2)}) collective-permute-start(f32[32,1536]{1,0:T(8,128)S(1)} %fusion.18), channel_id=1, source_target_pairs={{0,1},{1,0},{2,3},{3,2},{4,5},{5,4},{6,7},{7,6},{8,9},{9,8},{10,11... | collective-permute-start | bytes 589832 | tf_op jit(solution)/shard_map/ppermute | solution.py:19
  13.1 0.0 collective-permute-done.2
  13.1 1.0 %fusion.19 = f32[32,1536]{1,0:T(8,128)S(1)} fusion(bf16[32,1792]{1,0:T(8,128)(2,1)S(1)} %collective-permute-done.2, bf16[1792,1536]{1,0:T(8,128)(2,1)S(1)} %load_head.1.head_ref), kind=kOutput, calls=%fused_computation.74 | convolution fusion | flops 176160768 | bytes 5816320 | tf_op jit(solution)/shard_map/dot_general | solution.py:326
  14.1 0.4 collective-permute-start.3
  14.5 0.0 collective-permute-start.4
  14.5 0.9 %fusion.21.own_ref = f32[128,1536]{1,0:T(8,128)S(1)} fusion(bf16[128,1792]{1,0:T(8,128)(2,1)S(1)} %slice_select_fusion, bf16[1792,1536]{1,0:T(8,128)(2,1)S(1)} %load_head.1.head_ref), kind=kOutput, calls=%fused_computation.76 | convolution fusion | flops 704643072 | bytes 6750208 | tf_op jit(solution)/shard_map/dot_general | solution.py:332
  15.4 0.1 and_reduce_fusion
  15.6 0.3 fusion
  15.9 0.1 collective-permute-done.4
  16.0 1.1 %fusion.20 = f32[64,1536]{1,0:T(8,128)S(1)} fusion(bf16[64,1792]{1,0:T(8,128)(2,1)S(1)} %collective-permute-done.4, bf16[1792,1536]{1,0:T(8,128)(2,1)S(1)} %load_head.1.head_ref), kind=kOutput, calls=%fused_computation.75 | convolution fusion | flops 352321536 | bytes 6127616 | tf_op jit(solution)/shard_map/dot_general | solution.py:326
  17.0 1.8 %collective-permute-start.5 = (f32[64,1536]{1,0:T(8,128)S(1)}, f32[64,1536]{1,0:T(8,128)S(1)}, u32[]{:S(2)}, u32[]{:S(2)}) collective-permute-start(f32[64,1536]{1,0:T(8,128)S(1)} %fusion.20), channel_id=1, source_target_pairs={{0,1},{1,0},{2,3},{3,2},{4,5},{5,4},{6,7},{7,6},{8,9},{9,8},{10,11... | collective-permute-start | bytes 1179656 | tf_op jit(solution)/shard_map/ppermute | solution.py:19
  18.9 0.1 pad_maximum_fusion.refs_0_
  19.0 4.1 %collective-permute-done.3.refs_1_ = f32[32,1536]{1,0:T(8,128)S(1)} collective-permute-done((f32[32,1536]{1,0:T(8,128)S(1)}, f32[32,1536]{1,0:T(8,128)S(1)}, u32[]{:S(2)}, u32[]{:S(2)}) %collective-permute-start.3) | collective-permute-done | bytes 196640 | tf_op jit(solution)/shard_map/ppermute | solution.py:19
  23.0 0.0 collective-permute-done.1.refs_0_
  23.0 7.0 %collective-permute-done.5.refs_2_ = f32[64,1536]{1,0:T(8,128)S(1)} collective-permute-done((f32[64,1536]{1,0:T(8,128)S(1)}, f32[64,1536]{1,0:T(8,128)S(1)}, u32[]{:S(2)}, u32[]{:S(2)}) %collective-permute-start.5) | collective-permute-done | bytes 393248 | tf_op jit(solution)/shard_map/ppermute | solution.py:19
  30.0 0.4 local_stats.1
  30.4 0.0 collective-permute-start.6
  30.5 1.1 %collective-permute-done.6 = f32[1,4,128]{2,1,0:T(4,128)S(1)} collective-permute-done((f32[1,4,128]{2,1,0:T(4,128)S(1)}, f32[1,4,128]{2,1,0:T(4,128)S(1)}, u32[]{:S(2)}, u32[]{:S(2)}) %collective-permute-start.6) | collective-permute-done | bytes 2080 | tf_op jit(solution)/shard_map/ppermute | solution.py:23
  31.7 1.5 %collective-permute-start.9 = (f32[2,4,128]{2,1,0:T(4,128)S(1)}, f32[2,4,128]{2,1,0:T(4,128)S(1)}, u32[]{:S(2)}, u32[]{:S(2)}) collective-permute-start(f32[2,4,128]{2,1,0:T(4,128)S(1)} %pad_maximum_fusion.4), channel_id=1, source_target_pairs={{0,4},{2,6},{4,0},{6,2},{8,12},{10,14},{12,8},{14,10},{16,20},{18,... | collective-permute-start | bytes 12296 | tf_op jit(solution)/shard_map/ppermute | solution.py:23
  33.1 1.6 %collective-permute-start.8 = (f32[2,4,128]{2,1,0:T(4,128)S(1)}, f32[2,4,128]{2,1,0:T(4,128)S(1)}, u32[]{:S(2)}, u32[]{:S(2)}) collective-permute-start(f32[2,4,128]{2,1,0:T(4,128)S(1)} %pad_maximum_fusion.4), channel_id=1, source_target_pairs={{0,8},{2,10},{4,12},{6,14},{8,0},{10,2},{12,4},{14,6},{16,24},{18,... | collective-permute-start | bytes 12296 | tf_op jit(solution)/shard_map/ppermute | solution.py:23
  34.7 0.5 collective-permute-start.7
  35.2 0.1 collective-permute-done.9
  35.3 1.4 %collective-permute-done.8 = f32[2,4,128]{2,1,0:T(4,128)S(1)} collective-permute-done((f32[2,4,128]{2,1,0:T(4,128)S(1)}, f32[2,4,128]{2,1,0:T(4,128)S(1)}, u32[]{:S(2)}, u32[]{:S(2)}) %collective-permute-start.8) | collective-permute-done | bytes 4128 | tf_op jit(solution)/shard_map/ppermute | solution.py:23
  36.7 2.5 %collective-permute-done.7 = f32[2,4,128]{2,1,0:T(4,128)S(1)} collective-permute-done((f32[2,4,128]{2,1,0:T(4,128)S(1)}, f32[2,4,128]{2,1,0:T(4,128)S(1)}, u32[]{:S(2)}, u32[]{:S(2)}) %collective-permute-start.7) | collective-permute-done | bytes 4128 | tf_op jit(solution)/shard_map/ppermute | solution.py:23
  39.2 2.7 %collective-permute-start.10 = (f32[8,4,128]{2,1,0:T(4,128)S(1)}, f32[8,4,128]{2,1,0:T(4,128)S(1)}, u32[]{:S(2)}, u32[]{:S(2)}) collective-permute-start(f32[8,4,128]{2,1,0:T(4,128)S(1)} %pad_maximum_fusion.3), channel_id=1, source_target_pairs={{0,16},{2,18},{4,20},{6,22},{8,24},{10,26},{12,28},{14,30},{16,0},... | collective-permute-start | bytes 49160 | tf_op jit(solution)/shard_map/ppermute | solution.py:23
  41.9 2.1 %collective-permute-done.10 = f32[8,4,128]{2,1,0:T(4,128)S(1)} collective-permute-done((f32[8,4,128]{2,1,0:T(4,128)S(1)}, f32[8,4,128]{2,1,0:T(4,128)S(1)}, u32[]{:S(2)}, u32[]{:S(2)}) %collective-permute-start.10) | collective-permute-done | bytes 16416 | tf_op jit(solution)/shard_map/ppermute | solution.py:23
  44.0 0.9 %delta.1 = (bf16[128,1536]{1,0:T(8,128)(2,1)S(1)}, f32[1,128]{1,0:T(1,128)}, f32[1,128]{1,0:T(1,128)}) custom-call(f32[16,4,128]{2,1,0:T(4,128)S(1)} %pad_maximum_fusion.2.gathered_ref, f32[128,1536]{1,0:T(8,128)S(1)} %get-tuple-element.70.logits_ref, bf16[128,1536]{1,0:T(8,128)(2,1)S(1)} %get-tuple-element.64.kept_ref), custom_call_target="tpu_custom_call" | custom-call | flops 1572864 | bytes 1572864 | tf_op jit(solution)/shard_map/delta/pallas_call | solution.py:155
  44.9 1.5 %collective-permute-start.11 = (bf16[128,1536]{1,0:T(8,128)(2,1)S(1)}, bf16[128,1536]{1,0:T(8,128)(2,1)S(1)}, u32[]{:S(2)}, u32[]{:S(2)}) collective-permute-start(bf16[128,1536]{1,0:T(8,128)(2,1)S(1)} %get-tuple-element.74.delta_ref), channel_id=1, source_target_pairs={{0,1},{1,0},{2,3},{3,2},{4,5},{5,4},{6,7},{7,6},{8,9},{9,8},{10,11... | collective-permute-start | bytes 1179656 | tf_op jit(solution)/shard_map/ppermute | solution.py:19
  46.4 1.6 %partial_gradient.5 = f32[4,2,224,128]{3,2,1,0:T(8,128)S(1)} custom-call(bf16[1792,1536]{1,0:T(8,128)(2,1)S(1)} %load_head.1.head_ref, bf16[128,1536]{1,0:T(8,128)(2,1)S(1)} %get-tuple-element.74.delta_ref), custom_call_target="tpu_custom_call" | custom-call | flops 704643072 | bytes 5898240 | tf_op jit(solution)/shard_map/partial_gradient/pallas_call | solution.py:214
  48.0 0.1 fusion.8
  48.1 0.4 collective-permute-start.19
  48.5 1.5 %collective-permute-start.17 = (bf16[2,224,128]{2,1,0:T(8,128)(2,1)S(1)}, bf16[2,224,128]{2,1,0:T(8,128)(2,1)S(1)}, u32[]{:S(2)}, u32[]{:S(2)}) collective-permute-start(bf16[2,224,128]{2,1,0:T(8,128)(2,1)S(1)} %get-tuple-element.95), channel_id=1, source_target_pairs={{0,4},{2,6},{4,0},{6,2},{8,12},{10,14},{12,8},{14,10},{16,20},{18,... | collective-permute-start | bytes 344072 | tf_op jit(solution)/shard_map/ppermute | solution.py:23
  50.0 1.6 %collective-permute-start.18 = (bf16[2,224,128]{2,1,0:T(8,128)(2,1)S(1)}, bf16[2,224,128]{2,1,0:T(8,128)(2,1)S(1)}, u32[]{:S(2)}, u32[]{:S(2)}) collective-permute-start(bf16[2,224,128]{2,1,0:T(8,128)(2,1)S(1)} %get-tuple-element.96), channel_id=1, source_target_pairs={{0,8},{2,10},{4,12},{6,14},{8,0},{10,2},{12,4},{14,6},{16,24},{18,... | collective-permute-start | bytes 344072 | tf_op jit(solution)/shard_map/ppermute | solution.py:23
  51.6 1.6 %collective-permute-done.11.delta_ref = bf16[128,1536]{1,0:T(8,128)(2,1)S(1)} collective-permute-done((bf16[128,1536]{1,0:T(8,128)(2,1)S(1)}, bf16[128,1536]{1,0:T(8,128)(2,1)S(1)}, u32[]{:S(2)}, u32[]{:S(2)}) %collective-permute-start.11) | collective-permute-done | bytes 393248 | tf_op jit(solution)/shard_map/ppermute | solution.py:19
  53.2 0.9 %partial_gradient.3 = bf16[4,224,128]{2,1,0:T(8,128)(2,1)S(1)} custom-call(s32[1]{0:T(128)} %bitcast.1.core_ref, bf16[1792,1536]{1,0:T(8,128)(2,1)S(1)} %load_head.1.head_ref, bf16[128,1536]{1,0:T(8,128)(2,1)S(1)} %collective-permute-done.11.delta_ref), custom_call_target="tpu_custom_call" | custom-call | flops 704643072 | bytes 5898240 | tf_op jit(solution)/shard_map/partial_gradient/pallas_call | solution.py:214
  54.1 0.1 collective-permute-start.12
  54.2 0.9 %partial_gradient.4 = f32[4,224,128]{2,1,0:T(8,128)S(1)} custom-call(s32[1]{0:T(128)} %bitcast.1.core_ref, bf16[1792,1536]{1,0:T(8,128)(2,1)S(1)} %load_head.1.head_ref, bf16[128,1536]{1,0:T(8,128)(2,1)S(1)} %collective-permute-done.11.delta_ref), custom_call_target="tpu_custom_call" | custom-call | flops 704643072 | bytes 5898240 | tf_op jit(solution)/shard_map/partial_gradient/pallas_call | solution.py:214
  55.0 0.0 collective-permute-done.19
  55.1 0.0 collective-permute-done.18
  55.1 0.1 fusion.5
  55.2 0.6 collective-permute-start.20
  55.7 0.1 pad_maximum_fusion.1.refs_1_
  55.8 0.1 convert_add_fusion
  55.9 1.6 %collective-permute-start.13 = (bf16[224,128]{1,0:T(8,128)(2,1)S(1)}, bf16[224,128]{1,0:T(8,128)(2,1)S(1)}, u32[]{:S(2)}, u32[]{:S(2)}) collective-permute-start(bf16[224,128]{1,0:T(8,128)(2,1)S(1)} %get-tuple-element.76), channel_id=1, source_target_pairs={{0,1},{1,0},{2,3},{3,2},{4,5},{5,4},{6,7},{7,6},{8,9},{9,8},{10,11... | collective-permute-start | bytes 172040 | tf_op jit(solution)/shard_map/ppermute | solution.py:391
  57.5 0.6 collective-permute-start.14
  58.1 1.3 %collective-permute-start.15 = (bf16[224,128]{1,0:T(8,128)(2,1)S(1)}, bf16[224,128]{1,0:T(8,128)(2,1)S(1)}, u32[]{:S(2)}, u32[]{:S(2)}) collective-permute-start(bf16[224,128]{1,0:T(8,128)(2,1)S(1)} %get-tuple-element.78), channel_id=1, source_target_pairs={{0,9},{1,8},{2,11},{3,10},{4,13},{5,12},{6,15},{7,14},{8,1},{9,0},... | collective-permute-start | bytes 172040 | tf_op jit(solution)/shard_map/ppermute | solution.py:391
  59.3 2.5 %collective-permute-start.16 = (bf16[224,128]{1,0:T(8,128)(2,1)S(1)}, bf16[224,128]{1,0:T(8,128)(2,1)S(1)}, u32[]{:S(2)}, u32[]{:S(2)}) collective-permute-start(bf16[224,128]{1,0:T(8,128)(2,1)S(1)} %get-tuple-element.79), channel_id=1, source_target_pairs={{0,13},{1,12},{2,15},{3,14},{4,9},{5,8},{6,11},{7,10},{8,5},{9,4},... | collective-permute-start | bytes 172040 | tf_op jit(solution)/shard_map/ppermute | solution.py:391
  61.8 2.1 %head_gradient.2.refs_2_ = bf16[1792,1536]{1,0:T(8,128)(2,1)} custom-call(bf16[256,1792]{1,0:T(8,128)(2,1)S(1)} %pad_maximum_fusion.refs_0_, bf16[256,1536]{1,0:T(8,128)(2,1)S(1)} %pad_maximum_fusion.1.refs_1_), custom_call_target="tpu_custom_call" | custom-call | flops 805306368 | bytes 4849664 | tf_op jit(solution)/shard_map/head_gradient/pallas_call | solution.py:253
  63.9 0.0 collective-permute-done.14
  63.9 0.0 collective-permute-done.15
  63.9 1.4 %collective-permute-done.16 = bf16[224,128]{1,0:T(8,128)(2,1)S(1)} collective-permute-done((bf16[224,128]{1,0:T(8,128)(2,1)S(1)}, bf16[224,128]{1,0:T(8,128)(2,1)S(1)}, u32[]{:S(2)}, u32[]{:S(2)}) %collective-permute-start.16) | collective-permute-done | bytes 57376 | tf_op jit(solution)/shard_map/ppermute | solution.py:391
  65.3 0.0 collective-permute-done.20
  65.3 0.1 broadcast_select_fusion.2
  65.4 2.6 %collective-permute-start.21 = (bf16[224,128]{1,0:T(8,128)(2,1)S(1)}, bf16[224,128]{1,0:T(8,128)(2,1)S(1)}, u32[]{:S(2)}, u32[]{:S(2)}) collective-permute-start(bf16[224,128]{1,0:T(8,128)(2,1)S(1)} %broadcast_select_fusion.2), channel_id=1, source_target_pairs={{0,16},{2,18},{4,20},{6,22},{8,24},{10,26},{12,28},{14,30},{16,0},... | collective-permute-start | bytes 172040 | tf_op jit(solution)/shard_map/ppermute | solution.py:422
  68.0 1.8 %head_gradient.3 = bf16[1792,1536]{1,0:T(8,128)(2,1)} custom-call(bf16[256,1792]{1,0:T(8,128)(2,1)S(1)} %pad_maximum_fusion.refs_0_, bf16[256,1536]{1,0:T(8,128)(2,1)S(1)} %pad_maximum_fusion.1.refs_1_, bf16[1792,1536]{1,0:T(8,128)(2,1)} %head_gradient.2.refs_2_), custom_call_target="tpu_custom_call", output_to_operand_aliasing={{}: (2, {})} | custom-call | flops 603979776 | bytes 4063232 | tf_op jit(solution)/shard_map/head_gradient/pallas_call | solution.py:253
  69.8 0.7 collective-permute-done.21
  70.5 0.7 add_bitcast_fusion
  (23 shorter events, 0.2 us)
Async XLA Ops:
  1.6 11.4 %collective-permute-start.2 = (bf16[32,1792]{1,0:T(8,128)(2,1)S(1)}, bf16[32,1792]{1,0:T(8,128)(2,1)S(1)}, u32[]{:S(2)}, u32[]{:S(2)}) collective-permute-start(bf16[32,1792]{1,0:T(8,128)(2,1)S(1)} %get-tuple-element.97), channel_id=1, source_target_pairs={{0,1},{1,0},{2,3},{3,2},{4,5},{5,4},{6,7},{7,6},{8,9},{9,8},{10,11... | collective-permute-start | bytes 344072 | tf_op jit(solution)/shard_map/ppermute | solution.py:19
  4.7 5.6 %collective-permute-start = (bf16[32,1792]{1,0:T(8,128)(2,1)S(1)}, bf16[32,1792]{1,0:T(8,128)(2,1)S(1)}, u32[]{:S(2)}, u32[]{:S(2)}) collective-permute-start(bf16[32,1792]{1,0:T(8,128)(2,1)S(1)} %get-tuple-element.98), channel_id=1, source_target_pairs={{0,1},{1,0},{2,3},{3,2},{4,5},{5,4},{6,7},{7,6},{8,9},{9,8},{10,11... | collective-permute-start | bytes 344072 | tf_op jit(solution)/shard_map/ppermute | solution.py:19
  8.1 6.4 %copy-start = (bf16[128,3584]{1,0:T(8,128)(2,1)S(1)}, bf16[128,3584]{1,0:T(8,128)(2,1)}, u32[]{:S(2)}) copy-start(bf16[128,3584]{1,0:T(8,128)(2,1)} %param.5) | copy-start | bytes 2752516
  11.3 11.7 %collective-permute-start.1 = (f32[32,1536]{1,0:T(8,128)S(1)}, f32[32,1536]{1,0:T(8,128)S(1)}, u32[]{:S(2)}, u32[]{:S(2)}) collective-permute-start(f32[32,1536]{1,0:T(8,128)S(1)} %fusion.18), channel_id=1, source_target_pairs={{0,1},{1,0},{2,3},{3,2},{4,5},{5,4},{6,7},{7,6},{8,9},{9,8},{10,11... | collective-permute-start | bytes 589832 | tf_op jit(solution)/shard_map/ppermute | solution.py:19
  14.1 1.3 %copy-start.2 = (s32[1,16]{1,0:T(1,128)S(1)}, s32[1,16]{1,0:T(1,128)}, u32[]{:S(2)}) copy-start(s32[1,16]{1,0:T(1,128)} %param.8) | copy-start | bytes 196
  14.1 1.5 %copy-start.1 = (bf16[128,1536]{1,0:T(8,128)(2,1)S(1)}, bf16[128,1536]{1,0:T(8,128)(2,1)}, u32[]{:S(2)}) copy-start(bf16[128,1536]{1,0:T(8,128)(2,1)} %param.7) | copy-start | bytes 1179652
  14.1 8.9 %collective-permute-start.3 = (f32[32,1536]{1,0:T(8,128)S(1)}, f32[32,1536]{1,0:T(8,128)S(1)}, u32[]{:S(2)}, u32[]{:S(2)}) collective-permute-start(f32[32,1536]{1,0:T(8,128)S(1)} %fusion.19), channel_id=1, source_target_pairs={{0,1},{1,0},{2,3},{3,2},{4,5},{5,4},{6,7},{7,6},{8,9},{9,8},{10,11... | collective-permute-start | bytes 589832 | tf_op jit(solution)/shard_map/ppermute | solution.py:19
  14.5 1.5 %collective-permute-start.4 = (bf16[64,1792]{1,0:T(8,128)(2,1)S(1)}, bf16[64,1792]{1,0:T(8,128)(2,1)S(1)}, u32[]{:S(2)}, u32[]{:S(2)}) collective-permute-start(bf16[64,1792]{1,0:T(8,128)(2,1)S(1)} %constant_dynamic-update-slice_fusion), channel_id=1, source_target_pairs={{0,2},{2,0},{4,6},{6,4},{8,10},{10,8},{12,14},{14,12},{16,18},{18,... | collective-permute-start | bytes 688136 | tf_op jit(solution)/shard_map/ppermute | solution.py:23
  17.0 13.0 %collective-permute-start.5 = (f32[64,1536]{1,0:T(8,128)S(1)}, f32[64,1536]{1,0:T(8,128)S(1)}, u32[]{:S(2)}, u32[]{:S(2)}) collective-permute-start(f32[64,1536]{1,0:T(8,128)S(1)} %fusion.20), channel_id=1, source_target_pairs={{0,1},{1,0},{2,3},{3,2},{4,5},{5,4},{6,7},{7,6},{8,9},{9,8},{10,11... | collective-permute-start | bytes 1179656 | tf_op jit(solution)/shard_map/ppermute | solution.py:19
  30.4 1.2 %collective-permute-start.6 = (f32[1,4,128]{2,1,0:T(4,128)S(1)}, f32[1,4,128]{2,1,0:T(4,128)S(1)}, u32[]{:S(2)}, u32[]{:S(2)}) collective-permute-start(f32[1,4,128]{2,1,0:T(4,128)S(1)} %bitcast.50), channel_id=1, source_target_pairs={{0,2},{2,0},{4,6},{6,4},{8,10},{10,8},{12,14},{14,12},{16,18},{18,... | collective-permute-start | bytes 6152 | tf_op jit(solution)/shard_map/ppermute | solution.py:23
  31.7 3.7 %collective-permute-start.9 = (f32[2,4,128]{2,1,0:T(4,128)S(1)}, f32[2,4,128]{2,1,0:T(4,128)S(1)}, u32[]{:S(2)}, u32[]{:S(2)}) collective-permute-start(f32[2,4,128]{2,1,0:T(4,128)S(1)} %pad_maximum_fusion.4), channel_id=1, source_target_pairs={{0,4},{2,6},{4,0},{6,2},{8,12},{10,14},{12,8},{14,10},{16,20},{18,... | collective-permute-start | bytes 12296 | tf_op jit(solution)/shard_map/ppermute | solution.py:23
  33.1 3.6 %collective-permute-start.8 = (f32[2,4,128]{2,1,0:T(4,128)S(1)}, f32[2,4,128]{2,1,0:T(4,128)S(1)}, u32[]{:S(2)}, u32[]{:S(2)}) collective-permute-start(f32[2,4,128]{2,1,0:T(4,128)S(1)} %pad_maximum_fusion.4), channel_id=1, source_target_pairs={{0,8},{2,10},{4,12},{6,14},{8,0},{10,2},{12,4},{14,6},{16,24},{18,... | collective-permute-start | bytes 12296 | tf_op jit(solution)/shard_map/ppermute | solution.py:23
  34.7 4.5 %collective-permute-start.7 = (f32[2,4,128]{2,1,0:T(4,128)S(1)}, f32[2,4,128]{2,1,0:T(4,128)S(1)}, u32[]{:S(2)}, u32[]{:S(2)}) collective-permute-start(f32[2,4,128]{2,1,0:T(4,128)S(1)} %pad_maximum_fusion.4), channel_id=1, source_target_pairs={{0,12},{2,14},{4,8},{6,10},{8,4},{10,6},{12,0},{14,2},{16,28},{18,... | collective-permute-start | bytes 12296 | tf_op jit(solution)/shard_map/ppermute | solution.py:23
  39.2 4.8 %collective-permute-start.10 = (f32[8,4,128]{2,1,0:T(4,128)S(1)}, f32[8,4,128]{2,1,0:T(4,128)S(1)}, u32[]{:S(2)}, u32[]{:S(2)}) collective-permute-start(f32[8,4,128]{2,1,0:T(4,128)S(1)} %pad_maximum_fusion.3), channel_id=1, source_target_pairs={{0,16},{2,18},{4,20},{6,22},{8,24},{10,26},{12,28},{14,30},{16,0},... | collective-permute-start | bytes 49160 | tf_op jit(solution)/shard_map/ppermute | solution.py:23
  44.9 8.3 %collective-permute-start.11 = (bf16[128,1536]{1,0:T(8,128)(2,1)S(1)}, bf16[128,1536]{1,0:T(8,128)(2,1)S(1)}, u32[]{:S(2)}, u32[]{:S(2)}) collective-permute-start(bf16[128,1536]{1,0:T(8,128)(2,1)S(1)} %get-tuple-element.74.delta_ref), channel_id=1, source_target_pairs={{0,1},{1,0},{2,3},{3,2},{4,5},{5,4},{6,7},{7,6},{8,9},{9,8},{10,11... | collective-permute-start | bytes 1179656 | tf_op jit(solution)/shard_map/ppermute | solution.py:19
  48.1 7.0 %collective-permute-start.19 = (bf16[2,224,128]{2,1,0:T(8,128)(2,1)S(1)}, bf16[2,224,128]{2,1,0:T(8,128)(2,1)S(1)}, u32[]{:S(2)}, u32[]{:S(2)}) collective-permute-start(bf16[2,224,128]{2,1,0:T(8,128)(2,1)S(1)} %get-tuple-element.94), channel_id=1, source_target_pairs={{0,12},{2,14},{4,8},{6,10},{8,4},{10,6},{12,0},{14,2},{16,28},{18,... | collective-permute-start | bytes 344072 | tf_op jit(solution)/shard_map/ppermute | solution.py:23
  48.5 6.6 %collective-permute-start.17 = (bf16[2,224,128]{2,1,0:T(8,128)(2,1)S(1)}, bf16[2,224,128]{2,1,0:T(8,128)(2,1)S(1)}, u32[]{:S(2)}, u32[]{:S(2)}) collective-permute-start(bf16[2,224,128]{2,1,0:T(8,128)(2,1)S(1)} %get-tuple-element.95), channel_id=1, source_target_pairs={{0,4},{2,6},{4,0},{6,2},{8,12},{10,14},{12,8},{14,10},{16,20},{18,... | collective-permute-start | bytes 344072 | tf_op jit(solution)/shard_map/ppermute | solution.py:23
  50.0 5.1 %collective-permute-start.18 = (bf16[2,224,128]{2,1,0:T(8,128)(2,1)S(1)}, bf16[2,224,128]{2,1,0:T(8,128)(2,1)S(1)}, u32[]{:S(2)}, u32[]{:S(2)}) collective-permute-start(bf16[2,224,128]{2,1,0:T(8,128)(2,1)S(1)} %get-tuple-element.96), channel_id=1, source_target_pairs={{0,8},{2,10},{4,12},{6,14},{8,0},{10,2},{12,4},{14,6},{16,24},{18,... | collective-permute-start | bytes 344072 | tf_op jit(solution)/shard_map/ppermute | solution.py:23
  54.1 1.7 %collective-permute-start.12 = (bf16[4,224,128]{2,1,0:T(8,128)(2,1)S(1)}, bf16[4,224,128]{2,1,0:T(8,128)(2,1)S(1)}, u32[]{:S(2)}, u32[]{:S(2)}) collective-permute-start(bf16[4,224,128]{2,1,0:T(8,128)(2,1)S(1)} %partial_gradient.3), channel_id=1, source_target_pairs={{0,2},{2,0},{4,6},{6,4},{8,10},{10,8},{12,14},{14,12},{16,18},{18,... | collective-permute-start | bytes 688136 | tf_op jit(solution)/shard_map/ppermute | solution.py:23
  55.2 10.1 %collective-permute-start.20 = (bf16[224,128]{1,0:T(8,128)(2,1)S(1)}, bf16[224,128]{1,0:T(8,128)(2,1)S(1)}, u32[]{:S(2)}, u32[]{:S(2)}) collective-permute-start(bf16[224,128]{1,0:T(8,128)(2,1)S(1)} %fusion.13), channel_id=1, source_target_pairs={{0,2},{2,0},{4,6},{6,4},{8,10},{10,8},{12,14},{14,12},{16,18},{18,... | collective-permute-start | bytes 172040 | tf_op jit(solution)/shard_map/ppermute | solution.py:23
  55.9 8.0 %collective-permute-start.13 = (bf16[224,128]{1,0:T(8,128)(2,1)S(1)}, bf16[224,128]{1,0:T(8,128)(2,1)S(1)}, u32[]{:S(2)}, u32[]{:S(2)}) collective-permute-start(bf16[224,128]{1,0:T(8,128)(2,1)S(1)} %get-tuple-element.76), channel_id=1, source_target_pairs={{0,1},{1,0},{2,3},{3,2},{4,5},{5,4},{6,7},{7,6},{8,9},{9,8},{10,11... | collective-permute-start | bytes 172040 | tf_op jit(solution)/shard_map/ppermute | solution.py:391
  57.5 6.4 %collective-permute-start.14 = (bf16[224,128]{1,0:T(8,128)(2,1)S(1)}, bf16[224,128]{1,0:T(8,128)(2,1)S(1)}, u32[]{:S(2)}, u32[]{:S(2)}) collective-permute-start(bf16[224,128]{1,0:T(8,128)(2,1)S(1)} %get-tuple-element.77), channel_id=1, source_target_pairs={{0,5},{1,4},{2,7},{3,6},{4,1},{5,0},{6,3},{7,2},{8,13},{9,12},{10,... | collective-permute-start | bytes 172040 | tf_op jit(solution)/shard_map/ppermute | solution.py:391
  58.1 5.9 %collective-permute-start.15 = (bf16[224,128]{1,0:T(8,128)(2,1)S(1)}, bf16[224,128]{1,0:T(8,128)(2,1)S(1)}, u32[]{:S(2)}, u32[]{:S(2)}) collective-permute-start(bf16[224,128]{1,0:T(8,128)(2,1)S(1)} %get-tuple-element.78), channel_id=1, source_target_pairs={{0,9},{1,8},{2,11},{3,10},{4,13},{5,12},{6,15},{7,14},{8,1},{9,0},... | collective-permute-start | bytes 172040 | tf_op jit(solution)/shard_map/ppermute | solution.py:391
  59.3 6.0 %collective-permute-start.16 = (bf16[224,128]{1,0:T(8,128)(2,1)S(1)}, bf16[224,128]{1,0:T(8,128)(2,1)S(1)}, u32[]{:S(2)}, u32[]{:S(2)}) collective-permute-start(bf16[224,128]{1,0:T(8,128)(2,1)S(1)} %get-tuple-element.79), channel_id=1, source_target_pairs={{0,13},{1,12},{2,15},{3,14},{4,9},{5,8},{6,11},{7,10},{8,5},{9,4},... | collective-permute-start | bytes 172040 | tf_op jit(solution)/shard_map/ppermute | solution.py:391
  65.4 5.1 %collective-permute-start.21 = (bf16[224,128]{1,0:T(8,128)(2,1)S(1)}, bf16[224,128]{1,0:T(8,128)(2,1)S(1)}, u32[]{:S(2)}, u32[]{:S(2)}) collective-permute-start(bf16[224,128]{1,0:T(8,128)(2,1)S(1)} %broadcast_select_fusion.2), channel_id=1, source_target_pairs={{0,16},{2,18},{4,20},{6,22},{8,24},{10,26},{12,28},{14,30},{16,0},... | collective-permute-start | bytes 172040 | tf_op jit(solution)/shard_map/ppermute | solution.py:422

commit v16 on v15

--- a/solution.py
+++ b/solution.py
@@ -79,7 +79,7 @@
 
 
 def stats_kernel(core_ref, own_ref, kept_ref, early_ref, *refs):
-    parts, (logits_ref, stats_ref, turned_ref) = refs[:-3], refs[-3:]
+    parts, (powers_ref, stats_ref, turned_ref) = refs[:-3], refs[-3:]
     half = own_ref.shape[0] // 2
     lane = lax.broadcasted_iota(jnp.int32, (STEP, 128), 1)
     groups = [(core_ref[0], 0, half // 2), (core_ref[0], half // 2, half // 2)]
@@ -91,9 +91,10 @@
             logits = own_ref[rows, :]
             for part in parts[place::3]:
                 logits = logits + part[r : r + STEP, :]
-            logits_ref[rows, :] = logits
             top = jnp.max(logits, axis=1, keepdims=True)
-            total = jnp.sum(jnp.exp(logits - top), axis=1, keepdims=True)
+            powers = jnp.exp(logits - top)
+            powers_ref[rows, :] = powers
+            total = jnp.sum(powers, axis=1, keepdims=True)
             dot = jnp.sum(kept_ref[rows, :].astype(jnp.float32) * logits, axis=1, keepdims=True)
             turned_ref[rows, :] = jnp.where(lane == 0, top, jnp.where(lane == 1, total, dot))
     turned = turned_ref[...].T
@@ -127,7 +128,7 @@
     )(core, *arrays)
 
 
-def delta_kernel(gathered_ref, logits_ref, kept_ref, delta_ref, lse_ref, kl_ref):
+def delta_kernel(gathered_ref, stats_ref, powers_ref, kept_ref, delta_ref, lse_ref, kl_ref):
     shards = [gathered_ref[i] for i in range(gathered_ref.shape[0])]
     top = shards[0][0:1]
     for x in shards[1:]:
@@ -140,33 +141,34 @@
     lse_ref[...] = lse
     kl_ref[...] = part / mass - jnp.log(mass) + lse
     row = lax.broadcasted_iota(jnp.int32, (128, lse.shape[1]), 0)
-    turned = jnp.where(row == 0, lse, 1.0 / mass).T
-    lse_column, scale_column = turned[:, 0:1], turned[:, 1:2]
-    for r in range(0, logits_ref.shape[0], STEP):
+    student_scale = loss_scale * jnp.exp(stats_ref[0:1, :] - lse)
+    turned = jnp.where(row == 0, student_scale, loss_scale / mass).T
+    student_column, kept_column = turned[:, 0:1], turned[:, 1:2]
+    for r in range(0, powers_ref.shape[0], STEP):
         rows = slice(r, r + STEP)
-        student = jnp.exp(logits_ref[rows, :] - lse_column[rows])
-        kept = kept_ref[rows, :].astype(jnp.float32) * scale_column[rows]
-        delta_ref[rows, :] = (loss_scale * (student - kept)).astype(jnp.bfloat16)
-
-
-def finish(gathered, logits, kept):
-    tokens = logits.shape[0]
+        student = powers_ref[rows, :] * student_column[rows]
+        kept = kept_ref[rows, :].astype(jnp.float32) * kept_column[rows]
+        delta_ref[rows, :] = (student - kept).astype(jnp.bfloat16)
+
+
+def finish(gathered, stats, powers, kept):
+    tokens = powers.shape[0]
     in_vmem = pl.BlockSpec(memory_space=pltpu.VMEM)
     delta, lse, kl = pl.pallas_call(
         delta_kernel,
         out_shape=(
-            pltpu.VMEM(logits.shape, jnp.bfloat16),
+            pltpu.VMEM(powers.shape, jnp.bfloat16),
             jax.ShapeDtypeStruct((1, tokens), jnp.float32),
             jax.ShapeDtypeStruct((1, tokens), jnp.float32),
         ),
-        in_specs=[in_vmem] * 3,
+        in_specs=[in_vmem] * 4,
         out_specs=(in_vmem, in_vmem, in_vmem),
         compiler_params=pltpu.CompilerParams(vmem_limit_bytes=VMEM_LIMIT),
         cost_estimate=pl.CostEstimate(
-            flops=8 * logits.size, bytes_accessed=8 * logits.size, transcendentals=logits.size
+            flops=8 * powers.size, bytes_accessed=8 * powers.size, transcendentals=0
         ),
         name="delta",
-    )(*[pltpu.with_memory_space_constraint(x, pltpu.VMEM) for x in (gathered, logits, kept)])
+    )(*[pltpu.with_memory_space_constraint(x, pltpu.VMEM) for x in (gathered, stats, powers, kept)])
     return delta, lse.reshape(tokens), kl.reshape(tokens)
 
 
@@ -348,8 +350,9 @@
         (returned, all_features, logits, kept, early)
     )
     places = [i for i in range(1, len(upper)) if 1 << i < run]
-    logits, stats = local_stats(core_word, logits, kept, early, returned)
-    delta, lse, kl = finish(gather_vocab(stats, upper, places, vocab_size), logits, kept)
+    powers, stats = local_stats(core_word, logits, kept, early, returned)
+    gathered = gather_vocab(stats, upper, places, vocab_size)
+    delta, lse, kl = finish(gathered, stats, powers, kept)
 
     deltas = [delta] + [shift_tok(delta, d, tok_size) for d in range(1, tok_size)]
     flags = [upper[i] for i in places]

time: 71.4 us -> 71.3 us (level)
  no operation moved by 1% of the time
where the time goes in v16:
time: 71.3 us; the launch traced here: 71.2 us
  starting transfers between devices  27.5 us (39%)
  waiting for transfers between devices  24.2 us (34%)
  Pallas kernels  11.1 us (16%)
  matrix products  4.01 us (6%)
  other arithmetic  1.69 us (2%)
  between operations  1.6 us (2%)
  local copies, waits for them, and re-layouts  1.01 us (1%)
    ppermute x6, waiting for transfers between devices, shift_tok(): lax.ppermute(x, 'tok', [(i, (i + offset) % size) for i in range(size)])  14.8 us
    ppermute x11, starting transfers between devices, swap_vocab(): return lax.ppermute(x, 'vocab', [(i, i ^ bit) for i in range(size)])  10.5 us
    ppermute x6, starting transfers between devices, shift_tok(): lax.ppermute(x, 'tok', [(i, (i + offset) % size) for i in range(size)])  8.54 us
    ppermute x11, waiting for transfers between devices, swap_vocab(): return lax.ppermute(x, 'vocab', [(i, i ^ bit) for i in range(size)])  7.3 us
    ppermute x4, starting transfers between devices, per_device(): block.append(lax.ppermute(piece, ('vocab', 'tok'), pairs))  5.91 us
    pallas_call x2, Pallas kernels, head_gradient(): pl.pallas_call(functools.partial(head_gradient_kernel, steps, start, widt...  3.89 us
    pallas_call x3, Pallas kernels, gradient(): pl.pallas_call(kernel, out_shape=out, in_specs=([] if core is None else [...  3.31 us
    dot_general x3, matrix products, per_device(): jnp.dot(x, head_here, preferred_element_type=jnp.float32)  3.13 us
  transfers between devices with their start and end apart: 22, of which 12 were waited for; matrix products, arithmetic and copies ran while one was open for 7% of the time, Pallas kernels for 14%

profile of v16, /device:TPU:0, one launch (start us, length us, event | category | flops | bytes accessed | tf_op | source)
XLA Modules:
  0.0 71.2 jit_solution(4160381447488292629)
XLA Ops:
  0.6 1.0 %fusion.17 = (bf16[32,1792]{1,0:T(8,128)(2,1)S(1)}, bf16[32,1792]{1,0:T(8,128)(2,1)S(1)}) fusion(bf16[128,3584]{1,0:T(8,128)(2,1)} %param.5, s32[]{:T(128)S(6)} %select_n.253, s32[]{:T(128)S(6)} %select_n.252, s32[]{:T(128)S(6)} %select_n.251), kind=kLoop, calls=%fused_computation.72 | loop fusion | bytes 458764 | tf_op jit(solution)/shard_map/dynamic_slice | solution.py:287
  1.6 3.0 %collective-permute-start.2 = (bf16[32,1792]{1,0:T(8,128)(2,1)S(1)}, bf16[32,1792]{1,0:T(8,128)(2,1)S(1)}, u32[]{:S(2)}, u32[]{:S(2)}) collective-permute-start(bf16[32,1792]{1,0:T(8,128)(2,1)S(1)} %get-tuple-element.97), channel_id=1, source_target_pairs={{0,1},{1,0},{2,3},{3,2},{4,5},{5,4},{6,7},{7,6},{8,9},{9,8},{10,11... | collective-permute-start | bytes 344072 | tf_op jit(solution)/shard_map/ppermute | solution.py:19
  4.7 0.1 collective-permute-start
  5.4 2.6 %load_head.1.head_ref = bf16[1792,1536]{1,0:T(8,128)(2,1)S(1)} custom-call(bf16[1792,1536]{1,0:T(8,128)(2,1)} %head_ref), custom_call_target="tpu_custom_call" | custom-call | bytes 11010048 | tf_op jit(solution)/shard_map/load_head/pallas_call | solution.py:67
  8.1 0.0 copy-start
  8.1 2.2 %collective-permute-done = bf16[32,1792]{1,0:T(8,128)(2,1)S(1)} collective-permute-done((bf16[32,1792]{1,0:T(8,128)(2,1)S(1)}, bf16[32,1792]{1,0:T(8,128)(2,1)S(1)}, u32[]{:S(2)}, u32[]{:S(2)}) %collective-permute-start) | collective-permute-done | bytes 114720 | tf_op jit(solution)/shard_map/ppermute | solution.py:19
  10.3 1.0 %fusion.18 = f32[32,1536]{1,0:T(8,128)S(1)} fusion(bf16[32,1792]{1,0:T(8,128)(2,1)S(1)} %collective-permute-done, bf16[1792,1536]{1,0:T(8,128)(2,1)S(1)} %load_head.1.head_ref), kind=kOutput, calls=%fused_computation.73 | convolution fusion | flops 176160768 | bytes 5816320 | tf_op jit(solution)/shard_map/dot_general | solution.py:319
  11.3 1.8 %collective-permute-start.1 = (f32[32,1536]{1,0:T(8,128)S(1)}, f32[32,1536]{1,0:T(8,128)S(1)}, u32[]{:S(2)}, u32[]{:S(2)}) collective-permute-start(f32[32,1536]{1,0:T(8,128)S(1)} %fusion.18), channel_id=1, source_target_pairs={{0,1},{1,0},{2,3},{3,2},{4,5},{5,4},{6,7},{7,6},{8,9},{9,8},{10,11... | collective-permute-start | bytes 589832 | tf_op jit(solution)/shard_map/ppermute | solution.py:19
  13.1 0.0 collective-permute-done.2
  13.1 1.0 %fusion.19 = f32[32,1536]{1,0:T(8,128)S(1)} fusion(bf16[32,1792]{1,0:T(8,128)(2,1)S(1)} %collective-permute-done.2, bf16[1792,1536]{1,0:T(8,128)(2,1)S(1)} %load_head.1.head_ref), kind=kOutput, calls=%fused_computation.74 | convolution fusion | flops 176160768 | bytes 5816320 | tf_op jit(solution)/shard_map/dot_general | solution.py:328
  14.1 0.4 collective-permute-start.3
  14.5 0.0 collective-permute-start.4
  14.5 0.9 %fusion.21.own_ref = f32[128,1536]{1,0:T(8,128)S(1)} fusion(bf16[128,1792]{1,0:T(8,128)(2,1)S(1)} %slice_select_fusion, bf16[1792,1536]{1,0:T(8,128)(2,1)S(1)} %load_head.1.head_ref), kind=kOutput, calls=%fused_computation.76 | convolution fusion | flops 704643072 | bytes 6750208 | tf_op jit(solution)/shard_map/dot_general | solution.py:334
  15.4 0.1 and_reduce_fusion
  15.6 0.3 fusion
  15.9 0.1 collective-permute-done.4
  16.0 1.1 %fusion.20 = f32[64,1536]{1,0:T(8,128)S(1)} fusion(bf16[64,1792]{1,0:T(8,128)(2,1)S(1)} %collective-permute-done.4, bf16[1792,1536]{1,0:T(8,128)(2,1)S(1)} %load_head.1.head_ref), kind=kOutput, calls=%fused_computation.75 | convolution fusion | flops 352321536 | bytes 6127616 | tf_op jit(solution)/shard_map/dot_general | solution.py:328
  17.0 1.8 %collective-permute-start.5 = (f32[64,1536]{1,0:T(8,128)S(1)}, f32[64,1536]{1,0:T(8,128)S(1)}, u32[]{:S(2)}, u32[]{:S(2)}) collective-permute-start(f32[64,1536]{1,0:T(8,128)S(1)} %fusion.20), channel_id=1, source_target_pairs={{0,1},{1,0},{2,3},{3,2},{4,5},{5,4},{6,7},{7,6},{8,9},{9,8},{10,11... | collective-permute-start | bytes 1179656 | tf_op jit(solution)/shard_map/ppermute | solution.py:19
  18.9 0.1 pad_maximum_fusion.refs_0_
  19.0 4.1 %collective-permute-done.3.refs_1_ = f32[32,1536]{1,0:T(8,128)S(1)} collective-permute-done((f32[32,1536]{1,0:T(8,128)S(1)}, f32[32,1536]{1,0:T(8,128)S(1)}, u32[]{:S(2)}, u32[]{:S(2)}) %collective-permute-start.3) | collective-permute-done | bytes 196640 | tf_op jit(solution)/shard_map/ppermute | solution.py:19
  23.0 0.0 collective-permute-done.1.refs_0_
  23.0 7.0 %collective-permute-done.5.refs_2_ = f32[64,1536]{1,0:T(8,128)S(1)} collective-permute-done((f32[64,1536]{1,0:T(8,128)S(1)}, f32[64,1536]{1,0:T(8,128)S(1)}, u32[]{:S(2)}, u32[]{:S(2)}) %collective-permute-start.5) | collective-permute-done | bytes 393248 | tf_op jit(solution)/shard_map/ppermute | solution.py:19
  30.0 0.4 local_stats.1
  30.4 0.0 collective-permute-start.6
  30.5 1.1 %collective-permute-done.6 = f32[1,4,128]{2,1,0:T(4,128)S(1)} collective-permute-done((f32[1,4,128]{2,1,0:T(4,128)S(1)}, f32[1,4,128]{2,1,0:T(4,128)S(1)}, u32[]{:S(2)}, u32[]{:S(2)}) %collective-permute-start.6) | collective-permute-done | bytes 2080 | tf_op jit(solution)/shard_map/ppermute | solution.py:23
  31.6 1.5 %collective-permute-start.9 = (f32[2,4,128]{2,1,0:T(4,128)S(1)}, f32[2,4,128]{2,1,0:T(4,128)S(1)}, u32[]{:S(2)}, u32[]{:S(2)}) collective-permute-start(f32[2,4,128]{2,1,0:T(4,128)S(1)} %pad_maximum_fusion.4), channel_id=1, source_target_pairs={{0,4},{2,6},{4,0},{6,2},{8,12},{10,14},{12,8},{14,10},{16,20},{18,... | collective-permute-start | bytes 12296 | tf_op jit(solution)/shard_map/ppermute | solution.py:23
  33.1 1.6 %collective-permute-start.8 = (f32[2,4,128]{2,1,0:T(4,128)S(1)}, f32[2,4,128]{2,1,0:T(4,128)S(1)}, u32[]{:S(2)}, u32[]{:S(2)}) collective-permute-start(f32[2,4,128]{2,1,0:T(4,128)S(1)} %pad_maximum_fusion.4), channel_id=1, source_target_pairs={{0,8},{2,10},{4,12},{6,14},{8,0},{10,2},{12,4},{14,6},{16,24},{18,... | collective-permute-start | bytes 12296 | tf_op jit(solution)/shard_map/ppermute | solution.py:23
  34.7 0.5 collective-permute-start.7
  35.2 0.1 collective-permute-done.9
  35.3 1.4 %collective-permute-done.8 = f32[2,4,128]{2,1,0:T(4,128)S(1)} collective-permute-done((f32[2,4,128]{2,1,0:T(4,128)S(1)}, f32[2,4,128]{2,1,0:T(4,128)S(1)}, u32[]{:S(2)}, u32[]{:S(2)}) %collective-permute-start.8) | collective-permute-done | bytes 4128 | tf_op jit(solution)/shard_map/ppermute | solution.py:23
  36.7 2.5 %collective-permute-done.7 = f32[2,4,128]{2,1,0:T(4,128)S(1)} collective-permute-done((f32[2,4,128]{2,1,0:T(4,128)S(1)}, f32[2,4,128]{2,1,0:T(4,128)S(1)}, u32[]{:S(2)}, u32[]{:S(2)}) %collective-permute-start.7) | collective-permute-done | bytes 4128 | tf_op jit(solution)/shard_map/ppermute | solution.py:23
  39.2 2.7 %collective-permute-start.10 = (f32[8,4,128]{2,1,0:T(4,128)S(1)}, f32[8,4,128]{2,1,0:T(4,128)S(1)}, u32[]{:S(2)}, u32[]{:S(2)}) collective-permute-start(f32[8,4,128]{2,1,0:T(4,128)S(1)} %pad_maximum_fusion.3), channel_id=1, source_target_pairs={{0,16},{2,18},{4,20},{6,22},{8,24},{10,26},{12,28},{14,30},{16,0},... | collective-permute-start | bytes 49160 | tf_op jit(solution)/shard_map/ppermute | solution.py:23
  41.9 2.1 %collective-permute-done.10 = f32[8,4,128]{2,1,0:T(4,128)S(1)} collective-permute-done((f32[8,4,128]{2,1,0:T(4,128)S(1)}, f32[8,4,128]{2,1,0:T(4,128)S(1)}, u32[]{:S(2)}, u32[]{:S(2)}) %collective-permute-start.10) | collective-permute-done | bytes 16416 | tf_op jit(solution)/shard_map/ppermute | solution.py:23
  44.0 0.8 %delta.1 = (bf16[128,1536]{1,0:T(8,128)(2,1)S(1)}, f32[1,128]{1,0:T(1,128)}, f32[1,128]{1,0:T(1,128)}) custom-call(f32[16,4,128]{2,1,0:T(4,128)S(1)} %pad_maximum_fusion.2.gathered_ref, f32[4,128]{1,0:T(4,128)S(1)} %get-tuple-element.69.stats_ref, f32[128,1536]{1,0:T(8,128)S(1)} %get-tuple-element.70.powers_ref, bf16[128,1536]{1,0:T(8,128)(2,1)S(1)} %get-tuple-element.64.kept_ref), custom_call_target="tpu_custom_call" | custom-call | flops 1572864 | bytes 1572864 | tf_op jit(solution)/shard_map/delta/pallas_call | solution.py:157
  44.8 1.5 %collective-permute-start.11 = (bf16[128,1536]{1,0:T(8,128)(2,1)S(1)}, bf16[128,1536]{1,0:T(8,128)(2,1)S(1)}, u32[]{:S(2)}, u32[]{:S(2)}) collective-permute-start(bf16[128,1536]{1,0:T(8,128)(2,1)S(1)} %get-tuple-element.74.delta_ref), channel_id=1, source_target_pairs={{0,1},{1,0},{2,3},{3,2},{4,5},{5,4},{6,7},{7,6},{8,9},{9,8},{10,11... | collective-permute-start | bytes 1179656 | tf_op jit(solution)/shard_map/ppermute | solution.py:19
  46.3 1.6 %partial_gradient.5 = f32[4,2,224,128]{3,2,1,0:T(8,128)S(1)} custom-call(bf16[1792,1536]{1,0:T(8,128)(2,1)S(1)} %load_head.1.head_ref, bf16[128,1536]{1,0:T(8,128)(2,1)S(1)} %get-tuple-element.74.delta_ref), custom_call_target="tpu_custom_call" | custom-call | flops 704643072 | bytes 5898240 | tf_op jit(solution)/shard_map/partial_gradient/pallas_call | solution.py:216
  47.9 0.1 fusion.8
  48.0 0.4 collective-permute-start.19
  48.4 1.5 %collective-permute-start.17 = (bf16[2,224,128]{2,1,0:T(8,128)(2,1)S(1)}, bf16[2,224,128]{2,1,0:T(8,128)(2,1)S(1)}, u32[]{:S(2)}, u32[]{:S(2)}) collective-permute-start(bf16[2,224,128]{2,1,0:T(8,128)(2,1)S(1)} %get-tuple-element.95), channel_id=1, source_target_pairs={{0,4},{2,6},{4,0},{6,2},{8,12},{10,14},{12,8},{14,10},{16,20},{18,... | collective-permute-start | bytes 344072 | tf_op jit(solution)/shard_map/ppermute | solution.py:23
  49.9 1.6 %collective-permute-start.18 = (bf16[2,224,128]{2,1,0:T(8,128)(2,1)S(1)}, bf16[2,224,128]{2,1,0:T(8,128)(2,1)S(1)}, u32[]{:S(2)}, u32[]{:S(2)}) collective-permute-start(bf16[2,224,128]{2,1,0:T(8,128)(2,1)S(1)} %get-tuple-element.96), channel_id=1, source_target_pairs={{0,8},{2,10},{4,12},{6,14},{8,0},{10,2},{12,4},{14,6},{16,24},{18,... | collective-permute-start | bytes 344072 | tf_op jit(solution)/shard_map/ppermute | solution.py:23
  51.5 1.6 %collective-permute-done.11.delta_ref = bf16[128,1536]{1,0:T(8,128)(2,1)S(1)} collective-permute-done((bf16[128,1536]{1,0:T(8,128)(2,1)S(1)}, bf16[128,1536]{1,0:T(8,128)(2,1)S(1)}, u32[]{:S(2)}, u32[]{:S(2)}) %collective-permute-start.11) | collective-permute-done | bytes 393248 | tf_op jit(solution)/shard_map/ppermute | solution.py:19
  53.1 0.9 %partial_gradient.3 = bf16[4,224,128]{2,1,0:T(8,128)(2,1)S(1)} custom-call(s32[1]{0:T(128)} %bitcast.1.core_ref, bf16[1792,1536]{1,0:T(8,128)(2,1)S(1)} %load_head.1.head_ref, bf16[128,1536]{1,0:T(8,128)(2,1)S(1)} %collective-permute-done.11.delta_ref), custom_call_target="tpu_custom_call" | custom-call | flops 704643072 | bytes 5898240 | tf_op jit(solution)/shard_map/partial_gradient/pallas_call | solution.py:216
  54.0 0.1 collective-permute-start.12
  54.1 0.9 %partial_gradient.4 = f32[4,224,128]{2,1,0:T(8,128)S(1)} custom-call(s32[1]{0:T(128)} %bitcast.1.core_ref, bf16[1792,1536]{1,0:T(8,128)(2,1)S(1)} %load_head.1.head_ref, bf16[128,1536]{1,0:T(8,128)(2,1)S(1)} %collective-permute-done.11.delta_ref), custom_call_target="tpu_custom_call" | custom-call | flops 704643072 | bytes 5898240 | tf_op jit(solution)/shard_map/partial_gradient/pallas_call | solution.py:216
  55.0 0.0 collective-permute-done.19
  55.0 0.0 collective-permute-done.17
  55.0 0.0 collective-permute-done.18
  55.0 0.1 fusion.5
  55.1 0.6 collective-permute-start.20
  55.7 0.1 pad_maximum_fusion.1.refs_1_
  55.7 0.1 convert_add_fusion
  55.8 1.6 %collective-permute-start.13 = (bf16[224,128]{1,0:T(8,128)(2,1)S(1)}, bf16[224,128]{1,0:T(8,128)(2,1)S(1)}, u32[]{:S(2)}, u32[]{:S(2)}) collective-permute-start(bf16[224,128]{1,0:T(8,128)(2,1)S(1)} %get-tuple-element.76), channel_id=1, source_target_pairs={{0,1},{1,0},{2,3},{3,2},{4,5},{5,4},{6,7},{7,6},{8,9},{9,8},{10,11... | collective-permute-start | bytes 172040 | tf_op jit(solution)/shard_map/ppermute | solution.py:394
  57.4 0.6 collective-permute-start.14
  58.0 1.3 %collective-permute-start.15 = (bf16[224,128]{1,0:T(8,128)(2,1)S(1)}, bf16[224,128]{1,0:T(8,128)(2,1)S(1)}, u32[]{:S(2)}, u32[]{:S(2)}) collective-permute-start(bf16[224,128]{1,0:T(8,128)(2,1)S(1)} %get-tuple-element.78), channel_id=1, source_target_pairs={{0,9},{1,8},{2,11},{3,10},{4,13},{5,12},{6,15},{7,14},{8,1},{9,0},... | collective-permute-start | bytes 172040 | tf_op jit(solution)/shard_map/ppermute | solution.py:394
  59.3 2.5 %collective-permute-start.16 = (bf16[224,128]{1,0:T(8,128)(2,1)S(1)}, bf16[224,128]{1,0:T(8,128)(2,1)S(1)}, u32[]{:S(2)}, u32[]{:S(2)}) collective-permute-start(bf16[224,128]{1,0:T(8,128)(2,1)S(1)} %get-tuple-element.79), channel_id=1, source_target_pairs={{0,13},{1,12},{2,15},{3,14},{4,9},{5,8},{6,11},{7,10},{8,5},{9,4},... | collective-permute-start | bytes 172040 | tf_op jit(solution)/shard_map/ppermute | solution.py:394
  61.7 2.1 %head_gradient.2.refs_2_ = bf16[1792,1536]{1,0:T(8,128)(2,1)} custom-call(bf16[256,1792]{1,0:T(8,128)(2,1)S(1)} %pad_maximum_fusion.refs_0_, bf16[256,1536]{1,0:T(8,128)(2,1)S(1)} %pad_maximum_fusion.1.refs_1_), custom_call_target="tpu_custom_call" | custom-call | flops 805306368 | bytes 4849664 | tf_op jit(solution)/shard_map/head_gradient/pallas_call | solution.py:255
  63.8 0.0 collective-permute-done.13
  63.8 0.0 collective-permute-done.15
  63.9 1.4 %collective-permute-done.16 = bf16[224,128]{1,0:T(8,128)(2,1)S(1)} collective-permute-done((bf16[224,128]{1,0:T(8,128)(2,1)S(1)}, bf16[224,128]{1,0:T(8,128)(2,1)S(1)}, u32[]{:S(2)}, u32[]{:S(2)}) %collective-permute-start.16) | collective-permute-done | bytes 57376 | tf_op jit(solution)/shard_map/ppermute | solution.py:394
  65.2 0.1 broadcast_select_fusion.2
  65.3 2.6 %collective-permute-start.21 = (bf16[224,128]{1,0:T(8,128)(2,1)S(1)}, bf16[224,128]{1,0:T(8,128)(2,1)S(1)}, u32[]{:S(2)}, u32[]{:S(2)}) collective-permute-start(bf16[224,128]{1,0:T(8,128)(2,1)S(1)} %broadcast_select_fusion.2), channel_id=1, source_target_pairs={{0,16},{2,18},{4,20},{6,22},{8,24},{10,26},{12,28},{14,30},{16,0},... | collective-permute-start | bytes 172040 | tf_op jit(solution)/shard_map/ppermute | solution.py:425
  67.9 1.8 %head_gradient.3 = bf16[1792,1536]{1,0:T(8,128)(2,1)} custom-call(bf16[256,1792]{1,0:T(8,128)(2,1)S(1)} %pad_maximum_fusion.refs_0_, bf16[256,1536]{1,0:T(8,128)(2,1)S(1)} %pad_maximum_fusion.1.refs_1_, bf16[1792,1536]{1,0:T(8,128)(2,1)} %head_gradient.2.refs_2_), custom_call_target="tpu_custom_call", output_to_operand_aliasing={{}: (2, {})} | custom-call | flops 603979776 | bytes 4063232 | tf_op jit(solution)/shard_map/head_gradient/pallas_call | solution.py:255
  69.7 0.7 %collective-permute-done.21 = bf16[224,128]{1,0:T(8,128)(2,1)S(1)} collective-permute-done((bf16[224,128]{1,0:T(8,128)(2,1)S(1)}, bf16[224,128]{1,0:T(8,128)(2,1)S(1)}, u32[]{:S(2)}, u32[]{:S(2)}) %collective-permute-start.21) | collective-permute-done | bytes 57376 | tf_op jit(solution)/shard_map/ppermute | solution.py:425
  70.4 0.7 add_bitcast_fusion
  (23 shorter events, 0.2 us)
Async XLA Ops:
  1.6 11.4 %collective-permute-start.2 = (bf16[32,1792]{1,0:T(8,128)(2,1)S(1)}, bf16[32,1792]{1,0:T(8,128)(2,1)S(1)}, u32[]{:S(2)}, u32[]{:S(2)}) collective-permute-start(bf16[32,1792]{1,0:T(8,128)(2,1)S(1)} %get-tuple-element.97), channel_id=1, source_target_pairs={{0,1},{1,0},{2,3},{3,2},{4,5},{5,4},{6,7},{7,6},{8,9},{9,8},{10,11... | collective-permute-start | bytes 344072 | tf_op jit(solution)/shard_map/ppermute | solution.py:19
  4.7 5.6 %collective-permute-start = (bf16[32,1792]{1,0:T(8,128)(2,1)S(1)}, bf16[32,1792]{1,0:T(8,128)(2,1)S(1)}, u32[]{:S(2)}, u32[]{:S(2)}) collective-permute-start(bf16[32,1792]{1,0:T(8,128)(2,1)S(1)} %get-tuple-element.98), channel_id=1, source_target_pairs={{0,1},{1,0},{2,3},{3,2},{4,5},{5,4},{6,7},{7,6},{8,9},{9,8},{10,11... | collective-permute-start | bytes 344072 | tf_op jit(solution)/shard_map/ppermute | solution.py:19
  8.1 6.4 %copy-start = (bf16[128,3584]{1,0:T(8,128)(2,1)S(1)}, bf16[128,3584]{1,0:T(8,128)(2,1)}, u32[]{:S(2)}) copy-start(bf16[128,3584]{1,0:T(8,128)(2,1)} %param.5) | copy-start | bytes 2752516
  11.3 11.7 %collective-permute-start.1 = (f32[32,1536]{1,0:T(8,128)S(1)}, f32[32,1536]{1,0:T(8,128)S(1)}, u32[]{:S(2)}, u32[]{:S(2)}) collective-permute-start(f32[32,1536]{1,0:T(8,128)S(1)} %fusion.18), channel_id=1, source_target_pairs={{0,1},{1,0},{2,3},{3,2},{4,5},{5,4},{6,7},{7,6},{8,9},{9,8},{10,11... | collective-permute-start | bytes 589832 | tf_op jit(solution)/shard_map/ppermute | solution.py:19
  14.1 1.3 %copy-start.2 = (s32[1,16]{1,0:T(1,128)S(1)}, s32[1,16]{1,0:T(1,128)}, u32[]{:S(2)}) copy-start(s32[1,16]{1,0:T(1,128)} %param.8) | copy-start | bytes 196
  14.1 1.5 %copy-start.1 = (bf16[128,1536]{1,0:T(8,128)(2,1)S(1)}, bf16[128,1536]{1,0:T(8,128)(2,1)}, u32[]{:S(2)}) copy-start(bf16[128,1536]{1,0:T(8,128)(2,1)} %param.7) | copy-start | bytes 1179652
  14.1 8.9 %collective-permute-start.3 = (f32[32,1536]{1,0:T(8,128)S(1)}, f32[32,1536]{1,0:T(8,128)S(1)}, u32[]{:S(2)}, u32[]{:S(2)}) collective-permute-start(f32[32,1536]{1,0:T(8,128)S(1)} %fusion.19), channel_id=1, source_target_pairs={{0,1},{1,0},{2,3},{3,2},{4,5},{5,4},{6,7},{7,6},{8,9},{9,8},{10,11... | collective-permute-start | bytes 589832 | tf_op jit(solution)/shard_map/ppermute | solution.py:19
  14.5 1.5 %collective-permute-start.4 = (bf16[64,1792]{1,0:T(8,128)(2,1)S(1)}, bf16[64,1792]{1,0:T(8,128)(2,1)S(1)}, u32[]{:S(2)}, u32[]{:S(2)}) collective-permute-start(bf16[64,1792]{1,0:T(8,128)(2,1)S(1)} %constant_dynamic-update-slice_fusion), channel_id=1, source_target_pairs={{0,2},{2,0},{4,6},{6,4},{8,10},{10,8},{12,14},{14,12},{16,18},{18,... | collective-permute-start | bytes 688136 | tf_op jit(solution)/shard_map/ppermute | solution.py:23
  17.0 13.0 %collective-permute-start.5 = (f32[64,1536]{1,0:T(8,128)S(1)}, f32[64,1536]{1,0:T(8,128)S(1)}, u32[]{:S(2)}, u32[]{:S(2)}) collective-permute-start(f32[64,1536]{1,0:T(8,128)S(1)} %fusion.20), channel_id=1, source_target_pairs={{0,1},{1,0},{2,3},{3,2},{4,5},{5,4},{6,7},{7,6},{8,9},{9,8},{10,11... | collective-permute-start | bytes 1179656 | tf_op jit(solution)/shard_map/ppermute | solution.py:19
  30.4 1.2 %collective-permute-start.6 = (f32[1,4,128]{2,1,0:T(4,128)S(1)}, f32[1,4,128]{2,1,0:T(4,128)S(1)}, u32[]{:S(2)}, u32[]{:S(2)}) collective-permute-start(f32[1,4,128]{2,1,0:T(4,128)S(1)} %bitcast.50), channel_id=1, source_target_pairs={{0,2},{2,0},{4,6},{6,4},{8,10},{10,8},{12,14},{14,12},{16,18},{18,... | collective-permute-start | bytes 6152 | tf_op jit(solution)/shard_map/ppermute | solution.py:23
  31.6 3.7 %collective-permute-start.9 = (f32[2,4,128]{2,1,0:T(4,128)S(1)}, f32[2,4,128]{2,1,0:T(4,128)S(1)}, u32[]{:S(2)}, u32[]{:S(2)}) collective-permute-start(f32[2,4,128]{2,1,0:T(4,128)S(1)} %pad_maximum_fusion.4), channel_id=1, source_target_pairs={{0,4},{2,6},{4,0},{6,2},{8,12},{10,14},{12,8},{14,10},{16,20},{18,... | collective-permute-start | bytes 12296 | tf_op jit(solution)/shard_map/ppermute | solution.py:23
  33.1 3.6 %collective-permute-start.8 = (f32[2,4,128]{2,1,0:T(4,128)S(1)}, f32[2,4,128]{2,1,0:T(4,128)S(1)}, u32[]{:S(2)}, u32[]{:S(2)}) collective-permute-start(f32[2,4,128]{2,1,0:T(4,128)S(1)} %pad_maximum_fusion.4), channel_id=1, source_target_pairs={{0,8},{2,10},{4,12},{6,14},{8,0},{10,2},{12,4},{14,6},{16,24},{18,... | collective-permute-start | bytes 12296 | tf_op jit(solution)/shard_map/ppermute | solution.py:23
  34.7 4.5 %collective-permute-start.7 = (f32[2,4,128]{2,1,0:T(4,128)S(1)}, f32[2,4,128]{2,1,0:T(4,128)S(1)}, u32[]{:S(2)}, u32[]{:S(2)}) collective-permute-start(f32[2,4,128]{2,1,0:T(4,128)S(1)} %pad_maximum_fusion.4), channel_id=1, source_target_pairs={{0,12},{2,14},{4,8},{6,10},{8,4},{10,6},{12,0},{14,2},{16,28},{18,... | collective-permute-start | bytes 12296 | tf_op jit(solution)/shard_map/ppermute | solution.py:23
  39.2 4.8 %collective-permute-start.10 = (f32[8,4,128]{2,1,0:T(4,128)S(1)}, f32[8,4,128]{2,1,0:T(4,128)S(1)}, u32[]{:S(2)}, u32[]{:S(2)}) collective-permute-start(f32[8,4,128]{2,1,0:T(4,128)S(1)} %pad_maximum_fusion.3), channel_id=1, source_target_pairs={{0,16},{2,18},{4,20},{6,22},{8,24},{10,26},{12,28},{14,30},{16,0},... | collective-permute-start | bytes 49160 | tf_op jit(solution)/shard_map/ppermute | solution.py:23
  44.8 8.3 %collective-permute-start.11 = (bf16[128,1536]{1,0:T(8,128)(2,1)S(1)}, bf16[128,1536]{1,0:T(8,128)(2,1)S(1)}, u32[]{:S(2)}, u32[]{:S(2)}) collective-permute-start(bf16[128,1536]{1,0:T(8,128)(2,1)S(1)} %get-tuple-element.74.delta_ref), channel_id=1, source_target_pairs={{0,1},{1,0},{2,3},{3,2},{4,5},{5,4},{6,7},{7,6},{8,9},{9,8},{10,11... | collective-permute-start | bytes 1179656 | tf_op jit(solution)/shard_map/ppermute | solution.py:19
  48.0 7.0 %collective-permute-start.19 = (bf16[2,224,128]{2,1,0:T(8,128)(2,1)S(1)}, bf16[2,224,128]{2,1,0:T(8,128)(2,1)S(1)}, u32[]{:S(2)}, u32[]{:S(2)}) collective-permute-start(bf16[2,224,128]{2,1,0:T(8,128)(2,1)S(1)} %get-tuple-element.94), channel_id=1, source_target_pairs={{0,12},{2,14},{4,8},{6,10},{8,4},{10,6},{12,0},{14,2},{16,28},{18,... | collective-permute-start | bytes 344072 | tf_op jit(solution)/shard_map/ppermute | solution.py:23
  48.4 6.6 %collective-permute-start.17 = (bf16[2,224,128]{2,1,0:T(8,128)(2,1)S(1)}, bf16[2,224,128]{2,1,0:T(8,128)(2,1)S(1)}, u32[]{:S(2)}, u32[]{:S(2)}) collective-permute-start(bf16[2,224,128]{2,1,0:T(8,128)(2,1)S(1)} %get-tuple-element.95), channel_id=1, source_target_pairs={{0,4},{2,6},{4,0},{6,2},{8,12},{10,14},{12,8},{14,10},{16,20},{18,... | collective-permute-start | bytes 344072 | tf_op jit(solution)/shard_map/ppermute | solution.py:23
  49.9 5.1 %collective-permute-start.18 = (bf16[2,224,128]{2,1,0:T(8,128)(2,1)S(1)}, bf16[2,224,128]{2,1,0:T(8,128)(2,1)S(1)}, u32[]{:S(2)}, u32[]{:S(2)}) collective-permute-start(bf16[2,224,128]{2,1,0:T(8,128)(2,1)S(1)} %get-tuple-element.96), channel_id=1, source_target_pairs={{0,8},{2,10},{4,12},{6,14},{8,0},{10,2},{12,4},{14,6},{16,24},{18,... | collective-permute-start | bytes 344072 | tf_op jit(solution)/shard_map/ppermute | solution.py:23
  54.0 1.7 %collective-permute-start.12 = (bf16[4,224,128]{2,1,0:T(8,128)(2,1)S(1)}, bf16[4,224,128]{2,1,0:T(8,128)(2,1)S(1)}, u32[]{:S(2)}, u32[]{:S(2)}) collective-permute-start(bf16[4,224,128]{2,1,0:T(8,128)(2,1)S(1)} %partial_gradient.3), channel_id=1, source_target_pairs={{0,2},{2,0},{4,6},{6,4},{8,10},{10,8},{12,14},{14,12},{16,18},{18,... | collective-permute-start | bytes 688136 | tf_op jit(solution)/shard_map/ppermute | solution.py:23
  55.1 10.1 %collective-permute-start.20 = (bf16[224,128]{1,0:T(8,128)(2,1)S(1)}, bf16[224,128]{1,0:T(8,128)(2,1)S(1)}, u32[]{:S(2)}, u32[]{:S(2)}) collective-permute-start(bf16[224,128]{1,0:T(8,128)(2,1)S(1)} %fusion.13), channel_id=1, source_target_pairs={{0,2},{2,0},{4,6},{6,4},{8,10},{10,8},{12,14},{14,12},{16,18},{18,... | collective-permute-start | bytes 172040 | tf_op jit(solution)/shard_map/ppermute | solution.py:23
  55.8 8.0 %collective-permute-start.13 = (bf16[224,128]{1,0:T(8,128)(2,1)S(1)}, bf16[224,128]{1,0:T(8,128)(2,1)S(1)}, u32[]{:S(2)}, u32[]{:S(2)}) collective-permute-start(bf16[224,128]{1,0:T(8,128)(2,1)S(1)} %get-tuple-element.76), channel_id=1, source_target_pairs={{0,1},{1,0},{2,3},{3,2},{4,5},{5,4},{6,7},{7,6},{8,9},{9,8},{10,11... | collective-permute-start | bytes 172040 | tf_op jit(solution)/shard_map/ppermute | solution.py:394
  57.4 6.4 %collective-permute-start.14 = (bf16[224,128]{1,0:T(8,128)(2,1)S(1)}, bf16[224,128]{1,0:T(8,128)(2,1)S(1)}, u32[]{:S(2)}, u32[]{:S(2)}) collective-permute-start(bf16[224,128]{1,0:T(8,128)(2,1)S(1)} %get-tuple-element.77), channel_id=1, source_target_pairs={{0,5},{1,4},{2,7},{3,6},{4,1},{5,0},{6,3},{7,2},{8,13},{9,12},{10,... | collective-permute-start | bytes 172040 | tf_op jit(solution)/shard_map/ppermute | solution.py:394
  58.0 5.9 %collective-permute-start.15 = (bf16[224,128]{1,0:T(8,128)(2,1)S(1)}, bf16[224,128]{1,0:T(8,128)(2,1)S(1)}, u32[]{:S(2)}, u32[]{:S(2)}) collective-permute-start(bf16[224,128]{1,0:T(8,128)(2,1)S(1)} %get-tuple-element.78), channel_id=1, source_target_pairs={{0,9},{1,8},{2,11},{3,10},{4,13},{5,12},{6,15},{7,14},{8,1},{9,0},... | collective-permute-start | bytes 172040 | tf_op jit(solution)/shard_map/ppermute | solution.py:394
  59.3 6.0 %collective-permute-start.16 = (bf16[224,128]{1,0:T(8,128)(2,1)S(1)}, bf16[224,128]{1,0:T(8,128)(2,1)S(1)}, u32[]{:S(2)}, u32[]{:S(2)}) collective-permute-start(bf16[224,128]{1,0:T(8,128)(2,1)S(1)} %get-tuple-element.79), channel_id=1, source_target_pairs={{0,13},{1,12},{2,15},{3,14},{4,9},{5,8},{6,11},{7,10},{8,5},{9,4},... | collective-permute-start | bytes 172040 | tf_op jit(solution)/shard_map/ppermute | solution.py:394
  65.3 5.1 %collective-permute-start.21 = (bf16[224,128]{1,0:T(8,128)(2,1)S(1)}, bf16[224,128]{1,0:T(8,128)(2,1)S(1)}, u32[]{:S(2)}, u32[]{:S(2)}) collective-permute-start(bf16[224,128]{1,0:T(8,128)(2,1)S(1)} %broadcast_select_fusion.2), channel_id=1, source_target_pairs={{0,16},{2,18},{4,20},{6,22},{8,24},{10,26},{12,28},{14,30},{16,0},... | collective-permute-start | bytes 172040 | tf_op jit(solution)/shard_map/ppermute | solution.py:425

commit v17 on v16

--- a/solution.py
+++ b/solution.py
@@ -287,16 +287,18 @@
         return lax.dynamic_slice(hidden, (first, index * rows), (count, rows))
 
     quarter = half // 2
+    part = quarter // 2
+    second = lax.div(vocab_index, 2) & 1
     near, later = [
         [
             shift_tok(
-                columns_of(lax.rem(tok_index + d, tok_size), core * half + first, quarter),
+                columns_of(lax.rem(tok_index + d, tok_size), core * half + first, count),
                 d,
                 tok_size,
             )
             for d in range(1, tok_size)
         ]
-        for first in (0, quarter)
+        for first, count in ((0, quarter), (quarter + second * part, part))
     ]
     upper = []
     while 1 << len(upper) < vocab_size:
@@ -318,6 +320,7 @@
     )
     products = [jnp.dot(x, head_here, preferred_element_type=jnp.float32) for x in near]
     returned = [[shift_tok(x, -d, tok_size)] for d, x in enumerate(products, 1)]
+    later = [in_order(x, swap_vocab(x, 2, vocab_size), upper[1]) for x in later]
     later, _ = lax.optimization_barrier((later, products))
     near = [jnp.concatenate(pair, axis=0) for pair in zip(near, later)]
     far = [swap_vocab(x, 1, vocab_size) for x in near]

time: 71.3 us -> 71.7 us (level)
  waiting for transfers between devices: 24.2 us -> 22.8 us
  starting transfers between devices: 27.5 us -> 28.5 us
  local copies, waits for them, and re-layouts: 1.01 us -> 1.78 us
    ppermute x11 -> x12, starting transfers between devices: 10.5 us -> 12.5 us  [swap_vocab(): return lax.ppermute(x, 'vocab', [(i, i ^ bit) for i in range(size)])]
    ppermute x6, waiting for transfers between devices: 14.8 us -> 13.4 us  [shift_tok(): lax.ppermute(x, 'tok', [(i, (i + offset) % size) for i in range(size)])]
    ppermute x6, starting transfers between devices: 8.54 us -> 7.41 us  [shift_tok(): lax.ppermute(x, 'tok', [(i, (i + offset) % size) for i in range(size)])]
    dynamic_slice x1 -> x2, local copies, waits for them, and re-layouts: 0.98 us -> 1.74 us  [columns_of(): return lax.dynamic_slice(hidden, (first, index * rows), (count, rows))]
    ppermute x11 -> x12, waiting for transfers between devices: 7.3 us -> 7.28 us  [swap_vocab(): return lax.ppermute(x, 'vocab', [(i, i ^ bit) for i in range(size)])]
  transfers between devices with their start and end apart: 22 -> 23, of which waited for: 12 -> 11; matrix products, arithmetic and copies ran while one was open for 7% -> 8% of each run, Pallas kernels for 14% -> 14%
where the time goes in v17:
time: 71.7 us; the launch traced here: 71.5 us
  starting transfers between devices  28.5 us (40%)
  waiting for transfers between devices  22.8 us (32%)
  Pallas kernels  11.1 us (15%)
  matrix products  4.01 us (6%)
  local copies, waits for them, and re-layouts  1.78 us (2%)
  other arithmetic  1.71 us (2%)
  between operations  1.62 us (2%)
    ppermute x6, waiting for transfers between devices, shift_tok(): lax.ppermute(x, 'tok', [(i, (i + offset) % size) for i in range(size)])  13.4 us
    ppermute x12, starting transfers between devices, swap_vocab(): return lax.ppermute(x, 'vocab', [(i, i ^ bit) for i in range(size)])  12.5 us
    ppermute x6, starting transfers between devices, shift_tok(): lax.ppermute(x, 'tok', [(i, (i + offset) % size) for i in range(size)])  7.41 us
    ppermute x12, waiting for transfers between devices, swap_vocab(): return lax.ppermute(x, 'vocab', [(i, i ^ bit) for i in range(size)])  7.28 us
    ppermute x4, starting transfers between devices, per_device(): block.append(lax.ppermute(piece, ('vocab', 'tok'), pairs))  5.91 us
    pallas_call x2, Pallas kernels, head_gradient(): pl.pallas_call(functools.partial(head_gradient_kernel, steps, start, widt...  3.89 us
    pallas_call x3, Pallas kernels, gradient(): pl.pallas_call(kernel, out_shape=out, in_specs=([] if core is None else [...  3.31 us
    dot_general x3, matrix products, per_device(): jnp.dot(x, head_here, preferred_element_type=jnp.float32)  3.13 us
  transfers between devices with their start and end apart: 23, of which 11 were waited for; matrix products, arithmetic and copies ran while one was open for 8% of the time, Pallas kernels for 14%

profile of v17, /device:TPU:0, one launch (start us, length us, event | category | flops | bytes accessed | tf_op | source)
XLA Modules:
  0.0 71.5 jit_solution(17595920767128135031)
XLA Ops:
  0.6 0.8 %dynamic_slice.7 = bf16[16,1792]{1,0:T(8,128)(2,1)S(1)} dynamic-slice(bf16[128,3584]{1,0:T(8,128)(2,1)} %param.5, s32[]{:T(128)S(6)} %select_n.266, s32[]{:T(128)S(6)} %select_n.264), dynamic_slice_sizes={16,1792} | dynamic-slice | bytes 114692 | tf_op jit(solution)/shard_map/dynamic_slice | solution.py:287
  1.5 3.0 %collective-permute-start.2 = (bf16[16,1792]{1,0:T(8,128)(2,1)S(1)}, bf16[16,1792]{1,0:T(8,128)(2,1)S(1)}, u32[]{:S(2)}, u32[]{:S(2)}) collective-permute-start(bf16[16,1792]{1,0:T(8,128)(2,1)S(1)} %dynamic_slice.7), channel_id=1, source_target_pairs={{0,1},{1,0},{2,3},{3,2},{4,5},{5,4},{6,7},{7,6},{8,9},{9,8},{10,11... | collective-permute-start | bytes 172040 | tf_op jit(solution)/shard_map/ppermute | solution.py:19
  4.4 0.9 %dynamic_slice.6 = bf16[32,1792]{1,0:T(8,128)(2,1)S(1)} dynamic-slice(bf16[128,3584]{1,0:T(8,128)(2,1)} %param.5, s32[]{:T(128)S(6)} %select_n.263, s32[]{:T(128)S(6)} %select_n.264), dynamic_slice_sizes={32,1792} | dynamic-slice | bytes 229380 | tf_op jit(solution)/shard_map/dynamic_slice | solution.py:287
  5.4 0.0 collective-permute-start
  6.1 2.6 %load_head.1.head_ref = bf16[1792,1536]{1,0:T(8,128)(2,1)S(1)} custom-call(bf16[1792,1536]{1,0:T(8,128)(2,1)} %head_ref), custom_call_target="tpu_custom_call" | custom-call | bytes 11010048 | tf_op jit(solution)/shard_map/load_head/pallas_call | solution.py:67
  8.7 0.0 copy-start
  8.7 0.0 collective-permute-done.2
  8.7 2.0 %collective-permute-start.3 = (bf16[16,1792]{1,0:T(8,128)(2,1)S(1)}, bf16[16,1792]{1,0:T(8,128)(2,1)S(1)}, u32[]{:S(2)}, u32[]{:S(2)}) collective-permute-start(bf16[16,1792]{1,0:T(8,128)(2,1)S(1)} %collective-permute-done.2), channel_id=1, source_target_pairs={{0,4},{2,6},{4,0},{6,2},{8,12},{10,14},{12,8},{14,10},{16,20},{18,... | collective-permute-start | bytes 172040 | tf_op jit(solution)/shard_map/ppermute | solution.py:23
  10.8 1.0 %fusion.17 = f32[32,1536]{1,0:T(8,128)S(1)} fusion(bf16[32,1792]{1,0:T(8,128)(2,1)S(1)} %collective-permute-done, bf16[1792,1536]{1,0:T(8,128)(2,1)S(1)} %load_head.1.head_ref), kind=kOutput, calls=%fused_computation.75 | convolution fusion | flops 176160768 | bytes 5816320 | tf_op jit(solution)/shard_map/dot_general | solution.py:321
  11.8 1.6 %collective-permute-start.1 = (f32[32,1536]{1,0:T(8,128)S(1)}, f32[32,1536]{1,0:T(8,128)S(1)}, u32[]{:S(2)}, u32[]{:S(2)}) collective-permute-start(f32[32,1536]{1,0:T(8,128)S(1)} %fusion.17), channel_id=1, source_target_pairs={{0,1},{1,0},{2,3},{3,2},{4,5},{5,4},{6,7},{7,6},{8,9},{9,8},{10,11... | collective-permute-start | bytes 589832 | tf_op jit(solution)/shard_map/ppermute | solution.py:19
  13.4 0.0 collective-permute-done.3
  13.5 1.0 %fusion.18 = f32[32,1536]{1,0:T(8,128)S(1)} fusion(bf16[32,1792]{1,0:T(8,128)(2,1)S(1)} %pad_maximum_fusion.2, bf16[1792,1536]{1,0:T(8,128)(2,1)S(1)} %load_head.1.head_ref), kind=kOutput, calls=%fused_computation.76 | convolution fusion | flops 176160768 | bytes 5816320 | tf_op jit(solution)/shard_map/dot_general | solution.py:331
  14.5 1.6 %collective-permute-start.4 = (f32[32,1536]{1,0:T(8,128)S(1)}, f32[32,1536]{1,0:T(8,128)S(1)}, u32[]{:S(2)}, u32[]{:S(2)}) collective-permute-start(f32[32,1536]{1,0:T(8,128)S(1)} %fusion.18), channel_id=1, source_target_pairs={{0,1},{1,0},{2,3},{3,2},{4,5},{5,4},{6,7},{7,6},{8,9},{9,8},{10,11... | collective-permute-start | bytes 589832 | tf_op jit(solution)/shard_map/ppermute | solution.py:19
  16.1 0.0 collective-permute-start.5
  16.2 0.9 %fusion.20.own_ref = f32[128,1536]{1,0:T(8,128)S(1)} fusion(bf16[128,1792]{1,0:T(8,128)(2,1)S(1)} %slice_select_fusion, bf16[1792,1536]{1,0:T(8,128)(2,1)S(1)} %load_head.1.head_ref), kind=kOutput, calls=%fused_computation.78 | convolution fusion | flops 704643072 | bytes 6750208 | tf_op jit(solution)/shard_map/dot_general | solution.py:337
  17.1 0.1 and_reduce_fusion
  17.2 0.3 fusion
  17.5 0.1 collective-permute-done.5
  17.6 1.1 %fusion.19 = f32[64,1536]{1,0:T(8,128)S(1)} fusion(bf16[64,1792]{1,0:T(8,128)(2,1)S(1)} %collective-permute-done.5, bf16[1792,1536]{1,0:T(8,128)(2,1)S(1)} %load_head.1.head_ref), kind=kOutput, calls=%fused_computation.77 | convolution fusion | flops 352321536 | bytes 6127616 | tf_op jit(solution)/shard_map/dot_general | solution.py:331
  18.7 0.5 collective-permute-start.6
  19.3 0.1 pad_maximum_fusion.refs_0_
  19.3 2.7 %collective-permute-done.4.refs_1_ = f32[32,1536]{1,0:T(8,128)S(1)} collective-permute-done((f32[32,1536]{1,0:T(8,128)S(1)}, f32[32,1536]{1,0:T(8,128)S(1)}, u32[]{:S(2)}, u32[]{:S(2)}) %collective-permute-start.4) | collective-permute-done | bytes 196640 | tf_op jit(solution)/shard_map/ppermute | solution.py:19
  22.1 8.3 %collective-permute-done.6.refs_2_ = f32[64,1536]{1,0:T(8,128)S(1)} collective-permute-done((f32[64,1536]{1,0:T(8,128)S(1)}, f32[64,1536]{1,0:T(8,128)S(1)}, u32[]{:S(2)}, u32[]{:S(2)}) %collective-permute-start.6) | collective-permute-done | bytes 393248 | tf_op jit(solution)/shard_map/ppermute | solution.py:19
  30.3 0.4 local_stats.1
  30.7 0.0 collective-permute-start.7
  30.8 1.1 %collective-permute-done.7 = f32[1,4,128]{2,1,0:T(4,128)S(1)} collective-permute-done((f32[1,4,128]{2,1,0:T(4,128)S(1)}, f32[1,4,128]{2,1,0:T(4,128)S(1)}, u32[]{:S(2)}, u32[]{:S(2)}) %collective-permute-start.7) | collective-permute-done | bytes 2080 | tf_op jit(solution)/shard_map/ppermute | solution.py:23
  31.9 1.4 %collective-permute-start.10 = (f32[2,4,128]{2,1,0:T(4,128)S(1)}, f32[2,4,128]{2,1,0:T(4,128)S(1)}, u32[]{:S(2)}, u32[]{:S(2)}) collective-permute-start(f32[2,4,128]{2,1,0:T(4,128)S(1)} %pad_maximum_fusion.5), channel_id=1, source_target_pairs={{0,4},{2,6},{4,0},{6,2},{8,12},{10,14},{12,8},{14,10},{16,20},{18,... | collective-permute-start | bytes 12296 | tf_op jit(solution)/shard_map/ppermute | solution.py:23
  33.4 1.6 %collective-permute-start.9 = (f32[2,4,128]{2,1,0:T(4,128)S(1)}, f32[2,4,128]{2,1,0:T(4,128)S(1)}, u32[]{:S(2)}, u32[]{:S(2)}) collective-permute-start(f32[2,4,128]{2,1,0:T(4,128)S(1)} %pad_maximum_fusion.5), channel_id=1, source_target_pairs={{0,8},{2,10},{4,12},{6,14},{8,0},{10,2},{12,4},{14,6},{16,24},{18,... | collective-permute-start | bytes 12296 | tf_op jit(solution)/shard_map/ppermute | solution.py:23
  34.9 0.5 collective-permute-start.8
  35.5 0.1 collective-permute-done.10
  35.6 1.4 %collective-permute-done.9 = f32[2,4,128]{2,1,0:T(4,128)S(1)} collective-permute-done((f32[2,4,128]{2,1,0:T(4,128)S(1)}, f32[2,4,128]{2,1,0:T(4,128)S(1)}, u32[]{:S(2)}, u32[]{:S(2)}) %collective-permute-start.9) | collective-permute-done | bytes 4128 | tf_op jit(solution)/shard_map/ppermute | solution.py:23
  37.0 2.5 %collective-permute-done.8 = f32[2,4,128]{2,1,0:T(4,128)S(1)} collective-permute-done((f32[2,4,128]{2,1,0:T(4,128)S(1)}, f32[2,4,128]{2,1,0:T(4,128)S(1)}, u32[]{:S(2)}, u32[]{:S(2)}) %collective-permute-start.8) | collective-permute-done | bytes 4128 | tf_op jit(solution)/shard_map/ppermute | solution.py:23
  39.5 2.7 %collective-permute-start.11 = (f32[8,4,128]{2,1,0:T(4,128)S(1)}, f32[8,4,128]{2,1,0:T(4,128)S(1)}, u32[]{:S(2)}, u32[]{:S(2)}) collective-permute-start(f32[8,4,128]{2,1,0:T(4,128)S(1)} %pad_maximum_fusion.4), channel_id=1, source_target_pairs={{0,16},{2,18},{4,20},{6,22},{8,24},{10,26},{12,28},{14,30},{16,0},... | collective-permute-start | bytes 49160 | tf_op jit(solution)/shard_map/ppermute | solution.py:23
  42.2 2.1 %collective-permute-done.11 = f32[8,4,128]{2,1,0:T(4,128)S(1)} collective-permute-done((f32[8,4,128]{2,1,0:T(4,128)S(1)}, f32[8,4,128]{2,1,0:T(4,128)S(1)}, u32[]{:S(2)}, u32[]{:S(2)}) %collective-permute-start.11) | collective-permute-done | bytes 16416 | tf_op jit(solution)/shard_map/ppermute | solution.py:23
  44.3 0.8 %delta.1 = (bf16[128,1536]{1,0:T(8,128)(2,1)S(1)}, f32[1,128]{1,0:T(1,128)}, f32[1,128]{1,0:T(1,128)}) custom-call(f32[16,4,128]{2,1,0:T(4,128)S(1)} %pad_maximum_fusion.3.gathered_ref, f32[4,128]{1,0:T(4,128)S(1)} %get-tuple-element.69.stats_ref, f32[128,1536]{1,0:T(8,128)S(1)} %get-tuple-element.70.powers_ref, bf16[128,1536]{1,0:T(8,128)(2,1)S(1)} %get-tuple-element.64.kept_ref), custom_call_target="tpu_custom_call" | custom-call | flops 1572864 | bytes 1572864 | tf_op jit(solution)/shard_map/delta/pallas_call | solution.py:157
  45.1 0.7 collective-permute-start.12
  45.8 1.6 %partial_gradient.5 = f32[4,2,224,128]{3,2,1,0:T(8,128)S(1)} custom-call(bf16[1792,1536]{1,0:T(8,128)(2,1)S(1)} %load_head.1.head_ref, bf16[128,1536]{1,0:T(8,128)(2,1)S(1)} %get-tuple-element.74.delta_ref), custom_call_target="tpu_custom_call" | custom-call | flops 704643072 | bytes 5898240 | tf_op jit(solution)/shard_map/partial_gradient/pallas_call | solution.py:216
  47.4 0.1 fusion.8
  47.4 1.4 %collective-permute-start.20 = (bf16[2,224,128]{2,1,0:T(8,128)(2,1)S(1)}, bf16[2,224,128]{2,1,0:T(8,128)(2,1)S(1)}, u32[]{:S(2)}, u32[]{:S(2)}) collective-permute-start(bf16[2,224,128]{2,1,0:T(8,128)(2,1)S(1)} %get-tuple-element.94), channel_id=1, source_target_pairs={{0,12},{2,14},{4,8},{6,10},{8,4},{10,6},{12,0},{14,2},{16,28},{18,... | collective-permute-start | bytes 344072 | tf_op jit(solution)/shard_map/ppermute | solution.py:23
  48.8 0.6 collective-permute-start.18
  49.4 1.6 %collective-permute-start.19 = (bf16[2,224,128]{2,1,0:T(8,128)(2,1)S(1)}, bf16[2,224,128]{2,1,0:T(8,128)(2,1)S(1)}, u32[]{:S(2)}, u32[]{:S(2)}) collective-permute-start(bf16[2,224,128]{2,1,0:T(8,128)(2,1)S(1)} %get-tuple-element.96), channel_id=1, source_target_pairs={{0,8},{2,10},{4,12},{6,14},{8,0},{10,2},{12,4},{14,6},{16,24},{18,... | collective-permute-start | bytes 344072 | tf_op jit(solution)/shard_map/ppermute | solution.py:23
  51.0 2.4 %collective-permute-done.12.delta_ref = bf16[128,1536]{1,0:T(8,128)(2,1)S(1)} collective-permute-done((bf16[128,1536]{1,0:T(8,128)(2,1)S(1)}, bf16[128,1536]{1,0:T(8,128)(2,1)S(1)}, u32[]{:S(2)}, u32[]{:S(2)}) %collective-permute-start.12) | collective-permute-done | bytes 393248 | tf_op jit(solution)/shard_map/ppermute | solution.py:19
  53.4 0.9 %partial_gradient.3 = bf16[4,224,128]{2,1,0:T(8,128)(2,1)S(1)} custom-call(s32[1]{0:T(128)} %bitcast.1.core_ref, bf16[1792,1536]{1,0:T(8,128)(2,1)S(1)} %load_head.1.head_ref, bf16[128,1536]{1,0:T(8,128)(2,1)S(1)} %collective-permute-done.12.delta_ref), custom_call_target="tpu_custom_call" | custom-call | flops 704643072 | bytes 5898240 | tf_op jit(solution)/shard_map/partial_gradient/pallas_call | solution.py:216
  54.3 0.1 collective-permute-start.13
  54.3 0.9 %partial_gradient.4 = f32[4,224,128]{2,1,0:T(8,128)S(1)} custom-call(s32[1]{0:T(128)} %bitcast.1.core_ref, bf16[1792,1536]{1,0:T(8,128)(2,1)S(1)} %load_head.1.head_ref, bf16[128,1536]{1,0:T(8,128)(2,1)S(1)} %collective-permute-done.12.delta_ref), custom_call_target="tpu_custom_call" | custom-call | flops 704643072 | bytes 5898240 | tf_op jit(solution)/shard_map/partial_gradient/pallas_call | solution.py:216
  55.2 0.0 collective-permute-done.18
  55.2 0.0 collective-permute-done.19
  55.3 0.1 fusion.5
  55.4 0.6 collective-permute-start.21
  55.9 0.1 pad_maximum_fusion.1.refs_1_
  56.0 0.1 convert_add_fusion
  56.1 0.8 %collective-permute-start.14 = (bf16[224,128]{1,0:T(8,128)(2,1)S(1)}, bf16[224,128]{1,0:T(8,128)(2,1)S(1)}, u32[]{:S(2)}, u32[]{:S(2)}) collective-permute-start(bf16[224,128]{1,0:T(8,128)(2,1)S(1)} %get-tuple-element.76), channel_id=1, source_target_pairs={{0,1},{1,0},{2,3},{3,2},{4,5},{5,4},{6,7},{7,6},{8,9},{9,8},{10,11... | collective-permute-start | bytes 172040 | tf_op jit(solution)/shard_map/ppermute | solution.py:397
  56.9 1.5 %collective-permute-start.15 = (bf16[224,128]{1,0:T(8,128)(2,1)S(1)}, bf16[224,128]{1,0:T(8,128)(2,1)S(1)}, u32[]{:S(2)}, u32[]{:S(2)}) collective-permute-start(bf16[224,128]{1,0:T(8,128)(2,1)S(1)} %get-tuple-element.77), channel_id=1, source_target_pairs={{0,5},{1,4},{2,7},{3,6},{4,1},{5,0},{6,3},{7,2},{8,13},{9,12},{10,... | collective-permute-start | bytes 172040 | tf_op jit(solution)/shard_map/ppermute | solution.py:397
  58.3 1.3 %collective-permute-start.16 = (bf16[224,128]{1,0:T(8,128)(2,1)S(1)}, bf16[224,128]{1,0:T(8,128)(2,1)S(1)}, u32[]{:S(2)}, u32[]{:S(2)}) collective-permute-start(bf16[224,128]{1,0:T(8,128)(2,1)S(1)} %get-tuple-element.78), channel_id=1, source_target_pairs={{0,9},{1,8},{2,11},{3,10},{4,13},{5,12},{6,15},{7,14},{8,1},{9,0},... | collective-permute-start | bytes 172040 | tf_op jit(solution)/shard_map/ppermute | solution.py:397
  59.6 2.4 %collective-permute-start.17 = (bf16[224,128]{1,0:T(8,128)(2,1)S(1)}, bf16[224,128]{1,0:T(8,128)(2,1)S(1)}, u32[]{:S(2)}, u32[]{:S(2)}) collective-permute-start(bf16[224,128]{1,0:T(8,128)(2,1)S(1)} %get-tuple-element.79), channel_id=1, source_target_pairs={{0,13},{1,12},{2,15},{3,14},{4,9},{5,8},{6,11},{7,10},{8,5},{9,4},... | collective-permute-start | bytes 172040 | tf_op jit(solution)/shard_map/ppermute | solution.py:397
  62.0 2.1 %head_gradient.2.refs_2_ = bf16[1792,1536]{1,0:T(8,128)(2,1)} custom-call(bf16[256,1792]{1,0:T(8,128)(2,1)S(1)} %pad_maximum_fusion.refs_0_, bf16[256,1536]{1,0:T(8,128)(2,1)S(1)} %pad_maximum_fusion.1.refs_1_), custom_call_target="tpu_custom_call" | custom-call | flops 805306368 | bytes 4849664 | tf_op jit(solution)/shard_map/head_gradient/pallas_call | solution.py:255
  64.1 0.0 collective-permute-done.14
  64.1 0.0 collective-permute-done.16
  64.1 1.5 %collective-permute-done.17 = bf16[224,128]{1,0:T(8,128)(2,1)S(1)} collective-permute-done((bf16[224,128]{1,0:T(8,128)(2,1)S(1)}, bf16[224,128]{1,0:T(8,128)(2,1)S(1)}, u32[]{:S(2)}, u32[]{:S(2)}) %collective-permute-start.17) | collective-permute-done | bytes 57376 | tf_op jit(solution)/shard_map/ppermute | solution.py:397
  65.6 0.1 broadcast_select_fusion.2
  65.7 2.6 %collective-permute-start.22 = (bf16[224,128]{1,0:T(8,128)(2,1)S(1)}, bf16[224,128]{1,0:T(8,128)(2,1)S(1)}, u32[]{:S(2)}, u32[]{:S(2)}) collective-permute-start(bf16[224,128]{1,0:T(8,128)(2,1)S(1)} %broadcast_select_fusion.2), channel_id=1, source_target_pairs={{0,16},{2,18},{4,20},{6,22},{8,24},{10,26},{12,28},{14,30},{16,0},... | collective-permute-start | bytes 172040 | tf_op jit(solution)/shard_map/ppermute | solution.py:428
  68.3 1.8 %head_gradient.3 = bf16[1792,1536]{1,0:T(8,128)(2,1)} custom-call(bf16[256,1792]{1,0:T(8,128)(2,1)S(1)} %pad_maximum_fusion.refs_0_, bf16[256,1536]{1,0:T(8,128)(2,1)S(1)} %pad_maximum_fusion.1.refs_1_, bf16[1792,1536]{1,0:T(8,128)(2,1)} %head_gradient.2.refs_2_), custom_call_target="tpu_custom_call", output_to_operand_aliasing={{}: (2, {})} | custom-call | flops 603979776 | bytes 4063232 | tf_op jit(solution)/shard_map/head_gradient/pallas_call | solution.py:255
  70.1 0.7 collective-permute-done.22
  70.8 0.7 add_bitcast_fusion
  (28 shorter events, 0.3 us)
Async XLA Ops:
  1.5 7.2 %collective-permute-start.2 = (bf16[16,1792]{1,0:T(8,128)(2,1)S(1)}, bf16[16,1792]{1,0:T(8,128)(2,1)S(1)}, u32[]{:S(2)}, u32[]{:S(2)}) collective-permute-start(bf16[16,1792]{1,0:T(8,128)(2,1)S(1)} %dynamic_slice.7), channel_id=1, source_target_pairs={{0,1},{1,0},{2,3},{3,2},{4,5},{5,4},{6,7},{7,6},{8,9},{9,8},{10,11... | collective-permute-start | bytes 172040 | tf_op jit(solution)/shard_map/ppermute | solution.py:19
  5.4 5.4 %collective-permute-start = (bf16[32,1792]{1,0:T(8,128)(2,1)S(1)}, bf16[32,1792]{1,0:T(8,128)(2,1)S(1)}, u32[]{:S(2)}, u32[]{:S(2)}) collective-permute-start(bf16[32,1792]{1,0:T(8,128)(2,1)S(1)} %dynamic_slice.6), channel_id=1, source_target_pairs={{0,1},{1,0},{2,3},{3,2},{4,5},{5,4},{6,7},{7,6},{8,9},{9,8},{10,11... | collective-permute-start | bytes 344072 | tf_op jit(solution)/shard_map/ppermute | solution.py:19
  8.7 7.4 %copy-start = (bf16[128,3584]{1,0:T(8,128)(2,1)S(1)}, bf16[128,3584]{1,0:T(8,128)(2,1)}, u32[]{:S(2)}) copy-start(bf16[128,3584]{1,0:T(8,128)(2,1)} %param.5) | copy-start | bytes 2752516
  8.7 4.7 %collective-permute-start.3 = (bf16[16,1792]{1,0:T(8,128)(2,1)S(1)}, bf16[16,1792]{1,0:T(8,128)(2,1)S(1)}, u32[]{:S(2)}, u32[]{:S(2)}) collective-permute-start(bf16[16,1792]{1,0:T(8,128)(2,1)S(1)} %collective-permute-done.2), channel_id=1, source_target_pairs={{0,4},{2,6},{4,0},{6,2},{8,12},{10,14},{12,8},{14,10},{16,20},{18,... | collective-permute-start | bytes 172040 | tf_op jit(solution)/shard_map/ppermute | solution.py:23
  11.8 10.2 %collective-permute-start.1 = (f32[32,1536]{1,0:T(8,128)S(1)}, f32[32,1536]{1,0:T(8,128)S(1)}, u32[]{:S(2)}, u32[]{:S(2)}) collective-permute-start(f32[32,1536]{1,0:T(8,128)S(1)} %fusion.17), channel_id=1, source_target_pairs={{0,1},{1,0},{2,3},{3,2},{4,5},{5,4},{6,7},{7,6},{8,9},{9,8},{10,11... | collective-permute-start | bytes 589832 | tf_op jit(solution)/shard_map/ppermute | solution.py:19
  14.5 2.6 %copy-start.2 = (s32[1,16]{1,0:T(1,128)S(1)}, s32[1,16]{1,0:T(1,128)}, u32[]{:S(2)}) copy-start(s32[1,16]{1,0:T(1,128)} %param.8) | copy-start | bytes 196
  14.5 2.7 %copy-start.1 = (bf16[128,1536]{1,0:T(8,128)(2,1)S(1)}, bf16[128,1536]{1,0:T(8,128)(2,1)}, u32[]{:S(2)}) copy-start(bf16[128,1536]{1,0:T(8,128)(2,1)} %param.7) | copy-start | bytes 1179652
  14.5 7.5 %collective-permute-start.4 = (f32[32,1536]{1,0:T(8,128)S(1)}, f32[32,1536]{1,0:T(8,128)S(1)}, u32[]{:S(2)}, u32[]{:S(2)}) collective-permute-start(f32[32,1536]{1,0:T(8,128)S(1)} %fusion.18), channel_id=1, source_target_pairs={{0,1},{1,0},{2,3},{3,2},{4,5},{5,4},{6,7},{7,6},{8,9},{9,8},{10,11... | collective-permute-start | bytes 589832 | tf_op jit(solution)/shard_map/ppermute | solution.py:19
  16.1 1.5 %collective-permute-start.5 = (bf16[64,1792]{1,0:T(8,128)(2,1)S(1)}, bf16[64,1792]{1,0:T(8,128)(2,1)S(1)}, u32[]{:S(2)}, u32[]{:S(2)}) collective-permute-start(bf16[64,1792]{1,0:T(8,128)(2,1)S(1)} %constant_dynamic-update-slice_fusion), channel_id=1, source_target_pairs={{0,2},{2,0},{4,6},{6,4},{8,10},{10,8},{12,14},{14,12},{16,18},{18,... | collective-permute-start | bytes 688136 | tf_op jit(solution)/shard_map/ppermute | solution.py:23
  18.7 11.6 %collective-permute-start.6 = (f32[64,1536]{1,0:T(8,128)S(1)}, f32[64,1536]{1,0:T(8,128)S(1)}, u32[]{:S(2)}, u32[]{:S(2)}) collective-permute-start(f32[64,1536]{1,0:T(8,128)S(1)} %fusion.19), channel_id=1, source_target_pairs={{0,1},{1,0},{2,3},{3,2},{4,5},{5,4},{6,7},{7,6},{8,9},{9,8},{10,11... | collective-permute-start | bytes 1179656 | tf_op jit(solution)/shard_map/ppermute | solution.py:19
  30.7 1.2 %collective-permute-start.7 = (f32[1,4,128]{2,1,0:T(4,128)S(1)}, f32[1,4,128]{2,1,0:T(4,128)S(1)}, u32[]{:S(2)}, u32[]{:S(2)}) collective-permute-start(f32[1,4,128]{2,1,0:T(4,128)S(1)} %bitcast.50), channel_id=1, source_target_pairs={{0,2},{2,0},{4,6},{6,4},{8,10},{10,8},{12,14},{14,12},{16,18},{18,... | collective-permute-start | bytes 6152 | tf_op jit(solution)/shard_map/ppermute | solution.py:23
  31.9 3.7 %collective-permute-start.10 = (f32[2,4,128]{2,1,0:T(4,128)S(1)}, f32[2,4,128]{2,1,0:T(4,128)S(1)}, u32[]{:S(2)}, u32[]{:S(2)}) collective-permute-start(f32[2,4,128]{2,1,0:T(4,128)S(1)} %pad_maximum_fusion.5), channel_id=1, source_target_pairs={{0,4},{2,6},{4,0},{6,2},{8,12},{10,14},{12,8},{14,10},{16,20},{18,... | collective-permute-start | bytes 12296 | tf_op jit(solution)/shard_map/ppermute | solution.py:23
  33.4 3.6 %collective-permute-start.9 = (f32[2,4,128]{2,1,0:T(4,128)S(1)}, f32[2,4,128]{2,1,0:T(4,128)S(1)}, u32[]{:S(2)}, u32[]{:S(2)}) collective-permute-start(f32[2,4,128]{2,1,0:T(4,128)S(1)} %pad_maximum_fusion.5), channel_id=1, source_target_pairs={{0,8},{2,10},{4,12},{6,14},{8,0},{10,2},{12,4},{14,6},{16,24},{18,... | collective-permute-start | bytes 12296 | tf_op jit(solution)/shard_map/ppermute | solution.py:23
  34.9 4.5 %collective-permute-start.8 = (f32[2,4,128]{2,1,0:T(4,128)S(1)}, f32[2,4,128]{2,1,0:T(4,128)S(1)}, u32[]{:S(2)}, u32[]{:S(2)}) collective-permute-start(f32[2,4,128]{2,1,0:T(4,128)S(1)} %pad_maximum_fusion.5), channel_id=1, source_target_pairs={{0,12},{2,14},{4,8},{6,10},{8,4},{10,6},{12,0},{14,2},{16,28},{18,... | collective-permute-start | bytes 12296 | tf_op jit(solution)/shard_map/ppermute | solution.py:23
  39.5 4.8 %collective-permute-start.11 = (f32[8,4,128]{2,1,0:T(4,128)S(1)}, f32[8,4,128]{2,1,0:T(4,128)S(1)}, u32[]{:S(2)}, u32[]{:S(2)}) collective-permute-start(f32[8,4,128]{2,1,0:T(4,128)S(1)} %pad_maximum_fusion.4), channel_id=1, source_target_pairs={{0,16},{2,18},{4,20},{6,22},{8,24},{10,26},{12,28},{14,30},{16,0},... | collective-permute-start | bytes 49160 | tf_op jit(solution)/shard_map/ppermute | solution.py:23
  45.1 8.3 %collective-permute-start.12 = (bf16[128,1536]{1,0:T(8,128)(2,1)S(1)}, bf16[128,1536]{1,0:T(8,128)(2,1)S(1)}, u32[]{:S(2)}, u32[]{:S(2)}) collective-permute-start(bf16[128,1536]{1,0:T(8,128)(2,1)S(1)} %get-tuple-element.74.delta_ref), channel_id=1, source_target_pairs={{0,1},{1,0},{2,3},{3,2},{4,5},{5,4},{6,7},{7,6},{8,9},{9,8},{10,11... | collective-permute-start | bytes 1179656 | tf_op jit(solution)/shard_map/ppermute | solution.py:19
  47.4 7.8 %collective-permute-start.20 = (bf16[2,224,128]{2,1,0:T(8,128)(2,1)S(1)}, bf16[2,224,128]{2,1,0:T(8,128)(2,1)S(1)}, u32[]{:S(2)}, u32[]{:S(2)}) collective-permute-start(bf16[2,224,128]{2,1,0:T(8,128)(2,1)S(1)} %get-tuple-element.94), channel_id=1, source_target_pairs={{0,12},{2,14},{4,8},{6,10},{8,4},{10,6},{12,0},{14,2},{16,28},{18,... | collective-permute-start | bytes 344072 | tf_op jit(solution)/shard_map/ppermute | solution.py:23
  48.8 6.4 %collective-permute-start.18 = (bf16[2,224,128]{2,1,0:T(8,128)(2,1)S(1)}, bf16[2,224,128]{2,1,0:T(8,128)(2,1)S(1)}, u32[]{:S(2)}, u32[]{:S(2)}) collective-permute-start(bf16[2,224,128]{2,1,0:T(8,128)(2,1)S(1)} %get-tuple-element.95), channel_id=1, source_target_pairs={{0,4},{2,6},{4,0},{6,2},{8,12},{10,14},{12,8},{14,10},{16,20},{18,... | collective-permute-start | bytes 344072 | tf_op jit(solution)/shard_map/ppermute | solution.py:23
  49.4 5.9 %collective-permute-start.19 = (bf16[2,224,128]{2,1,0:T(8,128)(2,1)S(1)}, bf16[2,224,128]{2,1,0:T(8,128)(2,1)S(1)}, u32[]{:S(2)}, u32[]{:S(2)}) collective-permute-start(bf16[2,224,128]{2,1,0:T(8,128)(2,1)S(1)} %get-tuple-element.96), channel_id=1, source_target_pairs={{0,8},{2,10},{4,12},{6,14},{8,0},{10,2},{12,4},{14,6},{16,24},{18,... | collective-permute-start | bytes 344072 | tf_op jit(solution)/shard_map/ppermute | solution.py:23
  54.3 1.7 %collective-permute-start.13 = (bf16[4,224,128]{2,1,0:T(8,128)(2,1)S(1)}, bf16[4,224,128]{2,1,0:T(8,128)(2,1)S(1)}, u32[]{:S(2)}, u32[]{:S(2)}) collective-permute-start(bf16[4,224,128]{2,1,0:T(8,128)(2,1)S(1)} %partial_gradient.3), channel_id=1, source_target_pairs={{0,2},{2,0},{4,6},{6,4},{8,10},{10,8},{12,14},{14,12},{16,18},{18,... | collective-permute-start | bytes 688136 | tf_op jit(solution)/shard_map/ppermute | solution.py:23
  55.4 10.2 %collective-permute-start.21 = (bf16[224,128]{1,0:T(8,128)(2,1)S(1)}, bf16[224,128]{1,0:T(8,128)(2,1)S(1)}, u32[]{:S(2)}, u32[]{:S(2)}) collective-permute-start(bf16[224,128]{1,0:T(8,128)(2,1)S(1)} %fusion.13), channel_id=1, source_target_pairs={{0,2},{2,0},{4,6},{6,4},{8,10},{10,8},{12,14},{14,12},{16,18},{18,... | collective-permute-start | bytes 172040 | tf_op jit(solution)/shard_map/ppermute | solution.py:23
  56.1 8.0 %collective-permute-start.14 = (bf16[224,128]{1,0:T(8,128)(2,1)S(1)}, bf16[224,128]{1,0:T(8,128)(2,1)S(1)}, u32[]{:S(2)}, u32[]{:S(2)}) collective-permute-start(bf16[224,128]{1,0:T(8,128)(2,1)S(1)} %get-tuple-element.76), channel_id=1, source_target_pairs={{0,1},{1,0},{2,3},{3,2},{4,5},{5,4},{6,7},{7,6},{8,9},{9,8},{10,11... | collective-permute-start | bytes 172040 | tf_op jit(solution)/shard_map/ppermute | solution.py:397
  56.9 7.2 %collective-permute-start.15 = (bf16[224,128]{1,0:T(8,128)(2,1)S(1)}, bf16[224,128]{1,0:T(8,128)(2,1)S(1)}, u32[]{:S(2)}, u32[]{:S(2)}) collective-permute-start(bf16[224,128]{1,0:T(8,128)(2,1)S(1)} %get-tuple-element.77), channel_id=1, source_target_pairs={{0,5},{1,4},{2,7},{3,6},{4,1},{5,0},{6,3},{7,2},{8,13},{9,12},{10,... | collective-permute-start | bytes 172040 | tf_op jit(solution)/shard_map/ppermute | solution.py:397
  58.3 5.8 %collective-permute-start.16 = (bf16[224,128]{1,0:T(8,128)(2,1)S(1)}, bf16[224,128]{1,0:T(8,128)(2,1)S(1)}, u32[]{:S(2)}, u32[]{:S(2)}) collective-permute-start(bf16[224,128]{1,0:T(8,128)(2,1)S(1)} %get-tuple-element.78), channel_id=1, source_target_pairs={{0,9},{1,8},{2,11},{3,10},{4,13},{5,12},{6,15},{7,14},{8,1},{9,0},... | collective-permute-start | bytes 172040 | tf_op jit(solution)/shard_map/ppermute | solution.py:397
  59.6 6.0 %collective-permute-start.17 = (bf16[224,128]{1,0:T(8,128)(2,1)S(1)}, bf16[224,128]{1,0:T(8,128)(2,1)S(1)}, u32[]{:S(2)}, u32[]{:S(2)}) collective-permute-start(bf16[224,128]{1,0:T(8,128)(2,1)S(1)} %get-tuple-element.79), channel_id=1, source_target_pairs={{0,13},{1,12},{2,15},{3,14},{4,9},{5,8},{6,11},{7,10},{8,5},{9,4},... | collective-permute-start | bytes 172040 | tf_op jit(solution)/shard_map/ppermute | solution.py:397
  65.7 5.1 %collective-permute-start.22 = (bf16[224,128]{1,0:T(8,128)(2,1)S(1)}, bf16[224,128]{1,0:T(8,128)(2,1)S(1)}, u32[]{:S(2)}, u32[]{:S(2)}) collective-permute-start(bf16[224,128]{1,0:T(8,128)(2,1)S(1)} %broadcast_select_fusion.2), channel_id=1, source_target_pairs={{0,16},{2,18},{4,20},{6,22},{8,24},{10,26},{12,28},{14,30},{16,0},... | collective-permute-start | bytes 172040 | tf_op jit(solution)/shard_map/ppermute | solution.py:428

commit v18 on v16

--- a/solution.py
+++ b/solution.py
@@ -12,7 +12,7 @@
 
 loss_scale = 1024.0
 VMEM_LIMIT = 16 << 20
-STEP = 16
+STEP = 32
 
 
 def shift_tok(x, offset, size):

time: 71.3 us -> 71.3 us (level)
  no operation moved by 1% of the time
where the time goes in v18:
time: 71.3 us; the launch traced here: 71.2 us
  starting transfers between devices  27.6 us (39%)
  waiting for transfers between devices  24.2 us (34%)
  Pallas kernels  11.1 us (16%)
  matrix products  4.01 us (6%)
  other arithmetic  1.69 us (2%)
  between operations  1.6 us (2%)
  local copies, waits for them, and re-layouts  1.01 us (1%)
    ppermute x6, waiting for transfers between devices, shift_tok(): lax.ppermute(x, 'tok', [(i, (i + offset) % size) for i in range(size)])  14.8 us
    ppermute x11, starting transfers between devices, swap_vocab(): return lax.ppermute(x, 'vocab', [(i, i ^ bit) for i in range(size)])  10.5 us
    ppermute x6, starting transfers between devices, shift_tok(): lax.ppermute(x, 'tok', [(i, (i + offset) % size) for i in range(size)])  8.54 us
    ppermute x11, waiting for transfers between devices, swap_vocab(): return lax.ppermute(x, 'vocab', [(i, i ^ bit) for i in range(size)])  7.3 us
    ppermute x4, starting transfers between devices, per_device(): block.append(lax.ppermute(piece, ('vocab', 'tok'), pairs))  5.91 us
    pallas_call x2, Pallas kernels, head_gradient(): pl.pallas_call(functools.partial(head_gradient_kernel, steps, start, widt...  3.89 us
    pallas_call x3, Pallas kernels, gradient(): pl.pallas_call(kernel, out_shape=out, in_specs=([] if core is None else [...  3.32 us
    dot_general x3, matrix products, per_device(): jnp.dot(x, head_here, preferred_element_type=jnp.float32)  3.13 us
  transfers between devices with their start and end apart: 22, of which 12 were waited for; matrix products, arithmetic and copies ran while one was open for 7% of the time, Pallas kernels for 14%

profile of v18, /device:TPU:0, one launch (start us, length us, event | category | flops | bytes accessed | tf_op | source)
XLA Modules:
  0.0 71.2 jit_solution(9832405172839748382)
XLA Ops:
  0.6 1.0 %fusion.17 = (bf16[32,1792]{1,0:T(8,128)(2,1)S(1)}, bf16[32,1792]{1,0:T(8,128)(2,1)S(1)}) fusion(bf16[128,3584]{1,0:T(8,128)(2,1)} %param.5, s32[]{:T(128)S(6)} %select_n.253, s32[]{:T(128)S(6)} %select_n.252, s32[]{:T(128)S(6)} %select_n.251), kind=kLoop, calls=%fused_computation.72 | loop fusion | bytes 458764 | tf_op jit(solution)/shard_map/dynamic_slice | solution.py:287
  1.6 3.0 %collective-permute-start.2 = (bf16[32,1792]{1,0:T(8,128)(2,1)S(1)}, bf16[32,1792]{1,0:T(8,128)(2,1)S(1)}, u32[]{:S(2)}, u32[]{:S(2)}) collective-permute-start(bf16[32,1792]{1,0:T(8,128)(2,1)S(1)} %get-tuple-element.97), channel_id=1, source_target_pairs={{0,1},{1,0},{2,3},{3,2},{4,5},{5,4},{6,7},{7,6},{8,9},{9,8},{10,11... | collective-permute-start | bytes 344072 | tf_op jit(solution)/shard_map/ppermute | solution.py:19
  4.7 0.1 collective-permute-start
  5.4 2.6 %load_head.1.head_ref = bf16[1792,1536]{1,0:T(8,128)(2,1)S(1)} custom-call(bf16[1792,1536]{1,0:T(8,128)(2,1)} %head_ref), custom_call_target="tpu_custom_call" | custom-call | bytes 11010048 | tf_op jit(solution)/shard_map/load_head/pallas_call | solution.py:67
  8.1 0.0 copy-start
  8.1 2.2 %collective-permute-done = bf16[32,1792]{1,0:T(8,128)(2,1)S(1)} collective-permute-done((bf16[32,1792]{1,0:T(8,128)(2,1)S(1)}, bf16[32,1792]{1,0:T(8,128)(2,1)S(1)}, u32[]{:S(2)}, u32[]{:S(2)}) %collective-permute-start) | collective-permute-done | bytes 114720 | tf_op jit(solution)/shard_map/ppermute | solution.py:19
  10.3 1.0 %fusion.18 = f32[32,1536]{1,0:T(8,128)S(1)} fusion(bf16[32,1792]{1,0:T(8,128)(2,1)S(1)} %collective-permute-done, bf16[1792,1536]{1,0:T(8,128)(2,1)S(1)} %load_head.1.head_ref), kind=kOutput, calls=%fused_computation.73 | convolution fusion | flops 176160768 | bytes 5816320 | tf_op jit(solution)/shard_map/dot_general | solution.py:319
  11.3 1.8 %collective-permute-start.1 = (f32[32,1536]{1,0:T(8,128)S(1)}, f32[32,1536]{1,0:T(8,128)S(1)}, u32[]{:S(2)}, u32[]{:S(2)}) collective-permute-start(f32[32,1536]{1,0:T(8,128)S(1)} %fusion.18), channel_id=1, source_target_pairs={{0,1},{1,0},{2,3},{3,2},{4,5},{5,4},{6,7},{7,6},{8,9},{9,8},{10,11... | collective-permute-start | bytes 589832 | tf_op jit(solution)/shard_map/ppermute | solution.py:19
  13.1 0.0 collective-permute-done.2
  13.1 1.0 %fusion.19 = f32[32,1536]{1,0:T(8,128)S(1)} fusion(bf16[32,1792]{1,0:T(8,128)(2,1)S(1)} %collective-permute-done.2, bf16[1792,1536]{1,0:T(8,128)(2,1)S(1)} %load_head.1.head_ref), kind=kOutput, calls=%fused_computation.74 | convolution fusion | flops 176160768 | bytes 5816320 | tf_op jit(solution)/shard_map/dot_general | solution.py:328
  14.1 0.4 collective-permute-start.3
  14.5 0.0 collective-permute-start.4
  14.5 0.9 %fusion.21.own_ref = f32[128,1536]{1,0:T(8,128)S(1)} fusion(bf16[128,1792]{1,0:T(8,128)(2,1)S(1)} %slice_select_fusion, bf16[1792,1536]{1,0:T(8,128)(2,1)S(1)} %load_head.1.head_ref), kind=kOutput, calls=%fused_computation.76 | convolution fusion | flops 704643072 | bytes 6750208 | tf_op jit(solution)/shard_map/dot_general | solution.py:334
  15.4 0.1 and_reduce_fusion
  15.6 0.3 fusion
  15.9 0.1 collective-permute-done.4
  16.0 1.1 %fusion.20 = f32[64,1536]{1,0:T(8,128)S(1)} fusion(bf16[64,1792]{1,0:T(8,128)(2,1)S(1)} %collective-permute-done.4, bf16[1792,1536]{1,0:T(8,128)(2,1)S(1)} %load_head.1.head_ref), kind=kOutput, calls=%fused_computation.75 | convolution fusion | flops 352321536 | bytes 6127616 | tf_op jit(solution)/shard_map/dot_general | solution.py:328
  17.0 1.8 %collective-permute-start.5 = (f32[64,1536]{1,0:T(8,128)S(1)}, f32[64,1536]{1,0:T(8,128)S(1)}, u32[]{:S(2)}, u32[]{:S(2)}) collective-permute-start(f32[64,1536]{1,0:T(8,128)S(1)} %fusion.20), channel_id=1, source_target_pairs={{0,1},{1,0},{2,3},{3,2},{4,5},{5,4},{6,7},{7,6},{8,9},{9,8},{10,11... | collective-permute-start | bytes 1179656 | tf_op jit(solution)/shard_map/ppermute | solution.py:19
  18.9 0.1 pad_maximum_fusion.refs_0_
  19.0 4.1 %collective-permute-done.3.refs_1_ = f32[32,1536]{1,0:T(8,128)S(1)} collective-permute-done((f32[32,1536]{1,0:T(8,128)S(1)}, f32[32,1536]{1,0:T(8,128)S(1)}, u32[]{:S(2)}, u32[]{:S(2)}) %collective-permute-start.3) | collective-permute-done | bytes 196640 | tf_op jit(solution)/shard_map/ppermute | solution.py:19
  23.0 0.0 collective-permute-done.1.refs_0_
  23.0 7.0 %collective-permute-done.5.refs_2_ = f32[64,1536]{1,0:T(8,128)S(1)} collective-permute-done((f32[64,1536]{1,0:T(8,128)S(1)}, f32[64,1536]{1,0:T(8,128)S(1)}, u32[]{:S(2)}, u32[]{:S(2)}) %collective-permute-start.5) | collective-permute-done | bytes 393248 | tf_op jit(solution)/shard_map/ppermute | solution.py:19
  30.0 0.4 local_stats.1
  30.4 0.0 collective-permute-start.6
  30.5 1.1 %collective-permute-done.6 = f32[1,4,128]{2,1,0:T(4,128)S(1)} collective-permute-done((f32[1,4,128]{2,1,0:T(4,128)S(1)}, f32[1,4,128]{2,1,0:T(4,128)S(1)}, u32[]{:S(2)}, u32[]{:S(2)}) %collective-permute-start.6) | collective-permute-done | bytes 2080 | tf_op jit(solution)/shard_map/ppermute | solution.py:23
  31.6 1.5 %collective-permute-start.9 = (f32[2,4,128]{2,1,0:T(4,128)S(1)}, f32[2,4,128]{2,1,0:T(4,128)S(1)}, u32[]{:S(2)}, u32[]{:S(2)}) collective-permute-start(f32[2,4,128]{2,1,0:T(4,128)S(1)} %pad_maximum_fusion.4), channel_id=1, source_target_pairs={{0,4},{2,6},{4,0},{6,2},{8,12},{10,14},{12,8},{14,10},{16,20},{18,... | collective-permute-start | bytes 12296 | tf_op jit(solution)/shard_map/ppermute | solution.py:23
  33.1 1.6 %collective-permute-start.8 = (f32[2,4,128]{2,1,0:T(4,128)S(1)}, f32[2,4,128]{2,1,0:T(4,128)S(1)}, u32[]{:S(2)}, u32[]{:S(2)}) collective-permute-start(f32[2,4,128]{2,1,0:T(4,128)S(1)} %pad_maximum_fusion.4), channel_id=1, source_target_pairs={{0,8},{2,10},{4,12},{6,14},{8,0},{10,2},{12,4},{14,6},{16,24},{18,... | collective-permute-start | bytes 12296 | tf_op jit(solution)/shard_map/ppermute | solution.py:23
  34.7 0.5 collective-permute-start.7
  35.2 0.1 collective-permute-done.9
  35.3 1.4 %collective-permute-done.8 = f32[2,4,128]{2,1,0:T(4,128)S(1)} collective-permute-done((f32[2,4,128]{2,1,0:T(4,128)S(1)}, f32[2,4,128]{2,1,0:T(4,128)S(1)}, u32[]{:S(2)}, u32[]{:S(2)}) %collective-permute-start.8) | collective-permute-done | bytes 4128 | tf_op jit(solution)/shard_map/ppermute | solution.py:23
  36.7 2.5 %collective-permute-done.7 = f32[2,4,128]{2,1,0:T(4,128)S(1)} collective-permute-done((f32[2,4,128]{2,1,0:T(4,128)S(1)}, f32[2,4,128]{2,1,0:T(4,128)S(1)}, u32[]{:S(2)}, u32[]{:S(2)}) %collective-permute-start.7) | collective-permute-done | bytes 4128 | tf_op jit(solution)/shard_map/ppermute | solution.py:23
  39.2 2.7 %collective-permute-start.10 = (f32[8,4,128]{2,1,0:T(4,128)S(1)}, f32[8,4,128]{2,1,0:T(4,128)S(1)}, u32[]{:S(2)}, u32[]{:S(2)}) collective-permute-start(f32[8,4,128]{2,1,0:T(4,128)S(1)} %pad_maximum_fusion.3), channel_id=1, source_target_pairs={{0,16},{2,18},{4,20},{6,22},{8,24},{10,26},{12,28},{14,30},{16,0},... | collective-permute-start | bytes 49160 | tf_op jit(solution)/shard_map/ppermute | solution.py:23
  41.9 2.1 %collective-permute-done.10 = f32[8,4,128]{2,1,0:T(4,128)S(1)} collective-permute-done((f32[8,4,128]{2,1,0:T(4,128)S(1)}, f32[8,4,128]{2,1,0:T(4,128)S(1)}, u32[]{:S(2)}, u32[]{:S(2)}) %collective-permute-start.10) | collective-permute-done | bytes 16416 | tf_op jit(solution)/shard_map/ppermute | solution.py:23
  44.0 0.8 %delta.1 = (bf16[128,1536]{1,0:T(8,128)(2,1)S(1)}, f32[1,128]{1,0:T(1,128)}, f32[1,128]{1,0:T(1,128)}) custom-call(f32[16,4,128]{2,1,0:T(4,128)S(1)} %pad_maximum_fusion.2.gathered_ref, f32[4,128]{1,0:T(4,128)S(1)} %get-tuple-element.69.stats_ref, f32[128,1536]{1,0:T(8,128)S(1)} %get-tuple-element.70.powers_ref, bf16[128,1536]{1,0:T(8,128)(2,1)S(1)} %get-tuple-element.64.kept_ref), custom_call_target="tpu_custom_call" | custom-call | flops 1572864 | bytes 1572864 | tf_op jit(solution)/shard_map/delta/pallas_call | solution.py:157
  44.8 1.5 %collective-permute-start.11 = (bf16[128,1536]{1,0:T(8,128)(2,1)S(1)}, bf16[128,1536]{1,0:T(8,128)(2,1)S(1)}, u32[]{:S(2)}, u32[]{:S(2)}) collective-permute-start(bf16[128,1536]{1,0:T(8,128)(2,1)S(1)} %get-tuple-element.74.delta_ref), channel_id=1, source_target_pairs={{0,1},{1,0},{2,3},{3,2},{4,5},{5,4},{6,7},{7,6},{8,9},{9,8},{10,11... | collective-permute-start | bytes 1179656 | tf_op jit(solution)/shard_map/ppermute | solution.py:19
  46.4 1.6 %partial_gradient.5 = f32[4,2,224,128]{3,2,1,0:T(8,128)S(1)} custom-call(bf16[1792,1536]{1,0:T(8,128)(2,1)S(1)} %load_head.1.head_ref, bf16[128,1536]{1,0:T(8,128)(2,1)S(1)} %get-tuple-element.74.delta_ref), custom_call_target="tpu_custom_call" | custom-call | flops 704643072 | bytes 5898240 | tf_op jit(solution)/shard_map/partial_gradient/pallas_call | solution.py:216
  47.9 0.1 fusion.8
  48.0 0.4 collective-permute-start.19
  48.4 1.5 %collective-permute-start.17 = (bf16[2,224,128]{2,1,0:T(8,128)(2,1)S(1)}, bf16[2,224,128]{2,1,0:T(8,128)(2,1)S(1)}, u32[]{:S(2)}, u32[]{:S(2)}) collective-permute-start(bf16[2,224,128]{2,1,0:T(8,128)(2,1)S(1)} %get-tuple-element.95), channel_id=1, source_target_pairs={{0,4},{2,6},{4,0},{6,2},{8,12},{10,14},{12,8},{14,10},{16,20},{18,... | collective-permute-start | bytes 344072 | tf_op jit(solution)/shard_map/ppermute | solution.py:23
  49.9 1.6 %collective-permute-start.18 = (bf16[2,224,128]{2,1,0:T(8,128)(2,1)S(1)}, bf16[2,224,128]{2,1,0:T(8,128)(2,1)S(1)}, u32[]{:S(2)}, u32[]{:S(2)}) collective-permute-start(bf16[2,224,128]{2,1,0:T(8,128)(2,1)S(1)} %get-tuple-element.96), channel_id=1, source_target_pairs={{0,8},{2,10},{4,12},{6,14},{8,0},{10,2},{12,4},{14,6},{16,24},{18,... | collective-permute-start | bytes 344072 | tf_op jit(solution)/shard_map/ppermute | solution.py:23
  51.5 1.6 %collective-permute-done.11.delta_ref = bf16[128,1536]{1,0:T(8,128)(2,1)S(1)} collective-permute-done((bf16[128,1536]{1,0:T(8,128)(2,1)S(1)}, bf16[128,1536]{1,0:T(8,128)(2,1)S(1)}, u32[]{:S(2)}, u32[]{:S(2)}) %collective-permute-start.11) | collective-permute-done | bytes 393248 | tf_op jit(solution)/shard_map/ppermute | solution.py:19
  53.1 0.9 %partial_gradient.3 = bf16[4,224,128]{2,1,0:T(8,128)(2,1)S(1)} custom-call(s32[1]{0:T(128)} %bitcast.1.core_ref, bf16[1792,1536]{1,0:T(8,128)(2,1)S(1)} %load_head.1.head_ref, bf16[128,1536]{1,0:T(8,128)(2,1)S(1)} %collective-permute-done.11.delta_ref), custom_call_target="tpu_custom_call" | custom-call | flops 704643072 | bytes 5898240 | tf_op jit(solution)/shard_map/partial_gradient/pallas_call | solution.py:216
  54.0 0.1 collective-permute-start.12
  54.1 0.9 %partial_gradient.4 = f32[4,224,128]{2,1,0:T(8,128)S(1)} custom-call(s32[1]{0:T(128)} %bitcast.1.core_ref, bf16[1792,1536]{1,0:T(8,128)(2,1)S(1)} %load_head.1.head_ref, bf16[128,1536]{1,0:T(8,128)(2,1)S(1)} %collective-permute-done.11.delta_ref), custom_call_target="tpu_custom_call" | custom-call | flops 704643072 | bytes 5898240 | tf_op jit(solution)/shard_map/partial_gradient/pallas_call | solution.py:216
  55.0 0.0 collective-permute-done.19
  55.0 0.0 collective-permute-done.17
  55.0 0.1 fusion.5
  55.1 0.6 collective-permute-start.20
  55.7 0.1 pad_maximum_fusion.1.refs_1_
  55.7 0.0 collective-permute-done.12
  55.7 0.1 convert_add_fusion
  55.8 1.6 %collective-permute-start.13 = (bf16[224,128]{1,0:T(8,128)(2,1)S(1)}, bf16[224,128]{1,0:T(8,128)(2,1)S(1)}, u32[]{:S(2)}, u32[]{:S(2)}) collective-permute-start(bf16[224,128]{1,0:T(8,128)(2,1)S(1)} %get-tuple-element.76), channel_id=1, source_target_pairs={{0,1},{1,0},{2,3},{3,2},{4,5},{5,4},{6,7},{7,6},{8,9},{9,8},{10,11... | collective-permute-start | bytes 172040 | tf_op jit(solution)/shard_map/ppermute | solution.py:394
  57.4 0.6 collective-permute-start.14
  58.0 1.3 %collective-permute-start.15 = (bf16[224,128]{1,0:T(8,128)(2,1)S(1)}, bf16[224,128]{1,0:T(8,128)(2,1)S(1)}, u32[]{:S(2)}, u32[]{:S(2)}) collective-permute-start(bf16[224,128]{1,0:T(8,128)(2,1)S(1)} %get-tuple-element.78), channel_id=1, source_target_pairs={{0,9},{1,8},{2,11},{3,10},{4,13},{5,12},{6,15},{7,14},{8,1},{9,0},... | collective-permute-start | bytes 172040 | tf_op jit(solution)/shard_map/ppermute | solution.py:394
  59.3 2.5 %collective-permute-start.16 = (bf16[224,128]{1,0:T(8,128)(2,1)S(1)}, bf16[224,128]{1,0:T(8,128)(2,1)S(1)}, u32[]{:S(2)}, u32[]{:S(2)}) collective-permute-start(bf16[224,128]{1,0:T(8,128)(2,1)S(1)} %get-tuple-element.79), channel_id=1, source_target_pairs={{0,13},{1,12},{2,15},{3,14},{4,9},{5,8},{6,11},{7,10},{8,5},{9,4},... | collective-permute-start | bytes 172040 | tf_op jit(solution)/shard_map/ppermute | solution.py:394
  61.7 2.1 %head_gradient.2.refs_2_ = bf16[1792,1536]{1,0:T(8,128)(2,1)} custom-call(bf16[256,1792]{1,0:T(8,128)(2,1)S(1)} %pad_maximum_fusion.refs_0_, bf16[256,1536]{1,0:T(8,128)(2,1)S(1)} %pad_maximum_fusion.1.refs_1_), custom_call_target="tpu_custom_call" | custom-call | flops 805306368 | bytes 4849664 | tf_op jit(solution)/shard_map/head_gradient/pallas_call | solution.py:255
  63.8 0.0 collective-permute-done.13
  63.9 1.4 %collective-permute-done.16 = bf16[224,128]{1,0:T(8,128)(2,1)S(1)} collective-permute-done((bf16[224,128]{1,0:T(8,128)(2,1)S(1)}, bf16[224,128]{1,0:T(8,128)(2,1)S(1)}, u32[]{:S(2)}, u32[]{:S(2)}) %collective-permute-start.16) | collective-permute-done | bytes 57376 | tf_op jit(solution)/shard_map/ppermute | solution.py:394
  65.2 0.0 collective-permute-done.20
  65.2 0.1 broadcast_select_fusion.2
  65.3 2.6 %collective-permute-start.21 = (bf16[224,128]{1,0:T(8,128)(2,1)S(1)}, bf16[224,128]{1,0:T(8,128)(2,1)S(1)}, u32[]{:S(2)}, u32[]{:S(2)}) collective-permute-start(bf16[224,128]{1,0:T(8,128)(2,1)S(1)} %broadcast_select_fusion.2), channel_id=1, source_target_pairs={{0,16},{2,18},{4,20},{6,22},{8,24},{10,26},{12,28},{14,30},{16,0},... | collective-permute-start | bytes 172040 | tf_op jit(solution)/shard_map/ppermute | solution.py:425
  67.9 1.8 %head_gradient.3 = bf16[1792,1536]{1,0:T(8,128)(2,1)} custom-call(bf16[256,1792]{1,0:T(8,128)(2,1)S(1)} %pad_maximum_fusion.refs_0_, bf16[256,1536]{1,0:T(8,128)(2,1)S(1)} %pad_maximum_fusion.1.refs_1_, bf16[1792,1536]{1,0:T(8,128)(2,1)} %head_gradient.2.refs_2_), custom_call_target="tpu_custom_call", output_to_operand_aliasing={{}: (2, {})} | custom-call | flops 603979776 | bytes 4063232 | tf_op jit(solution)/shard_map/head_gradient/pallas_call | solution.py:255
  69.7 0.7 collective-permute-done.21
  70.4 0.7 add_bitcast_fusion
  (23 shorter events, 0.2 us)
Async XLA Ops:
  1.6 11.4 %collective-permute-start.2 = (bf16[32,1792]{1,0:T(8,128)(2,1)S(1)}, bf16[32,1792]{1,0:T(8,128)(2,1)S(1)}, u32[]{:S(2)}, u32[]{:S(2)}) collective-permute-start(bf16[32,1792]{1,0:T(8,128)(2,1)S(1)} %get-tuple-element.97), channel_id=1, source_target_pairs={{0,1},{1,0},{2,3},{3,2},{4,5},{5,4},{6,7},{7,6},{8,9},{9,8},{10,11... | collective-permute-start | bytes 344072 | tf_op jit(solution)/shard_map/ppermute | solution.py:19
  4.7 5.6 %collective-permute-start = (bf16[32,1792]{1,0:T(8,128)(2,1)S(1)}, bf16[32,1792]{1,0:T(8,128)(2,1)S(1)}, u32[]{:S(2)}, u32[]{:S(2)}) collective-permute-start(bf16[32,1792]{1,0:T(8,128)(2,1)S(1)} %get-tuple-element.98), channel_id=1, source_target_pairs={{0,1},{1,0},{2,3},{3,2},{4,5},{5,4},{6,7},{7,6},{8,9},{9,8},{10,11... | collective-permute-start | bytes 344072 | tf_op jit(solution)/shard_map/ppermute | solution.py:19
  8.1 6.4 %copy-start = (bf16[128,3584]{1,0:T(8,128)(2,1)S(1)}, bf16[128,3584]{1,0:T(8,128)(2,1)}, u32[]{:S(2)}) copy-start(bf16[128,3584]{1,0:T(8,128)(2,1)} %param.5) | copy-start | bytes 2752516
  11.3 11.7 %collective-permute-start.1 = (f32[32,1536]{1,0:T(8,128)S(1)}, f32[32,1536]{1,0:T(8,128)S(1)}, u32[]{:S(2)}, u32[]{:S(2)}) collective-permute-start(f32[32,1536]{1,0:T(8,128)S(1)} %fusion.18), channel_id=1, source_target_pairs={{0,1},{1,0},{2,3},{3,2},{4,5},{5,4},{6,7},{7,6},{8,9},{9,8},{10,11... | collective-permute-start | bytes 589832 | tf_op jit(solution)/shard_map/ppermute | solution.py:19
  14.1 1.3 %copy-start.2 = (s32[1,16]{1,0:T(1,128)S(1)}, s32[1,16]{1,0:T(1,128)}, u32[]{:S(2)}) copy-start(s32[1,16]{1,0:T(1,128)} %param.8) | copy-start | bytes 196
  14.1 1.5 %copy-start.1 = (bf16[128,1536]{1,0:T(8,128)(2,1)S(1)}, bf16[128,1536]{1,0:T(8,128)(2,1)}, u32[]{:S(2)}) copy-start(bf16[128,1536]{1,0:T(8,128)(2,1)} %param.7) | copy-start | bytes 1179652
  14.1 8.9 %collective-permute-start.3 = (f32[32,1536]{1,0:T(8,128)S(1)}, f32[32,1536]{1,0:T(8,128)S(1)}, u32[]{:S(2)}, u32[]{:S(2)}) collective-permute-start(f32[32,1536]{1,0:T(8,128)S(1)} %fusion.19), channel_id=1, source_target_pairs={{0,1},{1,0},{2,3},{3,2},{4,5},{5,4},{6,7},{7,6},{8,9},{9,8},{10,11... | collective-permute-start | bytes 589832 | tf_op jit(solution)/shard_map/ppermute | solution.py:19
  14.5 1.5 %collective-permute-start.4 = (bf16[64,1792]{1,0:T(8,128)(2,1)S(1)}, bf16[64,1792]{1,0:T(8,128)(2,1)S(1)}, u32[]{:S(2)}, u32[]{:S(2)}) collective-permute-start(bf16[64,1792]{1,0:T(8,128)(2,1)S(1)} %constant_dynamic-update-slice_fusion), channel_id=1, source_target_pairs={{0,2},{2,0},{4,6},{6,4},{8,10},{10,8},{12,14},{14,12},{16,18},{18,... | collective-permute-start | bytes 688136 | tf_op jit(solution)/shard_map/ppermute | solution.py:23
  17.0 13.0 %collective-permute-start.5 = (f32[64,1536]{1,0:T(8,128)S(1)}, f32[64,1536]{1,0:T(8,128)S(1)}, u32[]{:S(2)}, u32[]{:S(2)}) collective-permute-start(f32[64,1536]{1,0:T(8,128)S(1)} %fusion.20), channel_id=1, source_target_pairs={{0,1},{1,0},{2,3},{3,2},{4,5},{5,4},{6,7},{7,6},{8,9},{9,8},{10,11... | collective-permute-start | bytes 1179656 | tf_op jit(solution)/shard_map/ppermute | solution.py:19
  30.4 1.2 %collective-permute-start.6 = (f32[1,4,128]{2,1,0:T(4,128)S(1)}, f32[1,4,128]{2,1,0:T(4,128)S(1)}, u32[]{:S(2)}, u32[]{:S(2)}) collective-permute-start(f32[1,4,128]{2,1,0:T(4,128)S(1)} %bitcast.50), channel_id=1, source_target_pairs={{0,2},{2,0},{4,6},{6,4},{8,10},{10,8},{12,14},{14,12},{16,18},{18,... | collective-permute-start | bytes 6152 | tf_op jit(solution)/shard_map/ppermute | solution.py:23
  31.6 3.7 %collective-permute-start.9 = (f32[2,4,128]{2,1,0:T(4,128)S(1)}, f32[2,4,128]{2,1,0:T(4,128)S(1)}, u32[]{:S(2)}, u32[]{:S(2)}) collective-permute-start(f32[2,4,128]{2,1,0:T(4,128)S(1)} %pad_maximum_fusion.4), channel_id=1, source_target_pairs={{0,4},{2,6},{4,0},{6,2},{8,12},{10,14},{12,8},{14,10},{16,20},{18,... | collective-permute-start | bytes 12296 | tf_op jit(solution)/shard_map/ppermute | solution.py:23
  33.1 3.6 %collective-permute-start.8 = (f32[2,4,128]{2,1,0:T(4,128)S(1)}, f32[2,4,128]{2,1,0:T(4,128)S(1)}, u32[]{:S(2)}, u32[]{:S(2)}) collective-permute-start(f32[2,4,128]{2,1,0:T(4,128)S(1)} %pad_maximum_fusion.4), channel_id=1, source_target_pairs={{0,8},{2,10},{4,12},{6,14},{8,0},{10,2},{12,4},{14,6},{16,24},{18,... | collective-permute-start | bytes 12296 | tf_op jit(solution)/shard_map/ppermute | solution.py:23
  34.7 4.5 %collective-permute-start.7 = (f32[2,4,128]{2,1,0:T(4,128)S(1)}, f32[2,4,128]{2,1,0:T(4,128)S(1)}, u32[]{:S(2)}, u32[]{:S(2)}) collective-permute-start(f32[2,4,128]{2,1,0:T(4,128)S(1)} %pad_maximum_fusion.4), channel_id=1, source_target_pairs={{0,12},{2,14},{4,8},{6,10},{8,4},{10,6},{12,0},{14,2},{16,28},{18,... | collective-permute-start | bytes 12296 | tf_op jit(solution)/shard_map/ppermute | solution.py:23
  39.2 4.8 %collective-permute-start.10 = (f32[8,4,128]{2,1,0:T(4,128)S(1)}, f32[8,4,128]{2,1,0:T(4,128)S(1)}, u32[]{:S(2)}, u32[]{:S(2)}) collective-permute-start(f32[8,4,128]{2,1,0:T(4,128)S(1)} %pad_maximum_fusion.3), channel_id=1, source_target_pairs={{0,16},{2,18},{4,20},{6,22},{8,24},{10,26},{12,28},{14,30},{16,0},... | collective-permute-start | bytes 49160 | tf_op jit(solution)/shard_map/ppermute | solution.py:23
  44.8 8.3 %collective-permute-start.11 = (bf16[128,1536]{1,0:T(8,128)(2,1)S(1)}, bf16[128,1536]{1,0:T(8,128)(2,1)S(1)}, u32[]{:S(2)}, u32[]{:S(2)}) collective-permute-start(bf16[128,1536]{1,0:T(8,128)(2,1)S(1)} %get-tuple-element.74.delta_ref), channel_id=1, source_target_pairs={{0,1},{1,0},{2,3},{3,2},{4,5},{5,4},{6,7},{7,6},{8,9},{9,8},{10,11... | collective-permute-start | bytes 1179656 | tf_op jit(solution)/shard_map/ppermute | solution.py:19
  48.0 7.0 %collective-permute-start.19 = (bf16[2,224,128]{2,1,0:T(8,128)(2,1)S(1)}, bf16[2,224,128]{2,1,0:T(8,128)(2,1)S(1)}, u32[]{:S(2)}, u32[]{:S(2)}) collective-permute-start(bf16[2,224,128]{2,1,0:T(8,128)(2,1)S(1)} %get-tuple-element.94), channel_id=1, source_target_pairs={{0,12},{2,14},{4,8},{6,10},{8,4},{10,6},{12,0},{14,2},{16,28},{18,... | collective-permute-start | bytes 344072 | tf_op jit(solution)/shard_map/ppermute | solution.py:23
  48.4 6.6 %collective-permute-start.17 = (bf16[2,224,128]{2,1,0:T(8,128)(2,1)S(1)}, bf16[2,224,128]{2,1,0:T(8,128)(2,1)S(1)}, u32[]{:S(2)}, u32[]{:S(2)}) collective-permute-start(bf16[2,224,128]{2,1,0:T(8,128)(2,1)S(1)} %get-tuple-element.95), channel_id=1, source_target_pairs={{0,4},{2,6},{4,0},{6,2},{8,12},{10,14},{12,8},{14,10},{16,20},{18,... | collective-permute-start | bytes 344072 | tf_op jit(solution)/shard_map/ppermute | solution.py:23
  49.9 5.1 %collective-permute-start.18 = (bf16[2,224,128]{2,1,0:T(8,128)(2,1)S(1)}, bf16[2,224,128]{2,1,0:T(8,128)(2,1)S(1)}, u32[]{:S(2)}, u32[]{:S(2)}) collective-permute-start(bf16[2,224,128]{2,1,0:T(8,128)(2,1)S(1)} %get-tuple-element.96), channel_id=1, source_target_pairs={{0,8},{2,10},{4,12},{6,14},{8,0},{10,2},{12,4},{14,6},{16,24},{18,... | collective-permute-start | bytes 344072 | tf_op jit(solution)/shard_map/ppermute | solution.py:23
  54.0 1.7 %collective-permute-start.12 = (bf16[4,224,128]{2,1,0:T(8,128)(2,1)S(1)}, bf16[4,224,128]{2,1,0:T(8,128)(2,1)S(1)}, u32[]{:S(2)}, u32[]{:S(2)}) collective-permute-start(bf16[4,224,128]{2,1,0:T(8,128)(2,1)S(1)} %partial_gradient.3), channel_id=1, source_target_pairs={{0,2},{2,0},{4,6},{6,4},{8,10},{10,8},{12,14},{14,12},{16,18},{18,... | collective-permute-start | bytes 688136 | tf_op jit(solution)/shard_map/ppermute | solution.py:23
  55.1 10.1 %collective-permute-start.20 = (bf16[224,128]{1,0:T(8,128)(2,1)S(1)}, bf16[224,128]{1,0:T(8,128)(2,1)S(1)}, u32[]{:S(2)}, u32[]{:S(2)}) collective-permute-start(bf16[224,128]{1,0:T(8,128)(2,1)S(1)} %fusion.13), channel_id=1, source_target_pairs={{0,2},{2,0},{4,6},{6,4},{8,10},{10,8},{12,14},{14,12},{16,18},{18,... | collective-permute-start | bytes 172040 | tf_op jit(solution)/shard_map/ppermute | solution.py:23
  55.8 8.0 %collective-permute-start.13 = (bf16[224,128]{1,0:T(8,128)(2,1)S(1)}, bf16[224,128]{1,0:T(8,128)(2,1)S(1)}, u32[]{:S(2)}, u32[]{:S(2)}) collective-permute-start(bf16[224,128]{1,0:T(8,128)(2,1)S(1)} %get-tuple-element.76), channel_id=1, source_target_pairs={{0,1},{1,0},{2,3},{3,2},{4,5},{5,4},{6,7},{7,6},{8,9},{9,8},{10,11... | collective-permute-start | bytes 172040 | tf_op jit(solution)/shard_map/ppermute | solution.py:394
  57.4 6.4 %collective-permute-start.14 = (bf16[224,128]{1,0:T(8,128)(2,1)S(1)}, bf16[224,128]{1,0:T(8,128)(2,1)S(1)}, u32[]{:S(2)}, u32[]{:S(2)}) collective-permute-start(bf16[224,128]{1,0:T(8,128)(2,1)S(1)} %get-tuple-element.77), channel_id=1, source_target_pairs={{0,5},{1,4},{2,7},{3,6},{4,1},{5,0},{6,3},{7,2},{8,13},{9,12},{10,... | collective-permute-start | bytes 172040 | tf_op jit(solution)/shard_map/ppermute | solution.py:394
  58.0 5.9 %collective-permute-start.15 = (bf16[224,128]{1,0:T(8,128)(2,1)S(1)}, bf16[224,128]{1,0:T(8,128)(2,1)S(1)}, u32[]{:S(2)}, u32[]{:S(2)}) collective-permute-start(bf16[224,128]{1,0:T(8,128)(2,1)S(1)} %get-tuple-element.78), channel_id=1, source_target_pairs={{0,9},{1,8},{2,11},{3,10},{4,13},{5,12},{6,15},{7,14},{8,1},{9,0},... | collective-permute-start | bytes 172040 | tf_op jit(solution)/shard_map/ppermute | solution.py:394
  59.3 6.0 %collective-permute-start.16 = (bf16[224,128]{1,0:T(8,128)(2,1)S(1)}, bf16[224,128]{1,0:T(8,128)(2,1)S(1)}, u32[]{:S(2)}, u32[]{:S(2)}) collective-permute-start(bf16[224,128]{1,0:T(8,128)(2,1)S(1)} %get-tuple-element.79), channel_id=1, source_target_pairs={{0,13},{1,12},{2,15},{3,14},{4,9},{5,8},{6,11},{7,10},{8,5},{9,4},... | collective-permute-start | bytes 172040 | tf_op jit(solution)/shard_map/ppermute | solution.py:394
  65.3 5.1 %collective-permute-start.21 = (bf16[224,128]{1,0:T(8,128)(2,1)S(1)}, bf16[224,128]{1,0:T(8,128)(2,1)S(1)}, u32[]{:S(2)}, u32[]{:S(2)}) collective-permute-start(bf16[224,128]{1,0:T(8,128)(2,1)S(1)} %broadcast_select_fusion.2), channel_id=1, source_target_pairs={{0,16},{2,18},{4,20},{6,22},{8,24},{10,26},{12,28},{14,30},{16,0},... | collective-permute-start | bytes 172040 | tf_op jit(solution)/shard_map/ppermute | solution.py:425
